TPU v7x, 32 devices: a whole 2x2x4 slice. The times are simulated.
32 devices in a mesh: seq: 16 (over z, x, core), tp: 2 (over y).
Axes of the slice: x: 2, y: 2, z: 4, core: 2. Of those that a mesh axis runs over, the one named last changes fastest.
Arguments:
- queries: bfloat16 [4096, 4096], P(('seq', 'tp')), may hold values from -6 to 6
- key_states: bfloat16 [4096, 2048], P(('seq', 'tp')), may hold values from -6 to 6
- value_state_rows: bfloat16 [4096, 2048], P(('seq', 'tp')), may hold values from -6 to 6
- out_grad: bfloat16 [4096, 4096], P(('seq', 'tp')), may hold values from -6 to 6
- doc_lengths: int32 [4], replicated, may hold values from 1 to 2048, 4096 in all
Outputs:
- query_grad: bfloat16 [4096, 4096], P(('seq', 'tp'))
- key_gradient: bfloat16 [4096, 2048], P(('seq', 'tp'))
- value_gradient: bfloat16 [4096, 2048], P(('seq', 'tp'))
Inputs may be any that keep to these rules, and one draw needn't show every extreme that they name: `doc_lengths`: the documents lie one after another from position 0 and fill all 4096 positions; the longest has exactly 2048 tokens.
All inputs are finite; a program needn't handle non-finite values.
Results may differ from a plain program's by a relative error of at most 0.013.
Values may be sent and summed in bfloat16 or wider, within the bound.
No kernel may reach another device: no remote copies, remote signals or barrier semaphores. Data moves between devices by JAX's collectives and lax.ppermute only.
A program may use at most 64 MiB of HBM per device.

v0:
```python
import jax
import jax.numpy as jnp
from jax import lax
from jax.sharding import PartitionSpec as P

QUERY_HEADS = 32
KEY_HEADS = 16
HEAD_SIZE = 128
WINDOW = 1024


attn_scale = 168.0 ** (-0.5)
masked_floor = -1e30


def passed_along(value, axis, steps):
    count = lax.axis_size(axis)
    initial, last = (max(0, -steps), min(count, count - steps))
    return lax.ppermute(value, axis, [(source, source + steps) for source in range(initial, last)])


def run_stretch(stretch_index, work):
    if stretch_index == 0:
        return work()
    return work()


def per_device(queries, key_states, value_state_rows, out_grad, doc_lengths):
    query_matrix, key_matrix, value_matrix, grad_all = (
        lax.all_to_all(queries, "tp", split_axis=1, concat_axis=0, tiled=True),
        lax.all_to_all(key_states, "tp", split_axis=1, concat_axis=0, tiled=True),
        lax.all_to_all(value_state_rows, "tp", split_axis=1, concat_axis=0, tiled=True),
        lax.all_to_all(out_grad, "tp", split_axis=1, concat_axis=0, tiled=True),
    )
    stretch_rows = query_matrix.shape[0]
    kv_local = key_matrix.shape[1] // HEAD_SIZE
    group_width = QUERY_HEADS // KEY_HEADS
    halo_count = WINDOW // stretch_rows
    stretch_first = lax.axis_index("seq") * stretch_rows
    starts_arr = jnp.cumsum(doc_lengths) - doc_lengths

    def doc_of(positions):
        counted = jnp.sum((starts_arr[None, :] <= positions[:, None]).astype(jnp.int32), axis=1)
        return counted - 1

    offsets = jnp.arange(stretch_rows, dtype=jnp.int32)
    query_pos = stretch_first + offsets
    query_doc = doc_of(query_pos)
    query_four = query_matrix.reshape(stretch_rows, kv_local, group_width, HEAD_SIZE)
    grad_four = grad_all.reshape(stretch_rows, kv_local, group_width, HEAD_SIZE)
    kv_pair = jnp.stack([key_matrix, value_matrix])
    stretches = [kv_pair]
    for distance in range(1, halo_count + 1):
        stretches.append(passed_along(kv_pair, "seq", distance))

    def visible(stretch_index):
        key_pos = stretch_first - stretch_index * stretch_rows + offsets
        allowed = (key_pos[None, :] <= query_pos[:, None]) & (
            query_pos[:, None] - key_pos[None, :] < WINDOW
        )
        allowed = allowed & (key_pos[None, :] >= 0)
        allowed = allowed & (doc_of(key_pos)[None, :] == query_doc[:, None])
        return allowed[None, None, :, :]

    def split_pair(pair):
        return (
            pair[0].reshape(stretch_rows, kv_local, HEAD_SIZE),
            pair[1].reshape(stretch_rows, kv_local, HEAD_SIZE),
        )

    def scores_of(key_tile):
        return (
            jnp.einsum("qgrd,kgd->grqk", query_four, key_tile, preferred_element_type=jnp.float32)
            * attn_scale
        )

    stat_shape = (kv_local, group_width, stretch_rows)
    maxima = []
    totals = []
    for stretch_index in range(halo_count + 1):

        def stats_work(pair=stretches[stretch_index], stretch_index=stretch_index):
            key_tile, value_tile = split_pair(pair)
            allowed = visible(stretch_index)
            raw_scores = scores_of(key_tile)
            row_max = jnp.max(jnp.where(allowed, raw_scores, masked_floor), axis=-1)
            row_sum = jnp.sum(
                jnp.where(allowed, jnp.exp(raw_scores - row_max[..., None]), 0.0), axis=-1
            )
            return (row_max, row_sum)

        row_max, row_sum = run_stretch(stretch_index, stats_work)
        maxima.append(row_max)
        totals.append(row_sum)
    peak_max = maxima[0]
    for row_max in maxima[1:]:
        peak_max = jnp.maximum(peak_max, row_max)
    norm_sum = jnp.zeros(stat_shape, jnp.float32)
    for row_max, row_sum in zip(maxima, totals):
        norm_sum = norm_sum + row_sum * jnp.exp(row_max - peak_max)
    log_total = peak_max + jnp.log(norm_sum)

    def probs_of(raw_scores, allowed):
        return jnp.where(allowed, jnp.exp(raw_scores - log_total[..., None]), 0.0)

    out_shape = (stretch_rows, kv_local, group_width, HEAD_SIZE)
    attn_out = jnp.zeros(out_shape, jnp.float32)
    for stretch_index in range(halo_count + 1):

        def output_work(pair=stretches[stretch_index], stretch_index=stretch_index):
            key_tile, value_tile = split_pair(pair)
            probs_bf = probs_of(scores_of(key_tile), visible(stretch_index)).astype(jnp.bfloat16)
            return jnp.einsum(
                "grqk,kgd->qgrd", probs_bf, value_tile, preferred_element_type=jnp.float32
            )

        attn_out = attn_out + run_stretch(stretch_index, output_work)
    delta_rows = jnp.transpose(
        jnp.sum(grad_four.astype(jnp.float32) * attn_out, axis=-1), (1, 2, 0)
    )
    query_sum = jnp.zeros(out_shape, jnp.float32)
    terms = []
    for stretch_index in range(halo_count + 1):

        def grad_work(pair=stretches[stretch_index], stretch_index=stretch_index):
            key_tile, value_tile = split_pair(pair)
            probs = probs_of(scores_of(key_tile), visible(stretch_index))
            probs_bf = probs.astype(jnp.bfloat16)
            prob_grad = jnp.einsum(
                "qgrd,kgd->grqk", grad_four, value_tile, preferred_element_type=jnp.float32
            )
            grad_scores = (probs * (prob_grad - delta_rows[..., None]) * attn_scale).astype(
                jnp.bfloat16
            )
            query_part = jnp.einsum(
                "grqk,kgd->qgrd", grad_scores, key_tile, preferred_element_type=jnp.float32
            )
            key_part = jnp.einsum(
                "grqk,qgrd->kgd", grad_scores, query_four, preferred_element_type=jnp.float32
            )
            value_part = jnp.einsum(
                "grqk,qgrd->kgd", probs_bf, grad_four, preferred_element_type=jnp.float32
            )
            stacked = jnp.stack(
                [
                    key_part.reshape(stretch_rows, kv_local * HEAD_SIZE),
                    value_part.reshape(stretch_rows, kv_local * HEAD_SIZE),
                ]
            )
            return (query_part, stacked)

        query_part, stacked = run_stretch(stretch_index, grad_work)
        query_sum = query_sum + query_part
        terms.append(stacked)
    carried = terms[halo_count]
    for distance in range(halo_count - 1, -1, -1):
        carried = passed_along(carried, "seq", -1) + terms[distance]
    query_grad = query_sum.reshape(stretch_rows, kv_local * group_width * HEAD_SIZE).astype(
        jnp.bfloat16
    )
    key_gradient = carried[0].astype(jnp.bfloat16)
    value_gradient = carried[1].astype(jnp.bfloat16)
    return (
        lax.all_to_all(query_grad, "tp", split_axis=0, concat_axis=1, tiled=True),
        lax.all_to_all(key_gradient, "tp", split_axis=0, concat_axis=1, tiled=True),
        lax.all_to_all(value_gradient, "tp", split_axis=0, concat_axis=1, tiled=True),
    )


def solution(mesh):
    return jax.shard_map(
        per_device,
        mesh=mesh,
        in_specs=(
            P(("seq", "tp"), None),
            P(("seq", "tp"), None),
            P(("seq", "tp"), None),
            P(("seq", "tp"), None),
            P(),
        ),
        out_specs=(P(("seq", "tp"), None), P(("seq", "tp"), None), P(("seq", "tp"), None)),
        check_vma=False,
    )
```

profile of v0, /device:TPU:24, one launch (start us, length us, event | category | flops | bytes accessed | tf_op | source)
XLA Modules:
  0.0 266.3 jit_solution(3894638889041781022)
XLA Ops:
  0.6 2.0 copy.701
  2.6 3.5 %all-to-all-start = ((bf16[128,2,1024]{2,0,1:T(8,128)(2,1)}), bf16[128,2,1024]{2,0,1:T(8,128)(2,1)S(1)}, u32[]{:S(2)}, u32[]{:S(2)}) async-start(bf16[128,2,1024]{2,0,1:T(8,128)(2,1)} %bitcast.409), calls=%async_computation | async-start | bytes 1048576 | tf_op jit(solution)/shard_map/all_to_all | solution.py:31
  7.7 1.9 copy.700
  9.6 4.7 %all-to-all-done = bf16[128,2,1024]{2,0,1:T(8,128)(2,1)S(1)} async-done(((bf16[128,2,1024]{2,0,1:T(8,128)(2,1)}), bf16[128,2,1024]{2,0,1:T(8,128)(2,1)S(1)}, u32[]{:S(2)}, u32[]{:S(2)}) %all-to-all-start) | async-done | bytes 524320 | tf_op jit(solution)/shard_map/all_to_all | solution.py:31
  14.3 3.5 %all-to-all-start.2 = ((bf16[128,2,1024]{2,0,1:T(8,128)(2,1)}), bf16[128,2,1024]{2,0,1:T(8,128)(2,1)S(1)}, u32[]{:S(2)}, u32[]{:S(2)}) async-start(bf16[128,2,1024]{2,0,1:T(8,128)(2,1)} %bitcast.408), calls=%async_computation.2 | async-start | bytes 1048576 | tf_op jit(solution)/shard_map/all_to_all | solution.py:32
  17.9 1.1 copy.699
  18.9 6.2 %all-to-all-done.2 = bf16[128,2,1024]{2,0,1:T(8,128)(2,1)S(1)} async-done(((bf16[128,2,1024]{2,0,1:T(8,128)(2,1)}), bf16[128,2,1024]{2,0,1:T(8,128)(2,1)S(1)}, u32[]{:S(2)}, u32[]{:S(2)}) %all-to-all-start.2) | async-done | bytes 524320 | tf_op jit(solution)/shard_map/all_to_all | solution.py:32
  25.2 3.6 %all-to-all-start.1 = ((bf16[128,2,2048]{2,0,1:T(8,128)(2,1)}), bf16[128,2,2048]{2,0,1:T(8,128)(2,1)S(1)}, u32[]{:S(2)}, u32[]{:S(2)}) async-start(bf16[128,2,2048]{2,0,1:T(8,128)(2,1)} %bitcast.426), calls=%async_computation.1 | async-start | bytes 2097152 | tf_op jit(solution)/shard_map/all_to_all | solution.py:30
  28.8 2.3 copy.698
  31.6 1.1 pad_maximum_fusion.1
  32.6 3.4 %collective-permute-start.1 = (bf16[2,256,1024]{1,2,0:T(8,128)(2,1)}, bf16[2,256,1024]{1,2,0:T(8,128)(2,1)}, u32[]{:S(2)}, u32[]{:S(2)}) collective-permute-start(bf16[2,256,1024]{1,2,0:T(8,128)(2,1)} %pad_maximum_fusion.1), channel_id=1, source_target_pairs={{0,4},{2,6},{4,8},{6,10},{8,12},{10,14},{12,16},{14,18},{16,20},{1... | collective-permute-start | bytes 3145736 | tf_op jit(solution)/shard_map/ppermute | solution.py:19
  36.0 4.8 %all-to-all-done.1 = bf16[128,2,2048]{2,0,1:T(8,128)(2,1)S(1)} async-done(((bf16[128,2,2048]{2,0,1:T(8,128)(2,1)}), bf16[128,2,2048]{2,0,1:T(8,128)(2,1)S(1)}, u32[]{:S(2)}, u32[]{:S(2)}) %all-to-all-start.1) | async-done | bytes 1048608 | tf_op jit(solution)/shard_map/all_to_all | solution.py:30
  40.8 4.4 %all-to-all-start.3 = ((bf16[128,2,2048]{2,0,1:T(8,128)(2,1)}), bf16[128,2,2048]{2,0,1:T(8,128)(2,1)}, u32[]{:S(2)}, u32[]{:S(2)}) async-start(bf16[128,2,2048]{2,0,1:T(8,128)(2,1)} %bitcast.425), calls=%async_computation.3 | async-start | bytes 2097152 | tf_op jit(solution)/shard_map/all_to_all | solution.py:33
  46.0 1.9 collective-permute-start
  48.0 1.9 collective-permute-start.2
  49.9 1.3 collective-permute-start.3
  51.4 1.1 copy.579
  52.5 1.5 reshape.699
  54.1 2.4 copy.546
  56.5 2.8 %fusion.39 = (f32[8,2,256]{2,1,0:T(2,128)S(1)}, f32[8,256,256,2]{2,1,3,0:T(8,128)}) fusion(pred[256,256]{0,1:T(8,128)(4,1)S(1)} %get-tuple-element.36, bf16[256,8,2,128]{0,3,2,1:T(8,128)(2,1)S(1)} %copy.546, bf16[256,8,128,1]{2,1,0,3:T(8,128)(2,1)S(1)} %bitcast.410), kind=kOutput, calls=%fused_computation.59 | convolution fusion | flops 271577088 | bytes 5849088 | tf_op jit(solution)/shard_map/qgrd,kgd->grqk/dot_general | solution.py:73
  59.3 1.8 reshape.700
  61.1 1.2 copy.518
  62.3 3.4 %fusion.42 = f32[8,2,256]{2,1,0:T(2,128)S(1)} fusion(f32[8,256,256,2]{2,1,3,0:T(8,128)} %get-tuple-element.50, f32[8,2,256]{2,1,0:T(2,128)S(1)} %get-tuple-element.49, pred[256,256]{0,1:T(8,128)(4,1)S(1)} %get-tuple-element.36), kind=kLoop, calls=%fused_computation.62 | loop fusion | flops 4190208 | bytes 4292608 | tf_op jit(solution)/shard_map/reduce_sum | solution.py:87
  65.8 1.3 fusion.121
  67.9 10.4 %collective-permute-done = bf16[2,256,1024]{1,2,0:T(8,128)(2,1)} collective-permute-done((bf16[2,256,1024]{1,2,0:T(8,128)(2,1)}, bf16[2,256,1024]{1,2,0:T(8,128)(2,1)}, u32[]{:S(2)}, u32[]{:S(2)}) %collective-permute-start) | collective-permute-done | bytes 1048608 | tf_op jit(solution)/shard_map/ppermute | solution.py:19
  78.3 1.3 fusion.120
  81.4 1.3 fusion.122
  85.3 1.3 fusion.119
  92.8 2.1 fusion.79
  94.9 1.5 fusion.53
  96.4 1.6 fusion.2
  99.4 31.5 %collective-permute-start.4 = (f32[2,256,1024]{1,2,0:T(8,128)S(1)}, f32[2,256,1024]{1,2,0:T(8,128)S(1)}, u32[]{:S(2)}, u32[]{:S(2)}) collective-permute-start(f32[2,256,1024]{1,2,0:T(8,128)S(1)} %pad_maximum_fusion), channel_id=1, source_target_pairs={{2,0},{4,2},{6,4},{8,6},{10,8},{12,10},{14,12},{16,14},{18,16},{20... | collective-permute-start | bytes 6291464 | tf_op jit(solution)/shard_map/ppermute | solution.py:19
  130.9 1.6 fusion.5
  133.3 1.0 fusion.82
  134.3 20.1 %collective-permute-done.4 = f32[2,256,1024]{1,2,0:T(8,128)S(1)} collective-permute-done((f32[2,256,1024]{1,2,0:T(8,128)S(1)}, f32[2,256,1024]{1,2,0:T(8,128)S(1)}, u32[]{:S(2)}, u32[]{:S(2)}) %collective-permute-start.4) | collective-permute-done | bytes 2097184 | tf_op jit(solution)/shard_map/ppermute | solution.py:19
  154.7 4.7 %collective-permute-start.5 = (f32[2,256,1024]{1,2,0:T(8,128)S(1)}, f32[2,256,1024]{1,2,0:T(8,128)S(1)}, u32[]{:S(2)}, u32[]{:S(2)}) collective-permute-start(f32[2,256,1024]{1,2,0:T(8,128)S(1)} %maximum_add_fusion), channel_id=1, source_target_pairs={{2,0},{4,2},{6,4},{8,6},{10,8},{12,10},{14,12},{16,14},{18,16},{20... | collective-permute-start | bytes 6291464 | tf_op jit(solution)/shard_map/ppermute | solution.py:19
  159.4 1.6 fusion.8
  161.8 1.0 fusion.86
  162.8 20.1 %collective-permute-done.5 = f32[2,256,1024]{1,2,0:T(8,128)S(1)} collective-permute-done((f32[2,256,1024]{1,2,0:T(8,128)S(1)}, f32[2,256,1024]{1,2,0:T(8,128)S(1)}, u32[]{:S(2)}, u32[]{:S(2)}) %collective-permute-start.5) | collective-permute-done | bytes 2097184 | tf_op jit(solution)/shard_map/ppermute | solution.py:19
  183.3 5.0 %collective-permute-start.6 = (f32[2,256,1024]{1,2,0:T(8,128)S(1)}, f32[2,256,1024]{1,2,0:T(8,128)S(1)}, u32[]{:S(2)}, u32[]{:S(2)}) collective-permute-start(f32[2,256,1024]{1,2,0:T(8,128)S(1)} %maximum_add_fusion.1), channel_id=1, source_target_pairs={{2,0},{4,2},{6,4},{8,6},{10,8},{12,10},{14,12},{16,14},{18,16},{20... | collective-permute-start | bytes 6291464 | tf_op jit(solution)/shard_map/ppermute | solution.py:19
  188.2 1.6 fusion.11
  193.2 1.0 fusion.90
  194.2 17.3 %collective-permute-done.6 = f32[2,256,1024]{1,2,0:T(8,128)S(1)} collective-permute-done((f32[2,256,1024]{1,2,0:T(8,128)S(1)}, f32[2,256,1024]{1,2,0:T(8,128)S(1)}, u32[]{:S(2)}, u32[]{:S(2)}) %collective-permute-start.6) | collective-permute-done | bytes 2097184 | tf_op jit(solution)/shard_map/ppermute | solution.py:19
  211.5 1.6 maximum_add_fusion.2
  213.1 4.8 %collective-permute-start.7 = (f32[2,256,1024]{1,2,0:T(8,128)}, f32[2,256,1024]{1,2,0:T(8,128)}, u32[]{:S(2)}, u32[]{:S(2)}) collective-permute-start(f32[2,256,1024]{1,2,0:T(8,128)} %maximum_add_fusion.2), channel_id=1, source_target_pairs={{2,0},{4,2},{6,4},{8,6},{10,8},{12,10},{14,12},{16,14},{18,16},{20... | collective-permute-start | bytes 6291464 | tf_op jit(solution)/shard_map/ppermute | solution.py:19
  218.0 1.6 fusion.14
  220.4 1.1 fusion.51
  221.5 2.0 copy.543
  223.6 2.6 convert_element_type.98
  226.2 4.9 %all-to-all-start.4 = ((bf16[2,128,2048]{2,1,0:T(8,128)(2,1)}), bf16[2,128,2048]{2,1,0:T(8,128)(2,1)}, u32[]{:S(2)}, u32[]{:S(2)}) async-start(bf16[2,128,2048]{2,1,0:T(8,128)(2,1)} %convert_element_type.98), calls=%async_computation.4 | async-start | bytes 2097152 | tf_op jit(solution)/shard_map/all_to_all | solution.py:164
  231.9 1.4 copy-done.1
  233.3 2.2 fusion.94
  235.5 6.3 %collective-permute-done.7 = f32[2,256,1024]{1,2,0:T(8,128)} collective-permute-done((f32[2,256,1024]{1,2,0:T(8,128)}, f32[2,256,1024]{1,2,0:T(8,128)}, u32[]{:S(2)}, u32[]{:S(2)}) %collective-permute-start.7) | collective-permute-done | bytes 2097184 | tf_op jit(solution)/shard_map/ppermute | solution.py:19
  241.8 1.9 fusion.50
  243.8 1.0 copy.565
  244.8 3.5 %all-to-all-start.5 = ((bf16[2,128,1024]{2,1,0:T(8,128)(2,1)}), bf16[2,128,1024]{2,1,0:T(8,128)(2,1)S(1)}, u32[]{:S(2)}, u32[]{:S(2)}) async-start(bf16[2,128,1024]{2,1,0:T(8,128)(2,1)} %bitcast.107), calls=%async_computation.5 | async-start | bytes 1048576 | tf_op jit(solution)/shard_map/all_to_all | solution.py:165
  248.3 1.0 copy.567
  249.3 5.6 %all-to-all-done.5 = bf16[2,128,1024]{2,1,0:T(8,128)(2,1)S(1)} async-done(((bf16[2,128,1024]{2,1,0:T(8,128)(2,1)}), bf16[2,128,1024]{2,1,0:T(8,128)(2,1)S(1)}, u32[]{:S(2)}, u32[]{:S(2)}) %all-to-all-start.5) | async-done | bytes 524320 | tf_op jit(solution)/shard_map/all_to_all | solution.py:165
  254.8 3.5 %all-to-all-start.6 = ((bf16[2,128,1024]{2,1,0:T(8,128)(2,1)}), bf16[2,128,1024]{2,1,0:T(8,128)(2,1)S(1)}, u32[]{:S(2)}, u32[]{:S(2)}) async-start(bf16[2,128,1024]{2,1,0:T(8,128)(2,1)} %bitcast.110), calls=%async_computation.6 | async-start | bytes 1048576 | tf_op jit(solution)/shard_map/all_to_all | solution.py:166
  258.3 1.6 copy.544
  260.0 1.3 copy.569
  261.5 1.0 copy.570
  262.6 2.3 all-to-all-done.6
  265.2 1.0 copy.571
  (74 shorter events, 23.6 us)
Async XLA Ops:
  0.6 17.2 %copy-start.9 = (bf16[128,4096]{1,0:T(8,128)(2,1)S(1)}, bf16[128,4096]{1,0:T(8,128)(2,1)}, u32[]{:S(2)}) copy-start(bf16[128,4096]{1,0:T(8,128)(2,1)} %param.5) | copy-start | bytes 3145732
  2.6 11.7 %all-to-all-start = ((bf16[128,2,1024]{2,0,1:T(8,128)(2,1)}), bf16[128,2,1024]{2,0,1:T(8,128)(2,1)S(1)}, u32[]{:S(2)}, u32[]{:S(2)}) async-start(bf16[128,2,1024]{2,0,1:T(8,128)(2,1)} %bitcast.409), calls=%async_computation | async-start | bytes 1048576 | tf_op jit(solution)/shard_map/all_to_all | solution.py:31
  14.3 10.9 %all-to-all-start.2 = ((bf16[128,2,1024]{2,0,1:T(8,128)(2,1)}), bf16[128,2,1024]{2,0,1:T(8,128)(2,1)S(1)}, u32[]{:S(2)}, u32[]{:S(2)}) async-start(bf16[128,2,1024]{2,0,1:T(8,128)(2,1)} %bitcast.408), calls=%async_computation.2 | async-start | bytes 1048576 | tf_op jit(solution)/shard_map/all_to_all | solution.py:32
  25.2 15.6 %all-to-all-start.1 = ((bf16[128,2,2048]{2,0,1:T(8,128)(2,1)}), bf16[128,2,2048]{2,0,1:T(8,128)(2,1)S(1)}, u32[]{:S(2)}, u32[]{:S(2)}) async-start(bf16[128,2,2048]{2,0,1:T(8,128)(2,1)} %bitcast.426), calls=%async_computation.1 | async-start | bytes 2097152 | tf_op jit(solution)/shard_map/all_to_all | solution.py:30
  32.6 33.1 %collective-permute-start.1 = (bf16[2,256,1024]{1,2,0:T(8,128)(2,1)}, bf16[2,256,1024]{1,2,0:T(8,128)(2,1)}, u32[]{:S(2)}, u32[]{:S(2)}) collective-permute-start(bf16[2,256,1024]{1,2,0:T(8,128)(2,1)} %pad_maximum_fusion.1), channel_id=1, source_target_pairs={{0,4},{2,6},{4,8},{6,10},{8,12},{10,14},{12,16},{14,18},{16,20},{1... | collective-permute-start | bytes 3145736 | tf_op jit(solution)/shard_map/ppermute | solution.py:19
  40.8 18.4 %all-to-all-start.3 = ((bf16[128,2,2048]{2,0,1:T(8,128)(2,1)}), bf16[128,2,2048]{2,0,1:T(8,128)(2,1)}, u32[]{:S(2)}, u32[]{:S(2)}) async-start(bf16[128,2,2048]{2,0,1:T(8,128)(2,1)} %bitcast.425), calls=%async_computation.3 | async-start | bytes 2097152 | tf_op jit(solution)/shard_map/all_to_all | solution.py:33
  46.0 32.3 %collective-permute-start = (bf16[2,256,1024]{1,2,0:T(8,128)(2,1)}, bf16[2,256,1024]{1,2,0:T(8,128)(2,1)}, u32[]{:S(2)}, u32[]{:S(2)}) collective-permute-start(bf16[2,256,1024]{1,2,0:T(8,128)(2,1)} %pad_maximum_fusion.1), channel_id=1, source_target_pairs={{0,2},{2,4},{4,6},{6,8},{8,10},{10,12},{12,14},{14,16},{16,18},{18... | collective-permute-start | bytes 3145736 | tf_op jit(solution)/shard_map/ppermute | solution.py:19
  48.0 33.4 %collective-permute-start.2 = (bf16[2,256,1024]{1,2,0:T(8,128)(2,1)}, bf16[2,256,1024]{1,2,0:T(8,128)(2,1)}, u32[]{:S(2)}, u32[]{:S(2)}) collective-permute-start(bf16[2,256,1024]{1,2,0:T(8,128)(2,1)} %pad_maximum_fusion.1), channel_id=1, source_target_pairs={{0,6},{2,8},{4,10},{6,12},{8,14},{10,16},{12,18},{14,20},{16,22},{... | collective-permute-start | bytes 3145736 | tf_op jit(solution)/shard_map/ppermute | solution.py:19
  49.9 35.4 %collective-permute-start.3 = (bf16[2,256,1024]{1,2,0:T(8,128)(2,1)}, bf16[2,256,1024]{1,2,0:T(8,128)(2,1)}, u32[]{:S(2)}, u32[]{:S(2)}) collective-permute-start(bf16[2,256,1024]{1,2,0:T(8,128)(2,1)} %pad_maximum_fusion.1), channel_id=1, source_target_pairs={{0,8},{2,10},{4,12},{6,14},{8,16},{10,18},{12,20},{14,22},{16,24},... | collective-permute-start | bytes 3145736 | tf_op jit(solution)/shard_map/ppermute | solution.py:19
  51.3 8.0 %copy-start.2 = (bf16[32,8,8,128]{3,2,1,0:T(8,128)(2,1)}, bf16[32,8,8,128]{3,2,1,0:T(8,128)(2,1)S(1)}, u32[]{:S(2)}) copy-start(bf16[32,8,8,128]{3,2,1,0:T(8,128)(2,1)S(1)} %copy.656) | copy-start | bytes 1572868
  62.3 130.9 %copy-start.4 = (bf16[256,8,2,128]{0,3,2,1:T(8,128)(2,1)}, bf16[256,8,2,128]{0,3,2,1:T(8,128)(2,1)S(1)}, u32[]{:S(2)}) copy-start(bf16[256,8,2,128]{0,3,2,1:T(8,128)(2,1)S(1)} %copy.518) | copy-start | bytes 3145732
  82.6 9.2 %copy-start.7 = (bf16[1,256,1024]{1,2,0:T(8,128)(2,1)}, bf16[1,256,1024]{1,2,0:T(8,128)(2,1)S(1)}, u32[]{:S(2)}) copy-start(bf16[1,256,1024]{1,2,0:T(8,128)(2,1)S(1)} %get-tuple-element.34) | copy-start | bytes 1572868
  86.6 2.2 copy-start
  86.6 2.3 copy-start.6
  98.0 1.2 copy-start.10
  98.0 32.9 %copy-start.8 = (bf16[1,256,1024]{1,2,0:T(8,128)(2,1)S(1)}, bf16[1,256,1024]{1,2,0:T(8,128)(2,1)}, u32[]{:S(2)}) copy-start(bf16[1,256,1024]{1,2,0:T(8,128)(2,1)} %copy-done.7) | copy-start | bytes 1572868
  99.4 55.0 %collective-permute-start.4 = (f32[2,256,1024]{1,2,0:T(8,128)S(1)}, f32[2,256,1024]{1,2,0:T(8,128)S(1)}, u32[]{:S(2)}, u32[]{:S(2)}) collective-permute-start(f32[2,256,1024]{1,2,0:T(8,128)S(1)} %pad_maximum_fusion), channel_id=1, source_target_pairs={{2,0},{4,2},{6,4},{8,6},{10,8},{12,10},{14,12},{16,14},{18,16},{20... | collective-permute-start | bytes 6291464 | tf_op jit(solution)/shard_map/ppermute | solution.py:19
  154.7 28.3 %collective-permute-start.5 = (f32[2,256,1024]{1,2,0:T(8,128)S(1)}, f32[2,256,1024]{1,2,0:T(8,128)S(1)}, u32[]{:S(2)}, u32[]{:S(2)}) collective-permute-start(f32[2,256,1024]{1,2,0:T(8,128)S(1)} %maximum_add_fusion), channel_id=1, source_target_pairs={{2,0},{4,2},{6,4},{8,6},{10,8},{12,10},{14,12},{16,14},{18,16},{20... | collective-permute-start | bytes 6291464 | tf_op jit(solution)/shard_map/ppermute | solution.py:19
  183.3 28.3 %collective-permute-start.6 = (f32[2,256,1024]{1,2,0:T(8,128)S(1)}, f32[2,256,1024]{1,2,0:T(8,128)S(1)}, u32[]{:S(2)}, u32[]{:S(2)}) collective-permute-start(f32[2,256,1024]{1,2,0:T(8,128)S(1)} %maximum_add_fusion.1), channel_id=1, source_target_pairs={{2,0},{4,2},{6,4},{8,6},{10,8},{12,10},{14,12},{16,14},{18,16},{20... | collective-permute-start | bytes 6291464 | tf_op jit(solution)/shard_map/ppermute | solution.py:19
  194.2 23.7 %copy-start.5 = (bf16[256,8,2,128]{0,3,2,1:T(8,128)(2,1)S(1)}, bf16[256,8,2,128]{0,3,2,1:T(8,128)(2,1)}, u32[]{:S(2)}) copy-start(bf16[256,8,2,128]{0,3,2,1:T(8,128)(2,1)} %copy-done.4) | copy-start | bytes 3145732
  213.1 6.5 %copy-start.3 = (bf16[32,8,8,128]{3,2,1,0:T(8,128)(2,1)S(1)}, bf16[32,8,8,128]{3,2,1,0:T(8,128)(2,1)}, u32[]{:S(2)}) copy-start(bf16[32,8,8,128]{3,2,1,0:T(8,128)(2,1)} %copy-done.2) | copy-start | bytes 1572868
  213.1 28.7 %collective-permute-start.7 = (f32[2,256,1024]{1,2,0:T(8,128)}, f32[2,256,1024]{1,2,0:T(8,128)}, u32[]{:S(2)}, u32[]{:S(2)}) collective-permute-start(f32[2,256,1024]{1,2,0:T(8,128)} %maximum_add_fusion.2), channel_id=1, source_target_pairs={{2,0},{4,2},{6,4},{8,6},{10,8},{12,10},{14,12},{16,14},{18,16},{20... | collective-permute-start | bytes 6291464 | tf_op jit(solution)/shard_map/ppermute | solution.py:19
  226.2 18.6 %all-to-all-start.4 = ((bf16[2,128,2048]{2,1,0:T(8,128)(2,1)}), bf16[2,128,2048]{2,1,0:T(8,128)(2,1)}, u32[]{:S(2)}, u32[]{:S(2)}) async-start(bf16[2,128,2048]{2,1,0:T(8,128)(2,1)} %convert_element_type.98), calls=%async_computation.4 | async-start | bytes 2097152 | tf_op jit(solution)/shard_map/all_to_all | solution.py:164
  231.1 2.2 copy-start.1
  244.8 10.1 %all-to-all-start.5 = ((bf16[2,128,1024]{2,1,0:T(8,128)(2,1)}), bf16[2,128,1024]{2,1,0:T(8,128)(2,1)S(1)}, u32[]{:S(2)}, u32[]{:S(2)}) async-start(bf16[2,128,1024]{2,1,0:T(8,128)(2,1)} %bitcast.107), calls=%async_computation.5 | async-start | bytes 1048576 | tf_op jit(solution)/shard_map/all_to_all | solution.py:165
  254.8 10.1 %all-to-all-start.6 = ((bf16[2,128,1024]{2,1,0:T(8,128)(2,1)}), bf16[2,128,1024]{2,1,0:T(8,128)(2,1)S(1)}, u32[]{:S(2)}, u32[]{:S(2)}) async-start(bf16[2,128,1024]{2,1,0:T(8,128)(2,1)} %bitcast.110), calls=%async_computation.6 | async-start | bytes 1048576 | tf_op jit(solution)/shard_map/all_to_all | solution.py:166
where the time goes:
time: 271 us; the launch traced here: 266 us
  waiting for transfers between devices  97.9 us (36%)
  starting transfers between devices  81.4 us (30%)
  local copies, waits for them, and re-layouts  35.5 us (13%)
  matrix products  35.4 us (13%)
  other arithmetic  14.7 us (5%)
    ppermute x8, waiting for transfers between devices, passed_along(): lax.ppermute(value, axis, [(source, source + steps) for source in range(i...  74.2 us
    ppermute x8, starting transfers between devices, passed_along(): lax.ppermute(value, axis, [(source, source + steps) for source in range(i...  54.5 us
    dot_general x5, matrix products, grad_work(): jnp.einsum('qgrd,kgd->grqk', grad_four, value_tile, preferred_element_typ...  8.03 us
    dot_general x5, matrix products, grad_work(): jnp.einsum('grqk,qgrd->kgd', probs_bf, grad_four, preferred_element_type=...  7.26 us
    reduce_sum x5, other arithmetic, stats_work(): jnp.sum(jnp.where(allowed, jnp.exp(raw_scores - row_max[..., None]), 0.0)...  6.98 us
    dot_general x5, matrix products, scores_of(): jnp.einsum('qgrd,kgd->grqk', query_four, key_tile, preferred_element_type...  6.27 us
    all_to_all x1, waiting for transfers between devices, per_device(): lax.all_to_all(value_state_rows, 'tp', split_axis=1, concat_axis=0, tiled...  6.25 us
    unnamed x27, local copies, waits for them, and re-layouts  5.79 us
  transfers between devices with their start and end apart: 15, of which 10 were waited for; matrix products, arithmetic and copies ran while one was open for 24% of the time, Pallas kernels for 0%

commit v1 on v0

v1 whole, which is shorter than its diff:
```python
import functools
import math

import jax
import jax.numpy as jnp
from jax import lax
from jax.experimental import pallas as pl
from jax.experimental.pallas import tpu as pltpu
from jax.sharding import PartitionSpec as P

QUERY_HEADS = 32
KEY_HEADS = 16
HEAD_SIZE = 128
WINDOW = 1024
GROUP = QUERY_HEADS // KEY_HEADS
AXES = ("seq", "tp")

attn_scale = 168.0 ** (-0.5)
masked_floor = -1e30

CHUNKS = 2
ANY = pl.BlockSpec(memory_space=pl.ANY)
VMEM = pl.BlockSpec(memory_space=pltpu.VMEM)
SMEM = pl.BlockSpec(memory_space=pltpu.SMEM)


class Plan:
    def __init__(self, rows):
        self.seq, self.tp = lax.axis_size("seq"), lax.axis_size("tp")
        self.rows = rows
        self.block = rows * self.tp
        self.slab = WINDOW // self.block
        self.cores = min(2, self.slab)
        self.ways = self.slab // self.cores
        self.groups = self.ways * self.tp
        self.key_heads = KEY_HEADS // self.groups
        self.chunks = min(CHUNKS, self.key_heads)
        self.heads = self.key_heads // self.chunks
        self.key_cols = self.heads * HEAD_SIZE
        self.query_cols = self.key_cols * GROUP
        self.pieces = self.slab * self.tp

    def place(self):
        seq, tp = lax.axis_index("seq"), lax.axis_index("tp")
        inner = lax.rem(seq, self.slab)
        core = lax.rem(inner, self.cores)
        return seq - inner, core, (inner // self.cores) * self.tp + tp

    def routes(self, move):
        pairs = []
        for seq in range(self.seq):
            for tp in range(self.tp):
                slab, inner = divmod(seq, self.slab)
                way, core = divmod(inner, self.cores)
                to = move(slab, core, way * self.tp + tp)
                if to is not None and 0 <= to[0] < self.seq // self.slab:
                    target = (to[0] * self.slab + (to[2] // self.tp) * self.cores + to[1]) * self.tp + to[2] % self.tp
                    pairs.append((seq * self.tp + tp, target))
        return pairs

    def to_group(self, value, flip):
        return lax.ppermute(value, AXES, self.routes(lambda slab, core, group: (slab, core, group ^ flip)))

    def to_core(self, value):
        return lax.ppermute(value, AXES, self.routes(lambda slab, core, group: (slab, self.cores - 1 - core, group)))

    def to_slab(self, value, step):
        return lax.ppermute(value, AXES, self.routes(lambda slab, core, group: (slab + step, core, group)))


def run_copies(copies):
    for copy in copies:
        copy.start()
    for copy in copies:
        copy.wait()


def traffic(count):
    return pl.CostEstimate(flops=0, bytes_accessed=count, transcendentals=0)


def columns(start, width):
    return pl.ds(pl.multiple_of(start, HEAD_SIZE), width)


def split_columns(plan, arrays, width, chunks, name):
    chunk_width = width // chunks

    def kernel(*refs):
        sources, targets, sem = refs[: len(arrays)], refs[len(arrays) : -1], refs[-1]
        _, _, group = plan.place()
        copies = []
        for chunk in range(chunks):
            for flip in range(plan.groups):
                start = (group ^ flip) * width + chunk * chunk_width
                for index, source in enumerate(sources):
                    copies.append(
                        pltpu.make_async_copy(
                            source.at[:, columns(start, chunk_width)],
                            targets[chunk * plan.groups + flip].at[index],
                            sem.at[len(copies)],
                        )
                    )
        run_copies(copies)

    count = chunks * plan.groups
    shape = jax.ShapeDtypeStruct((len(arrays), plan.rows, chunk_width), jnp.bfloat16)
    out = pl.pallas_call(
        kernel,
        out_shape=[shape] * count,
        in_specs=[ANY] * len(arrays),
        out_specs=[VMEM] * count,
        scratch_shapes=[pltpu.SemaphoreType.DMA((count * len(arrays),))],
        cost_estimate=traffic(2 * sum(array.nbytes for array in arrays)),
        name=name,
    )(*arrays)
    return [out[chunk * plan.groups : (chunk + 1) * plan.groups] for chunk in range(chunks)]


def gather_pieces(plan, pieces):
    def kernel(*refs):
        sources, target, sem = refs[:-2], refs[-2], refs[-1]
        _, _, group = plan.place()
        run_copies(
            [pltpu.make_async_copy(source, target.at[group ^ flip], sem.at[flip]) for flip, source in enumerate(sources)]
        )

    return pl.pallas_call(
        kernel,
        out_shape=jax.ShapeDtypeStruct((plan.groups,) + pieces[0].shape, jnp.bfloat16),
        in_specs=[ANY] * plan.groups,
        out_specs=VMEM,
        scratch_shapes=[pltpu.SemaphoreType.DMA((plan.groups,))],
        cost_estimate=traffic(2 * sum(piece.nbytes for piece in pieces)),
        name="gather_keys",
    )(*pieces)


def join_columns(plan, chunked, count, width, name):
    chunks = len(chunked)
    chunk_width = width // chunks
    flat = [piece for pieces in chunked for piece in pieces]

    def kernel(*refs):
        sources, targets, sem = refs[: len(flat)], refs[len(flat) : -1], refs[-1]
        _, _, group = plan.place()
        copies = []
        for chunk in range(chunks):
            for flip in range(plan.groups):
                start = (group ^ flip) * width + chunk * chunk_width
                for index, target in enumerate(targets):
                    copies.append(
                        pltpu.make_async_copy(
                            sources[chunk * plan.groups + flip].at[index],
                            target.at[:, columns(start, chunk_width)],
                            sem.at[len(copies)],
                        )
                    )
        run_copies(copies)

    return pl.pallas_call(
        kernel,
        out_shape=[jax.ShapeDtypeStruct((plan.rows, width * plan.groups), jnp.bfloat16)] * count,
        in_specs=[ANY] * len(flat),
        out_specs=[VMEM] * count,
        scratch_shapes=[pltpu.SemaphoreType.DMA((len(flat) * count,))],
        cost_estimate=traffic(2 * sum(piece.nbytes for piece in flat)),
        name=name,
    )(*flat)


def backward(plan, chunk, doc_lengths, query_pieces, own, own_other, before, before_other):
    tiles = plan.slab + 1
    block, groups, tp, cores = plan.block, plan.groups, plan.tp, plan.cores
    wide = GROUP * block
    exponent_scale = attn_scale * math.log2(math.e)

    def kernel(docs, *refs):
        pieces = refs[:groups]
        key_refs = refs[groups : groups + 4]
        refs = refs[groups + 4 :]
        query_out, refs = refs[:groups], refs[groups:]
        own_mine, own_far, before_mine, before_far = refs[:4]
        q_s, o_s, k_s, v_s, dq_s, dk_s, dv_s, score_s, prob_grad_s, sem = refs[4:]
        slab_seq, core, group = plan.place()

        copies = []

        def add(source, target):
            copies.append(pltpu.make_async_copy(source, target, sem.at[len(copies)]))

        for flip, piece in enumerate(pieces):
            add(piece.at[0], q_s.at[group ^ flip])
            add(piece.at[1], o_s.at[group ^ flip])
        cols = pl.ds(chunk * plan.key_cols, plan.key_cols)
        for source, late, far in zip(key_refs, (1, 1, 0, 0), (0, 1, 0, 1)):
            side = core + far * (cores - 1 - 2 * core)
            for way in range(plan.ways):
                start = late * plan.pieces + (way * cores + side) * tp
                for index, target in enumerate((k_s, v_s)):
                    add(source.at[pl.ds(way * tp, tp), index, :, cols], target.at[pl.ds(start, tp)])
        for copy in copies:
            copy.start()
        dk_s[...] = jnp.zeros_like(dk_s)
        dv_s[...] = jnp.zeros_like(dv_s)
        for copy in copies:
            copy.wait()

        def step(index, carry):
            head, way = index // plan.ways, lax.rem(index, plan.ways)
            key_at = (way * cores + core) * tp
            key_cols = columns(head * HEAD_SIZE, HEAD_SIZE)
            rows_at = pl.ds(way * tp, tp)

            def both(ref):
                parts = [
                    ref[rows_at, :, columns((head * GROUP + member) * HEAD_SIZE, HEAD_SIZE)].reshape(block, HEAD_SIZE)
                    for member in range(GROUP)
                ]
                return jnp.concatenate(parts, axis=0)

            queries, grads = both(q_s), both(o_s)
            inner = lax.broadcasted_iota(jnp.int32, (1, block), 1)
            inner = jnp.concatenate([inner] * GROUP, axis=1)
            first = (slab_seq + way * cores + core) * block
            position = inner + first
            lowest = position - (WINDOW - 1)
            start = jnp.int32(0)
            for doc in range(docs.shape[0]):
                lowest = jnp.where(position >= start, jnp.maximum(lowest, start), lowest)
                start = start + docs[doc]
            lowest = lowest - (first - WINDOW)

            def key_rows(ref, tile):
                return ref[pl.ds(key_at + tile * tp, tp), :, key_cols].reshape(block, HEAD_SIZE)

            def tile_rows(tile):
                return pl.ds(tile * block, block)

            peak = jnp.full((1, wide), masked_floor, jnp.float32)
            for tile in range(tiles):
                scores = lax.dot_general(
                    key_rows(k_s, tile), queries, (((1,), (1,)), ((), ())), preferred_element_type=jnp.float32
                )
                row = lax.broadcasted_iota(jnp.int32, (block, wide), 0)
                allowed = row >= lowest - tile * block
                if tile == tiles - 1:
                    allowed = allowed & (row <= inner)
                scores = jnp.where(allowed, scores, masked_floor)
                peak = jnp.maximum(peak, jnp.max(scores, axis=0, keepdims=True))
                score_s[tile_rows(tile), :] = scores
            peak = peak * exponent_scale
            total = jnp.zeros((1, wide), jnp.float32)
            delta = jnp.zeros((1, wide), jnp.float32)
            for tile in range(tiles):
                raised = jnp.exp2(score_s[tile_rows(tile), :] * exponent_scale - peak)
                prob_grad = lax.dot_general(
                    key_rows(v_s, tile), grads, (((1,), (1,)), ((), ())), preferred_element_type=jnp.float32
                )
                total = total + jnp.sum(raised, axis=0, keepdims=True)
                delta = delta + jnp.sum(raised * prob_grad, axis=0, keepdims=True)
                score_s[tile_rows(tile), :] = raised
                prob_grad_s[tile_rows(tile), :] = prob_grad
            inverse = 1.0 / total
            delta = delta * inverse
            query_sum = jnp.zeros((HEAD_SIZE, wide), jnp.float32)
            for tile in range(tiles):
                probs = score_s[tile_rows(tile), :] * inverse
                grad_scores = (probs * (prob_grad_s[tile_rows(tile), :] - delta) * attn_scale).astype(jnp.bfloat16)
                at = pl.ds(key_at + tile * tp, tp)
                value_part = jnp.dot(probs.astype(jnp.bfloat16), grads, preferred_element_type=jnp.float32)
                dv_s[at, :, key_cols] += value_part.reshape(tp, plan.rows, HEAD_SIZE)
                key_part = jnp.dot(grad_scores, queries, preferred_element_type=jnp.float32)
                dk_s[at, :, key_cols] += key_part.reshape(tp, plan.rows, HEAD_SIZE)
                query_sum += lax.dot_general(
                    key_rows(k_s, tile), grad_scores, (((0,), (0,)), ((), ())), preferred_element_type=jnp.float32
                )
            query_rows = query_sum.T.astype(jnp.bfloat16)
            for member in range(GROUP):
                dq_s[rows_at, :, columns((head * GROUP + member) * HEAD_SIZE, HEAD_SIZE)] = query_rows[
                    member * block : (member + 1) * block
                ].reshape(tp, plan.rows, HEAD_SIZE)
            return carry

        lax.fori_loop(0, plan.heads * plan.ways, step, 0)
        for flip in range(groups):
            query_out[flip][0] = dq_s[group ^ flip]
        for late, far, target in ((1, 0, own_mine), (1, 1, own_far), (0, 0, before_mine), (0, 1, before_far)):
            side = core + far * (cores - 1 - 2 * core)
            for way in range(plan.ways):
                at = pl.ds(late * plan.pieces + (way * cores + side) * tp, tp)
                for index, source in enumerate((dk_s, dv_s)):
                    target[pl.ds(way * tp, tp), index] = source[at].astype(target.dtype)

    part = (groups, 2, plan.rows, plan.key_cols)
    bf, fl = jnp.bfloat16, jnp.float32
    span = 2 * plan.pieces
    pairs = tiles * block * wide * plan.heads * plan.ways
    out = pl.pallas_call(
        kernel,
        out_shape=[jax.ShapeDtypeStruct((1, plan.rows, plan.query_cols), bf)] * groups
        + [jax.ShapeDtypeStruct(part, dtype) for dtype in (fl, bf, fl, bf)],
        in_specs=[SMEM] + [ANY] * (groups + 4),
        out_specs=[VMEM] * (groups + 4),
        scratch_shapes=[
            pltpu.VMEM((groups, plan.rows, plan.query_cols), bf),
            pltpu.VMEM((groups, plan.rows, plan.query_cols), bf),
            pltpu.VMEM((span, plan.rows, plan.key_cols), bf),
            pltpu.VMEM((span, plan.rows, plan.key_cols), bf),
            pltpu.VMEM((groups, plan.rows, plan.query_cols), bf),
            pltpu.VMEM((span, plan.rows, plan.key_cols), fl),
            pltpu.VMEM((span, plan.rows, plan.key_cols), fl),
            pltpu.VMEM((tiles * block, wide), fl),
            pltpu.VMEM((tiles * block, wide), fl),
            pltpu.SemaphoreType.DMA((2 * groups + 8 * plan.ways,)),
        ],
        compiler_params=pltpu.CompilerParams(vmem_limit_bytes=40 * 1024 * 1024),
        cost_estimate=pl.CostEstimate(flops=10 * pairs * HEAD_SIZE, bytes_accessed=6 << 20, transcendentals=pairs),
        name="backward",
    )(doc_lengths, *query_pieces, own, own_other, before, before_other)
    return out[:groups], out[groups:]


def add_up(plan, mine, far, later):
    def kernel(mine_ref, far_ref, later_ref, *targets):
        _, _, group = plan.place()
        for flip, target in enumerate(targets):
            at = group ^ flip
            total = mine_ref[at] + far_ref[at].astype(jnp.float32) + later_ref[at].astype(jnp.float32)
            target[...] = total.astype(jnp.bfloat16)

    shape = jax.ShapeDtypeStruct(mine.shape[1:], jnp.bfloat16)
    return pl.pallas_call(
        kernel,
        out_shape=[shape] * plan.groups,
        in_specs=[VMEM] * 3,
        out_specs=[VMEM] * plan.groups,
        cost_estimate=traffic(mine.nbytes + far.nbytes * 3),
        name="add_up",
    )(mine, far, later)


def per_device(queries, key_states, value_state_rows, out_grad, doc_lengths):
    plan = Plan(queries.shape[0])
    key_width = KEY_HEADS * HEAD_SIZE // plan.groups
    query_width = QUERY_HEADS * HEAD_SIZE // plan.groups

    def exchange(pieces):
        return [pieces[0]] + [plan.to_group(pieces[flip], flip) for flip in range(1, plan.groups)]

    key_pieces = exchange(split_columns(plan, (key_states, value_state_rows), key_width, 1, "split_keys")[0])
    query_chunks = split_columns(plan, (queries, out_grad), query_width, plan.chunks, "split_queries")
    key_pieces, query_chunks = lax.optimization_barrier((key_pieces, query_chunks))
    own = gather_pieces(plan, key_pieces)
    before = plan.to_slab(own, 1)
    own_other = plan.to_core(own)
    arrived = [exchange(query_chunks[0])]
    before, own_other, arrived[0] = lax.optimization_barrier((before, own_other, arrived[0]))
    before_other = plan.to_core(before)
    for chunk in range(1, plan.chunks):
        arrived.append(exchange(query_chunks[chunk]))
    query_results, key_results = [], []
    for chunk in range(plan.chunks):
        pieces = arrived[chunk]
        query_out, (own_mine, own_far, before_mine, before_far) = backward(
            plan, chunk, doc_lengths, pieces, own, own_other, before, before_other
        )
        before_sum = (before_mine + plan.to_core(before_far).astype(jnp.float32)).astype(jnp.bfloat16)
        later = plan.to_slab(before_sum, -1)
        far = plan.to_core(own_far)
        query_results.append(exchange(query_out))
        key_results.append(exchange(add_up(plan, own_mine, far, later)))
    (query_grad,) = join_columns(plan, query_results, 1, query_width, "join_queries")
    key_gradient, value_gradient = join_columns(plan, key_results, 2, key_width, "join_keys")
    return query_grad, key_gradient, value_gradient


def solution(mesh):
    split = P(("seq", "tp"), None)
    return jax.shard_map(
        per_device,
        mesh=mesh,
        in_specs=(split, split, split, split, P()),
        out_specs=(split, split, split),
        check_vma=False,
    )
```

time: 271 us -> 145 us (0.54)
  the two profiles are of different devices: /device:TPU:24 before, /device:TPU:0 now
where the time goes in v1:
time: 145 us; the launch traced here: 144 us
  waiting for transfers between devices  57.7 us (40%)
  Pallas kernels  45.5 us (31%)
  starting transfers between devices  35.5 us (24%)
  local copies, waits for them, and re-layouts  4.37 us (3%)
    ppermute x21, waiting for transfers between devices, to_group(): lax.ppermute(value, AXES, self.routes(lambda slab, core, group: (slab, co...  38.2 us
    pallas_call x2, Pallas kernels, backward(): pl.pallas_call(kernel, out_shape=[jax.ShapeDtypeStruct((1, plan.rows, pla...  28.2 us
    ppermute x21, starting transfers between devices, to_group(): lax.ppermute(value, AXES, self.routes(lambda slab, core, group: (slab, co...  28.1 us
    ppermute x3, waiting for transfers between devices, to_slab(): lax.ppermute(value, AXES, self.routes(lambda slab, core, group: (slab + s...  19.4 us
    ppermute x3, starting transfers between devices, to_slab(): lax.ppermute(value, AXES, self.routes(lambda slab, core, group: (slab + s...  6.28 us
    pallas_call x2, Pallas kernels, split_columns(): pl.pallas_call(kernel, out_shape=[shape] * count, in_specs=[ANY] * len(ar...  5.42 us
    pallas_call x2, Pallas kernels, add_up(): pl.pallas_call(kernel, out_shape=[shape] * plan.groups, in_specs=[VMEM] *...  4.84 us
    pallas_call x2, Pallas kernels, join_columns(): pl.pallas_call(kernel, out_shape=[jax.ShapeDtypeStruct((plan.rows, width...  4.68 us
  transfers between devices with their start and end apart: 30, of which 16 were waited for; matrix products, arithmetic and copies ran while one was open for 0% of the time, Pallas kernels for 17%

profile of v1, /device:TPU:0, one launch (start us, length us, event | category | flops | bytes accessed | tf_op | source)
XLA Modules:
  0.0 144.3 jit_solution(9962993022422437433)
XLA Ops:
  0.6 2.4 %split_keys.1 = (bf16[2,128,512]{2,1,0:T(8,128)(2,1)}, bf16[2,128,512]{2,1,0:T(8,128)(2,1)}, bf16[2,128,512]{2,1,0:T(8,128)(2,1)}, bf16[2,128,512]{2,1,0:T(8,128)(2,1)}) custom-call(bf16[128,2048]{1,0:T(8,128)(2,1)} %refs_0_.2, bf16[128,2048]{1,0:T(8,128)(2,1)} %refs_1_.2), custom_call_target="tpu_custom_call" | custom-call | bytes 2097152 | tf_op jit(solution)/shard_map/split_keys/pallas_call | solution.py:108
  3.0 3.0 %collective-permute-start = (bf16[2,128,512]{2,1,0:T(8,128)(2,1)}, bf16[2,128,512]{2,1,0:T(8,128)(2,1)S(1)}, u32[]{:S(2)}, u32[]{:S(2)}) collective-permute-start(bf16[2,128,512]{2,1,0:T(8,128)(2,1)} %get-tuple-element.60), channel_id=1, source_target_pairs={{0,1},{1,0},{2,3},{3,2},{4,5},{5,4},{6,7},{7,6},{8,9},{9,8},{10,11... | collective-permute-start | bytes 786440 | tf_op jit(solution)/shard_map/ppermute | solution.py:62
  6.0 1.5 %collective-permute-start.1 = (bf16[2,128,512]{2,1,0:T(8,128)(2,1)}, bf16[2,128,512]{2,1,0:T(8,128)(2,1)S(1)}, u32[]{:S(2)}, u32[]{:S(2)}) collective-permute-start(bf16[2,128,512]{2,1,0:T(8,128)(2,1)} %get-tuple-element.61), channel_id=1, source_target_pairs={{0,4},{1,5},{2,6},{3,7},{4,0},{5,1},{6,2},{7,3},{8,12},{9,13},{10,... | collective-permute-start | bytes 786440 | tf_op jit(solution)/shard_map/ppermute | solution.py:62
  7.5 0.0 collective-permute-start.2
  7.6 3.1 %split_queries.1 = (bf16[2,128,512]{2,1,0:T(8,128)(2,1)}, bf16[2,128,512]{2,1,0:T(8,128)(2,1)}, bf16[2,128,512]{2,1,0:T(8,128)(2,1)}, bf16[2,128,512]{2,1,0:T(8,...) custom-call(bf16[128,4096]{1,0:T(8,128)(2,1)} %refs_0_.3, ...), custom_call_target="tpu_custom_call" | custom-call | bytes 4194304 | tf_op jit(solution)/shard_map/split_queries/pallas_call | solution.py:108
  10.6 1.9 %collective-permute-done.refs_1_ = bf16[2,128,512]{2,1,0:T(8,128)(2,1)S(1)} collective-permute-done((bf16[2,128,512]{2,1,0:T(8,128)(2,1)}, bf16[2,128,512]{2,1,0:T(8,128)(2,1)S(1)}, u32[]{:S(2)}, u32[]{:S(2)}) %collective-permute-start) | collective-permute-done | bytes 262176 | tf_op jit(solution)/shard_map/ppermute | solution.py:62
  12.5 2.9 %collective-permute-done.1.refs_2_ = bf16[2,128,512]{2,1,0:T(8,128)(2,1)S(1)} collective-permute-done((bf16[2,128,512]{2,1,0:T(8,128)(2,1)}, bf16[2,128,512]{2,1,0:T(8,128)(2,1)S(1)}, u32[]{:S(2)}, u32[]{:S(2)}) %collective-permute-start.1) | collective-permute-done | bytes 262176 | tf_op jit(solution)/shard_map/ppermute | solution.py:62
  15.5 3.9 %collective-permute-done.2.refs_3_ = bf16[2,128,512]{2,1,0:T(8,128)(2,1)S(1)} collective-permute-done((bf16[2,128,512]{2,1,0:T(8,128)(2,1)}, bf16[2,128,512]{2,1,0:T(8,128)(2,1)S(1)}, u32[]{:S(2)}, u32[]{:S(2)}) %collective-permute-start.2) | collective-permute-done | bytes 262176 | tf_op jit(solution)/shard_map/ppermute | solution.py:62
  19.4 0.7 copy-done.14
  20.2 0.0 copy-start.7
  20.2 0.0 copy-start.5
  20.2 2.3 %gather_keys.1.refs_4_ = bf16[4,2,128,512]{3,2,1,0:T(8,128)(2,1)} custom-call(bf16[2,128,512]{2,1,0:T(8,128)(2,1)} %get-tuple-element.71.refs_0_, bf16[2,128,512]{2,1,0:T(8,128)(2,1)} %copy-done.12, bf16[2,128,512]{2,1,0:T(8,128)(2,1)} %copy-done.13, bf16[2,128,512]{2,1,0:T(8,128)(2,1)} %copy-done.14), custom_call_target="tpu_custom_call" | custom-call | bytes 2097152 | tf_op jit(solution)/shard_map/gather_keys/pallas_call | solution.py:128
  22.5 3.7 %collective-permute-start.3 = (bf16[4,2,128,512]{3,2,1,0:T(8,128)(2,1)}, bf16[4,2,128,512]{3,2,1,0:T(8,128)(2,1)S(1)}, u32[]{:S(2)}, u32[]{:S(2)}) collective-permute-start(bf16[4,2,128,512]{3,2,1,0:T(8,128)(2,1)} %gather_keys.1.refs_4_), channel_id=1, source_target_pairs={{0,8},{1,9},{2,10},{3,11},{4,12},{5,13},{6,14},{7,15},{8,16},{9,17... | collective-permute-start | bytes 3145736 | tf_op jit(solution)/shard_map/ppermute | solution.py:68
  26.2 0.1 collective-permute-start.4
  26.3 1.6 %collective-permute-start.5 = (bf16[2,128,512]{2,1,0:T(8,128)(2,1)}, bf16[2,128,512]{2,1,0:T(8,128)(2,1)S(1)}, u32[]{:S(2)}, u32[]{:S(2)}) collective-permute-start(bf16[2,128,512]{2,1,0:T(8,128)(2,1)} %get-tuple-element.76), channel_id=1, source_target_pairs={{0,1},{1,0},{2,3},{3,2},{4,5},{5,4},{6,7},{7,6},{8,9},{9,8},{10,11... | collective-permute-start | bytes 786440 | tf_op jit(solution)/shard_map/ppermute | solution.py:62
  27.9 1.5 %collective-permute-start.6 = (bf16[2,128,512]{2,1,0:T(8,128)(2,1)S(1)}, bf16[2,128,512]{2,1,0:T(8,128)(2,1)S(1)}, u32[]{:S(2)}, u32[]{:S(2)}) collective-permute-start(bf16[2,128,512]{2,1,0:T(8,128)(2,1)S(1)} %copy-done.31), channel_id=1, source_target_pairs={{0,4},{1,5},{2,6},{3,7},{4,0},{5,1},{6,2},{7,3},{8,12},{9,13},{10,... | collective-permute-start | bytes 786440 | tf_op jit(solution)/shard_map/ppermute | solution.py:62
  29.4 0.5 collective-permute-start.7
  29.9 5.4 %collective-permute-done.5.refs_1_ = bf16[2,128,512]{2,1,0:T(8,128)(2,1)S(1)} collective-permute-done((bf16[2,128,512]{2,1,0:T(8,128)(2,1)}, bf16[2,128,512]{2,1,0:T(8,128)(2,1)S(1)}, u32[]{:S(2)}, u32[]{:S(2)}) %collective-permute-start.5) | collective-permute-done | bytes 262176 | tf_op jit(solution)/shard_map/ppermute | solution.py:62
  35.3 1.8 %collective-permute-done.6.refs_2_ = bf16[2,128,512]{2,1,0:T(8,128)(2,1)S(1)} collective-permute-done((bf16[2,128,512]{2,1,0:T(8,128)(2,1)S(1)}, bf16[2,128,512]{2,1,0:T(8,128)(2,1)S(1)}, u32[]{:S(2)}, u32[]{:S(2)}) %collective-permute-start.6) | collective-permute-done | bytes 262176 | tf_op jit(solution)/shard_map/ppermute | solution.py:62
  37.1 4.8 %collective-permute-done.7.refs_3_ = bf16[2,128,512]{2,1,0:T(8,128)(2,1)S(1)} collective-permute-done((bf16[2,128,512]{2,1,0:T(8,128)(2,1)S(1)}, bf16[2,128,512]{2,1,0:T(8,128)(2,1)S(1)}, u32[]{:S(2)}, u32[]{:S(2)}) %collective-permute-start.7) | collective-permute-done | bytes 262176 | tf_op jit(solution)/shard_map/ppermute | solution.py:62
  41.8 5.9 %collective-permute-done.3.refs_6_ = bf16[4,2,128,512]{3,2,1,0:T(8,128)(2,1)S(1)} collective-permute-done((bf16[4,2,128,512]{3,2,1,0:T(8,128)(2,1)}, bf16[4,2,128,512]{3,2,1,0:T(8,128)(2,1)S(1)}, u32[]{:S(2)}, u32[]{:S(2)}) %collective-permute-start.3) | collective-permute-done | bytes 1048608 | tf_op jit(solution)/shard_map/ppermute | solution.py:68
  47.7 1.6 %collective-permute-start.12 = (bf16[2,128,512]{2,1,0:T(8,128)(2,1)S(1)}, bf16[2,128,512]{2,1,0:T(8,128)(2,1)S(1)}, u32[]{:S(2)}, u32[]{:S(2)}) collective-permute-start(bf16[2,128,512]{2,1,0:T(8,128)(2,1)S(1)} %copy-done.29), channel_id=1, source_target_pairs={{0,1},{1,0},{2,3},{3,2},{4,5},{5,4},{6,7},{7,6},{8,9},{9,8},{10,11... | collective-permute-start | bytes 786440 | tf_op jit(solution)/shard_map/ppermute | solution.py:62
  49.3 1.5 %collective-permute-start.13 = (bf16[2,128,512]{2,1,0:T(8,128)(2,1)S(1)}, bf16[2,128,512]{2,1,0:T(8,128)(2,1)S(1)}, u32[]{:S(2)}, u32[]{:S(2)}) collective-permute-start(bf16[2,128,512]{2,1,0:T(8,128)(2,1)S(1)} %copy-done.28), channel_id=1, source_target_pairs={{0,4},{1,5},{2,6},{3,7},{4,0},{5,1},{6,2},{7,3},{8,12},{9,13},{10,... | collective-permute-start | bytes 786440 | tf_op jit(solution)/shard_map/ppermute | solution.py:62
  50.8 0.5 collective-permute-start.14
  51.3 5.2 %collective-permute-done.12.refs_1_ = bf16[2,128,512]{2,1,0:T(8,128)(2,1)S(1)} collective-permute-done((bf16[2,128,512]{2,1,0:T(8,128)(2,1)S(1)}, bf16[2,128,512]{2,1,0:T(8,128)(2,1)S(1)}, u32[]{:S(2)}, u32[]{:S(2)}) %collective-permute-start.12) | collective-permute-done | bytes 262176 | tf_op jit(solution)/shard_map/ppermute | solution.py:62
  56.4 2.0 %collective-permute-done.13.refs_2_ = bf16[2,128,512]{2,1,0:T(8,128)(2,1)S(1)} collective-permute-done((bf16[2,128,512]{2,1,0:T(8,128)(2,1)S(1)}, bf16[2,128,512]{2,1,0:T(8,128)(2,1)S(1)}, u32[]{:S(2)}, u32[]{:S(2)}) %collective-permute-start.13) | collective-permute-done | bytes 262176 | tf_op jit(solution)/shard_map/ppermute | solution.py:62
  58.5 4.8 %collective-permute-done.14.refs_3_ = bf16[2,128,512]{2,1,0:T(8,128)(2,1)S(1)} collective-permute-done((bf16[2,128,512]{2,1,0:T(8,128)(2,1)S(1)}, bf16[2,128,512]{2,1,0:T(8,128)(2,1)S(1)}, u32[]{:S(2)}, u32[]{:S(2)}) %collective-permute-start.14) | collective-permute-done | bytes 262176 | tf_op jit(solution)/shard_map/ppermute | solution.py:62
  63.2 0.0 copy-start.1
  63.3 1.2 copy-done.1
  64.5 14.1 %backward.3 = (bf16[1,128,512]{2,1,0:T(8,128)(2,1)S(1)}, bf16[1,128,512]{2,1,0:T(8,128)(2,1)S(1)}, bf16[1,128,512]{2,1,0:T(8,128)(2,1)S(1)}, bf16[1,128,512]{2,1...) custom-call(s32[4]{0:T(128)S(1)} %copy-done.7, ...), custom_call_target="tpu_custom_call" | custom-call | flops 3355443200 | bytes 6291456 | tf_op jit(solution)/shard_map/backward/pallas_call | solution.py:299
  78.6 1.0 copy-done.2
  79.6 0.7 copy-done.3
  80.3 14.1 %backward.2 = (bf16[1,128,512]{2,1,0:T(8,128)(2,1)S(1)}, bf16[1,128,512]{2,1,0:T(8,128)(2,1)S(1)}, bf16[1,128,512]{2,1,0:T(8,128)(2,1)S(1)}, bf16[1,128,512]{2,1...) custom-call(s32[4]{0:T(128)S(1)} %copy-done.7, ...), custom_call_target="tpu_custom_call" | custom-call | flops 3355443200 | bytes 6291456 | tf_op jit(solution)/shard_map/backward/pallas_call | solution.py:299
  94.4 0.0 copy-start
  94.5 0.6 collective-permute-start.19
  95.0 0.1 collective-permute-start.24
  95.1 0.4 collective-permute-start.18
  95.5 0.2 add_convert_fusion
  95.7 1.3 collective-permute-start.26
  97.0 0.1 add_convert_fusion.1
  97.1 1.3 collective-permute-start.20
  98.4 1.6 %collective-permute-start.15 = (bf16[1,128,512]{2,1,0:T(8,128)(2,1)S(1)}, bf16[1,128,512]{2,1,0:T(8,128)(2,1)S(1)}, u32[]{:S(2)}, u32[]{:S(2)}) collective-permute-start(bf16[1,128,512]{2,1,0:T(8,128)(2,1)S(1)} %get-tuple-element.94), channel_id=1, source_target_pairs={{0,1},{1,0},{2,3},{3,2},{4,5},{5,4},{6,7},{7,6},{8,9},{9,8},{10,11... | collective-permute-start | bytes 393224 | tf_op jit(solution)/shard_map/ppermute | solution.py:62
  100.0 1.5 %collective-permute-start.16 = (bf16[1,128,512]{2,1,0:T(8,128)(2,1)S(1)}, bf16[1,128,512]{2,1,0:T(8,128)(2,1)S(1)}, u32[]{:S(2)}, u32[]{:S(2)}) collective-permute-start(bf16[1,128,512]{2,1,0:T(8,128)(2,1)S(1)} %get-tuple-element.95), channel_id=1, source_target_pairs={{0,4},{1,5},{2,6},{3,7},{4,0},{5,1},{6,2},{7,3},{8,12},{9,13},{10,... | collective-permute-start | bytes 393224 | tf_op jit(solution)/shard_map/ppermute | solution.py:62
  101.5 11.2 %collective-permute-done.26.later_ref = bf16[4,2,128,256]{3,2,1,0:T(8,128)(2,1)S(1)} collective-permute-done((bf16[4,2,128,256]{3,2,1,0:T(8,128)(2,1)S(1)}, bf16[4,2,128,256]{3,2,1,0:T(8,128)(2,1)S(1)}, u32[]{:S(2)}, u32[]{:S(2)}) %collective-permute-start.26) | collective-permute-done | bytes 524320 | tf_op jit(solution)/shard_map/ppermute | solution.py:68
  112.7 2.4 %collective-permute-start.17 = (bf16[1,128,512]{2,1,0:T(8,128)(2,1)S(1)}, bf16[1,128,512]{2,1,0:T(8,128)(2,1)S(1)}, u32[]{:S(2)}, u32[]{:S(2)}) collective-permute-start(bf16[1,128,512]{2,1,0:T(8,128)(2,1)S(1)} %get-tuple-element.96), channel_id=1, source_target_pairs={{0,5},{1,4},{2,7},{3,6},{4,1},{5,0},{6,3},{7,2},{8,13},{9,12},{10,... | collective-permute-start | bytes 393224 | tf_op jit(solution)/shard_map/ppermute | solution.py:62
  115.1 2.4 %add_up.3 = (bf16[2,128,256]{2,1,0:T(8,128)(2,1)}, bf16[2,128,256]{2,1,0:T(8,128)(2,1)}, bf16[2,128,256]{2,1,0:T(8,128)(2,1)}, bf16[2,128,256]{2,1,0:T(8,128)(2,1)}) custom-call(f32[4,2,128,256]{3,2,1,0:T(8,128)} %copy-done.2, bf16[4,2,128,256]{3,2,1,0:T(8,128)(2,1)} %copy-done.10, bf16[4,2,128,256]{3,2,1,0:T(8,128)(2,1)} %copy-done.11), custom_call_target="tpu_custom_call" | custom-call | bytes 2621440 | tf_op jit(solution)/shard_map/add_up/pallas_call | solution.py:333
  117.5 0.6 collective-permute-start.10
  118.1 1.4 collective-permute-start.11
  119.6 1.5 %collective-permute-start.9 = (bf16[1,128,512]{2,1,0:T(8,128)(2,1)S(1)}, bf16[1,128,512]{2,1,0:T(8,128)(2,1)S(1)}, u32[]{:S(2)}, u32[]{:S(2)}) collective-permute-start(bf16[1,128,512]{2,1,0:T(8,128)(2,1)S(1)} %get-tuple-element.86), channel_id=1, source_target_pairs={{0,1},{1,0},{2,3},{3,2},{4,5},{5,4},{6,7},{7,6},{8,9},{9,8},{10,11... | collective-permute-start | bytes 393224 | tf_op jit(solution)/shard_map/ppermute | solution.py:62
  121.1 2.4 %collective-permute-done.20.later_ref = bf16[4,2,128,256]{3,2,1,0:T(8,128)(2,1)S(1)} collective-permute-done((bf16[4,2,128,256]{3,2,1,0:T(8,128)(2,1)S(1)}, bf16[4,2,128,256]{3,2,1,0:T(8,128)(2,1)S(1)}, u32[]{:S(2)}, u32[]{:S(2)}) %collective-permute-start.20) | collective-permute-done | bytes 524320 | tf_op jit(solution)/shard_map/ppermute | solution.py:68
  123.5 1.5 %collective-permute-start.27 = (bf16[2,128,256]{2,1,0:T(8,128)(2,1)}, bf16[2,128,256]{2,1,0:T(8,128)(2,1)S(1)}, u32[]{:S(2)}, u32[]{:S(2)}) collective-permute-start(bf16[2,128,256]{2,1,0:T(8,128)(2,1)} %get-tuple-element.110), channel_id=1, source_target_pairs={{0,1},{1,0},{2,3},{3,2},{4,5},{5,4},{6,7},{7,6},{8,9},{9,8},{10,11... | collective-permute-start | bytes 393224 | tf_op jit(solution)/shard_map/ppermute | solution.py:62
  125.0 2.5 %add_up.2 = (bf16[2,128,256]{2,1,0:T(8,128)(2,1)}, bf16[2,128,256]{2,1,0:T(8,128)(2,1)}, bf16[2,128,256]{2,1,0:T(8,128)(2,1)}, bf16[2,128,256]{2,1,0:T(8,128)(2,1)}) custom-call(f32[4,2,128,256]{3,2,1,0:T(8,128)} %copy-done, bf16[4,2,128,256]{3,2,1,0:T(8,128)(2,1)} %copy-done.8, bf16[4,2,128,256]{3,2,1,0:T(8,128)(2,1)} %copy-done.9), custom_call_target="tpu_custom_call" | custom-call | bytes 2621440 | tf_op jit(solution)/shard_map/add_up/pallas_call | solution.py:333
  127.5 1.6 %collective-permute-start.28 = (bf16[2,128,256]{2,1,0:T(8,128)(2,1)S(1)}, bf16[2,128,256]{2,1,0:T(8,128)(2,1)S(1)}, u32[]{:S(2)}, u32[]{:S(2)}) collective-permute-start(bf16[2,128,256]{2,1,0:T(8,128)(2,1)S(1)} %copy-done.33), channel_id=1, source_target_pairs={{0,4},{1,5},{2,6},{3,7},{4,0},{5,1},{6,2},{7,3},{8,12},{9,13},{10,... | collective-permute-start | bytes 393224 | tf_op jit(solution)/shard_map/ppermute | solution.py:62
  129.1 0.8 collective-permute-start.29
  129.9 1.2 collective-permute-start.21
  131.2 1.5 %collective-permute-start.22 = (bf16[2,128,256]{2,1,0:T(8,128)(2,1)}, bf16[2,128,256]{2,1,0:T(8,128)(2,1)S(1)}, u32[]{:S(2)}, u32[]{:S(2)}) collective-permute-start(bf16[2,128,256]{2,1,0:T(8,128)(2,1)} %get-tuple-element.103), channel_id=1, source_target_pairs={{0,4},{1,5},{2,6},{3,7},{4,0},{5,1},{6,2},{7,3},{8,12},{9,13},{10,... | collective-permute-start | bytes 393224 | tf_op jit(solution)/shard_map/ppermute | solution.py:62
  132.7 0.7 collective-permute-start.23
  133.4 2.3 %join_queries.1 = bf16[128,4096]{1,0:T(8,128)(2,1)} custom-call(bf16[1,128,512]{2,1,0:T(8,128)(2,1)} %copy-done.4, bf16[1,128,512]{2,1,0:T(8,128)(2,1)} %copy-done.20, bf16[1,128,512]{2,1,0:T(8,128)(2,1)} %copy-done.18, bf16[1,128,512]{2,1,0:T(8,128)(2,1)} %copy-done.19, bf16[1,128,512]{2,1,0:T(8,128)(2,1)} %copy-done.3, bf16[1,128,512]{2,1,0:T(8,128)(2,1)} %copy-done.15, ...), custom_call_target="tpu_custom_call" | custom-call | bytes 2097152 | tf_op jit(solution)/shard_map/join_queries/pallas_call | solution.py:161
  135.8 1.0 collective-permute-done.29.refs_7_
  136.8 0.6 collective-permute-done.21.refs_1_
  137.5 1.9 %collective-permute-done.22.refs_2_ = bf16[2,128,256]{2,1,0:T(8,128)(2,1)S(1)} collective-permute-done((bf16[2,128,256]{2,1,0:T(8,128)(2,1)}, bf16[2,128,256]{2,1,0:T(8,128)(2,1)S(1)}, u32[]{:S(2)}, u32[]{:S(2)}) %collective-permute-start.22) | collective-permute-done | bytes 131104 | tf_op jit(solution)/shard_map/ppermute | solution.py:62
  139.4 2.0 %collective-permute-done.23.refs_3_ = bf16[2,128,256]{2,1,0:T(8,128)(2,1)S(1)} collective-permute-done((bf16[2,128,256]{2,1,0:T(8,128)(2,1)}, bf16[2,128,256]{2,1,0:T(8,128)(2,1)S(1)}, u32[]{:S(2)}, u32[]{:S(2)}) %collective-permute-start.23) | collective-permute-done | bytes 131104 | tf_op jit(solution)/shard_map/ppermute | solution.py:62
  141.4 0.6 copy-done.26
  142.0 2.3 %join_keys.1 = (bf16[128,2048]{1,0:T(8,128)(2,1)}, bf16[128,2048]{1,0:T(8,128)(2,1)}) custom-call(bf16[2,128,256]{2,1,0:T(8,128)(2,1)} %get-tuple-element.101.refs_0_, bf16[2,128,256]{2,1,0:T(8,128)(2,1)} %copy-done.24, bf16[2,128,256]{2,1,0:T(8,128)(2,1)} %copy-done.25, bf16[2,128,256]{2,1,0:T(8,128)(2,1)} %copy-done.26, ...), custom_call_target="tpu_custom_call" | custom-call | bytes 2097152 | tf_op jit(solution)/shard_map/join_keys/pallas_call | solution.py:161
  (75 shorter events, 0.2 us)
Async XLA Ops:
  3.0 9.5 %collective-permute-start = (bf16[2,128,512]{2,1,0:T(8,128)(2,1)}, bf16[2,128,512]{2,1,0:T(8,128)(2,1)S(1)}, u32[]{:S(2)}, u32[]{:S(2)}) collective-permute-start(bf16[2,128,512]{2,1,0:T(8,128)(2,1)} %get-tuple-element.60), channel_id=1, source_target_pairs={{0,1},{1,0},{2,3},{3,2},{4,5},{5,4},{6,7},{7,6},{8,9},{9,8},{10,11... | collective-permute-start | bytes 786440 | tf_op jit(solution)/shard_map/ppermute | solution.py:62
  6.0 9.4 %collective-permute-start.1 = (bf16[2,128,512]{2,1,0:T(8,128)(2,1)}, bf16[2,128,512]{2,1,0:T(8,128)(2,1)S(1)}, u32[]{:S(2)}, u32[]{:S(2)}) collective-permute-start(bf16[2,128,512]{2,1,0:T(8,128)(2,1)} %get-tuple-element.61), channel_id=1, source_target_pairs={{0,4},{1,5},{2,6},{3,7},{4,0},{5,1},{6,2},{7,3},{8,12},{9,13},{10,... | collective-permute-start | bytes 786440 | tf_op jit(solution)/shard_map/ppermute | solution.py:62
  7.5 11.9 %collective-permute-start.2 = (bf16[2,128,512]{2,1,0:T(8,128)(2,1)}, bf16[2,128,512]{2,1,0:T(8,128)(2,1)S(1)}, u32[]{:S(2)}, u32[]{:S(2)}) collective-permute-start(bf16[2,128,512]{2,1,0:T(8,128)(2,1)} %get-tuple-element.62), channel_id=1, source_target_pairs={{0,5},{1,4},{2,7},{3,6},{4,1},{5,0},{6,3},{7,2},{8,13},{9,12},{10,... | collective-permute-start | bytes 786440 | tf_op jit(solution)/shard_map/ppermute | solution.py:62
  12.5 6.9 %copy-start.12 = (bf16[2,128,512]{2,1,0:T(8,128)(2,1)}, bf16[2,128,512]{2,1,0:T(8,128)(2,1)S(1)}, u32[]{:S(2)}) copy-start(bf16[2,128,512]{2,1,0:T(8,128)(2,1)S(1)} %collective-permute-done.refs_1_) | copy-start | bytes 786436
  15.5 4.0 %copy-start.13 = (bf16[2,128,512]{2,1,0:T(8,128)(2,1)}, bf16[2,128,512]{2,1,0:T(8,128)(2,1)S(1)}, u32[]{:S(2)}) copy-start(bf16[2,128,512]{2,1,0:T(8,128)(2,1)S(1)} %collective-permute-done.1.refs_2_) | copy-start | bytes 786436
  19.4 0.7 copy-start.14
  20.1 7.8 %copy-start.31 = (bf16[2,128,512]{2,1,0:T(8,128)(2,1)S(1)}, bf16[2,128,512]{2,1,0:T(8,128)(2,1)}, u32[]{:S(2)}) copy-start(bf16[2,128,512]{2,1,0:T(8,128)(2,1)} %get-tuple-element.77) | copy-start | bytes 786436
  20.1 9.3 %copy-start.30 = (bf16[2,128,512]{2,1,0:T(8,128)(2,1)S(1)}, bf16[2,128,512]{2,1,0:T(8,128)(2,1)}, u32[]{:S(2)}) copy-start(bf16[2,128,512]{2,1,0:T(8,128)(2,1)} %get-tuple-element.78) | copy-start | bytes 786436
  20.1 27.6 %copy-start.29 = (bf16[2,128,512]{2,1,0:T(8,128)(2,1)S(1)}, bf16[2,128,512]{2,1,0:T(8,128)(2,1)}, u32[]{:S(2)}) copy-start(bf16[2,128,512]{2,1,0:T(8,128)(2,1)} %get-tuple-element.90) | copy-start | bytes 786436
  20.2 29.1 %copy-start.28 = (bf16[2,128,512]{2,1,0:T(8,128)(2,1)S(1)}, bf16[2,128,512]{2,1,0:T(8,128)(2,1)}, u32[]{:S(2)}) copy-start(bf16[2,128,512]{2,1,0:T(8,128)(2,1)} %get-tuple-element.91) | copy-start | bytes 786436
  20.2 30.6 %copy-start.27 = (bf16[2,128,512]{2,1,0:T(8,128)(2,1)S(1)}, bf16[2,128,512]{2,1,0:T(8,128)(2,1)}, u32[]{:S(2)}) copy-start(bf16[2,128,512]{2,1,0:T(8,128)(2,1)} %get-tuple-element.92) | copy-start | bytes 786436
  20.2 43.1 %copy-start.6 = (bf16[2,128,512]{2,1,0:T(8,128)(2,1)S(1)}, bf16[2,128,512]{2,1,0:T(8,128)(2,1)}, u32[]{:S(2)}) copy-start(bf16[2,128,512]{2,1,0:T(8,128)(2,1)} %get-tuple-element.89.refs_0_) | copy-start | bytes 786436
  20.2 43.1 %copy-start.7 = (s32[4]{0:T(128)S(1)}, s32[4]{0:T(128)}, u32[]{:S(2)}) copy-start(s32[4]{0:T(128)} %docs.3) | copy-start | bytes 52
  20.2 60.1 %copy-start.5 = (bf16[2,128,512]{2,1,0:T(8,128)(2,1)S(1)}, bf16[2,128,512]{2,1,0:T(8,128)(2,1)}, u32[]{:S(2)}) copy-start(bf16[2,128,512]{2,1,0:T(8,128)(2,1)} %get-tuple-element.79.refs_0_) | copy-start | bytes 786436
  22.5 25.2 %collective-permute-start.3 = (bf16[4,2,128,512]{3,2,1,0:T(8,128)(2,1)}, bf16[4,2,128,512]{3,2,1,0:T(8,128)(2,1)S(1)}, u32[]{:S(2)}, u32[]{:S(2)}) collective-permute-start(bf16[4,2,128,512]{3,2,1,0:T(8,128)(2,1)} %gather_keys.1.refs_4_), channel_id=1, source_target_pairs={{0,8},{1,9},{2,10},{3,11},{4,12},{5,13},{6,14},{7,15},{8,16},{9,17... | collective-permute-start | bytes 3145736 | tf_op jit(solution)/shard_map/ppermute | solution.py:68
  26.2 21.5 %collective-permute-start.4 = (bf16[4,2,128,512]{3,2,1,0:T(8,128)(2,1)}, bf16[4,2,128,512]{3,2,1,0:T(8,128)(2,1)S(1)}, u32[]{:S(2)}, u32[]{:S(2)}) collective-permute-start(bf16[4,2,128,512]{3,2,1,0:T(8,128)(2,1)} %gather_keys.1.refs_4_), channel_id=1, source_target_pairs={{0,2},{1,3},{2,0},{3,1},{4,6},{5,7},{6,4},{7,5},{8,10},{9,11},{10,... | collective-permute-start | bytes 3145736 | tf_op jit(solution)/shard_map/ppermute | solution.py:65
  26.3 8.9 %collective-permute-start.5 = (bf16[2,128,512]{2,1,0:T(8,128)(2,1)}, bf16[2,128,512]{2,1,0:T(8,128)(2,1)S(1)}, u32[]{:S(2)}, u32[]{:S(2)}) collective-permute-start(bf16[2,128,512]{2,1,0:T(8,128)(2,1)} %get-tuple-element.76), channel_id=1, source_target_pairs={{0,1},{1,0},{2,3},{3,2},{4,5},{5,4},{6,7},{7,6},{8,9},{9,8},{10,11... | collective-permute-start | bytes 786440 | tf_op jit(solution)/shard_map/ppermute | solution.py:62
  27.9 9.2 %collective-permute-start.6 = (bf16[2,128,512]{2,1,0:T(8,128)(2,1)S(1)}, bf16[2,128,512]{2,1,0:T(8,128)(2,1)S(1)}, u32[]{:S(2)}, u32[]{:S(2)}) collective-permute-start(bf16[2,128,512]{2,1,0:T(8,128)(2,1)S(1)} %copy-done.31), channel_id=1, source_target_pairs={{0,4},{1,5},{2,6},{3,7},{4,0},{5,1},{6,2},{7,3},{8,12},{9,13},{10,... | collective-permute-start | bytes 786440 | tf_op jit(solution)/shard_map/ppermute | solution.py:62
  29.4 12.4 %collective-permute-start.7 = (bf16[2,128,512]{2,1,0:T(8,128)(2,1)S(1)}, bf16[2,128,512]{2,1,0:T(8,128)(2,1)S(1)}, u32[]{:S(2)}, u32[]{:S(2)}) collective-permute-start(bf16[2,128,512]{2,1,0:T(8,128)(2,1)S(1)} %copy-done.30), channel_id=1, source_target_pairs={{0,5},{1,4},{2,7},{3,6},{4,1},{5,0},{6,3},{7,2},{8,13},{9,12},{10,... | collective-permute-start | bytes 786440 | tf_op jit(solution)/shard_map/ppermute | solution.py:62
  47.7 15.5 %collective-permute-start.8 = (bf16[4,2,128,512]{3,2,1,0:T(8,128)(2,1)S(1)}, bf16[4,2,128,512]{3,2,1,0:T(8,128)(2,1)S(1)}, u32[]{:S(2)}, u32[]{:S(2)}) collective-permute-start(bf16[4,2,128,512]{3,2,1,0:T(8,128)(2,1)S(1)} %collective-permute-done.3.refs_6_), channel_id=1, source_target_pairs={{0,2},{1,3},{2,0},{3,1},{4,6},{5,7},{6,4},{7,5},{8,10},{9,11},{10,... | collective-permute-start | bytes 3145736 | tf_op jit(solution)/shard_map/ppermute | solution.py:65
  47.7 8.7 %collective-permute-start.12 = (bf16[2,128,512]{2,1,0:T(8,128)(2,1)S(1)}, bf16[2,128,512]{2,1,0:T(8,128)(2,1)S(1)}, u32[]{:S(2)}, u32[]{:S(2)}) collective-permute-start(bf16[2,128,512]{2,1,0:T(8,128)(2,1)S(1)} %copy-done.29), channel_id=1, source_target_pairs={{0,1},{1,0},{2,3},{3,2},{4,5},{5,4},{6,7},{7,6},{8,9},{9,8},{10,11... | collective-permute-start | bytes 786440 | tf_op jit(solution)/shard_map/ppermute | solution.py:62
  49.3 9.2 %collective-permute-start.13 = (bf16[2,128,512]{2,1,0:T(8,128)(2,1)S(1)}, bf16[2,128,512]{2,1,0:T(8,128)(2,1)S(1)}, u32[]{:S(2)}, u32[]{:S(2)}) collective-permute-start(bf16[2,128,512]{2,1,0:T(8,128)(2,1)S(1)} %copy-done.28), channel_id=1, source_target_pairs={{0,4},{1,5},{2,6},{3,7},{4,0},{5,1},{6,2},{7,3},{8,12},{9,13},{10,... | collective-permute-start | bytes 786440 | tf_op jit(solution)/shard_map/ppermute | solution.py:62
  50.8 12.4 %collective-permute-start.14 = (bf16[2,128,512]{2,1,0:T(8,128)(2,1)S(1)}, bf16[2,128,512]{2,1,0:T(8,128)(2,1)S(1)}, u32[]{:S(2)}, u32[]{:S(2)}) collective-permute-start(bf16[2,128,512]{2,1,0:T(8,128)(2,1)S(1)} %copy-done.27), channel_id=1, source_target_pairs={{0,5},{1,4},{2,7},{3,6},{4,1},{5,0},{6,3},{7,2},{8,13},{9,12},{10,... | collective-permute-start | bytes 786440 | tf_op jit(solution)/shard_map/ppermute | solution.py:62
  63.2 1.2 copy-start.1
  78.6 1.0 copy-start.2
  79.6 0.7 copy-start.3
  80.3 15.2 %collective-permute-start.25 = (bf16[4,2,128,256]{3,2,1,0:T(8,128)(2,1)S(1)}, bf16[4,2,128,256]{3,2,1,0:T(8,128)(2,1)S(1)}, u32[]{:S(2)}, u32[]{:S(2)}) collective-permute-start(bf16[4,2,128,256]{3,2,1,0:T(8,128)(2,1)S(1)} %get-tuple-element.108), channel_id=1, source_target_pairs={{0,2},{1,3},{2,0},{3,1},{4,6},{5,7},{6,4},{7,5},{8,10},{9,11},{10,... | collective-permute-start | bytes 1572872 | tf_op jit(solution)/shard_map/ppermute | solution.py:65
  94.4 1.3 copy-start
  94.4 1.3 copy-start.4
  94.5 2.6 %collective-permute-start.19 = (bf16[4,2,128,256]{3,2,1,0:T(8,128)(2,1)S(1)}, bf16[4,2,128,256]{3,2,1,0:T(8,128)(2,1)S(1)}, u32[]{:S(2)}, u32[]{:S(2)}) collective-permute-start(bf16[4,2,128,256]{3,2,1,0:T(8,128)(2,1)S(1)} %get-tuple-element.100), channel_id=1, source_target_pairs={{0,2},{1,3},{2,0},{3,1},{4,6},{5,7},{6,4},{7,5},{8,10},{9,11},{10,... | collective-permute-start | bytes 1572872 | tf_op jit(solution)/shard_map/ppermute | solution.py:65
  95.0 5.0 %collective-permute-start.24 = (bf16[4,2,128,256]{3,2,1,0:T(8,128)(2,1)S(1)}, bf16[4,2,128,256]{3,2,1,0:T(8,128)(2,1)S(1)}, u32[]{:S(2)}, u32[]{:S(2)}) collective-permute-start(bf16[4,2,128,256]{3,2,1,0:T(8,128)(2,1)S(1)} %get-tuple-element.106), channel_id=1, source_target_pairs={{0,2},{1,3},{2,0},{3,1},{4,6},{5,7},{6,4},{7,5},{8,10},{9,11},{10,... | collective-permute-start | bytes 1572872 | tf_op jit(solution)/shard_map/ppermute | solution.py:65
  95.1 24.5 %collective-permute-start.18 = (bf16[4,2,128,256]{3,2,1,0:T(8,128)(2,1)S(1)}, bf16[4,2,128,256]{3,2,1,0:T(8,128)(2,1)S(1)}, u32[]{:S(2)}, u32[]{:S(2)}) collective-permute-start(bf16[4,2,128,256]{3,2,1,0:T(8,128)(2,1)S(1)} %get-tuple-element.98), channel_id=1, source_target_pairs={{0,2},{1,3},{2,0},{3,1},{4,6},{5,7},{6,4},{7,5},{8,10},{9,11},{10,... | collective-permute-start | bytes 1572872 | tf_op jit(solution)/shard_map/ppermute | solution.py:65
  95.7 17.0 %collective-permute-start.26 = (bf16[4,2,128,256]{3,2,1,0:T(8,128)(2,1)S(1)}, bf16[4,2,128,256]{3,2,1,0:T(8,128)(2,1)S(1)}, u32[]{:S(2)}, u32[]{:S(2)}) collective-permute-start(bf16[4,2,128,256]{3,2,1,0:T(8,128)(2,1)S(1)} %add_convert_fusion), channel_id=1, source_target_pairs={{8,0},{9,1},{10,2},{11,3},{12,4},{13,5},{14,6},{15,7},{16,8},{17,9... | collective-permute-start | bytes 1572872 | tf_op jit(solution)/shard_map/ppermute | solution.py:68
  97.1 26.4 %collective-permute-start.20 = (bf16[4,2,128,256]{3,2,1,0:T(8,128)(2,1)S(1)}, bf16[4,2,128,256]{3,2,1,0:T(8,128)(2,1)S(1)}, u32[]{:S(2)}, u32[]{:S(2)}) collective-permute-start(bf16[4,2,128,256]{3,2,1,0:T(8,128)(2,1)S(1)} %add_convert_fusion.1), channel_id=1, source_target_pairs={{8,0},{9,1},{10,2},{11,3},{12,4},{13,5},{14,6},{15,7},{16,8},{17,9... | collective-permute-start | bytes 1572872 | tf_op jit(solution)/shard_map/ppermute | solution.py:68
  98.4 19.1 %collective-permute-start.15 = (bf16[1,128,512]{2,1,0:T(8,128)(2,1)S(1)}, bf16[1,128,512]{2,1,0:T(8,128)(2,1)S(1)}, u32[]{:S(2)}, u32[]{:S(2)}) collective-permute-start(bf16[1,128,512]{2,1,0:T(8,128)(2,1)S(1)} %get-tuple-element.94), channel_id=1, source_target_pairs={{0,1},{1,0},{2,3},{3,2},{4,5},{5,4},{6,7},{7,6},{8,9},{9,8},{10,11... | collective-permute-start | bytes 393224 | tf_op jit(solution)/shard_map/ppermute | solution.py:62
  100.0 15.1 %copy-start.10 = (bf16[4,2,128,256]{3,2,1,0:T(8,128)(2,1)}, bf16[4,2,128,256]{3,2,1,0:T(8,128)(2,1)S(1)}, u32[]{:S(2)}) copy-start(bf16[4,2,128,256]{3,2,1,0:T(8,128)(2,1)S(1)} %collective-permute-done.24.far_ref) | copy-start | bytes 1572868
  100.0 18.1 %collective-permute-start.16 = (bf16[1,128,512]{2,1,0:T(8,128)(2,1)S(1)}, bf16[1,128,512]{2,1,0:T(8,128)(2,1)S(1)}, u32[]{:S(2)}, u32[]{:S(2)}) collective-permute-start(bf16[1,128,512]{2,1,0:T(8,128)(2,1)S(1)} %get-tuple-element.95), channel_id=1, source_target_pairs={{0,4},{1,5},{2,6},{3,7},{4,0},{5,1},{6,2},{7,3},{8,12},{9,13},{10,... | collective-permute-start | bytes 393224 | tf_op jit(solution)/shard_map/ppermute | solution.py:62
  112.7 2.5 %copy-start.11 = (bf16[4,2,128,256]{3,2,1,0:T(8,128)(2,1)}, bf16[4,2,128,256]{3,2,1,0:T(8,128)(2,1)S(1)}, u32[]{:S(2)}) copy-start(bf16[4,2,128,256]{3,2,1,0:T(8,128)(2,1)S(1)} %collective-permute-done.26.later_ref) | copy-start | bytes 1572868
  112.7 14.8 %collective-permute-start.17 = (bf16[1,128,512]{2,1,0:T(8,128)(2,1)S(1)}, bf16[1,128,512]{2,1,0:T(8,128)(2,1)S(1)}, u32[]{:S(2)}, u32[]{:S(2)}) collective-permute-start(bf16[1,128,512]{2,1,0:T(8,128)(2,1)S(1)} %get-tuple-element.96), channel_id=1, source_target_pairs={{0,5},{1,4},{2,7},{3,6},{4,1},{5,0},{6,3},{7,2},{8,13},{9,12},{10,... | collective-permute-start | bytes 393224 | tf_op jit(solution)/shard_map/ppermute | solution.py:62
  117.5 9.9 %copy-start.15 = (bf16[1,128,512]{2,1,0:T(8,128)(2,1)}, bf16[1,128,512]{2,1,0:T(8,128)(2,1)S(1)}, u32[]{:S(2)}) copy-start(bf16[1,128,512]{2,1,0:T(8,128)(2,1)S(1)} %collective-permute-done.15.refs_5_) | copy-start | bytes 393220
  117.5 11.5 %collective-permute-start.10 = (bf16[1,128,512]{2,1,0:T(8,128)(2,1)S(1)}, bf16[1,128,512]{2,1,0:T(8,128)(2,1)S(1)}, u32[]{:S(2)}, u32[]{:S(2)}) collective-permute-start(bf16[1,128,512]{2,1,0:T(8,128)(2,1)S(1)} %get-tuple-element.87), channel_id=1, source_target_pairs={{0,4},{1,5},{2,6},{3,7},{4,0},{5,1},{6,2},{7,3},{8,12},{9,13},{10,... | collective-permute-start | bytes 393224 | tf_op jit(solution)/shard_map/ppermute | solution.py:62
  118.1 9.4 %copy-start.16 = (bf16[1,128,512]{2,1,0:T(8,128)(2,1)}, bf16[1,128,512]{2,1,0:T(8,128)(2,1)S(1)}, u32[]{:S(2)}) copy-start(bf16[1,128,512]{2,1,0:T(8,128)(2,1)S(1)} %collective-permute-done.16.refs_6_) | copy-start | bytes 393220
  118.1 11.8 %collective-permute-start.11 = (bf16[1,128,512]{2,1,0:T(8,128)(2,1)S(1)}, bf16[1,128,512]{2,1,0:T(8,128)(2,1)S(1)}, u32[]{:S(2)}, u32[]{:S(2)}) collective-permute-start(bf16[1,128,512]{2,1,0:T(8,128)(2,1)S(1)} %get-tuple-element.88), channel_id=1, source_target_pairs={{0,5},{1,4},{2,7},{3,6},{4,1},{5,0},{6,3},{7,2},{8,13},{9,12},{10,... | collective-permute-start | bytes 393224 | tf_op jit(solution)/shard_map/ppermute | solution.py:62
  119.6 5.4 %copy-start.8 = (bf16[4,2,128,256]{3,2,1,0:T(8,128)(2,1)}, bf16[4,2,128,256]{3,2,1,0:T(8,128)(2,1)S(1)}, u32[]{:S(2)}) copy-start(bf16[4,2,128,256]{3,2,1,0:T(8,128)(2,1)S(1)} %collective-permute-done.18.far_ref) | copy-start | bytes 1572868
  119.6 11.6 %collective-permute-start.9 = (bf16[1,128,512]{2,1,0:T(8,128)(2,1)S(1)}, bf16[1,128,512]{2,1,0:T(8,128)(2,1)S(1)}, u32[]{:S(2)}, u32[]{:S(2)}) collective-permute-start(bf16[1,128,512]{2,1,0:T(8,128)(2,1)S(1)} %get-tuple-element.86), channel_id=1, source_target_pairs={{0,1},{1,0},{2,3},{3,2},{4,5},{5,4},{6,7},{7,6},{8,9},{9,8},{10,11... | collective-permute-start | bytes 393224 | tf_op jit(solution)/shard_map/ppermute | solution.py:62
  123.5 1.5 %copy-start.9 = (bf16[4,2,128,256]{3,2,1,0:T(8,128)(2,1)}, bf16[4,2,128,256]{3,2,1,0:T(8,128)(2,1)S(1)}, u32[]{:S(2)}) copy-start(bf16[4,2,128,256]{3,2,1,0:T(8,128)(2,1)S(1)} %collective-permute-done.20.later_ref) | copy-start | bytes 1572868
  123.5 9.1 %collective-permute-start.27 = (bf16[2,128,256]{2,1,0:T(8,128)(2,1)}, bf16[2,128,256]{2,1,0:T(8,128)(2,1)S(1)}, u32[]{:S(2)}, u32[]{:S(2)}) collective-permute-start(bf16[2,128,256]{2,1,0:T(8,128)(2,1)} %get-tuple-element.110), channel_id=1, source_target_pairs={{0,1},{1,0},{2,3},{3,2},{4,5},{5,4},{6,7},{7,6},{8,9},{9,8},{10,11... | collective-permute-start | bytes 393224 | tf_op jit(solution)/shard_map/ppermute | solution.py:62
  125.0 2.5 %copy-start.33 = (bf16[2,128,256]{2,1,0:T(8,128)(2,1)S(1)}, bf16[2,128,256]{2,1,0:T(8,128)(2,1)}, u32[]{:S(2)}) copy-start(bf16[2,128,256]{2,1,0:T(8,128)(2,1)} %get-tuple-element.111) | copy-start | bytes 393220
  125.0 4.1 %copy-start.32 = (bf16[2,128,256]{2,1,0:T(8,128)(2,1)S(1)}, bf16[2,128,256]{2,1,0:T(8,128)(2,1)}, u32[]{:S(2)}) copy-start(bf16[2,128,256]{2,1,0:T(8,128)(2,1)} %get-tuple-element.112) | copy-start | bytes 393220
  127.5 5.9 %copy-start.17 = (bf16[1,128,512]{2,1,0:T(8,128)(2,1)}, bf16[1,128,512]{2,1,0:T(8,128)(2,1)S(1)}, u32[]{:S(2)}) copy-start(bf16[1,128,512]{2,1,0:T(8,128)(2,1)S(1)} %collective-permute-done.17.refs_7_) | copy-start | bytes 393220
  127.5 8.3 %collective-permute-start.28 = (bf16[2,128,256]{2,1,0:T(8,128)(2,1)S(1)}, bf16[2,128,256]{2,1,0:T(8,128)(2,1)S(1)}, u32[]{:S(2)}, u32[]{:S(2)}) collective-permute-start(bf16[2,128,256]{2,1,0:T(8,128)(2,1)S(1)} %copy-done.33), channel_id=1, source_target_pairs={{0,4},{1,5},{2,6},{3,7},{4,0},{5,1},{6,2},{7,3},{8,12},{9,13},{10,... | collective-permute-start | bytes 393224 | tf_op jit(solution)/shard_map/ppermute | solution.py:62
  129.1 4.3 %copy-start.18 = (bf16[1,128,512]{2,1,0:T(8,128)(2,1)}, bf16[1,128,512]{2,1,0:T(8,128)(2,1)S(1)}, u32[]{:S(2)}) copy-start(bf16[1,128,512]{2,1,0:T(8,128)(2,1)S(1)} %collective-permute-done.10.refs_2_) | copy-start | bytes 393220
  129.1 7.7 %collective-permute-start.29 = (bf16[2,128,256]{2,1,0:T(8,128)(2,1)S(1)}, bf16[2,128,256]{2,1,0:T(8,128)(2,1)S(1)}, u32[]{:S(2)}, u32[]{:S(2)}) collective-permute-start(bf16[2,128,256]{2,1,0:T(8,128)(2,1)S(1)} %copy-done.32), channel_id=1, source_target_pairs={{0,5},{1,4},{2,7},{3,6},{4,1},{5,0},{6,3},{7,2},{8,13},{9,12},{10,... | collective-permute-start | bytes 393224 | tf_op jit(solution)/shard_map/ppermute | solution.py:62
  129.9 3.5 %copy-start.19 = (bf16[1,128,512]{2,1,0:T(8,128)(2,1)}, bf16[1,128,512]{2,1,0:T(8,128)(2,1)S(1)}, u32[]{:S(2)}) copy-start(bf16[1,128,512]{2,1,0:T(8,128)(2,1)S(1)} %collective-permute-done.11.refs_3_) | copy-start | bytes 393220
  129.9 7.5 %collective-permute-start.21 = (bf16[2,128,256]{2,1,0:T(8,128)(2,1)}, bf16[2,128,256]{2,1,0:T(8,128)(2,1)S(1)}, u32[]{:S(2)}, u32[]{:S(2)}) collective-permute-start(bf16[2,128,256]{2,1,0:T(8,128)(2,1)} %get-tuple-element.102), channel_id=1, source_target_pairs={{0,1},{1,0},{2,3},{3,2},{4,5},{5,4},{6,7},{7,6},{8,9},{9,8},{10,11... | collective-permute-start | bytes 393224 | tf_op jit(solution)/shard_map/ppermute | solution.py:62
  131.2 2.3 %copy-start.20 = (bf16[1,128,512]{2,1,0:T(8,128)(2,1)}, bf16[1,128,512]{2,1,0:T(8,128)(2,1)S(1)}, u32[]{:S(2)}) copy-start(bf16[1,128,512]{2,1,0:T(8,128)(2,1)S(1)} %collective-permute-done.9.refs_1_) | copy-start | bytes 393220
  131.2 8.2 %collective-permute-start.22 = (bf16[2,128,256]{2,1,0:T(8,128)(2,1)}, bf16[2,128,256]{2,1,0:T(8,128)(2,1)S(1)}, u32[]{:S(2)}, u32[]{:S(2)}) collective-permute-start(bf16[2,128,256]{2,1,0:T(8,128)(2,1)} %get-tuple-element.103), channel_id=1, source_target_pairs={{0,4},{1,5},{2,6},{3,7},{4,0},{5,1},{6,2},{7,3},{8,12},{9,13},{10,... | collective-permute-start | bytes 393224 | tf_op jit(solution)/shard_map/ppermute | solution.py:62
  132.7 3.1 %copy-start.21 = (bf16[2,128,256]{2,1,0:T(8,128)(2,1)}, bf16[2,128,256]{2,1,0:T(8,128)(2,1)S(1)}, u32[]{:S(2)}) copy-start(bf16[2,128,256]{2,1,0:T(8,128)(2,1)S(1)} %collective-permute-done.27.refs_5_) | copy-start | bytes 393220
  132.7 8.7 %collective-permute-start.23 = (bf16[2,128,256]{2,1,0:T(8,128)(2,1)}, bf16[2,128,256]{2,1,0:T(8,128)(2,1)S(1)}, u32[]{:S(2)}, u32[]{:S(2)}) collective-permute-start(bf16[2,128,256]{2,1,0:T(8,128)(2,1)} %get-tuple-element.104), channel_id=1, source_target_pairs={{0,5},{1,4},{2,7},{3,6},{4,1},{5,0},{6,3},{7,2},{8,13},{9,12},{10,... | collective-permute-start | bytes 393224 | tf_op jit(solution)/shard_map/ppermute | solution.py:62
  135.8 5.5 %copy-start.22 = (bf16[2,128,256]{2,1,0:T(8,128)(2,1)}, bf16[2,128,256]{2,1,0:T(8,128)(2,1)S(1)}, u32[]{:S(2)}) copy-start(bf16[2,128,256]{2,1,0:T(8,128)(2,1)S(1)} %collective-permute-done.28.refs_6_) | copy-start | bytes 393220
  136.8 4.5 %copy-start.23 = (bf16[2,128,256]{2,1,0:T(8,128)(2,1)}, bf16[2,128,256]{2,1,0:T(8,128)(2,1)S(1)}, u32[]{:S(2)}) copy-start(bf16[2,128,256]{2,1,0:T(8,128)(2,1)S(1)} %collective-permute-done.29.refs_7_) | copy-start | bytes 393220
  137.5 3.9 %copy-start.24 = (bf16[2,128,256]{2,1,0:T(8,128)(2,1)}, bf16[2,128,256]{2,1,0:T(8,128)(2,1)S(1)}, u32[]{:S(2)}) copy-start(bf16[2,128,256]{2,1,0:T(8,128)(2,1)S(1)} %collective-permute-done.21.refs_1_) | copy-start | bytes 393220
  139.3 2.0 %copy-start.25 = (bf16[2,128,256]{2,1,0:T(8,128)(2,1)}, bf16[2,128,256]{2,1,0:T(8,128)(2,1)S(1)}, u32[]{:S(2)}) copy-start(bf16[2,128,256]{2,1,0:T(8,128)(2,1)S(1)} %collective-permute-done.22.refs_2_) | copy-start | bytes 393220
  141.3 0.7 copy-start.26

commit v2 on v1

v2 whole, which is shorter than its diff:
```python
import itertools
import math

import jax
import jax.numpy as jnp
from jax import lax
from jax.experimental import pallas as pl
from jax.experimental.pallas import tpu as pltpu
from jax.sharding import PartitionSpec as P

QUERY_HEADS = 32
KEY_HEADS = 16
HEAD_SIZE = 128
WINDOW = 1024
GROUP = QUERY_HEADS // KEY_HEADS
AXES = ("seq", "tp")

attn_scale = 168.0 ** (-0.5)
masked_floor = -1e30

CHUNKS = 2
VMEM_LIMIT = 56 * 1024 * 1024
ANY = pl.BlockSpec(memory_space=pl.ANY)
VMEM = pl.BlockSpec(memory_space=pltpu.VMEM)
SMEM = pl.BlockSpec(memory_space=pltpu.SMEM)


class Plan:
    def __init__(self, rows):
        self.seq, self.tp = lax.axis_size("seq"), lax.axis_size("tp")
        self.rows = rows
        self.block = rows * self.tp
        self.slab = WINDOW // self.block
        self.cores = min(2, self.slab)
        self.ways = self.slab // self.cores
        self.groups = self.ways * self.tp
        self.key_heads = KEY_HEADS // self.groups
        self.chunks = min(CHUNKS, self.key_heads)
        self.heads = self.key_heads // self.chunks
        self.key_cols = self.heads * HEAD_SIZE
        self.query_cols = self.key_cols * GROUP
        self.pieces = self.slab * self.tp

    def place(self):
        seq, tp = lax.axis_index("seq"), lax.axis_index("tp")
        inner = lax.rem(seq, self.slab)
        core = lax.rem(inner, self.cores)
        return seq - inner, core, (inner // self.cores) * self.tp + tp

    def routes(self, move):
        pairs = []
        for seq in range(self.seq):
            for tp in range(self.tp):
                slab, inner = divmod(seq, self.slab)
                way, core = divmod(inner, self.cores)
                to_slab, to_core, to_group = move(slab, core, way * self.tp + tp)
                to_slab %= self.seq // self.slab
                target = (to_slab * self.slab + to_group // self.tp * self.cores + to_core) * self.tp + to_group % self.tp
                pairs.append((seq * self.tp + tp, target))
        return pairs

    def to_group(self, value, flip):
        return lax.ppermute(value, AXES, self.routes(lambda slab, core, group: (slab, core, group ^ flip)))

    def to_core(self, value):
        return lax.ppermute(value, AXES, self.routes(lambda slab, core, group: (slab, self.cores - 1 - core, group)))

    def to_slab(self, value, step):
        return lax.ppermute(value, AXES, self.routes(lambda slab, core, group: (slab + step, core, group)))


def run_copies(copies):
    for copy in copies:
        copy.start()
    for copy in copies:
        copy.wait()


def traffic(count):
    return pl.CostEstimate(flops=0, bytes_accessed=count, transcendentals=0)


def columns(start, width):
    return pl.ds(pl.multiple_of(start, HEAD_SIZE), width)


def split_columns(plan, arrays, width, chunks, name, after=()):
    chunk_width = width // chunks

    def kernel(*refs):
        sources, targets, sem = refs[: len(arrays)], refs[len(arrays) + len(after) : -1], refs[-1]
        _, _, group = plan.place()
        copies = []
        for chunk in range(chunks):
            for flip in range(plan.groups):
                start = (group ^ flip) * width + chunk * chunk_width
                for index, source in enumerate(sources):
                    copies.append(
                        pltpu.make_async_copy(
                            source.at[:, columns(start, chunk_width)],
                            targets[chunk * plan.groups + flip].at[index],
                            sem.at[len(copies)],
                        )
                    )
        run_copies(copies)

    count = chunks * plan.groups
    shape = jax.ShapeDtypeStruct((len(arrays), plan.rows, chunk_width), jnp.bfloat16)
    out = pl.pallas_call(
        kernel,
        out_shape=[shape] * count,
        in_specs=[ANY] * (len(arrays) + len(after)),
        out_specs=[VMEM] * count,
        scratch_shapes=[pltpu.SemaphoreType.DMA((count * len(arrays),))],
        cost_estimate=traffic(2 * sum(array.nbytes for array in arrays)),
        name=name,
    )(*arrays, *after)
    return [out[chunk * plan.groups : (chunk + 1) * plan.groups] for chunk in range(chunks)]


def join_columns(plan, chunked, count, width, name):
    chunks = len(chunked)
    chunk_width = width // chunks
    flat = [piece for pieces in chunked for piece in pieces]

    def kernel(*refs):
        sources, targets, sem = refs[: len(flat)], refs[len(flat) : -1], refs[-1]
        _, _, group = plan.place()
        copies = []
        for chunk in range(chunks):
            for flip in range(plan.groups):
                start = (group ^ flip) * width + chunk * chunk_width
                for index, target in enumerate(targets):
                    copies.append(
                        pltpu.make_async_copy(
                            sources[chunk * plan.groups + flip].at[index],
                            target.at[:, columns(start, chunk_width)],
                            sem.at[len(copies)],
                        )
                    )
        run_copies(copies)

    return pl.pallas_call(
        kernel,
        out_shape=[jax.ShapeDtypeStruct((plan.rows, width * plan.groups), jnp.bfloat16)] * count,
        in_specs=[ANY] * len(flat),
        out_specs=[VMEM] * count,
        scratch_shapes=[pltpu.SemaphoreType.DMA((len(flat) * count,))],
        cost_estimate=traffic(2 * sum(piece.nbytes for piece in flat)),
        name=name,
    )(*flat)


def backward(plan, chunk, first_head, heads, doc_lengths, query_pieces, key_pieces, earlier, after):
    tiles = plan.slab + 1
    block, groups, tp, cores = plan.block, plan.groups, plan.tp, plan.cores
    wide = GROUP * block
    query_width = HEAD_SIZE * GROUP
    key_cols, query_cols = heads * HEAD_SIZE, heads * query_width
    done_cols = first_head * query_width
    exponent_scale = attn_scale * math.log2(math.e)

    def kernel(docs, *refs):
        pieces, refs = refs[:groups], refs[groups:]
        key_refs, refs = refs[: 4 * groups], refs[4 * groups :]
        done, refs = refs[: len(earlier)], refs[len(earlier) + len(after) :]
        query_out, refs = refs[:groups], refs[groups:]
        mine, far, q_s, o_s, k_s, v_s, dq_s, dk_s, dv_s, score_s, prob_grad_s, prob_s, grad_s, sem = refs
        slab_seq, core, group = plan.place()

        copies = []

        def add(source, target):
            copies.append(pltpu.make_async_copy(source, target, sem.at[len(copies)]))

        for flip, piece in enumerate(pieces):
            add(piece.at[0, :, pl.ds(done_cols, query_cols)], q_s.at[group ^ flip])
            add(piece.at[1, :, pl.ds(done_cols, query_cols)], o_s.at[group ^ flip])
        cols = pl.ds((chunk * plan.heads + first_head) * HEAD_SIZE, key_cols)
        for source, (late, away, flip) in zip(key_refs, itertools.product((1, 0), (0, 1), range(groups))):
            side = core + away * (cores - 1 - 2 * core)
            way, lane = (group ^ flip) // tp, lax.rem(group ^ flip, tp)
            start = late * plan.pieces + (way * cores + side) * tp + lane
            for index, target in enumerate((k_s, v_s)):
                add(source.at[index, :, cols], target.at[start])
        for source, target in zip(done, query_out):
            add(source.at[0, :, pl.ds(0, done_cols)], target.at[0, :, pl.ds(0, done_cols)])
        for copy in copies:
            copy.start()
        dk_s[...] = jnp.zeros_like(dk_s)
        dv_s[...] = jnp.zeros_like(dv_s)
        for copy in copies:
            copy.wait()

        def step(index, carry):
            head, way = index // plan.ways, lax.rem(index, plan.ways)
            key_at = (way * cores + core) * tp
            head_cols = columns(head * HEAD_SIZE, HEAD_SIZE)
            rows_at = pl.ds(way * tp, tp)

            def both(ref):
                parts = [
                    ref[rows_at, :, columns((head * GROUP + member) * HEAD_SIZE, HEAD_SIZE)].reshape(block, HEAD_SIZE)
                    for member in range(GROUP)
                ]
                return jnp.concatenate(parts, axis=0)

            queries, grads = both(q_s), both(o_s)
            inner = lax.broadcasted_iota(jnp.int32, (1, block), 1)
            inner = jnp.concatenate([inner] * GROUP, axis=1)
            first = (slab_seq + way * cores + core) * block
            position = inner + first
            lowest = position - (WINDOW - 1)
            start = jnp.int32(0)
            for doc in range(docs.shape[0]):
                lowest = jnp.where(position >= start, jnp.maximum(lowest, start), lowest)
                start = start + docs[doc]
            lowest = lowest - (first - WINDOW)

            def key_rows(ref, tile):
                return ref[pl.ds(key_at + tile * tp, tp), :, head_cols].reshape(block, HEAD_SIZE)

            def tile_rows(tile):
                return pl.ds(tile * block, block)

            peak = jnp.full((1, wide), masked_floor, jnp.float32)
            for tile in range(tiles):
                scores = lax.dot_general(
                    key_rows(k_s, tile), queries, (((1,), (1,)), ((), ())), preferred_element_type=jnp.float32
                )
                row = lax.broadcasted_iota(jnp.int32, (block, wide), 0)
                allowed = row >= lowest - tile * block
                if tile == tiles - 1:
                    allowed = allowed & (row <= inner)
                scores = jnp.where(allowed, scores, masked_floor)
                peak = jnp.maximum(peak, jnp.max(scores, axis=0, keepdims=True))
                score_s[tile_rows(tile), :] = scores
            peak = peak * exponent_scale
            total = jnp.zeros((1, wide), jnp.float32)
            delta = jnp.zeros((1, wide), jnp.float32)
            for tile in range(tiles):
                raised = jnp.exp2(score_s[tile_rows(tile), :] * exponent_scale - peak)
                prob_grad = lax.dot_general(
                    key_rows(v_s, tile), grads, (((1,), (1,)), ((), ())), preferred_element_type=jnp.float32
                )
                total = total + jnp.sum(raised, axis=0, keepdims=True)
                delta = delta + jnp.sum(raised * prob_grad, axis=0, keepdims=True)
                score_s[tile_rows(tile), :] = raised
                prob_grad_s[tile_rows(tile), :] = prob_grad
            inverse = 1.0 / total
            delta = delta * inverse
            for tile in range(tiles):
                probs = score_s[tile_rows(tile), :] * inverse
                prob_s[tile_rows(tile), :] = probs.astype(jnp.bfloat16)
                grad_scores = probs * (prob_grad_s[tile_rows(tile), :] - delta) * attn_scale
                grad_s[tile_rows(tile), :] = grad_scores.astype(jnp.bfloat16)
            at = pl.ds(key_at, tiles * tp)
            shape = (tiles * tp, plan.rows, HEAD_SIZE)
            dv_s[at, :, head_cols] += jnp.dot(prob_s[...], grads, preferred_element_type=jnp.float32).reshape(shape)
            dk_s[at, :, head_cols] += jnp.dot(grad_s[...], queries, preferred_element_type=jnp.float32).reshape(shape)
            query_sum = lax.dot_general(
                k_s[at, :, head_cols].reshape(tiles * block, HEAD_SIZE),
                grad_s[...],
                (((0,), (0,)), ((), ())),
                preferred_element_type=jnp.float32,
            )
            query_rows = query_sum.T.astype(jnp.bfloat16)
            for member in range(GROUP):
                dq_s[rows_at, :, columns((head * GROUP + member) * HEAD_SIZE, HEAD_SIZE)] = query_rows[
                    member * block : (member + 1) * block
                ].reshape(tp, plan.rows, HEAD_SIZE)
            return carry

        lax.fori_loop(0, heads * plan.ways, step, 0)
        for flip in range(groups):
            query_out[flip][0, :, done_cols:] = dq_s[group ^ flip]
        for late, away, piece in itertools.product((0, 1), (0, 1), range(groups)):
            side = core + away * (cores - 1 - 2 * core)
            at = late * plan.pieces + (piece // tp * cores + side) * tp + piece % tp
            for index, source in enumerate((dk_s, dv_s)):
                target = (mine, far)[away]
                target[late, piece, index] = source[at].astype(target.dtype)

    part = (2, groups, 2, plan.rows, key_cols)
    bf, fl = jnp.bfloat16, jnp.float32
    span = 2 * plan.pieces
    pairs = tiles * block * wide * heads * plan.ways
    out = pl.pallas_call(
        kernel,
        out_shape=[jax.ShapeDtypeStruct((1, plan.rows, done_cols + query_cols), bf)] * groups
        + [jax.ShapeDtypeStruct(part, fl), jax.ShapeDtypeStruct(part, bf)],
        in_specs=[SMEM] + [ANY] * (5 * groups + len(earlier) + len(after)),
        out_specs=[VMEM] * (groups + 2),
        scratch_shapes=[
            pltpu.VMEM((groups, plan.rows, query_cols), bf),
            pltpu.VMEM((groups, plan.rows, query_cols), bf),
            pltpu.VMEM((span, plan.rows, key_cols), bf),
            pltpu.VMEM((span, plan.rows, key_cols), bf),
            pltpu.VMEM((groups, plan.rows, query_cols), bf),
            pltpu.VMEM((span, plan.rows, key_cols), fl),
            pltpu.VMEM((span, plan.rows, key_cols), fl),
            pltpu.VMEM((tiles * block, wide), fl),
            pltpu.VMEM((tiles * block, wide), fl),
            pltpu.VMEM((tiles * block, wide), bf),
            pltpu.VMEM((tiles * block, wide), bf),
            pltpu.SemaphoreType.DMA((10 * groups + len(earlier),)),
        ],
        compiler_params=pltpu.CompilerParams(vmem_limit_bytes=VMEM_LIMIT),
        cost_estimate=pl.CostEstimate(flops=160 * pairs * HEAD_SIZE, bytes_accessed=6 << 20, transcendentals=pairs),
        name="backward",
    )(doc_lengths, *query_pieces, *key_pieces, *earlier, *after)
    return out[:groups], out[groups], out[groups + 1]


def half(array, late):
    block = (1,) + array.shape[1:]
    return pl.BlockSpec(block, lambda step: (late,) + (0,) * (len(block) - 1))


def add_before(plan, mine, far, after):
    parts = len(mine)

    def kernel(*refs):
        target = refs[-1]
        at = 0
        for mine_ref, far_ref in zip(refs[:parts], refs[parts : 2 * parts]):
            width = mine_ref.shape[-1]
            total = mine_ref[0] + far_ref[0].astype(jnp.float32)
            target[:, :, :, at : at + width] = total.astype(jnp.bfloat16)
            at += width

    shape = mine[0].shape[1:-1] + (plan.key_cols,)
    return pl.pallas_call(
        kernel,
        grid=(1,),
        out_shape=jax.ShapeDtypeStruct(shape, jnp.bfloat16),
        in_specs=[half(array, 0) for array in (*mine, *far)] + [ANY] * len(after),
        out_specs=pl.BlockSpec(shape, lambda step: (0,) * len(shape)),
        cost_estimate=traffic(8 * math.prod(shape)),
        name="add_before",
    )(*mine, *far, *after)


def add_up(plan, mine, far, later):
    parts = len(mine)

    def kernel(*refs):
        later_ref, targets = refs[2 * parts], refs[2 * parts + 1 :]
        _, _, group = plan.place()
        for flip, target in enumerate(targets):
            piece = group ^ flip
            at = 0
            for mine_ref, far_ref in zip(refs[:parts], refs[parts : 2 * parts]):
                width = mine_ref.shape[-1]
                total = mine_ref[0, piece] + far_ref[0, piece].astype(jnp.float32)
                total = total + later_ref[piece, :, :, at : at + width].astype(jnp.float32)
                target[:, :, at : at + width] = total.astype(jnp.bfloat16)
                at += width

    shape = later.shape[1:]
    return pl.pallas_call(
        kernel,
        grid=(1,),
        out_shape=[jax.ShapeDtypeStruct(shape, jnp.bfloat16)] * plan.groups,
        in_specs=[half(array, 1) for array in (*mine, *far)] + [pl.BlockSpec(later.shape, lambda step: (0,) * later.ndim)],
        out_specs=[pl.BlockSpec(shape, lambda step: (0,) * len(shape))] * plan.groups,
        cost_estimate=traffic(10 * math.prod(later.shape)),
        name="add_up",
    )(*mine, *far, later)


def per_device(queries, key_states, value_state_rows, out_grad, doc_lengths):
    plan = Plan(queries.shape[0])
    key_width = KEY_HEADS * HEAD_SIZE // plan.groups
    query_width = QUERY_HEADS * HEAD_SIZE // plan.groups

    def exchange(pieces):
        return [pieces[0]] + [plan.to_group(pieces[flip], flip) for flip in range(1, plan.groups)]

    key_parts = split_columns(plan, (key_states, value_state_rows), key_width, 1, "split_keys")[0]
    query_chunks = split_columns(
        plan, (queries, out_grad), query_width, plan.chunks, "split_queries", after=(key_parts[0],)
    )
    own = exchange(key_parts)
    arrived = [exchange(parts) for parts in query_chunks]
    before = [plan.to_slab(piece, 1) for piece in own]
    key_pieces = own + [plan.to_core(piece) for piece in own] + before + [plan.to_core(piece) for piece in before]
    query_results, key_results, after = [], [], ()
    for chunk in range(plan.chunks):
        split = chunk > 0 and plan.heads > 1
        calls = [(head, 1) for head in range(plan.heads)] if split else [(0, plan.heads)]
        query_out, mine, far = (), [], []
        for first_head, heads in calls:
            query_out, mine_part, far_part = backward(
                plan, chunk, first_head, heads, doc_lengths, arrived[chunk], key_pieces, query_out, after
            )
            after = (far_part,) if not far and chunk == 0 else after
            mine.append(mine_part)
            far.append(plan.to_core(far_part))
            if split and len(far) == 1:
                after = sent
        before_sum = add_before(plan, mine, far, (later,) if key_results else ())
        later = plan.to_slab(before_sum, -1)
        query_results.append(exchange(query_out))
        key_results.append(exchange(add_up(plan, mine, far, later)))
        sent = (before_sum, *query_results[-1][1:])
    (query_grad,) = join_columns(plan, query_results, 1, query_width, "join_queries")
    key_gradient, value_gradient = join_columns(plan, key_results, 2, key_width, "join_keys")
    return query_grad, key_gradient, value_gradient


def solution(mesh):
    split = P(("seq", "tp"), None)
    return jax.shard_map(
        per_device,
        mesh=mesh,
        in_specs=(split, split, split, split, P()),
        out_specs=(split, split, split),
        check_vma=False,
    )
```

time: 145 us -> 129 us (0.89)
  waiting for transfers between devices: 57.7 us -> 27.7 us
  Pallas kernels: 45.5 us -> 52.9 us
  starting transfers between devices: 35.5 us -> 41.6 us
    ppermute x21, waiting for transfers between devices: 38.2 us -> 11.4 us  [to_group(): lax.ppermute(value, AXES, self.routes(lambda slab, core, group: (slab, co...]
    pallas_call x7 -> x9, Pallas kernels: 40.8 us -> 48.2 us  [the longest x3 33.5 us: backward(): pl.pallas_call(kernel, out_shape=[jax.ShapeDtypeStruct((1, plan.rows, don...]
    ppermute x3 -> x6, starting transfers between devices: 6.28 us -> 12.8 us  [to_slab(): lax.ppermute(value, AXES, self.routes(lambda slab, core, group: (slab + s...]
    ppermute x3 -> x6, waiting for transfers between devices: 19.4 us -> 16.2 us  [to_slab(): lax.ppermute(value, AXES, self.routes(lambda slab, core, group: (slab + s...]
    unnamed x68 -> x84, local copies, waits for them, and re-layouts: 4.37 us -> 5.01 us
  transfers between devices with their start and end apart: 30 -> 38, of which waited for: 16 -> 12; matrix products, arithmetic and copies ran while one was open for 0% -> 0% of each run, Pallas kernels for 17% -> 36%
where the time goes in v2:
time: 129 us; the launch traced here: 128 us
  Pallas kernels  52.9 us (41%)
  starting transfers between devices  41.6 us (32%)
  waiting for transfers between devices  27.7 us (21%)
  local copies, waits for them, and re-layouts  5.01 us (4%)
    pallas_call x3, Pallas kernels, backward(): pl.pallas_call(kernel, out_shape=[jax.ShapeDtypeStruct((1, plan.rows, don...  33.5 us
    ppermute x21, starting transfers between devices, to_group(): lax.ppermute(value, AXES, self.routes(lambda slab, core, group: (slab, co...  27.2 us
    ppermute x6, waiting for transfers between devices, to_slab(): lax.ppermute(value, AXES, self.routes(lambda slab, core, group: (slab + s...  16.2 us
    ppermute x6, starting transfers between devices, to_slab(): lax.ppermute(value, AXES, self.routes(lambda slab, core, group: (slab + s...  12.8 us
    ppermute x21, waiting for transfers between devices, to_group(): lax.ppermute(value, AXES, self.routes(lambda slab, core, group: (slab, co...  11.4 us
    pallas_call x2, Pallas kernels, split_columns(): pl.pallas_call(kernel, out_shape=[shape] * count, in_specs=[ANY] * (len(a...  5.42 us
    unnamed x84, local copies, waits for them, and re-layouts  5.01 us
    pallas_call x2, Pallas kernels, add_up(): pl.pallas_call(kernel, grid=(1,), out_shape=[jax.ShapeDtypeStruct(shape,...  4.78 us
  transfers between devices with their start and end apart: 38, of which 12 were waited for; matrix products, arithmetic and copies ran while one was open for 0% of the time, Pallas kernels for 36%

profile of v2, /device:TPU:0, one launch (start us, length us, event | category | flops | bytes accessed | tf_op | source)
XLA Modules:
  0.0 128.4 jit_solution(17550389458442962224)
XLA Ops:
  0.6 2.3 %split_keys.1 = (bf16[2,128,512]{2,1,0:T(8,128)(2,1)}, bf16[2,128,512]{2,1,0:T(8,128)(2,1)}, bf16[2,128,512]{2,1,0:T(8,128)(2,1)}, bf16[2,128,512]{2,1,0:T(8,128)(2,1)}) custom-call(bf16[128,2048]{1,0:T(8,128)(2,1)} %refs_0_.2, bf16[128,2048]{1,0:T(8,128)(2,1)} %refs_1_.2), custom_call_target="tpu_custom_call" | custom-call | bytes 2097152 | tf_op jit(solution)/shard_map/split_keys/pallas_call | solution.py:109
  3.0 3.0 %collective-permute-start.3 = (bf16[2,128,512]{2,1,0:T(8,128)(2,1)}, bf16[2,128,512]{2,1,0:T(8,128)(2,1)S(1)}, u32[]{:S(2)}, u32[]{:S(2)}) collective-permute-start(bf16[2,128,512]{2,1,0:T(8,128)(2,1)} %get-tuple-element.48), channel_id=1, source_target_pairs={{0,1},{1,0},{2,3},{3,2},{4,5},{5,4},{6,7},{7,6},{8,9},{9,8},{10,11... | collective-permute-start | bytes 786440 | tf_op jit(solution)/shard_map/ppermute | solution.py:63
  6.0 1.5 %collective-permute-start.4 = (bf16[2,128,512]{2,1,0:T(8,128)(2,1)}, bf16[2,128,512]{2,1,0:T(8,128)(2,1)S(1)}, u32[]{:S(2)}, u32[]{:S(2)}) collective-permute-start(bf16[2,128,512]{2,1,0:T(8,128)(2,1)} %get-tuple-element.49), channel_id=1, source_target_pairs={{0,4},{1,5},{2,6},{3,7},{4,0},{5,1},{6,2},{7,3},{8,12},{9,13},{10,... | collective-permute-start | bytes 786440 | tf_op jit(solution)/shard_map/ppermute | solution.py:63
  7.6 2.0 %collective-permute-start.10 = (bf16[2,128,512]{2,1,0:T(8,128)(2,1)}, bf16[2,128,512]{2,1,0:T(8,128)(2,1)S(1)}, u32[]{:S(2)}, u32[]{:S(2)}) collective-permute-start(bf16[2,128,512]{2,1,0:T(8,128)(2,1)} %get-tuple-element.43.refs_2_.refs_4_), channel_id=1, source_target_pairs={{0,8},{1,9},{2,10},{3,11},{4,12},{5,13},{6,14},{7,15},{8,16},{9,17... | collective-permute-start | bytes 786440 | tf_op jit(solution)/shard_map/ppermute | solution.py:69
  9.6 3.1 %split_queries.1 = (bf16[2,128,512]{2,1,0:T(8,128)(2,1)}, bf16[2,128,512]{2,1,0:T(8,128)(2,1)}, bf16[2,128,512]{2,1,0:T(8,128)(2,1)}, bf16[2,128,512]{2,1,0:T(8,...) custom-call(bf16[128,4096]{1,0:T(8,128)(2,1)} %refs_0_.3, ...), custom_call_target="tpu_custom_call" | custom-call | bytes 4194304 | tf_op jit(solution)/shard_map/split_queries/pallas_call | solution.py:109
  12.7 1.9 %collective-permute-start = (bf16[2,128,512]{2,1,0:T(8,128)(2,1)}, bf16[2,128,512]{2,1,0:T(8,128)(2,1)S(1)}, u32[]{:S(2)}, u32[]{:S(2)}) collective-permute-start(bf16[2,128,512]{2,1,0:T(8,128)(2,1)} %get-tuple-element.45), channel_id=1, source_target_pairs={{0,1},{1,0},{2,3},{3,2},{4,5},{5,4},{6,7},{7,6},{8,9},{9,8},{10,11... | collective-permute-start | bytes 786440 | tf_op jit(solution)/shard_map/ppermute | solution.py:63
  14.5 0.9 collective-permute-done.4.refs_6_
  15.5 1.5 %collective-permute-start.1 = (bf16[2,128,512]{2,1,0:T(8,128)(2,1)}, bf16[2,128,512]{2,1,0:T(8,128)(2,1)S(1)}, u32[]{:S(2)}, u32[]{:S(2)}) collective-permute-start(bf16[2,128,512]{2,1,0:T(8,128)(2,1)} %get-tuple-element.46), channel_id=1, source_target_pairs={{0,4},{1,5},{2,6},{3,7},{4,0},{5,1},{6,2},{7,3},{8,12},{9,13},{10,... | collective-permute-start | bytes 786440 | tf_op jit(solution)/shard_map/ppermute | solution.py:63
  16.9 3.6 %collective-permute-done.5.refs_7_ = bf16[2,128,512]{2,1,0:T(8,128)(2,1)S(1)} collective-permute-done((bf16[2,128,512]{2,1,0:T(8,128)(2,1)}, bf16[2,128,512]{2,1,0:T(8,128)(2,1)S(1)}, u32[]{:S(2)}, u32[]{:S(2)}) %collective-permute-start.5) | collective-permute-done | bytes 262176 | tf_op jit(solution)/shard_map/ppermute | solution.py:63
  20.6 2.9 %collective-permute-start.2 = (bf16[2,128,512]{2,1,0:T(8,128)(2,1)}, bf16[2,128,512]{2,1,0:T(8,128)(2,1)S(1)}, u32[]{:S(2)}, u32[]{:S(2)}) collective-permute-start(bf16[2,128,512]{2,1,0:T(8,128)(2,1)} %get-tuple-element.47), channel_id=1, source_target_pairs={{0,5},{1,4},{2,7},{3,6},{4,1},{5,0},{6,3},{7,2},{8,13},{9,12},{10,... | collective-permute-start | bytes 786440 | tf_op jit(solution)/shard_map/ppermute | solution.py:63
  23.5 1.6 %collective-permute-start.11 = (bf16[2,128,512]{2,1,0:T(8,128)(2,1)S(1)}, bf16[2,128,512]{2,1,0:T(8,128)(2,1)S(1)}, u32[]{:S(2)}, u32[]{:S(2)}) collective-permute-start(bf16[2,128,512]{2,1,0:T(8,128)(2,1)S(1)} %collective-permute-done.3.refs_5_), channel_id=1, source_target_pairs={{0,8},{1,9},{2,10},{3,11},{4,12},{5,13},{6,14},{7,15},{8,16},{9,17... | collective-permute-start | bytes 786440 | tf_op jit(solution)/shard_map/ppermute | solution.py:69
  25.1 1.0 collective-permute-done.refs_1_
  26.1 2.0 %collective-permute-start.12 = (bf16[2,128,512]{2,1,0:T(8,128)(2,1)S(1)}, bf16[2,128,512]{2,1,0:T(8,128)(2,1)S(1)}, u32[]{:S(2)}, u32[]{:S(2)}) collective-permute-start(bf16[2,128,512]{2,1,0:T(8,128)(2,1)S(1)} %collective-permute-done.4.refs_6_), channel_id=1, source_target_pairs={{0,8},{1,9},{2,10},{3,11},{4,12},{5,13},{6,14},{7,15},{8,16},{9,17... | collective-permute-start | bytes 786440 | tf_op jit(solution)/shard_map/ppermute | solution.py:69
  28.2 2.5 %collective-permute-done.2.refs_3_ = bf16[2,128,512]{2,1,0:T(8,128)(2,1)S(1)} collective-permute-done((bf16[2,128,512]{2,1,0:T(8,128)(2,1)}, bf16[2,128,512]{2,1,0:T(8,128)(2,1)S(1)}, u32[]{:S(2)}, u32[]{:S(2)}) %collective-permute-start.2) | collective-permute-done | bytes 262176 | tf_op jit(solution)/shard_map/ppermute | solution.py:63
  30.7 1.7 %collective-permute-start.13 = (bf16[2,128,512]{2,1,0:T(8,128)(2,1)S(1)}, bf16[2,128,512]{2,1,0:T(8,128)(2,1)S(1)}, u32[]{:S(2)}, u32[]{:S(2)}) collective-permute-start(bf16[2,128,512]{2,1,0:T(8,128)(2,1)S(1)} %collective-permute-done.5.refs_7_), channel_id=1, source_target_pairs={{0,8},{1,9},{2,10},{3,11},{4,12},{5,13},{6,14},{7,15},{8,16},{9,17... | collective-permute-start | bytes 786440 | tf_op jit(solution)/shard_map/ppermute | solution.py:69
  32.4 0.4 collective-permute-done.11.refs_13_
  32.8 0.5 collective-permute-start.14
  33.3 5.1 %collective-permute-done.12.refs_14_ = bf16[2,128,512]{2,1,0:T(8,128)(2,1)S(1)} collective-permute-done((bf16[2,128,512]{2,1,0:T(8,128)(2,1)S(1)}, bf16[2,128,512]{2,1,0:T(8,128)(2,1)S(1)}, u32[]{:S(2)}, u32[]{:S(2)}) %collective-permute-start.12) | collective-permute-done | bytes 262176 | tf_op jit(solution)/shard_map/ppermute | solution.py:69
  38.4 0.5 collective-permute-start.16
  38.9 4.0 %collective-permute-done.13.refs_15_ = bf16[2,128,512]{2,1,0:T(8,128)(2,1)S(1)} collective-permute-done((bf16[2,128,512]{2,1,0:T(8,128)(2,1)S(1)}, bf16[2,128,512]{2,1,0:T(8,128)(2,1)S(1)}, u32[]{:S(2)}, u32[]{:S(2)}) %collective-permute-start.13) | collective-permute-done | bytes 262176 | tf_op jit(solution)/shard_map/ppermute | solution.py:69
  42.9 0.9 collective-permute-start.21
  43.8 1.5 %collective-permute-start.22 = (bf16[2,128,512]{2,1,0:T(8,128)(2,1)}, bf16[2,128,512]{2,1,0:T(8,128)(2,1)S(1)}, u32[]{:S(2)}, u32[]{:S(2)}) collective-permute-start(bf16[2,128,512]{2,1,0:T(8,128)(2,1)} %get-tuple-element.57), channel_id=1, source_target_pairs={{0,4},{1,5},{2,6},{3,7},{4,0},{5,1},{6,2},{7,3},{8,12},{9,13},{10,... | collective-permute-start | bytes 786440 | tf_op jit(solution)/shard_map/ppermute | solution.py:63
  45.3 1.2 collective-permute-start.23
  46.7 0.5 copy-done.30
  47.2 0.1 copy-done.32
  47.3 15.5 %backward.3 = (bf16[1,128,512]{2,1,0:T(8,128)(2,1)}, bf16[1,128,512]{2,1,0:T(8,128)(2,1)}, bf16[1,128,512]{2,1,0:T(8,128)(2,1)}, bf16[1,128,512]{2,1,0:T(8,128)(...) custom-call(s32[4]{0:T(128)} %docs.5, bf16[2,128,512]{2,1,0:T(8,128)(2,1)} %get-tuple-element.44.refs_0_, ...), custom_call_target="tpu_custom_call" | custom-call | flops 53687091200 | bytes 6291456 | tf_op jit(solution)/shard_map/backward/pallas_call | solution.py:288
  62.7 0.9 collective-permute-start.18
  63.6 1.5 %collective-permute-start.19 = (bf16[1,128,512]{2,1,0:T(8,128)(2,1)}, bf16[1,128,512]{2,1,0:T(8,128)(2,1)S(1)}, u32[]{:S(2)}, u32[]{:S(2)}) collective-permute-start(bf16[1,128,512]{2,1,0:T(8,128)(2,1)} %get-tuple-element.53), channel_id=1, source_target_pairs={{0,4},{1,5},{2,6},{3,7},{4,0},{5,1},{6,2},{7,3},{8,12},{9,13},{10,... | collective-permute-start | bytes 393224 | tf_op jit(solution)/shard_map/ppermute | solution.py:63
  65.1 1.2 collective-permute-start.20
  66.4 0.7 copy-done.36
  67.0 0.1 copy-done.37
  67.1 8.9 %backward.4 = (bf16[1,128,256]{2,1,0:T(8,128)(2,1)}, bf16[1,128,256]{2,1,0:T(8,128)(2,1)}, bf16[1,128,256]{2,1,0:T(8,128)(2,1)}, bf16[1,128,256]{2,1,0:T(8,128)(...) custom-call(s32[4]{0:T(128)} %docs.5, bf16[2,128,512]{2,1,0:T(8,128)(2,1)} %get-tuple-element.55.refs_0_, ...), custom_call_target="tpu_custom_call" | custom-call | flops 26843545600 | bytes 6291456 | tf_op jit(solution)/shard_map/backward/pallas_call | solution.py:288
  76.0 0.5 collective-permute-start.32
  76.5 1.0 copy-done
  77.4 2.2 %add_before.2.refs_24_ = bf16[4,2,128,256]{3,2,1,0:T(8,128)(2,1)} custom-call(f32[2,4,2,128,256]{4,3,2,1,0:T(8,128)} %get-tuple-element.64.refs_0_, bf16[2,4,2,128,256]{4,3,2,1,0:T(8,128)(2,1)} %copy-done), custom_call_target="tpu_custom_call" | custom-call | bytes 2097152 | tf_op jit(solution)/shard_map/add_before/pallas_call | solution.py:333
  79.7 1.8 %collective-permute-start.28 = (bf16[4,2,128,256]{3,2,1,0:T(8,128)(2,1)}, bf16[4,2,128,256]{3,2,1,0:T(8,128)(2,1)S(1)}, u32[]{:S(2)}, u32[]{:S(2)}) collective-permute-start(bf16[4,2,128,256]{3,2,1,0:T(8,128)(2,1)} %add_before.2.refs_24_), channel_id=1, source_target_pairs={{0,24},{1,25},{2,26},{3,27},{4,28},{5,29},{6,30},{7,31},{8,0},{9,1... | collective-permute-start | bytes 1572872 | tf_op jit(solution)/shard_map/ppermute | solution.py:69
  81.5 0.6 copy-done.5
  82.2 0.1 copy-done.7
  82.2 9.2 %backward.5 = (bf16[1,128,512]{2,1,0:T(8,128)(2,1)}, bf16[1,128,512]{2,1,0:T(8,128)(2,1)}, bf16[1,128,512]{2,1,0:T(8,128)(2,1)}, bf16[1,128,512]{2,1,0:T(8,128)(...) custom-call(s32[4]{0:T(128)} %docs.5, bf16[2,128,512]{2,1,0:T(8,128)(2,1)} %get-tuple-element.55.refs_0_, ...), custom_call_target="tpu_custom_call" | custom-call | flops 26843545600 | bytes 6291456 | tf_op jit(solution)/shard_map/backward/pallas_call | solution.py:288
  91.4 0.1 collective-permute-start.33
  91.5 2.3 %collective-permute-done.28.refs_2_.refs_4_ = bf16[4,2,128,256]{3,2,1,0:T(8,128)(2,1)S(1)} collective-permute-done((bf16[4,2,128,256]{3,2,1,0:T(8,128)(2,1)}, bf16[4,2,128,256]{3,2,1,0:T(8,128)(2,1)S(1)}, u32[]{:S(2)}, u32[]{:S(2)}) %collective-permute-start.28) | collective-permute-done | bytes 524320 | tf_op jit(solution)/shard_map/ppermute | solution.py:69
  93.8 0.8 copy-done.2
  94.6 0.2 copy-done.3
  94.8 2.3 %add_before.3 = bf16[4,2,128,256]{3,2,1,0:T(8,128)(2,1)} custom-call(f32[2,4,2,128,128]{4,3,2,1,0:T(8,128)} %get-tuple-element.73.refs_0_, f32[2,4,2,128,128]{4,3,2,1,0:T(8,128)} %get-tuple-element.74.refs_1_, bf16[2,4,2,128,128]{4,3,2,1,0:T(8,128)(2,1)} %copy-done.1, bf16[2,4,2,128,128]{4,3,2,1,0:T(8,128)(2,1)} %copy-done.3, bf16[4,2,128,256]{3,2,1,0:T(8,128)(2,1)} %copy-done.2), custom_call_target="tpu_custom_call" | custom-call | bytes 2097152 | tf_op jit(solution)/shard_map/add_before/pallas_call | solution.py:333
  97.1 3.6 %collective-permute-start.34 = (bf16[4,2,128,256]{3,2,1,0:T(8,128)(2,1)}, bf16[4,2,128,256]{3,2,1,0:T(8,128)(2,1)S(1)}, u32[]{:S(2)}, u32[]{:S(2)}) collective-permute-start(bf16[4,2,128,256]{3,2,1,0:T(8,128)(2,1)} %add_before.3), channel_id=1, source_target_pairs={{0,24},{1,25},{2,26},{3,27},{4,28},{5,29},{6,30},{7,31},{8,0},{9,1... | collective-permute-start | bytes 1572872 | tf_op jit(solution)/shard_map/ppermute | solution.py:69
  100.7 0.5 collective-permute-start.25
  101.2 0.5 collective-permute-start.26
  101.7 2.5 %collective-permute-start.27 = (bf16[1,128,512]{2,1,0:T(8,128)(2,1)S(1)}, bf16[1,128,512]{2,1,0:T(8,128)(2,1)S(1)}, u32[]{:S(2)}, u32[]{:S(2)}) collective-permute-start(bf16[1,128,512]{2,1,0:T(8,128)(2,1)S(1)} %copy-done.38), channel_id=1, source_target_pairs={{0,5},{1,4},{2,7},{3,6},{4,1},{5,0},{6,3},{7,2},{8,13},{9,12},{10,... | collective-permute-start | bytes 393224 | tf_op jit(solution)/shard_map/ppermute | solution.py:63
  104.2 2.4 %add_up.2 = (bf16[2,128,256]{2,1,0:T(8,128)(2,1)}, bf16[2,128,256]{2,1,0:T(8,128)(2,1)}, bf16[2,128,256]{2,1,0:T(8,128)(2,1)}, bf16[2,128,256]{2,1,0:T(8,128)(2,1)}) custom-call(f32[2,4,2,128,256]{4,3,2,1,0:T(8,128)} %get-tuple-element.64.refs_0_, bf16[2,4,2,128,256]{4,3,2,1,0:T(8,128)(2,1)} %copy-done, bf16[4,2,128,256]{3,2,1,0:T(8,128)(2,1)} %copy-done.2), custom_call_target="tpu_custom_call" | custom-call | bytes 2621440 | tf_op jit(solution)/shard_map/add_up/pallas_call | solution.py:361
  106.6 0.5 collective-permute-start.29
  107.1 4.5 %collective-permute-done.34.refs_4_ = bf16[4,2,128,256]{3,2,1,0:T(8,128)(2,1)S(1)} collective-permute-done((bf16[4,2,128,256]{3,2,1,0:T(8,128)(2,1)}, bf16[4,2,128,256]{3,2,1,0:T(8,128)(2,1)S(1)}, u32[]{:S(2)}, u32[]{:S(2)}) %collective-permute-start.34) | collective-permute-done | bytes 524320 | tf_op jit(solution)/shard_map/ppermute | solution.py:69
  111.6 0.5 collective-permute-start.30
  112.1 0.3 copy-done.4
  112.4 2.4 %add_up.3 = (bf16[2,128,256]{2,1,0:T(8,128)(2,1)}, bf16[2,128,256]{2,1,0:T(8,128)(2,1)}, bf16[2,128,256]{2,1,0:T(8,128)(2,1)}, bf16[2,128,256]{2,1,0:T(8,128)(2,1)}) custom-call(f32[2,4,2,128,128]{4,3,2,1,0:T(8,128)} %get-tuple-element.73.refs_0_, f32[2,4,2,128,128]{4,3,2,1,0:T(8,128)} %get-tuple-element.74.refs_1_, bf16[2,4,2,128,128]{4,3,2,1,0:T(8,128)(2,1)} %copy-done.1, ...), custom_call_target="tpu_custom_call" | custom-call | bytes 2621440 | tf_op jit(solution)/shard_map/add_up/pallas_call | solution.py:361
  114.8 1.2 collective-permute-start.31
  116.0 1.5 %collective-permute-start.35 = (bf16[2,128,256]{2,1,0:T(8,128)(2,1)}, bf16[2,128,256]{2,1,0:T(8,128)(2,1)S(1)}, u32[]{:S(2)}, u32[]{:S(2)}) collective-permute-start(bf16[2,128,256]{2,1,0:T(8,128)(2,1)} %get-tuple-element.78), channel_id=1, source_target_pairs={{0,1},{1,0},{2,3},{3,2},{4,5},{5,4},{6,7},{7,6},{8,9},{9,8},{10,11... | collective-permute-start | bytes 393224 | tf_op jit(solution)/shard_map/ppermute | solution.py:63
  117.5 0.8 collective-permute-start.36
  118.3 1.2 collective-permute-start.37
  119.5 2.3 %join_queries.1 = bf16[128,4096]{1,0:T(8,128)(2,1)} custom-call(bf16[1,128,512]{2,1,0:T(8,128)(2,1)} %get-tuple-element.51.refs_0_, bf16[1,128,512]{2,1,0:T(8,128)(2,1)} %copy-done.5, bf16[1,128,512]{2,1,0:T(8,128)(2,1)} %copy-done.6, bf16[1,128,512]{2,1,0:T(8,128)(2,1)} %copy-done.7, bf16[1,128,512]{2,1,0:T(8,128)(2,1)} %get-tuple-element.65.refs_4_, ...), custom_call_target="tpu_custom_call" | custom-call | bytes 2097152 | tf_op jit(solution)/shard_map/join_queries/pallas_call | solution.py:143
  121.9 0.4 collective-permute-done.31.refs_3_
  122.3 1.5 %collective-permute-done.35.refs_5_ = bf16[2,128,256]{2,1,0:T(8,128)(2,1)S(1)} collective-permute-done((bf16[2,128,256]{2,1,0:T(8,128)(2,1)}, bf16[2,128,256]{2,1,0:T(8,128)(2,1)S(1)}, u32[]{:S(2)}, u32[]{:S(2)}) %collective-permute-start.35) | collective-permute-done | bytes 131104 | tf_op jit(solution)/shard_map/ppermute | solution.py:63
  123.8 1.4 %collective-permute-done.37.refs_7_ = bf16[2,128,256]{2,1,0:T(8,128)(2,1)S(1)} collective-permute-done((bf16[2,128,256]{2,1,0:T(8,128)(2,1)}, bf16[2,128,256]{2,1,0:T(8,128)(2,1)S(1)}, u32[]{:S(2)}, u32[]{:S(2)}) %collective-permute-start.37) | collective-permute-done | bytes 131104 | tf_op jit(solution)/shard_map/ppermute | solution.py:63
  125.3 0.6 copy-done.16
  125.9 2.3 %join_keys.1 = (bf16[128,2048]{1,0:T(8,128)(2,1)}, bf16[128,2048]{1,0:T(8,128)(2,1)}) custom-call(bf16[2,128,256]{2,1,0:T(8,128)(2,1)} %get-tuple-element.69.refs_0_, bf16[2,128,256]{2,1,0:T(8,128)(2,1)} %copy-done.11, bf16[2,128,256]{2,1,0:T(8,128)(2,1)} %copy-done.12, bf16[2,128,256]{2,1,0:T(8,128)(2,1)} %copy-done.13, ...), custom_call_target="tpu_custom_call" | custom-call | bytes 2097152 | tf_op jit(solution)/shard_map/join_keys/pallas_call | solution.py:143
  (107 shorter events, 0.3 us)
Async XLA Ops:
  3.0 9.7 %collective-permute-start.3 = (bf16[2,128,512]{2,1,0:T(8,128)(2,1)}, bf16[2,128,512]{2,1,0:T(8,128)(2,1)S(1)}, u32[]{:S(2)}, u32[]{:S(2)}) collective-permute-start(bf16[2,128,512]{2,1,0:T(8,128)(2,1)} %get-tuple-element.48), channel_id=1, source_target_pairs={{0,1},{1,0},{2,3},{3,2},{4,5},{5,4},{6,7},{7,6},{8,9},{9,8},{10,11... | collective-permute-start | bytes 786440 | tf_op jit(solution)/shard_map/ppermute | solution.py:63
  6.0 9.4 %collective-permute-start.4 = (bf16[2,128,512]{2,1,0:T(8,128)(2,1)}, bf16[2,128,512]{2,1,0:T(8,128)(2,1)S(1)}, u32[]{:S(2)}, u32[]{:S(2)}) collective-permute-start(bf16[2,128,512]{2,1,0:T(8,128)(2,1)} %get-tuple-element.49), channel_id=1, source_target_pairs={{0,4},{1,5},{2,6},{3,7},{4,0},{5,1},{6,2},{7,3},{8,12},{9,13},{10,... | collective-permute-start | bytes 786440 | tf_op jit(solution)/shard_map/ppermute | solution.py:63
  7.5 13.1 %collective-permute-start.5 = (bf16[2,128,512]{2,1,0:T(8,128)(2,1)}, bf16[2,128,512]{2,1,0:T(8,128)(2,1)S(1)}, u32[]{:S(2)}, u32[]{:S(2)}) collective-permute-start(bf16[2,128,512]{2,1,0:T(8,128)(2,1)} %get-tuple-element.50), channel_id=1, source_target_pairs={{0,5},{1,4},{2,7},{3,6},{4,1},{5,0},{6,3},{7,2},{8,13},{9,12},{10,... | collective-permute-start | bytes 786440 | tf_op jit(solution)/shard_map/ppermute | solution.py:63
  7.6 16.0 %collective-permute-start.10 = (bf16[2,128,512]{2,1,0:T(8,128)(2,1)}, bf16[2,128,512]{2,1,0:T(8,128)(2,1)S(1)}, u32[]{:S(2)}, u32[]{:S(2)}) collective-permute-start(bf16[2,128,512]{2,1,0:T(8,128)(2,1)} %get-tuple-element.43.refs_2_.refs_4_), channel_id=1, source_target_pairs={{0,8},{1,9},{2,10},{3,11},{4,12},{5,13},{6,14},{7,15},{8,16},{9,17... | collective-permute-start | bytes 786440 | tf_op jit(solution)/shard_map/ppermute | solution.py:69
  9.6 15.5 %collective-permute-start.6 = (bf16[2,128,512]{2,1,0:T(8,128)(2,1)}, bf16[2,128,512]{2,1,0:T(8,128)(2,1)S(1)}, u32[]{:S(2)}, u32[]{:S(2)}) collective-permute-start(bf16[2,128,512]{2,1,0:T(8,128)(2,1)} %get-tuple-element.43.refs_2_.refs_4_), channel_id=1, source_target_pairs={{0,2},{1,3},{2,0},{3,1},{4,6},{5,7},{6,4},{7,5},{8,10},{9,11},{10,... | collective-permute-start | bytes 786440 | tf_op jit(solution)/shard_map/ppermute | solution.py:66
  12.7 33.9 %copy-start.17 = (bf16[2,128,512]{2,1,0:T(8,128)(2,1)}, bf16[2,128,512]{2,1,0:T(8,128)(2,1)S(1)}, u32[]{:S(2)}) copy-start(bf16[2,128,512]{2,1,0:T(8,128)(2,1)S(1)} %collective-permute-done.3.refs_5_) | copy-start | bytes 786436
  12.7 13.5 %collective-permute-start = (bf16[2,128,512]{2,1,0:T(8,128)(2,1)}, bf16[2,128,512]{2,1,0:T(8,128)(2,1)S(1)}, u32[]{:S(2)}, u32[]{:S(2)}) collective-permute-start(bf16[2,128,512]{2,1,0:T(8,128)(2,1)} %get-tuple-element.45), channel_id=1, source_target_pairs={{0,1},{1,0},{2,3},{3,2},{4,5},{5,4},{6,7},{7,6},{8,9},{9,8},{10,11... | collective-permute-start | bytes 786440 | tf_op jit(solution)/shard_map/ppermute | solution.py:63
  15.5 31.1 %copy-start.18 = (bf16[2,128,512]{2,1,0:T(8,128)(2,1)}, bf16[2,128,512]{2,1,0:T(8,128)(2,1)S(1)}, u32[]{:S(2)}) copy-start(bf16[2,128,512]{2,1,0:T(8,128)(2,1)S(1)} %collective-permute-done.4.refs_6_) | copy-start | bytes 786436
  15.5 12.7 %collective-permute-start.1 = (bf16[2,128,512]{2,1,0:T(8,128)(2,1)}, bf16[2,128,512]{2,1,0:T(8,128)(2,1)S(1)}, u32[]{:S(2)}, u32[]{:S(2)}) collective-permute-start(bf16[2,128,512]{2,1,0:T(8,128)(2,1)} %get-tuple-element.46), channel_id=1, source_target_pairs={{0,4},{1,5},{2,6},{3,7},{4,0},{5,1},{6,2},{7,3},{8,12},{9,13},{10,... | collective-permute-start | bytes 786440 | tf_op jit(solution)/shard_map/ppermute | solution.py:63
  20.6 26.0 %copy-start.19 = (bf16[2,128,512]{2,1,0:T(8,128)(2,1)}, bf16[2,128,512]{2,1,0:T(8,128)(2,1)S(1)}, u32[]{:S(2)}) copy-start(bf16[2,128,512]{2,1,0:T(8,128)(2,1)S(1)} %collective-permute-done.5.refs_7_) | copy-start | bytes 786436
  20.6 10.1 %collective-permute-start.2 = (bf16[2,128,512]{2,1,0:T(8,128)(2,1)}, bf16[2,128,512]{2,1,0:T(8,128)(2,1)S(1)}, u32[]{:S(2)}, u32[]{:S(2)}) collective-permute-start(bf16[2,128,512]{2,1,0:T(8,128)(2,1)} %get-tuple-element.47), channel_id=1, source_target_pairs={{0,5},{1,4},{2,7},{3,6},{4,1},{5,0},{6,3},{7,2},{8,13},{9,12},{10,... | collective-permute-start | bytes 786440 | tf_op jit(solution)/shard_map/ppermute | solution.py:63
  23.5 23.0 %copy-start.20 = (bf16[2,128,512]{2,1,0:T(8,128)(2,1)}, bf16[2,128,512]{2,1,0:T(8,128)(2,1)S(1)}, u32[]{:S(2)}) copy-start(bf16[2,128,512]{2,1,0:T(8,128)(2,1)S(1)} %collective-permute-done.10.refs_12_) | copy-start | bytes 786436
  23.5 9.2 %collective-permute-start.11 = (bf16[2,128,512]{2,1,0:T(8,128)(2,1)S(1)}, bf16[2,128,512]{2,1,0:T(8,128)(2,1)S(1)}, u32[]{:S(2)}, u32[]{:S(2)}) collective-permute-start(bf16[2,128,512]{2,1,0:T(8,128)(2,1)S(1)} %collective-permute-done.3.refs_5_), channel_id=1, source_target_pairs={{0,8},{1,9},{2,10},{3,11},{4,12},{5,13},{6,14},{7,15},{8,16},{9,17... | collective-permute-start | bytes 786440 | tf_op jit(solution)/shard_map/ppermute | solution.py:69
  25.1 21.5 %copy-start.21 = (bf16[2,128,512]{2,1,0:T(8,128)(2,1)}, bf16[2,128,512]{2,1,0:T(8,128)(2,1)S(1)}, u32[]{:S(2)}) copy-start(bf16[2,128,512]{2,1,0:T(8,128)(2,1)S(1)} %collective-permute-done.6.refs_8_) | copy-start | bytes 786436
  25.1 7.7 %collective-permute-start.7 = (bf16[2,128,512]{2,1,0:T(8,128)(2,1)S(1)}, bf16[2,128,512]{2,1,0:T(8,128)(2,1)S(1)}, u32[]{:S(2)}, u32[]{:S(2)}) collective-permute-start(bf16[2,128,512]{2,1,0:T(8,128)(2,1)S(1)} %collective-permute-done.3.refs_5_), channel_id=1, source_target_pairs={{0,2},{1,3},{2,0},{3,1},{4,6},{5,7},{6,4},{7,5},{8,10},{9,11},{10,... | collective-permute-start | bytes 786440 | tf_op jit(solution)/shard_map/ppermute | solution.py:66
  26.1 20.5 %copy-start.31 = (bf16[2,128,512]{2,1,0:T(8,128)(2,1)}, bf16[2,128,512]{2,1,0:T(8,128)(2,1)S(1)}, u32[]{:S(2)}) copy-start(bf16[2,128,512]{2,1,0:T(8,128)(2,1)S(1)} %collective-permute-done.refs_1_) | copy-start | bytes 786436
  26.1 12.3 %collective-permute-start.12 = (bf16[2,128,512]{2,1,0:T(8,128)(2,1)S(1)}, bf16[2,128,512]{2,1,0:T(8,128)(2,1)S(1)}, u32[]{:S(2)}, u32[]{:S(2)}) collective-permute-start(bf16[2,128,512]{2,1,0:T(8,128)(2,1)S(1)} %collective-permute-done.4.refs_6_), channel_id=1, source_target_pairs={{0,8},{1,9},{2,10},{3,11},{4,12},{5,13},{6,14},{7,15},{8,16},{9,17... | collective-permute-start | bytes 786440 | tf_op jit(solution)/shard_map/ppermute | solution.py:69
  28.2 18.4 %copy-start.33 = (bf16[2,128,512]{2,1,0:T(8,128)(2,1)}, bf16[2,128,512]{2,1,0:T(8,128)(2,1)S(1)}, u32[]{:S(2)}) copy-start(bf16[2,128,512]{2,1,0:T(8,128)(2,1)S(1)} %collective-permute-done.1.refs_2_) | copy-start | bytes 786436
  28.2 10.2 %collective-permute-start.8 = (bf16[2,128,512]{2,1,0:T(8,128)(2,1)S(1)}, bf16[2,128,512]{2,1,0:T(8,128)(2,1)S(1)}, u32[]{:S(2)}, u32[]{:S(2)}) collective-permute-start(bf16[2,128,512]{2,1,0:T(8,128)(2,1)S(1)} %collective-permute-done.4.refs_6_), channel_id=1, source_target_pairs={{0,2},{1,3},{2,0},{3,1},{4,6},{5,7},{6,4},{7,5},{8,10},{9,11},{10,... | collective-permute-start | bytes 786440 | tf_op jit(solution)/shard_map/ppermute | solution.py:66
  30.7 15.9 %copy-start.35 = (bf16[2,128,512]{2,1,0:T(8,128)(2,1)}, bf16[2,128,512]{2,1,0:T(8,128)(2,1)S(1)}, u32[]{:S(2)}) copy-start(bf16[2,128,512]{2,1,0:T(8,128)(2,1)S(1)} %collective-permute-done.2.refs_3_) | copy-start | bytes 786436
  30.7 12.2 %collective-permute-start.13 = (bf16[2,128,512]{2,1,0:T(8,128)(2,1)S(1)}, bf16[2,128,512]{2,1,0:T(8,128)(2,1)S(1)}, u32[]{:S(2)}, u32[]{:S(2)}) collective-permute-start(bf16[2,128,512]{2,1,0:T(8,128)(2,1)S(1)} %collective-permute-done.5.refs_7_), channel_id=1, source_target_pairs={{0,8},{1,9},{2,10},{3,11},{4,12},{5,13},{6,14},{7,15},{8,16},{9,17... | collective-permute-start | bytes 786440 | tf_op jit(solution)/shard_map/ppermute | solution.py:69
  32.8 13.9 %copy-start.22 = (bf16[2,128,512]{2,1,0:T(8,128)(2,1)}, bf16[2,128,512]{2,1,0:T(8,128)(2,1)S(1)}, u32[]{:S(2)}) copy-start(bf16[2,128,512]{2,1,0:T(8,128)(2,1)S(1)} %collective-permute-done.11.refs_13_) | copy-start | bytes 786436
  32.8 10.2 %collective-permute-start.9 = (bf16[2,128,512]{2,1,0:T(8,128)(2,1)S(1)}, bf16[2,128,512]{2,1,0:T(8,128)(2,1)S(1)}, u32[]{:S(2)}, u32[]{:S(2)}) collective-permute-start(bf16[2,128,512]{2,1,0:T(8,128)(2,1)S(1)} %collective-permute-done.5.refs_7_), channel_id=1, source_target_pairs={{0,2},{1,3},{2,0},{3,1},{4,6},{5,7},{6,4},{7,5},{8,10},{9,11},{10,... | collective-permute-start | bytes 786440 | tf_op jit(solution)/shard_map/ppermute | solution.py:66
  32.8 13.8 %copy-start.23 = (bf16[2,128,512]{2,1,0:T(8,128)(2,1)}, bf16[2,128,512]{2,1,0:T(8,128)(2,1)S(1)}, u32[]{:S(2)}) copy-start(bf16[2,128,512]{2,1,0:T(8,128)(2,1)S(1)} %collective-permute-done.7.refs_9_) | copy-start | bytes 786436
  32.8 11.0 %collective-permute-start.14 = (bf16[2,128,512]{2,1,0:T(8,128)(2,1)S(1)}, bf16[2,128,512]{2,1,0:T(8,128)(2,1)S(1)}, u32[]{:S(2)}, u32[]{:S(2)}) collective-permute-start(bf16[2,128,512]{2,1,0:T(8,128)(2,1)S(1)} %collective-permute-done.10.refs_12_), channel_id=1, source_target_pairs={{0,2},{1,3},{2,0},{3,1},{4,6},{5,7},{6,4},{7,5},{8,10},{9,11},{10,... | collective-permute-start | bytes 786440 | tf_op jit(solution)/shard_map/ppermute | solution.py:66
  38.4 8.3 %copy-start.24 = (bf16[2,128,512]{2,1,0:T(8,128)(2,1)}, bf16[2,128,512]{2,1,0:T(8,128)(2,1)S(1)}, u32[]{:S(2)}) copy-start(bf16[2,128,512]{2,1,0:T(8,128)(2,1)S(1)} %collective-permute-done.12.refs_14_) | copy-start | bytes 786436
  38.4 6.9 %collective-permute-start.15 = (bf16[2,128,512]{2,1,0:T(8,128)(2,1)S(1)}, bf16[2,128,512]{2,1,0:T(8,128)(2,1)S(1)}, u32[]{:S(2)}, u32[]{:S(2)}) collective-permute-start(bf16[2,128,512]{2,1,0:T(8,128)(2,1)S(1)} %collective-permute-done.11.refs_13_), channel_id=1, source_target_pairs={{0,2},{1,3},{2,0},{3,1},{4,6},{5,7},{6,4},{7,5},{8,10},{9,11},{10,... | collective-permute-start | bytes 786440 | tf_op jit(solution)/shard_map/ppermute | solution.py:66
  38.4 8.3 %copy-start.25 = (bf16[2,128,512]{2,1,0:T(8,128)(2,1)}, bf16[2,128,512]{2,1,0:T(8,128)(2,1)S(1)}, u32[]{:S(2)}) copy-start(bf16[2,128,512]{2,1,0:T(8,128)(2,1)S(1)} %collective-permute-done.8.refs_10_) | copy-start | bytes 786436
  38.4 8.1 %collective-permute-start.16 = (bf16[2,128,512]{2,1,0:T(8,128)(2,1)S(1)}, bf16[2,128,512]{2,1,0:T(8,128)(2,1)S(1)}, u32[]{:S(2)}, u32[]{:S(2)}) collective-permute-start(bf16[2,128,512]{2,1,0:T(8,128)(2,1)S(1)} %collective-permute-done.12.refs_14_), channel_id=1, source_target_pairs={{0,2},{1,3},{2,0},{3,1},{4,6},{5,7},{6,4},{7,5},{8,10},{9,11},{10,... | collective-permute-start | bytes 786440 | tf_op jit(solution)/shard_map/ppermute | solution.py:66
  42.9 3.7 %copy-start.26 = (bf16[2,128,512]{2,1,0:T(8,128)(2,1)}, bf16[2,128,512]{2,1,0:T(8,128)(2,1)S(1)}, u32[]{:S(2)}) copy-start(bf16[2,128,512]{2,1,0:T(8,128)(2,1)S(1)} %collective-permute-done.13.refs_15_) | copy-start | bytes 786436
  42.9 3.6 %collective-permute-start.17 = (bf16[2,128,512]{2,1,0:T(8,128)(2,1)S(1)}, bf16[2,128,512]{2,1,0:T(8,128)(2,1)S(1)}, u32[]{:S(2)}, u32[]{:S(2)}) collective-permute-start(bf16[2,128,512]{2,1,0:T(8,128)(2,1)S(1)} %collective-permute-done.13.refs_15_), channel_id=1, source_target_pairs={{0,2},{1,3},{2,0},{3,1},{4,6},{5,7},{6,4},{7,5},{8,10},{9,11},{10,... | collective-permute-start | bytes 786440 | tf_op jit(solution)/shard_map/ppermute | solution.py:66
  42.9 3.7 %copy-start.27 = (bf16[2,128,512]{2,1,0:T(8,128)(2,1)}, bf16[2,128,512]{2,1,0:T(8,128)(2,1)S(1)}, u32[]{:S(2)}) copy-start(bf16[2,128,512]{2,1,0:T(8,128)(2,1)S(1)} %collective-permute-done.9.refs_11_) | copy-start | bytes 786436
  42.9 22.2 %collective-permute-start.21 = (bf16[2,128,512]{2,1,0:T(8,128)(2,1)}, bf16[2,128,512]{2,1,0:T(8,128)(2,1)S(1)}, u32[]{:S(2)}, u32[]{:S(2)}) collective-permute-start(bf16[2,128,512]{2,1,0:T(8,128)(2,1)} %get-tuple-element.56), channel_id=1, source_target_pairs={{0,1},{1,0},{2,3},{3,2},{4,5},{5,4},{6,7},{7,6},{8,9},{9,8},{10,11... | collective-permute-start | bytes 786440 | tf_op jit(solution)/shard_map/ppermute | solution.py:63
  43.8 2.9 %copy-start.28 = (bf16[2,128,512]{2,1,0:T(8,128)(2,1)}, bf16[2,128,512]{2,1,0:T(8,128)(2,1)S(1)}, u32[]{:S(2)}) copy-start(bf16[2,128,512]{2,1,0:T(8,128)(2,1)S(1)} %collective-permute-done.14.refs_16_) | copy-start | bytes 786436
  43.8 22.5 %collective-permute-start.22 = (bf16[2,128,512]{2,1,0:T(8,128)(2,1)}, bf16[2,128,512]{2,1,0:T(8,128)(2,1)S(1)}, u32[]{:S(2)}, u32[]{:S(2)}) collective-permute-start(bf16[2,128,512]{2,1,0:T(8,128)(2,1)} %get-tuple-element.57), channel_id=1, source_target_pairs={{0,4},{1,5},{2,6},{3,7},{4,0},{5,1},{6,2},{7,3},{8,12},{9,13},{10,... | collective-permute-start | bytes 786440 | tf_op jit(solution)/shard_map/ppermute | solution.py:63
  45.3 21.0 %collective-permute-start.23 = (bf16[2,128,512]{2,1,0:T(8,128)(2,1)}, bf16[2,128,512]{2,1,0:T(8,128)(2,1)S(1)}, u32[]{:S(2)}, u32[]{:S(2)}) collective-permute-start(bf16[2,128,512]{2,1,0:T(8,128)(2,1)} %get-tuple-element.58), channel_id=1, source_target_pairs={{0,5},{1,4},{2,7},{3,6},{4,1},{5,0},{6,3},{7,2},{8,13},{9,12},{10,... | collective-permute-start | bytes 786440 | tf_op jit(solution)/shard_map/ppermute | solution.py:63
  62.7 18.7 %collective-permute-start.18 = (bf16[1,128,512]{2,1,0:T(8,128)(2,1)}, bf16[1,128,512]{2,1,0:T(8,128)(2,1)S(1)}, u32[]{:S(2)}, u32[]{:S(2)}) collective-permute-start(bf16[1,128,512]{2,1,0:T(8,128)(2,1)} %get-tuple-element.52), channel_id=1, source_target_pairs={{0,1},{1,0},{2,3},{3,2},{4,5},{5,4},{6,7},{7,6},{8,9},{9,8},{10,11... | collective-permute-start | bytes 393224 | tf_op jit(solution)/shard_map/ppermute | solution.py:63
  63.6 17.9 %collective-permute-start.19 = (bf16[1,128,512]{2,1,0:T(8,128)(2,1)}, bf16[1,128,512]{2,1,0:T(8,128)(2,1)S(1)}, u32[]{:S(2)}, u32[]{:S(2)}) collective-permute-start(bf16[1,128,512]{2,1,0:T(8,128)(2,1)} %get-tuple-element.53), channel_id=1, source_target_pairs={{0,4},{1,5},{2,6},{3,7},{4,0},{5,1},{6,2},{7,3},{8,12},{9,13},{10,... | collective-permute-start | bytes 393224 | tf_op jit(solution)/shard_map/ppermute | solution.py:63
  65.1 16.4 %collective-permute-start.20 = (bf16[1,128,512]{2,1,0:T(8,128)(2,1)}, bf16[1,128,512]{2,1,0:T(8,128)(2,1)S(1)}, u32[]{:S(2)}, u32[]{:S(2)}) collective-permute-start(bf16[1,128,512]{2,1,0:T(8,128)(2,1)} %get-tuple-element.54), channel_id=1, source_target_pairs={{0,5},{1,4},{2,7},{3,6},{4,1},{5,0},{6,3},{7,2},{8,13},{9,12},{10,... | collective-permute-start | bytes 393224 | tf_op jit(solution)/shard_map/ppermute | solution.py:63
  66.3 10.2 %collective-permute-start.24 = (bf16[2,4,2,128,256]{4,3,2,1,0:T(8,128)(2,1)}, bf16[2,4,2,128,256]{4,3,2,1,0:T(8,128)(2,1)S(1)}, u32[]{:S(2)}, u32[]{:S(2)}) collective-permute-start(bf16[2,4,2,128,256]{4,3,2,1,0:T(8,128)(2,1)} %get-tuple-element.59.refs_20_), channel_id=1, source_target_pairs={{0,2},{1,3},{2,0},{3,1},{4,6},{5,7},{6,4},{7,5},{8,10},{9,11},{10,... | collective-permute-start | bytes 3145736 | tf_op jit(solution)/shard_map/ppermute | solution.py:66
  76.0 15.5 %collective-permute-start.32 = (bf16[2,4,2,128,128]{4,3,2,1,0:T(8,128)(2,1)}, bf16[2,4,2,128,128]{4,3,2,1,0:T(8,128)(2,1)S(1)}, u32[]{:S(2)}, u32[]{:S(2)}) collective-permute-start(bf16[2,4,2,128,128]{4,3,2,1,0:T(8,128)(2,1)} %get-tuple-element.75), channel_id=1, source_target_pairs={{0,2},{1,3},{2,0},{3,1},{4,6},{5,7},{6,4},{7,5},{8,10},{9,11},{10,... | collective-permute-start | bytes 1572872 | tf_op jit(solution)/shard_map/ppermute | solution.py:66
  79.7 14.1 %collective-permute-start.28 = (bf16[4,2,128,256]{3,2,1,0:T(8,128)(2,1)}, bf16[4,2,128,256]{3,2,1,0:T(8,128)(2,1)S(1)}, u32[]{:S(2)}, u32[]{:S(2)}) collective-permute-start(bf16[4,2,128,256]{3,2,1,0:T(8,128)(2,1)} %add_before.2.refs_24_), channel_id=1, source_target_pairs={{0,24},{1,25},{2,26},{3,27},{4,28},{5,29},{6,30},{7,31},{8,0},{9,1... | collective-permute-start | bytes 1572872 | tf_op jit(solution)/shard_map/ppermute | solution.py:69
  91.4 2.4 %collective-permute-start.33 = (bf16[2,4,2,128,128]{4,3,2,1,0:T(8,128)(2,1)}, bf16[2,4,2,128,128]{4,3,2,1,0:T(8,128)(2,1)S(1)}, u32[]{:S(2)}, u32[]{:S(2)}) collective-permute-start(bf16[2,4,2,128,128]{4,3,2,1,0:T(8,128)(2,1)} %get-tuple-element.76), channel_id=1, source_target_pairs={{0,2},{1,3},{2,0},{3,1},{4,6},{5,7},{6,4},{7,5},{8,10},{9,11},{10,... | collective-permute-start | bytes 1572872 | tf_op jit(solution)/shard_map/ppermute | solution.py:66
  91.5 2.3 %copy-start.1 = (bf16[2,4,2,128,128]{4,3,2,1,0:T(8,128)(2,1)}, bf16[2,4,2,128,128]{4,3,2,1,0:T(8,128)(2,1)S(1)}, u32[]{:S(2)}) copy-start(bf16[2,4,2,128,128]{4,3,2,1,0:T(8,128)(2,1)S(1)} %collective-permute-done.32.refs_2_) | copy-start | bytes 1572868
  94.8 5.9 %copy-start.40 = (bf16[1,128,512]{2,1,0:T(8,128)(2,1)S(1)}, bf16[1,128,512]{2,1,0:T(8,128)(2,1)}, u32[]{:S(2)}) copy-start(bf16[1,128,512]{2,1,0:T(8,128)(2,1)} %get-tuple-element.66) | copy-start | bytes 393220
  94.8 6.4 %copy-start.39 = (bf16[1,128,512]{2,1,0:T(8,128)(2,1)S(1)}, bf16[1,128,512]{2,1,0:T(8,128)(2,1)}, u32[]{:S(2)}) copy-start(bf16[1,128,512]{2,1,0:T(8,128)(2,1)} %get-tuple-element.67) | copy-start | bytes 393220
  94.8 6.9 %copy-start.38 = (bf16[1,128,512]{2,1,0:T(8,128)(2,1)S(1)}, bf16[1,128,512]{2,1,0:T(8,128)(2,1)}, u32[]{:S(2)}) copy-start(bf16[1,128,512]{2,1,0:T(8,128)(2,1)} %get-tuple-element.68) | copy-start | bytes 393220
  97.1 14.5 %collective-permute-start.34 = (bf16[4,2,128,256]{3,2,1,0:T(8,128)(2,1)}, bf16[4,2,128,256]{3,2,1,0:T(8,128)(2,1)S(1)}, u32[]{:S(2)}, u32[]{:S(2)}) collective-permute-start(bf16[4,2,128,256]{3,2,1,0:T(8,128)(2,1)} %add_before.3), channel_id=1, source_target_pairs={{0,24},{1,25},{2,26},{3,27},{4,28},{5,29},{6,30},{7,31},{8,0},{9,1... | collective-permute-start | bytes 1572872 | tf_op jit(solution)/shard_map/ppermute | solution.py:69
  100.7 14.1 %collective-permute-start.25 = (bf16[1,128,512]{2,1,0:T(8,128)(2,1)S(1)}, bf16[1,128,512]{2,1,0:T(8,128)(2,1)S(1)}, u32[]{:S(2)}, u32[]{:S(2)}) collective-permute-start(bf16[1,128,512]{2,1,0:T(8,128)(2,1)S(1)} %copy-done.40), channel_id=1, source_target_pairs={{0,1},{1,0},{2,3},{3,2},{4,5},{5,4},{6,7},{7,6},{8,9},{9,8},{10,11... | collective-permute-start | bytes 393224 | tf_op jit(solution)/shard_map/ppermute | solution.py:63
  101.2 14.8 %collective-permute-start.26 = (bf16[1,128,512]{2,1,0:T(8,128)(2,1)S(1)}, bf16[1,128,512]{2,1,0:T(8,128)(2,1)S(1)}, u32[]{:S(2)}, u32[]{:S(2)}) collective-permute-start(bf16[1,128,512]{2,1,0:T(8,128)(2,1)S(1)} %copy-done.39), channel_id=1, source_target_pairs={{0,4},{1,5},{2,6},{3,7},{4,0},{5,1},{6,2},{7,3},{8,12},{9,13},{10,... | collective-permute-start | bytes 393224 | tf_op jit(solution)/shard_map/ppermute | solution.py:63
  101.7 15.8 %collective-permute-start.27 = (bf16[1,128,512]{2,1,0:T(8,128)(2,1)S(1)}, bf16[1,128,512]{2,1,0:T(8,128)(2,1)S(1)}, u32[]{:S(2)}, u32[]{:S(2)}) collective-permute-start(bf16[1,128,512]{2,1,0:T(8,128)(2,1)S(1)} %copy-done.38), channel_id=1, source_target_pairs={{0,5},{1,4},{2,7},{3,6},{4,1},{5,0},{6,3},{7,2},{8,13},{9,12},{10,... | collective-permute-start | bytes 393224 | tf_op jit(solution)/shard_map/ppermute | solution.py:63
  106.6 8.2 %copy-start.41 = (bf16[2,128,256]{2,1,0:T(8,128)(2,1)S(1)}, bf16[2,128,256]{2,1,0:T(8,128)(2,1)}, u32[]{:S(2)}) copy-start(bf16[2,128,256]{2,1,0:T(8,128)(2,1)} %get-tuple-element.72) | copy-start | bytes 393220
  106.6 11.8 %collective-permute-start.29 = (bf16[2,128,256]{2,1,0:T(8,128)(2,1)}, bf16[2,128,256]{2,1,0:T(8,128)(2,1)S(1)}, u32[]{:S(2)}, u32[]{:S(2)}) collective-permute-start(bf16[2,128,256]{2,1,0:T(8,128)(2,1)} %get-tuple-element.70), channel_id=1, source_target_pairs={{0,1},{1,0},{2,3},{3,2},{4,5},{5,4},{6,7},{7,6},{8,9},{9,8},{10,11... | collective-permute-start | bytes 393224 | tf_op jit(solution)/shard_map/ppermute | solution.py:63
  111.6 10.3 %collective-permute-start.30 = (bf16[2,128,256]{2,1,0:T(8,128)(2,1)}, bf16[2,128,256]{2,1,0:T(8,128)(2,1)S(1)}, u32[]{:S(2)}, u32[]{:S(2)}) collective-permute-start(bf16[2,128,256]{2,1,0:T(8,128)(2,1)} %get-tuple-element.71), channel_id=1, source_target_pairs={{0,4},{1,5},{2,6},{3,7},{4,0},{5,1},{6,2},{7,3},{8,12},{9,13},{10,... | collective-permute-start | bytes 393224 | tf_op jit(solution)/shard_map/ppermute | solution.py:63
  114.8 4.8 %copy-start.8 = (bf16[1,128,512]{2,1,0:T(8,128)(2,1)}, bf16[1,128,512]{2,1,0:T(8,128)(2,1)S(1)}, u32[]{:S(2)}) copy-start(bf16[1,128,512]{2,1,0:T(8,128)(2,1)S(1)} %collective-permute-done.25.refs_5_) | copy-start | bytes 393220
  114.8 7.5 %collective-permute-start.31 = (bf16[2,128,256]{2,1,0:T(8,128)(2,1)S(1)}, bf16[2,128,256]{2,1,0:T(8,128)(2,1)S(1)}, u32[]{:S(2)}, u32[]{:S(2)}) collective-permute-start(bf16[2,128,256]{2,1,0:T(8,128)(2,1)S(1)} %copy-done.41), channel_id=1, source_target_pairs={{0,5},{1,4},{2,7},{3,6},{4,1},{5,0},{6,3},{7,2},{8,13},{9,12},{10,... | collective-permute-start | bytes 393224 | tf_op jit(solution)/shard_map/ppermute | solution.py:63
  116.0 3.5 %copy-start.9 = (bf16[1,128,512]{2,1,0:T(8,128)(2,1)}, bf16[1,128,512]{2,1,0:T(8,128)(2,1)S(1)}, u32[]{:S(2)}) copy-start(bf16[1,128,512]{2,1,0:T(8,128)(2,1)S(1)} %collective-permute-done.26.refs_6_) | copy-start | bytes 393220
  116.0 7.8 %collective-permute-start.35 = (bf16[2,128,256]{2,1,0:T(8,128)(2,1)}, bf16[2,128,256]{2,1,0:T(8,128)(2,1)S(1)}, u32[]{:S(2)}, u32[]{:S(2)}) collective-permute-start(bf16[2,128,256]{2,1,0:T(8,128)(2,1)} %get-tuple-element.78), channel_id=1, source_target_pairs={{0,1},{1,0},{2,3},{3,2},{4,5},{5,4},{6,7},{7,6},{8,9},{9,8},{10,11... | collective-permute-start | bytes 393224 | tf_op jit(solution)/shard_map/ppermute | solution.py:63
  117.5 2.0 %copy-start.10 = (bf16[1,128,512]{2,1,0:T(8,128)(2,1)}, bf16[1,128,512]{2,1,0:T(8,128)(2,1)S(1)}, u32[]{:S(2)}) copy-start(bf16[1,128,512]{2,1,0:T(8,128)(2,1)S(1)} %collective-permute-done.27.refs_7_) | copy-start | bytes 393220
  117.5 6.2 %collective-permute-start.36 = (bf16[2,128,256]{2,1,0:T(8,128)(2,1)}, bf16[2,128,256]{2,1,0:T(8,128)(2,1)S(1)}, u32[]{:S(2)}, u32[]{:S(2)}) collective-permute-start(bf16[2,128,256]{2,1,0:T(8,128)(2,1)} %get-tuple-element.79), channel_id=1, source_target_pairs={{0,4},{1,5},{2,6},{3,7},{4,0},{5,1},{6,2},{7,3},{8,12},{9,13},{10,... | collective-permute-start | bytes 393224 | tf_op jit(solution)/shard_map/ppermute | solution.py:63
  118.3 6.9 %copy-start.11 = (bf16[2,128,256]{2,1,0:T(8,128)(2,1)}, bf16[2,128,256]{2,1,0:T(8,128)(2,1)S(1)}, u32[]{:S(2)}) copy-start(bf16[2,128,256]{2,1,0:T(8,128)(2,1)S(1)} %collective-permute-done.29.refs_1_) | copy-start | bytes 393220
  118.3 6.9 %collective-permute-start.37 = (bf16[2,128,256]{2,1,0:T(8,128)(2,1)}, bf16[2,128,256]{2,1,0:T(8,128)(2,1)S(1)}, u32[]{:S(2)}, u32[]{:S(2)}) collective-permute-start(bf16[2,128,256]{2,1,0:T(8,128)(2,1)} %get-tuple-element.80), channel_id=1, source_target_pairs={{0,5},{1,4},{2,7},{3,6},{4,1},{5,0},{6,3},{7,2},{8,13},{9,12},{10,... | collective-permute-start | bytes 393224 | tf_op jit(solution)/shard_map/ppermute | solution.py:63
  121.9 3.3 %copy-start.12 = (bf16[2,128,256]{2,1,0:T(8,128)(2,1)}, bf16[2,128,256]{2,1,0:T(8,128)(2,1)S(1)}, u32[]{:S(2)}) copy-start(bf16[2,128,256]{2,1,0:T(8,128)(2,1)S(1)} %collective-permute-done.30.refs_2_) | copy-start | bytes 393220
  122.3 3.0 %copy-start.13 = (bf16[2,128,256]{2,1,0:T(8,128)(2,1)}, bf16[2,128,256]{2,1,0:T(8,128)(2,1)S(1)}, u32[]{:S(2)}) copy-start(bf16[2,128,256]{2,1,0:T(8,128)(2,1)S(1)} %collective-permute-done.31.refs_3_) | copy-start | bytes 393220
  (16 other events, 14.7 us)

commit v3 on v2

v3 whole, which is shorter than its diff:
```python
import itertools
import math

import jax
import jax.numpy as jnp
from jax import lax
from jax.experimental import pallas as pl
from jax.experimental.pallas import tpu as pltpu
from jax.sharding import PartitionSpec as P

QUERY_HEADS = 32
KEY_HEADS = 16
HEAD_SIZE = 128
WINDOW = 1024
GROUP = QUERY_HEADS // KEY_HEADS
AXES = ("seq", "tp")

attn_scale = 168.0 ** (-0.5)
masked_floor = -1e30

CHUNKS = 2
EASY, HARD = 1 << 21, 1 << 25
VMEM_LIMIT = 56 * 1024 * 1024
ANY = pl.BlockSpec(memory_space=pl.ANY)
VMEM = pl.BlockSpec(memory_space=pltpu.VMEM)
SMEM = pl.BlockSpec(memory_space=pltpu.SMEM)


class Plan:
    def __init__(self, rows):
        self.seq, self.tp = lax.axis_size("seq"), lax.axis_size("tp")
        self.rows = rows
        self.block = rows * self.tp
        self.slab = WINDOW // self.block
        self.cores = min(2, self.slab)
        self.ways = self.slab // self.cores
        self.groups = self.ways * self.tp
        self.key_heads = KEY_HEADS // self.groups
        self.chunks = min(CHUNKS, self.key_heads)
        self.heads = self.key_heads // self.chunks
        self.key_cols = self.heads * HEAD_SIZE
        self.query_cols = self.key_cols * GROUP
        self.pieces = self.slab * self.tp
        self.flips = sorted(range(self.groups), key=lambda flip: (flip > 0, -bin(flip).count("1")))

    def place(self):
        seq, tp = lax.axis_index("seq"), lax.axis_index("tp")
        inner = lax.rem(seq, self.slab)
        core = lax.rem(inner, self.cores)
        return seq - inner, core, (inner // self.cores) * self.tp + tp

    def routes(self, move):
        pairs = []
        for seq in range(self.seq):
            for tp in range(self.tp):
                slab, inner = divmod(seq, self.slab)
                way, core = divmod(inner, self.cores)
                to_slab, to_core, to_group = move(slab, core, way * self.tp + tp)
                to_slab %= self.seq // self.slab
                target = (to_slab * self.slab + to_group // self.tp * self.cores + to_core) * self.tp + to_group % self.tp
                pairs.append((seq * self.tp + tp, target))
        return pairs

    def to_group(self, value, flip):
        return lax.ppermute(value, AXES, self.routes(lambda slab, core, group: (slab, core, group ^ flip)))

    def to_core(self, value):
        return lax.ppermute(value, AXES, self.routes(lambda slab, core, group: (slab, self.cores - 1 - core, group)))

    def to_slab(self, value, step):
        return lax.ppermute(value, AXES, self.routes(lambda slab, core, group: (slab + step, core, group)))


def run_copies(copies):
    for copy in copies:
        copy.start()
    for copy in copies:
        copy.wait()


def traffic(count):
    return pl.CostEstimate(flops=0, bytes_accessed=count, transcendentals=0)


def columns(start, width):
    return pl.ds(pl.multiple_of(start, HEAD_SIZE), width)


def split_columns(plan, arrays, width, chunks, name, after=()):
    chunk_width = width // chunks

    def kernel(*refs):
        sources, targets, sem = refs[: len(arrays)], refs[len(arrays) + len(after) : -1], refs[-1]
        _, _, group = plan.place()
        copies = []
        for chunk in range(chunks):
            for at, flip in enumerate(plan.flips):
                start = (group ^ flip) * width + chunk * chunk_width
                for index, source in enumerate(sources):
                    copies.append(
                        pltpu.make_async_copy(
                            source.at[:, columns(start, chunk_width)],
                            targets[chunk * plan.groups + at].at[index],
                            sem.at[len(copies)],
                        )
                    )
        run_copies(copies)

    count = chunks * plan.groups
    shape = jax.ShapeDtypeStruct((len(arrays), plan.rows, chunk_width), jnp.bfloat16)
    out = pl.pallas_call(
        kernel,
        out_shape=[shape] * count,
        in_specs=[ANY] * (len(arrays) + len(after)),
        out_specs=[VMEM] * count,
        scratch_shapes=[pltpu.SemaphoreType.DMA((count * len(arrays),))],
        cost_estimate=traffic(2 * sum(array.nbytes for array in arrays)),
        name=name,
    )(*arrays, *after)
    return [out[chunk * plan.groups : (chunk + 1) * plan.groups] for chunk in range(chunks)]


def gather_pieces(plan, pieces, cost, after=()):
    def kernel(*refs):
        sources, target, sem = refs[: plan.groups], refs[-2], refs[-1]
        _, _, group = plan.place()
        run_copies(
            [
                pltpu.make_async_copy(source, target.at[group ^ flip], sem.at[flip])
                for flip, source in zip(plan.flips, sources)
            ]
        )

    return pl.pallas_call(
        kernel,
        out_shape=jax.ShapeDtypeStruct((plan.groups,) + pieces[0].shape, jnp.bfloat16),
        in_specs=[ANY] * (plan.groups + len(after)),
        out_specs=VMEM,
        scratch_shapes=[pltpu.SemaphoreType.DMA((plan.groups,))],
        cost_estimate=traffic(cost),
        name="gather_keys",
    )(*pieces, *after)


def backward(plan, chunk, doc_lengths, query_pieces, key_arrays, after):
    tiles = plan.slab + 1
    block, groups, tp, cores = plan.block, plan.groups, plan.tp, plan.cores
    heads, key_cols, query_cols = plan.heads, plan.key_cols, plan.query_cols
    wide = GROUP * block
    query_width = HEAD_SIZE * GROUP
    exponent_scale = attn_scale * math.log2(math.e)
    loads = heads * (2 * groups + 8 * plan.ways)
    stores = heads * (2 * groups + 3)

    def kernel(docs, *refs):
        pieces, refs = refs[:groups], refs[groups:]
        key_refs, refs = refs[:4], refs[4:]
        refs = refs[len(after) :]
        query_out, refs = refs[:groups], refs[groups:]
        before_mine, own_mine, own_far, refs = *refs[:3], refs[3:]
        parts = (before_mine, None, own_mine, own_far)
        before_far, refs = refs[:groups], refs[groups:]
        q_s, o_s, k_s, v_s, dq_s, dk_s, dv_s, part_s, score_s, prob_grad_s, prob_s, grad_s, sem, out_sem = refs
        slab_seq, core, group = plan.place()

        copies, results = [], []

        def load(source, target):
            copies.append(pltpu.make_async_copy(source, target, sem.at[len(copies)]))
            copies[-1].start()

        def store(source, target):
            results.append(pltpu.make_async_copy(source, target, out_sem.at[len(results)]))
            results[-1].start()

        for head in range(heads):
            here, there = pl.ds(head * query_width, query_width), pl.ds((chunk * heads + head) * query_width, query_width)
            for flip, piece in zip(plan.flips, pieces):
                load(piece.at[0, :, there], q_s.at[group ^ flip, :, here])
                load(piece.at[1, :, there], o_s.at[group ^ flip, :, here])
            here, there = pl.ds(head * HEAD_SIZE, HEAD_SIZE), pl.ds((chunk * heads + head) * HEAD_SIZE, HEAD_SIZE)
            for source, (late, away) in zip(key_refs, itertools.product((1, 0), (0, 1))):
                side = core + away * (cores - 1 - 2 * core)
                for way in range(plan.ways):
                    start = late * plan.pieces + (way * cores + side) * tp
                    for index, target in enumerate((k_s, v_s)):
                        load(source.at[pl.ds(way * tp, tp), index, :, there], target.at[pl.ds(start, tp), :, here])
        dk_s[...] = jnp.zeros_like(dk_s)
        dv_s[...] = jnp.zeros_like(dv_s)

        def step(head, way):
            key_at = (way * cores + core) * tp
            head_cols = pl.ds(head * HEAD_SIZE, HEAD_SIZE)
            rows_at = pl.ds(way * tp, tp)

            def both(ref):
                parts = [
                    ref[rows_at, :, pl.ds((head * GROUP + member) * HEAD_SIZE, HEAD_SIZE)].reshape(block, HEAD_SIZE)
                    for member in range(GROUP)
                ]
                return jnp.concatenate(parts, axis=0)

            queries, grads = both(q_s), both(o_s)
            inner = lax.broadcasted_iota(jnp.int32, (1, block), 1)
            inner = jnp.concatenate([inner] * GROUP, axis=1)
            first = (slab_seq + way * cores + core) * block
            position = inner + first
            lowest = position - (WINDOW - 1)
            start = jnp.int32(0)
            for doc in range(docs.shape[0]):
                lowest = jnp.where(position >= start, jnp.maximum(lowest, start), lowest)
                start = start + docs[doc]
            lowest = lowest - (first - WINDOW)

            def key_rows(ref, tile):
                return ref[pl.ds(key_at + tile * tp, tp), :, head_cols].reshape(block, HEAD_SIZE)

            def tile_rows(tile):
                return pl.ds(tile * block, block)

            peak = jnp.full((1, wide), masked_floor, jnp.float32)
            for tile in range(tiles):
                scores = lax.dot_general(
                    key_rows(k_s, tile), queries, (((1,), (1,)), ((), ())), preferred_element_type=jnp.float32
                )
                row = lax.broadcasted_iota(jnp.int32, (block, wide), 0)
                allowed = row >= lowest - tile * block
                if tile == tiles - 1:
                    allowed = allowed & (row <= inner)
                scores = jnp.where(allowed, scores, masked_floor)
                peak = jnp.maximum(peak, jnp.max(scores, axis=0, keepdims=True))
                score_s[tile_rows(tile), :] = scores
            peak = peak * exponent_scale
            total = jnp.zeros((1, wide), jnp.float32)
            delta = jnp.zeros((1, wide), jnp.float32)
            for tile in range(tiles):
                raised = jnp.exp2(score_s[tile_rows(tile), :] * exponent_scale - peak)
                prob_grad = lax.dot_general(
                    key_rows(v_s, tile), grads, (((1,), (1,)), ((), ())), preferred_element_type=jnp.float32
                )
                total = total + jnp.sum(raised, axis=0, keepdims=True)
                delta = delta + jnp.sum(raised * prob_grad, axis=0, keepdims=True)
                score_s[tile_rows(tile), :] = raised
                prob_grad_s[tile_rows(tile), :] = prob_grad
            inverse = 1.0 / total
            delta = delta * inverse
            for tile in range(tiles):
                probs = score_s[tile_rows(tile), :] * inverse
                prob_s[tile_rows(tile), :] = probs.astype(jnp.bfloat16)
                grad_scores = probs * (prob_grad_s[tile_rows(tile), :] - delta) * attn_scale
                grad_s[tile_rows(tile), :] = grad_scores.astype(jnp.bfloat16)
            at = pl.ds(key_at, tiles * tp)
            shape = (tiles * tp, plan.rows, HEAD_SIZE)
            dv_s[at, :, head_cols] += jnp.dot(prob_s[...], grads, preferred_element_type=jnp.float32).reshape(shape)
            dk_s[at, :, head_cols] += jnp.dot(grad_s[...], queries, preferred_element_type=jnp.float32).reshape(shape)
            query_sum = lax.dot_general(
                k_s[at, :, head_cols].reshape(tiles * block, HEAD_SIZE),
                grad_s[...],
                (((0,), (0,)), ((), ())),
                preferred_element_type=jnp.float32,
            )
            query_rows = query_sum.T.astype(jnp.bfloat16)
            for member in range(GROUP):
                dq_s[rows_at, :, pl.ds((head * GROUP + member) * HEAD_SIZE, HEAD_SIZE)] = query_rows[
                    member * block : (member + 1) * block
                ].reshape(tp, plan.rows, HEAD_SIZE)

        for head in range(heads):
            for copy in copies[head * loads // heads : (head + 1) * loads // heads]:
                copy.wait()
            for way in range(plan.ways):
                step(head, way)
            head_cols = pl.ds(head * HEAD_SIZE, HEAD_SIZE)
            for late, away in itertools.product((0, 1), (0, 1)):
                side = core + away * (cores - 1 - 2 * core)
                staged = part_s.at[late, away]
                for way, index in itertools.product(range(plan.ways), (0, 1)):
                    at = pl.ds(late * plan.pieces + (way * cores + side) * tp, tp)
                    total = (dk_s, dv_s)[index][at, :, head_cols]
                    staged[pl.ds(way * tp, tp), index, :, head_cols] = total.astype(jnp.bfloat16)
                if late or not away:
                    store(staged.at[:, :, :, head_cols], parts[2 * late + away].at[:, :, :, head_cols])
                else:
                    for piece in range(groups):
                        store(staged.at[piece, :, :, head_cols], before_far[piece].at[:, :, head_cols])
            done_part = pl.ds(head * query_width, query_width)
            for at, flip in enumerate(plan.flips):
                store(dq_s.at[group ^ flip, :, done_part], query_out[at].at[0, :, done_part])
        for copy in results:
            copy.wait()

    part = (groups, 2, plan.rows, key_cols)
    bf, fl = jnp.bfloat16, jnp.float32
    span = 2 * plan.pieces
    pairs = tiles * block * wide * heads * plan.ways
    out = pl.pallas_call(
        kernel,
        out_shape=[jax.ShapeDtypeStruct((1, plan.rows, query_cols), bf)] * groups
        + [jax.ShapeDtypeStruct(part, bf)] * 3
        + [jax.ShapeDtypeStruct(part[1:], bf)] * groups,
        in_specs=[SMEM] + [ANY] * (groups + 4 + len(after)),
        out_specs=[ANY] * (2 * groups + 3),
        scratch_shapes=[
            pltpu.VMEM((groups, plan.rows, query_cols), bf),
            pltpu.VMEM((groups, plan.rows, query_cols), bf),
            pltpu.VMEM((span, plan.rows, key_cols), bf),
            pltpu.VMEM((span, plan.rows, key_cols), bf),
            pltpu.VMEM((groups, plan.rows, query_cols), bf),
            pltpu.VMEM((span, plan.rows, key_cols), fl),
            pltpu.VMEM((span, plan.rows, key_cols), fl),
            pltpu.VMEM((2, 2) + part, bf),
            pltpu.VMEM((tiles * block, wide), fl),
            pltpu.VMEM((tiles * block, wide), fl),
            pltpu.VMEM((tiles * block, wide), bf),
            pltpu.VMEM((tiles * block, wide), bf),
            pltpu.SemaphoreType.DMA((loads,)),
            pltpu.SemaphoreType.DMA((stores,)),
        ],
        compiler_params=pltpu.CompilerParams(vmem_limit_bytes=VMEM_LIMIT),
        cost_estimate=pl.CostEstimate(flops=160 * pairs * HEAD_SIZE, bytes_accessed=6 << 20, transcendentals=pairs),
        name="backward",
    )(doc_lengths, *query_pieces, *key_arrays, *after)
    return out[:groups], out[groups : groups + 3], out[groups + 3 :]


def add_before(plan, mine, far, after):
    def kernel(mine_ref, *refs):
        for piece in range(plan.groups):
            total = mine_ref[piece].astype(jnp.float32) + refs[piece][...].astype(jnp.float32)
            refs[-1][piece] = total.astype(jnp.bfloat16)

    return pl.pallas_call(
        kernel,
        out_shape=jax.ShapeDtypeStruct(mine.shape, jnp.bfloat16),
        in_specs=[VMEM] * (1 + plan.groups) + [ANY] * len(after),
        out_specs=VMEM,
        cost_estimate=traffic(3 * mine.nbytes),
        name="add_before",
    )(mine, *far, *after)


def add_up(plan, mine, far, later, cost, riders):
    def kernel(mine_ref, far_ref, later_ref, *refs):
        _, _, group = plan.place()
        for at, flip in enumerate(plan.flips):
            piece, target = group ^ flip, refs[len(riders) + at]
            total = mine_ref[piece].astype(jnp.float32) + far_ref[piece].astype(jnp.float32)
            total = (total + later_ref[piece].astype(jnp.float32)).astype(jnp.bfloat16)
            if riders:
                target[0] = refs[at][0]
                target[1, :, : plan.key_cols] = total[0]
                target[1, :, plan.key_cols :] = total[1]
            else:
                target[...] = total

    shape = (2, plan.rows, 2 * plan.key_cols if riders else plan.key_cols)
    return pl.pallas_call(
        kernel,
        out_shape=[jax.ShapeDtypeStruct(shape, jnp.bfloat16)] * plan.groups,
        in_specs=[VMEM] * (3 + len(riders)),
        out_specs=[VMEM] * plan.groups,
        cost_estimate=traffic(cost),
        name="add_up",
    )(mine, far, later, *riders)


def join_columns(plan, sources, targets, width, name):
    flat = [piece for pieces in sources for piece in pieces]
    chunks = len(targets[0])
    chunk_width = width // chunks

    def kernel(*refs):
        pieces, outs, sem = refs[: len(flat)], refs[len(flat) : -1], refs[-1]
        _, _, group = plan.place()
        copies = []
        for out, parts in zip(outs, targets):
            for chunk, (which, row, column) in enumerate(parts):
                for at, flip in enumerate(plan.flips):
                    start = (group ^ flip) * width + chunk * chunk_width
                    copies.append(
                        pltpu.make_async_copy(
                            pieces[which * plan.groups + at].at[row, :, pl.ds(column, chunk_width)],
                            out.at[:, columns(start, chunk_width)],
                            sem.at[len(copies)],
                        )
                    )
        run_copies(copies)

    return pl.pallas_call(
        kernel,
        out_shape=[jax.ShapeDtypeStruct((plan.rows, width * plan.groups), jnp.bfloat16)] * len(targets),
        in_specs=[ANY] * len(flat),
        out_specs=[VMEM] * len(targets),
        scratch_shapes=[pltpu.SemaphoreType.DMA((len(targets) * chunks * plan.groups,))],
        cost_estimate=traffic(2 * sum(piece.nbytes for piece in flat)),
        name=name,
    )(*flat)


def per_device(queries, key_states, value_state_rows, out_grad, doc_lengths):
    plan = Plan(queries.shape[0])
    key_width = KEY_HEADS * HEAD_SIZE // plan.groups
    query_width = QUERY_HEADS * HEAD_SIZE // plan.groups

    def exchange(pieces):
        return [pieces[0]] + [plan.to_group(piece, flip) for piece, flip in zip(pieces[1:], plan.flips[1:])]

    key_parts = split_columns(plan, (key_states, value_state_rows), key_width, 1, "split_keys")[0]
    query_parts = split_columns(plan, (queries, out_grad), query_width, 1, "split_queries", after=(key_parts[0],))[0]
    pieces = exchange(key_parts)
    arrived = exchange(query_parts)
    own = gather_pieces(plan, pieces, HARD)
    before = gather_pieces(plan, [plan.to_slab(piece, 1) for piece in pieces], HARD, (own, *arrived[1:]))
    key_arrays = (own, plan.to_core(own), before, plan.to_core(before))
    after, wait = (), ()
    sums, query_outs, sent = [], [], []
    for chunk in range(plan.chunks):
        query_out, (before_mine, own_mine, own_far), before_far = backward(plan, chunk, doc_lengths, arrived, key_arrays, after)
        before_sum = add_before(plan, before_mine, [plan.to_core(piece) for piece in before_far], wait)
        later = plan.to_slab(before_sum, -1)
        sums.append((own_mine, plan.to_core(own_far), later))
        query_outs.append(query_out)
        if chunk < plan.chunks - 1 or plan.chunks == 1:
            sent.append(exchange(query_out))
            after = (before_sum, *sent[-1][1:])
        wait = (later,)
    query_from, key_from, value_from = ([(chunk, 0, 0) for chunk in range(len(sent))], [], [])
    for chunk in range(plan.chunks):
        last, first = chunk == plan.chunks - 1, chunk == 0
        riders = query_outs[-1] if first and not last else ()
        sent.append(exchange(add_up(plan, *sums[chunk], EASY if last else HARD, riders)))
        at = len(sent) - 1
        if riders:
            query_from.append((at, 0, 0))
        key_from.append((at, 1, 0) if riders else (at, 0, 0))
        value_from.append((at, 1, plan.key_cols) if riders else (at, 1, 0))
    (query_grad,) = join_columns(plan, sent[: plan.chunks], [query_from], query_width, "join_queries")
    key_gradient, value_gradient = join_columns(plan, sent, [key_from, value_from], key_width, "join_keys")
    return query_grad, key_gradient, value_gradient


def solution(mesh):
    split = P(("seq", "tp"), None)
    return jax.shard_map(
        per_device,
        mesh=mesh,
        in_specs=(split, split, split, split, P()),
        out_specs=(split, split, split),
        check_vma=False,
    )
```

time: 129 us -> 127 us (0.984)
  starting transfers between devices: 41.6 us -> 35.2 us
  local copies, waits for them, and re-layouts: 5.01 us -> 8.22 us
  waiting for transfers between devices: 27.7 us -> 29.8 us
    ppermute x21 -> x15, starting transfers between devices: 27.2 us -> 19.9 us  [to_group(): lax.ppermute(value, AXES, self.routes(lambda slab, core, group: (slab, co...]
    ppermute x11 -> x12, waiting for transfers between devices: 0.03 us -> 4.57 us  [to_core(): lax.ppermute(value, AXES, self.routes(lambda slab, core, group: (slab, se...]
    unnamed x84 -> x66, local copies, waits for them, and re-layouts: 5.01 us -> 8.22 us
    ppermute x21 -> x15, waiting for transfers between devices: 11.4 us -> 10.1 us  [to_group(): lax.ppermute(value, AXES, self.routes(lambda slab, core, group: (slab, co...]
    ppermute x11 -> x12, starting transfers between devices: 1.57 us -> 2.76 us  [to_core(): lax.ppermute(value, AXES, self.routes(lambda slab, core, group: (slab, se...]
    pallas_call x7 -> x8, Pallas kernels: 42.8 us -> 42.2 us  [the longest x2 28.4 us: backward(): pl.pallas_call(kernel, out_shape=[jax.ShapeDtypeStruct((1, plan.rows, que...]
  transfers between devices with their start and end apart: 38 -> 33, of which waited for: 12 -> 14; matrix products, arithmetic and copies ran while one was open for 0% -> 0% of each run, Pallas kernels for 36% -> 26%
where the time goes in v3:
time: 127 us; the launch traced here: 126 us
  Pallas kernels  52.1 us (41%)
  starting transfers between devices  35.2 us (28%)
  waiting for transfers between devices  29.8 us (23%)
  local copies, waits for them, and re-layouts  8.22 us (6%)
    pallas_call x2, Pallas kernels, backward(): pl.pallas_call(kernel, out_shape=[jax.ShapeDtypeStruct((1, plan.rows, que...  28.4 us
    ppermute x15, starting transfers between devices, to_group(): lax.ppermute(value, AXES, self.routes(lambda slab, core, group: (slab, co...  19.9 us
    ppermute x6, waiting for transfers between devices, to_slab(): lax.ppermute(value, AXES, self.routes(lambda slab, core, group: (slab + s...  15.1 us
    ppermute x6, starting transfers between devices, to_slab(): lax.ppermute(value, AXES, self.routes(lambda slab, core, group: (slab + s...  12.5 us
    ppermute x15, waiting for transfers between devices, to_group(): lax.ppermute(value, AXES, self.routes(lambda slab, core, group: (slab, co...  10.1 us
    unnamed x66, local copies, waits for them, and re-layouts  8.22 us
    pallas_call x2, Pallas kernels, split_columns(): pl.pallas_call(kernel, out_shape=[shape] * count, in_specs=[ANY] * (len(a...  5.23 us
    pallas_call x2, Pallas kernels, add_up(): pl.pallas_call(kernel, out_shape=[jax.ShapeDtypeStruct(shape, jnp.bfloat1...  4.88 us
  transfers between devices with their start and end apart: 33, of which 14 were waited for; matrix products, arithmetic and copies ran while one was open for 0% of the time, Pallas kernels for 26%

profile of v3, /device:TPU:0, one launch (start us, length us, event | category | flops | bytes accessed | tf_op | source)
XLA Modules:
  0.0 126.2 jit_solution(8206379488852219891)
XLA Ops:
  0.6 2.3 %split_keys.1 = (bf16[2,128,512]{2,1,0:T(8,128)(2,1)}, bf16[2,128,512]{2,1,0:T(8,128)(2,1)}, bf16[2,128,512]{2,1,0:T(8,128)(2,1)}, bf16[2,128,512]{2,1,0:T(8,128)(2,1)}) custom-call(bf16[128,2048]{1,0:T(8,128)(2,1)} %refs_0_.2, bf16[128,2048]{1,0:T(8,128)(2,1)} %refs_1_.2), custom_call_target="tpu_custom_call" | custom-call | bytes 2097152 | tf_op jit(solution)/shard_map/split_keys/pallas_call | solution.py:111
  3.0 4.0 %collective-permute-start.3 = (bf16[2,128,512]{2,1,0:T(8,128)(2,1)}, bf16[2,128,512]{2,1,0:T(8,128)(2,1)S(1)}, u32[]{:S(2)}, u32[]{:S(2)}) collective-permute-start(bf16[2,128,512]{2,1,0:T(8,128)(2,1)} %get-tuple-element.48), channel_id=1, source_target_pairs={{0,5},{1,4},{2,7},{3,6},{4,1},{5,0},{6,3},{7,2},{8,13},{9,12},{10,... | collective-permute-start | bytes 786440 | tf_op jit(solution)/shard_map/ppermute | solution.py:65
  6.9 0.5 collective-permute-start.4
  7.6 2.0 %collective-permute-start.7 = (bf16[2,128,512]{2,1,0:T(8,128)(2,1)}, bf16[2,128,512]{2,1,0:T(8,128)(2,1)S(1)}, u32[]{:S(2)}, u32[]{:S(2)}) collective-permute-start(bf16[2,128,512]{2,1,0:T(8,128)(2,1)} %get-tuple-element.43.refs_2_.refs_0_), channel_id=1, source_target_pairs={{0,8},{1,9},{2,10},{3,11},{4,12},{5,13},{6,14},{7,15},{8,16},{9,17... | collective-permute-start | bytes 786440 | tf_op jit(solution)/shard_map/ppermute | solution.py:71
  9.5 2.9 %split_queries.1 = (bf16[2,128,1024]{2,1,0:T(8,128)(2,1)}, bf16[2,128,1024]{2,1,0:T(8,128)(2,1)}, bf16[2,128,1024]{2,1,0:T(8,128)(2,1)}, bf16[2,128,1024]{2,1,0:T(8,128)(2,1)}) custom-call(bf16[128,4096]{1,0:T(8,128)(2,1)} %refs_0_.3, bf16[128,4096]{1,0:T(8,128)(2,1)} %refs_1_.3, bf16[2,128,512]{2,1,0:T(8,128)(2,1)} %get-tuple-element.43.refs_2_.refs_0_), custom_call_target="tpu_custom_call" | custom-call | bytes 4194304 | tf_op jit(solution)/shard_map/split_queries/pallas_call | solution.py:111
  12.5 2.5 %collective-permute-start = (bf16[2,128,1024]{2,1,0:T(8,128)(2,1)}, bf16[2,128,1024]{2,1,0:T(8,128)(2,1)S(1)}, u32[]{:S(2)}, u32[]{:S(2)}) collective-permute-start(bf16[2,128,1024]{2,1,0:T(8,128)(2,1)} %get-tuple-element.45), channel_id=1, source_target_pairs={{0,5},{1,4},{2,7},{3,6},{4,1},{5,0},{6,3},{7,2},{8,13},{9,12},{10,... | collective-permute-start | bytes 1572872 | tf_op jit(solution)/shard_map/ppermute | solution.py:65
  15.0 1.6 %collective-permute-start.8 = (bf16[2,128,512]{2,1,0:T(8,128)(2,1)S(1)}, bf16[2,128,512]{2,1,0:T(8,128)(2,1)S(1)}, u32[]{:S(2)}, u32[]{:S(2)}) collective-permute-start(bf16[2,128,512]{2,1,0:T(8,128)(2,1)S(1)} %collective-permute-done.3.refs_1_), channel_id=1, source_target_pairs={{0,8},{1,9},{2,10},{3,11},{4,12},{5,13},{6,14},{7,15},{8,16},{9,17... | collective-permute-start | bytes 786440 | tf_op jit(solution)/shard_map/ppermute | solution.py:71
  16.6 3.3 %collective-permute-done.4.refs_2_ = bf16[2,128,512]{2,1,0:T(8,128)(2,1)S(1)} collective-permute-done((bf16[2,128,512]{2,1,0:T(8,128)(2,1)}, bf16[2,128,512]{2,1,0:T(8,128)(2,1)S(1)}, u32[]{:S(2)}, u32[]{:S(2)}) %collective-permute-start.4) | collective-permute-done | bytes 262176 | tf_op jit(solution)/shard_map/ppermute | solution.py:65
  19.8 2.0 %collective-permute-start.1 = (bf16[2,128,1024]{2,1,0:T(8,128)(2,1)}, bf16[2,128,1024]{2,1,0:T(8,128)(2,1)S(1)}, u32[]{:S(2)}, u32[]{:S(2)}) collective-permute-start(bf16[2,128,1024]{2,1,0:T(8,128)(2,1)} %get-tuple-element.46), channel_id=1, source_target_pairs={{0,1},{1,0},{2,3},{3,2},{4,5},{5,4},{6,7},{7,6},{8,9},{9,8},{10,11... | collective-permute-start | bytes 1572872 | tf_op jit(solution)/shard_map/ppermute | solution.py:65
  22.0 1.6 %collective-permute-start.9 = (bf16[2,128,512]{2,1,0:T(8,128)(2,1)S(1)}, bf16[2,128,512]{2,1,0:T(8,128)(2,1)S(1)}, u32[]{:S(2)}, u32[]{:S(2)}) collective-permute-start(bf16[2,128,512]{2,1,0:T(8,128)(2,1)S(1)} %collective-permute-done.4.refs_2_), channel_id=1, source_target_pairs={{0,8},{1,9},{2,10},{3,11},{4,12},{5,13},{6,14},{7,15},{8,16},{9,17... | collective-permute-start | bytes 786440 | tf_op jit(solution)/shard_map/ppermute | solution.py:71
  23.5 1.6 %collective-permute-start.10 = (bf16[2,128,512]{2,1,0:T(8,128)(2,1)S(1)}, bf16[2,128,512]{2,1,0:T(8,128)(2,1)S(1)}, u32[]{:S(2)}, u32[]{:S(2)}) collective-permute-start(bf16[2,128,512]{2,1,0:T(8,128)(2,1)S(1)} %collective-permute-done.5.refs_3_), channel_id=1, source_target_pairs={{0,8},{1,9},{2,10},{3,11},{4,12},{5,13},{6,14},{7,15},{8,16},{9,17... | collective-permute-start | bytes 786440 | tf_op jit(solution)/shard_map/ppermute | solution.py:71
  25.1 2.2 %gather_keys.2.refs_4_ = bf16[4,2,128,512]{3,2,1,0:T(8,128)(2,1)} custom-call(bf16[2,128,512]{2,1,0:T(8,128)(2,1)} %get-tuple-element.43.refs_2_.refs_0_, bf16[2,128,512]{2,1,0:T(8,128)(2,1)} %copy-done.18, bf16[2,128,512]{2,1,0:T(8,128)(2,1)} %copy-done.19, bf16[2,128,512]{2,1,0:T(8,128)(2,1)} %copy-done.17), custom_call_target="tpu_custom_call" | custom-call | bytes 33554432 | tf_op jit(solution)/shard_map/gather_keys/pallas_call | solution.py:134
  27.4 5.6 %collective-permute-done.9.refs_2_ = bf16[2,128,512]{2,1,0:T(8,128)(2,1)S(1)} collective-permute-done((bf16[2,128,512]{2,1,0:T(8,128)(2,1)S(1)}, bf16[2,128,512]{2,1,0:T(8,128)(2,1)S(1)}, u32[]{:S(2)}, u32[]{:S(2)}) %collective-permute-start.9) | collective-permute-done | bytes 262176 | tf_op jit(solution)/shard_map/ppermute | solution.py:71
  33.0 4.3 %collective-permute-done.10.refs_3_ = bf16[2,128,512]{2,1,0:T(8,128)(2,1)S(1)} collective-permute-done((bf16[2,128,512]{2,1,0:T(8,128)(2,1)S(1)}, bf16[2,128,512]{2,1,0:T(8,128)(2,1)S(1)}, u32[]{:S(2)}, u32[]{:S(2)}) %collective-permute-start.10) | collective-permute-done | bytes 262176 | tf_op jit(solution)/shard_map/ppermute | solution.py:71
  37.3 4.3 %collective-permute-done.1.refs_6_.refs_2_ = bf16[2,128,1024]{2,1,0:T(8,128)(2,1)S(1)} collective-permute-done((bf16[2,128,1024]{2,1,0:T(8,128)(2,1)}, bf16[2,128,1024]{2,1,0:T(8,128)(2,1)S(1)}, u32[]{:S(2)}, u32[]{:S(2)}) %collective-permute-start.1) | collective-permute-done | bytes 524320 | tf_op jit(solution)/shard_map/ppermute | solution.py:65
  41.6 0.3 collective-permute-done.2.refs_7_.refs_3_
  41.9 0.5 copy-done.5
  42.4 0.8 copy-done.6
  43.2 2.2 %gather_keys.3.refs_6_ = bf16[4,2,128,512]{3,2,1,0:T(8,128)(2,1)} custom-call(bf16[2,128,512]{2,1,0:T(8,128)(2,1)} %copy-done.13, bf16[2,128,512]{2,1,0:T(8,128)(2,1)} %copy-done.14, bf16[2,128,512]{2,1,0:T(8,128)(2,1)} %copy-done.15, bf16[2,128,512]{2,1,0:T(8,128)(2,1)} %copy-done.16, bf16[4,2,128,512]{3,2,1,0:T(8,128)(2,1)} %gather_keys.2.refs_4_, ...), custom_call_target="tpu_custom_call" | custom-call | bytes 33554432 | tf_op jit(solution)/shard_map/gather_keys/pallas_call | solution.py:134
  45.5 2.8 %collective-permute-done.11.refs_7_ = bf16[4,2,128,512]{3,2,1,0:T(8,128)(2,1)S(1)} collective-permute-done((bf16[4,2,128,512]{3,2,1,0:T(8,128)(2,1)}, bf16[4,2,128,512]{3,2,1,0:T(8,128)(2,1)S(1)}, u32[]{:S(2)}, u32[]{:S(2)}) %collective-permute-start.11) | collective-permute-done | bytes 1048608 | tf_op jit(solution)/shard_map/ppermute | solution.py:68
  48.3 1.0 copy-done.31
  49.3 14.2 %backward.2 = (bf16[1,128,512]{2,1,0:T(8,128)(2,1)}, bf16[1,128,512]{2,1,0:T(8,128)(2,1)}, bf16[1,128,512]{2,1,0:T(8,128)(2,1)}, bf16[1,128,512]{2,1,0:T(8,128)(...) custom-call(s32[4]{0:T(128)} %docs.3, ...), custom_call_target="tpu_custom_call" | custom-call | flops 53687091200 | bytes 6291456 | tf_op jit(solution)/shard_map/backward/pallas_call | solution.py:296
  63.5 0.2 collective-permute-start.16
  63.7 0.4 collective-permute-start.17
  64.1 2.6 %collective-permute-start.12 = (bf16[1,128,512]{2,1,0:T(8,128)(2,1)}, bf16[1,128,512]{2,1,0:T(8,128)(2,1)S(1)}, u32[]{:S(2)}, u32[]{:S(2)}) collective-permute-start(bf16[1,128,512]{2,1,0:T(8,128)(2,1)} %get-tuple-element.52), channel_id=1, source_target_pairs={{0,5},{1,4},{2,7},{3,6},{4,1},{5,0},{6,3},{7,2},{8,13},{9,12},{10,... | collective-permute-start | bytes 393224 | tf_op jit(solution)/shard_map/ppermute | solution.py:65
  66.7 0.5 collective-permute-start.19
  67.3 0.5 collective-permute-start.13
  67.8 0.6 collective-permute-start.14
  68.5 0.5 copy-done.27
  69.0 0.2 copy-done.29
  69.2 2.3 %add_before.2.refs_8_ = bf16[4,2,128,256]{3,2,1,0:T(8,128)(2,1)} custom-call(bf16[4,2,128,256]{3,2,1,0:T(8,128)(2,1)} %get-tuple-element.57.mine_ref, bf16[2,128,256]{2,1,0:T(8,128)(2,1)} %copy-done.22, bf16[2,128,256]{2,1,0:T(8,128)(2,1)} %copy-done.24, bf16[2,128,256]{2,1,0:T(8,128)(2,1)} %copy-done.27, bf16[2,128,256]{2,1,0:T(8,128)(2,1)} %copy-done.29), custom_call_target="tpu_custom_call" | custom-call | bytes 1572864 | tf_op jit(solution)/shard_map/add_before/pallas_call | solution.py:332
  71.5 3.6 %collective-permute-start.20 = (bf16[4,2,128,256]{3,2,1,0:T(8,128)(2,1)}, bf16[4,2,128,256]{3,2,1,0:T(8,128)(2,1)S(1)}, u32[]{:S(2)}, u32[]{:S(2)}) collective-permute-start(bf16[4,2,128,256]{3,2,1,0:T(8,128)(2,1)} %add_before.2.refs_8_), channel_id=1, source_target_pairs={{0,24},{1,25},{2,26},{3,27},{4,28},{5,29},{6,30},{7,31},{8,0},{9,1... | collective-permute-start | bytes 1572872 | tf_op jit(solution)/shard_map/ppermute | solution.py:71
  75.2 0.6 copy-done.9
  75.8 0.6 copy-done.11
  76.5 14.2 %backward.3 = (bf16[1,128,512]{2,1,0:T(8,128)(2,1)}, bf16[1,128,512]{2,1,0:T(8,128)(2,1)}, bf16[1,128,512]{2,1,0:T(8,128)(2,1)}, bf16[1,128,512]{2,1,0:T(8,128)(...) custom-call(s32[4]{0:T(128)} %docs.3, ...), custom_call_target="tpu_custom_call" | custom-call | flops 53687091200 | bytes 6291456 | tf_op jit(solution)/shard_map/backward/pallas_call | solution.py:296
  90.8 0.5 collective-permute-start.15
  91.4 0.4 collective-permute-start.27
  91.8 0.5 collective-permute-done.25.refs_0_
  92.3 0.1 collective-permute-start.28
  92.5 0.8 collective-permute-done.26.refs_1_
  93.3 0.3 collective-permute-start.24
  93.6 0.3 collective-permute-done.28.refs_3_
  93.9 0.3 copy-done.28
  94.3 0.3 copy-done.30
  94.6 0.2 copy-done
  94.7 2.1 %add_before.3 = bf16[4,2,128,256]{3,2,1,0:T(8,128)(2,1)} custom-call(bf16[4,2,128,256]{3,2,1,0:T(8,128)(2,1)} %get-tuple-element.72.mine_ref, bf16[2,128,256]{2,1,0:T(8,128)(2,1)} %copy-done.23, bf16[2,128,256]{2,1,0:T(8,128)(2,1)} %copy-done.26, bf16[2,128,256]{2,1,0:T(8,128)(2,1)} %copy-done.28, bf16[2,128,256]{2,1,0:T(8,128)(2,1)} %copy-done.30, ...), custom_call_target="tpu_custom_call" | custom-call | bytes 1572864 | tf_op jit(solution)/shard_map/add_before/pallas_call | solution.py:332
  96.9 2.2 %collective-permute-start.29 = (bf16[4,2,128,256]{3,2,1,0:T(8,128)(2,1)}, bf16[4,2,128,256]{3,2,1,0:T(8,128)(2,1)S(1)}, u32[]{:S(2)}, u32[]{:S(2)}) collective-permute-start(bf16[4,2,128,256]{3,2,1,0:T(8,128)(2,1)} %add_before.3), channel_id=1, source_target_pairs={{0,24},{1,25},{2,26},{3,27},{4,28},{5,29},{6,30},{7,31},{8,0},{9,1... | collective-permute-start | bytes 1572872 | tf_op jit(solution)/shard_map/ppermute | solution.py:71
  99.1 0.8 copy-done.12
  99.8 2.6 %add_up.2 = (bf16[2,128,512]{2,1,0:T(8,128)(2,1)}, bf16[2,128,512]{2,1,0:T(8,128)(2,1)}, bf16[2,128,512]{2,1,0:T(8,128)(2,1)}, bf16[2,128,512]{2,1,0:T(8,128)(2,1)}) custom-call(bf16[4,2,128,256]{3,2,1,0:T(8,128)(2,1)} %get-tuple-element.55.mine_ref, bf16[4,2,128,256]{3,2,1,0:T(8,128)(2,1)} %copy-done.12, bf16[4,2,128,256]{3,2,1,0:T(8,128)(2,1)} %copy-done, ...), custom_call_target="tpu_custom_call" | custom-call | bytes 33554432 | tf_op jit(solution)/shard_map/add_up/pallas_call | solution.py:357
  102.5 2.5 %collective-permute-start.21 = (bf16[2,128,512]{2,1,0:T(8,128)(2,1)}, bf16[2,128,512]{2,1,0:T(8,128)(2,1)S(1)}, u32[]{:S(2)}, u32[]{:S(2)}) collective-permute-start(bf16[2,128,512]{2,1,0:T(8,128)(2,1)} %get-tuple-element.67), channel_id=1, source_target_pairs={{0,5},{1,4},{2,7},{3,6},{4,1},{5,0},{6,3},{7,2},{8,13},{9,12},{10,... | collective-permute-start | bytes 786440 | tf_op jit(solution)/shard_map/ppermute | solution.py:65
  104.9 0.5 collective-permute-start.22
  105.4 0.5 collective-permute-start.23
  106.0 5.1 %collective-permute-done.29.later_ref = bf16[4,2,128,256]{3,2,1,0:T(8,128)(2,1)S(1)} collective-permute-done((bf16[4,2,128,256]{3,2,1,0:T(8,128)(2,1)}, bf16[4,2,128,256]{3,2,1,0:T(8,128)(2,1)S(1)}, u32[]{:S(2)}, u32[]{:S(2)}) %collective-permute-start.29) | collective-permute-done | bytes 524320 | tf_op jit(solution)/shard_map/ppermute | solution.py:71
  111.1 0.8 copy-done.8
  111.9 2.3 %add_up.3 = (bf16[2,128,256]{2,1,0:T(8,128)(2,1)}, bf16[2,128,256]{2,1,0:T(8,128)(2,1)}, bf16[2,128,256]{2,1,0:T(8,128)(2,1)}, bf16[2,128,256]{2,1,0:T(8,128)(2,1)}) custom-call(bf16[4,2,128,256]{3,2,1,0:T(8,128)(2,1)} %get-tuple-element.70.mine_ref, bf16[4,2,128,256]{3,2,1,0:T(8,128)(2,1)} %copy-done.7, bf16[4,2,128,256]{3,2,1,0:T(8,128)(2,1)} %copy-done.8), custom_call_target="tpu_custom_call" | custom-call | bytes 2097152 | tf_op jit(solution)/shard_map/add_up/pallas_call | solution.py:357
  114.1 2.3 %collective-permute-start.30 = (bf16[2,128,256]{2,1,0:T(8,128)(2,1)}, bf16[2,128,256]{2,1,0:T(8,128)(2,1)S(1)}, u32[]{:S(2)}, u32[]{:S(2)}) collective-permute-start(bf16[2,128,256]{2,1,0:T(8,128)(2,1)} %get-tuple-element.78), channel_id=1, source_target_pairs={{0,5},{1,4},{2,7},{3,6},{4,1},{5,0},{6,3},{7,2},{8,13},{9,12},{10,... | collective-permute-start | bytes 393224 | tf_op jit(solution)/shard_map/ppermute | solution.py:65
  116.4 0.5 collective-permute-start.31
  116.9 0.7 collective-permute-start.32
  117.7 0.7 copy-done.2
  118.4 2.3 %join_queries.1 = bf16[128,4096]{1,0:T(8,128)(2,1)} custom-call(bf16[1,128,512]{2,1,0:T(8,128)(2,1)} %get-tuple-element.51.refs_0_, bf16[1,128,512]{2,1,0:T(8,128)(2,1)} %copy-done.9, bf16[1,128,512]{2,1,0:T(8,128)(2,1)} %copy-done.10, bf16[1,128,512]{2,1,0:T(8,128)(2,1)} %copy-done.11, bf16[2,128,512]{2,1,0:T(8,128)(2,1)} %get-tuple-element.66.refs_4_, ...), custom_call_target="tpu_custom_call" | custom-call | bytes 3145728 | tf_op jit(solution)/shard_map/join_queries/pallas_call | solution.py:389
  120.8 0.3 collective-permute-done.30.refs_9_
  121.0 1.9 %collective-permute-done.31.refs_10_ = bf16[2,128,256]{2,1,0:T(8,128)(2,1)S(1)} collective-permute-done((bf16[2,128,256]{2,1,0:T(8,128)(2,1)}, bf16[2,128,256]{2,1,0:T(8,128)(2,1)S(1)}, u32[]{:S(2)}, u32[]{:S(2)}) %collective-permute-start.31) | collective-permute-done | bytes 131104 | tf_op jit(solution)/shard_map/ppermute | solution.py:65
  123.0 0.5 copy-done.21
  123.7 2.3 %join_keys.1 = (bf16[128,2048]{1,0:T(8,128)(2,1)}, bf16[128,2048]{1,0:T(8,128)(2,1)}) custom-call(bf16[1,128,512]{2,1,0:T(8,128)(2,1)} %get-tuple-element.51.refs_0_, bf16[1,128,512]{2,1,0:T(8,128)(2,1)} %copy-done.9, bf16[1,128,512]{2,1,0:T(8,128)(2,1)} %copy-done.10, bf16[1,128,512]{2,1,0:T(8,128)(2,1)} %copy-done.11, ...), custom_call_target="tpu_custom_call" | custom-call | bytes 4194304 | tf_op jit(solution)/shard_map/join_keys/pallas_call | solution.py:389
  (80 shorter events, 1.2 us)
Async XLA Ops:
  3.0 12.0 %collective-permute-start.3 = (bf16[2,128,512]{2,1,0:T(8,128)(2,1)}, bf16[2,128,512]{2,1,0:T(8,128)(2,1)S(1)}, u32[]{:S(2)}, u32[]{:S(2)}) collective-permute-start(bf16[2,128,512]{2,1,0:T(8,128)(2,1)} %get-tuple-element.48), channel_id=1, source_target_pairs={{0,5},{1,4},{2,7},{3,6},{4,1},{5,0},{6,3},{7,2},{8,13},{9,12},{10,... | collective-permute-start | bytes 786440 | tf_op jit(solution)/shard_map/ppermute | solution.py:65
  6.9 12.9 %collective-permute-start.4 = (bf16[2,128,512]{2,1,0:T(8,128)(2,1)}, bf16[2,128,512]{2,1,0:T(8,128)(2,1)S(1)}, u32[]{:S(2)}, u32[]{:S(2)}) collective-permute-start(bf16[2,128,512]{2,1,0:T(8,128)(2,1)} %get-tuple-element.49), channel_id=1, source_target_pairs={{0,1},{1,0},{2,3},{3,2},{4,5},{5,4},{6,7},{7,6},{8,9},{9,8},{10,11... | collective-permute-start | bytes 786440 | tf_op jit(solution)/shard_map/ppermute | solution.py:65
  7.4 14.4 %collective-permute-start.5 = (bf16[2,128,512]{2,1,0:T(8,128)(2,1)}, bf16[2,128,512]{2,1,0:T(8,128)(2,1)S(1)}, u32[]{:S(2)}, u32[]{:S(2)}) collective-permute-start(bf16[2,128,512]{2,1,0:T(8,128)(2,1)} %get-tuple-element.50), channel_id=1, source_target_pairs={{0,4},{1,5},{2,6},{3,7},{4,0},{5,1},{6,2},{7,3},{8,12},{9,13},{10,... | collective-permute-start | bytes 786440 | tf_op jit(solution)/shard_map/ppermute | solution.py:65
  7.6 14.4 %collective-permute-start.7 = (bf16[2,128,512]{2,1,0:T(8,128)(2,1)}, bf16[2,128,512]{2,1,0:T(8,128)(2,1)S(1)}, u32[]{:S(2)}, u32[]{:S(2)}) collective-permute-start(bf16[2,128,512]{2,1,0:T(8,128)(2,1)} %get-tuple-element.43.refs_2_.refs_0_), channel_id=1, source_target_pairs={{0,8},{1,9},{2,10},{3,11},{4,12},{5,13},{6,14},{7,15},{8,16},{9,17... | collective-permute-start | bytes 786440 | tf_op jit(solution)/shard_map/ppermute | solution.py:71
  12.5 24.8 %collective-permute-start = (bf16[2,128,1024]{2,1,0:T(8,128)(2,1)}, bf16[2,128,1024]{2,1,0:T(8,128)(2,1)S(1)}, u32[]{:S(2)}, u32[]{:S(2)}) collective-permute-start(bf16[2,128,1024]{2,1,0:T(8,128)(2,1)} %get-tuple-element.45), channel_id=1, source_target_pairs={{0,5},{1,4},{2,7},{3,6},{4,1},{5,0},{6,3},{7,2},{8,13},{9,12},{10,... | collective-permute-start | bytes 1572872 | tf_op jit(solution)/shard_map/ppermute | solution.py:65
  15.0 10.1 %copy-start.18 = (bf16[2,128,512]{2,1,0:T(8,128)(2,1)}, bf16[2,128,512]{2,1,0:T(8,128)(2,1)S(1)}, u32[]{:S(2)}) copy-start(bf16[2,128,512]{2,1,0:T(8,128)(2,1)S(1)} %collective-permute-done.3.refs_1_) | copy-start | bytes 786436
  15.0 8.6 %collective-permute-start.8 = (bf16[2,128,512]{2,1,0:T(8,128)(2,1)S(1)}, bf16[2,128,512]{2,1,0:T(8,128)(2,1)S(1)}, u32[]{:S(2)}, u32[]{:S(2)}) collective-permute-start(bf16[2,128,512]{2,1,0:T(8,128)(2,1)S(1)} %collective-permute-done.3.refs_1_), channel_id=1, source_target_pairs={{0,8},{1,9},{2,10},{3,11},{4,12},{5,13},{6,14},{7,15},{8,16},{9,17... | collective-permute-start | bytes 786440 | tf_op jit(solution)/shard_map/ppermute | solution.py:71
  19.8 5.3 %copy-start.19 = (bf16[2,128,512]{2,1,0:T(8,128)(2,1)}, bf16[2,128,512]{2,1,0:T(8,128)(2,1)S(1)}, u32[]{:S(2)}) copy-start(bf16[2,128,512]{2,1,0:T(8,128)(2,1)S(1)} %collective-permute-done.4.refs_2_) | copy-start | bytes 786436
  19.8 21.7 %collective-permute-start.1 = (bf16[2,128,1024]{2,1,0:T(8,128)(2,1)}, bf16[2,128,1024]{2,1,0:T(8,128)(2,1)S(1)}, u32[]{:S(2)}, u32[]{:S(2)}) collective-permute-start(bf16[2,128,1024]{2,1,0:T(8,128)(2,1)} %get-tuple-element.46), channel_id=1, source_target_pairs={{0,1},{1,0},{2,3},{3,2},{4,5},{5,4},{6,7},{7,6},{8,9},{9,8},{10,11... | collective-permute-start | bytes 1572872 | tf_op jit(solution)/shard_map/ppermute | solution.py:65
  21.9 3.2 %copy-start.17 = (bf16[2,128,512]{2,1,0:T(8,128)(2,1)}, bf16[2,128,512]{2,1,0:T(8,128)(2,1)S(1)}, u32[]{:S(2)}) copy-start(bf16[2,128,512]{2,1,0:T(8,128)(2,1)S(1)} %collective-permute-done.5.refs_3_) | copy-start | bytes 786436
  21.9 20.0 %collective-permute-start.2 = (bf16[2,128,1024]{2,1,0:T(8,128)(2,1)}, bf16[2,128,1024]{2,1,0:T(8,128)(2,1)S(1)}, u32[]{:S(2)}, u32[]{:S(2)}) collective-permute-start(bf16[2,128,1024]{2,1,0:T(8,128)(2,1)} %get-tuple-element.47), channel_id=1, source_target_pairs={{0,4},{1,5},{2,6},{3,7},{4,0},{5,1},{6,2},{7,3},{8,12},{9,13},{10,... | collective-permute-start | bytes 1572872 | tf_op jit(solution)/shard_map/ppermute | solution.py:65
  22.0 5.4 %copy-start.13 = (bf16[2,128,512]{2,1,0:T(8,128)(2,1)}, bf16[2,128,512]{2,1,0:T(8,128)(2,1)S(1)}, u32[]{:S(2)}) copy-start(bf16[2,128,512]{2,1,0:T(8,128)(2,1)S(1)} %collective-permute-done.7.refs_0_) | copy-start | bytes 786436
  22.0 11.0 %collective-permute-start.9 = (bf16[2,128,512]{2,1,0:T(8,128)(2,1)S(1)}, bf16[2,128,512]{2,1,0:T(8,128)(2,1)S(1)}, u32[]{:S(2)}, u32[]{:S(2)}) collective-permute-start(bf16[2,128,512]{2,1,0:T(8,128)(2,1)S(1)} %collective-permute-done.4.refs_2_), channel_id=1, source_target_pairs={{0,8},{1,9},{2,10},{3,11},{4,12},{5,13},{6,14},{7,15},{8,16},{9,17... | collective-permute-start | bytes 786440 | tf_op jit(solution)/shard_map/ppermute | solution.py:71
  23.5 3.8 %copy-start.14 = (bf16[2,128,512]{2,1,0:T(8,128)(2,1)}, bf16[2,128,512]{2,1,0:T(8,128)(2,1)S(1)}, u32[]{:S(2)}) copy-start(bf16[2,128,512]{2,1,0:T(8,128)(2,1)S(1)} %collective-permute-done.8.refs_1_) | copy-start | bytes 786436
  23.5 13.7 %collective-permute-start.10 = (bf16[2,128,512]{2,1,0:T(8,128)(2,1)S(1)}, bf16[2,128,512]{2,1,0:T(8,128)(2,1)S(1)}, u32[]{:S(2)}, u32[]{:S(2)}) collective-permute-start(bf16[2,128,512]{2,1,0:T(8,128)(2,1)S(1)} %collective-permute-done.5.refs_3_), channel_id=1, source_target_pairs={{0,8},{1,9},{2,10},{3,11},{4,12},{5,13},{6,14},{7,15},{8,16},{9,17... | collective-permute-start | bytes 786440 | tf_op jit(solution)/shard_map/ppermute | solution.py:71
  33.0 8.9 %copy-start.15 = (bf16[2,128,512]{2,1,0:T(8,128)(2,1)}, bf16[2,128,512]{2,1,0:T(8,128)(2,1)S(1)}, u32[]{:S(2)}) copy-start(bf16[2,128,512]{2,1,0:T(8,128)(2,1)S(1)} %collective-permute-done.9.refs_2_) | copy-start | bytes 786436
  33.0 12.5 %collective-permute-start.6 = (bf16[4,2,128,512]{3,2,1,0:T(8,128)(2,1)}, bf16[4,2,128,512]{3,2,1,0:T(8,128)(2,1)}, u32[]{:S(2)}, u32[]{:S(2)}) collective-permute-start(bf16[4,2,128,512]{3,2,1,0:T(8,128)(2,1)} %gather_keys.2.refs_4_), channel_id=1, source_target_pairs={{0,2},{1,3},{2,0},{3,1},{4,6},{5,7},{6,4},{7,5},{8,10},{9,11},{10,... | collective-permute-start | bytes 3145736 | tf_op jit(solution)/shard_map/ppermute | solution.py:68
  37.3 4.6 %copy-start.16 = (bf16[2,128,512]{2,1,0:T(8,128)(2,1)}, bf16[2,128,512]{2,1,0:T(8,128)(2,1)S(1)}, u32[]{:S(2)}) copy-start(bf16[2,128,512]{2,1,0:T(8,128)(2,1)S(1)} %collective-permute-done.10.refs_3_) | copy-start | bytes 786436
  37.3 4.6 %copy-start.4 = (bf16[2,128,1024]{2,1,0:T(8,128)(2,1)}, bf16[2,128,1024]{2,1,0:T(8,128)(2,1)S(1)}, u32[]{:S(2)}) copy-start(bf16[2,128,1024]{2,1,0:T(8,128)(2,1)S(1)} %collective-permute-done.refs_5_.refs_1_) | copy-start | bytes 1572868
  41.6 0.8 copy-start.5
  42.4 0.8 copy-start.6
  45.4 2.9 %collective-permute-start.11 = (bf16[4,2,128,512]{3,2,1,0:T(8,128)(2,1)}, bf16[4,2,128,512]{3,2,1,0:T(8,128)(2,1)S(1)}, u32[]{:S(2)}, u32[]{:S(2)}) collective-permute-start(bf16[4,2,128,512]{3,2,1,0:T(8,128)(2,1)} %gather_keys.3.refs_6_), channel_id=1, source_target_pairs={{0,2},{1,3},{2,0},{3,1},{4,6},{5,7},{6,4},{7,5},{8,10},{9,11},{10,... | collective-permute-start | bytes 3145736 | tf_op jit(solution)/shard_map/ppermute | solution.py:68
  48.3 1.0 copy-start.31
  63.5 3.7 %collective-permute-start.16 = (bf16[2,128,256]{2,1,0:T(8,128)(2,1)}, bf16[2,128,256]{2,1,0:T(8,128)(2,1)S(1)}, u32[]{:S(2)}, u32[]{:S(2)}) collective-permute-start(bf16[2,128,256]{2,1,0:T(8,128)(2,1)} %get-tuple-element.58), channel_id=1, source_target_pairs={{0,2},{1,3},{2,0},{3,1},{4,6},{5,7},{6,4},{7,5},{8,10},{9,11},{10,... | collective-permute-start | bytes 393224 | tf_op jit(solution)/shard_map/ppermute | solution.py:68
  63.7 4.0 %collective-permute-start.17 = (bf16[2,128,256]{2,1,0:T(8,128)(2,1)}, bf16[2,128,256]{2,1,0:T(8,128)(2,1)S(1)}, u32[]{:S(2)}, u32[]{:S(2)}) collective-permute-start(bf16[2,128,256]{2,1,0:T(8,128)(2,1)} %get-tuple-element.59), channel_id=1, source_target_pairs={{0,2},{1,3},{2,0},{3,1},{4,6},{5,7},{6,4},{7,5},{8,10},{9,11},{10,... | collective-permute-start | bytes 393224 | tf_op jit(solution)/shard_map/ppermute | solution.py:68
  64.1 11.0 %collective-permute-start.12 = (bf16[1,128,512]{2,1,0:T(8,128)(2,1)}, bf16[1,128,512]{2,1,0:T(8,128)(2,1)S(1)}, u32[]{:S(2)}, u32[]{:S(2)}) collective-permute-start(bf16[1,128,512]{2,1,0:T(8,128)(2,1)} %get-tuple-element.52), channel_id=1, source_target_pairs={{0,5},{1,4},{2,7},{3,6},{4,1},{5,0},{6,3},{7,2},{8,13},{9,12},{10,... | collective-permute-start | bytes 393224 | tf_op jit(solution)/shard_map/ppermute | solution.py:65
  66.7 1.6 %collective-permute-start.18 = (bf16[2,128,256]{2,1,0:T(8,128)(2,1)}, bf16[2,128,256]{2,1,0:T(8,128)(2,1)S(1)}, u32[]{:S(2)}, u32[]{:S(2)}) collective-permute-start(bf16[2,128,256]{2,1,0:T(8,128)(2,1)} %get-tuple-element.60), channel_id=1, source_target_pairs={{0,2},{1,3},{2,0},{3,1},{4,6},{5,7},{6,4},{7,5},{8,10},{9,11},{10,... | collective-permute-start | bytes 393224 | tf_op jit(solution)/shard_map/ppermute | solution.py:68
  66.7 1.7 %collective-permute-start.19 = (bf16[2,128,256]{2,1,0:T(8,128)(2,1)}, bf16[2,128,256]{2,1,0:T(8,128)(2,1)S(1)}, u32[]{:S(2)}, u32[]{:S(2)}) collective-permute-start(bf16[2,128,256]{2,1,0:T(8,128)(2,1)} %get-tuple-element.61), channel_id=1, source_target_pairs={{0,2},{1,3},{2,0},{3,1},{4,6},{5,7},{6,4},{7,5},{8,10},{9,11},{10,... | collective-permute-start | bytes 393224 | tf_op jit(solution)/shard_map/ppermute | solution.py:68
  67.3 1.2 copy-start.22
  67.3 7.9 %collective-permute-start.13 = (bf16[1,128,512]{2,1,0:T(8,128)(2,1)}, bf16[1,128,512]{2,1,0:T(8,128)(2,1)S(1)}, u32[]{:S(2)}, u32[]{:S(2)}) collective-permute-start(bf16[1,128,512]{2,1,0:T(8,128)(2,1)} %get-tuple-element.53), channel_id=1, source_target_pairs={{0,1},{1,0},{2,3},{3,2},{4,5},{5,4},{6,7},{7,6},{8,9},{9,8},{10,11... | collective-permute-start | bytes 393224 | tf_op jit(solution)/shard_map/ppermute | solution.py:65
  67.8 0.7 copy-start.24
  67.8 7.4 %collective-permute-start.14 = (bf16[1,128,512]{2,1,0:T(8,128)(2,1)}, bf16[1,128,512]{2,1,0:T(8,128)(2,1)S(1)}, u32[]{:S(2)}, u32[]{:S(2)}) collective-permute-start(bf16[1,128,512]{2,1,0:T(8,128)(2,1)} %get-tuple-element.54), channel_id=1, source_target_pairs={{0,4},{1,5},{2,6},{3,7},{4,0},{5,1},{6,2},{7,3},{8,12},{9,13},{10,... | collective-permute-start | bytes 393224 | tf_op jit(solution)/shard_map/ppermute | solution.py:65
  68.4 0.7 copy-start.27
  68.5 0.7 copy-start.29
  71.5 19.3 %copy-start.32 = (bf16[4,2,128,256]{3,2,1,0:T(8,128)(2,1)S(1)}, bf16[4,2,128,256]{3,2,1,0:T(8,128)(2,1)}, u32[]{:S(2)}) copy-start(bf16[4,2,128,256]{3,2,1,0:T(8,128)(2,1)} %get-tuple-element.56) | copy-start | bytes 1572868
  71.5 22.4 %collective-permute-start.20 = (bf16[4,2,128,256]{3,2,1,0:T(8,128)(2,1)}, bf16[4,2,128,256]{3,2,1,0:T(8,128)(2,1)S(1)}, u32[]{:S(2)}, u32[]{:S(2)}) collective-permute-start(bf16[4,2,128,256]{3,2,1,0:T(8,128)(2,1)} %add_before.2.refs_8_), channel_id=1, source_target_pairs={{0,24},{1,25},{2,26},{3,27},{4,28},{5,29},{6,30},{7,31},{8,0},{9,1... | collective-permute-start | bytes 1572872 | tf_op jit(solution)/shard_map/ppermute | solution.py:71
  75.1 0.7 copy-start.10
  75.8 0.7 copy-start.11
  90.7 1.6 %collective-permute-start.25 = (bf16[2,128,256]{2,1,0:T(8,128)(2,1)}, bf16[2,128,256]{2,1,0:T(8,128)(2,1)S(1)}, u32[]{:S(2)}, u32[]{:S(2)}) collective-permute-start(bf16[2,128,256]{2,1,0:T(8,128)(2,1)} %get-tuple-element.73), channel_id=1, source_target_pairs={{0,2},{1,3},{2,0},{3,1},{4,6},{5,7},{6,4},{7,5},{8,10},{9,11},{10,... | collective-permute-start | bytes 393224 | tf_op jit(solution)/shard_map/ppermute | solution.py:68
  90.8 8.2 %collective-permute-start.15 = (bf16[4,2,128,256]{3,2,1,0:T(8,128)(2,1)S(1)}, bf16[4,2,128,256]{3,2,1,0:T(8,128)(2,1)S(1)}, u32[]{:S(2)}, u32[]{:S(2)}) collective-permute-start(bf16[4,2,128,256]{3,2,1,0:T(8,128)(2,1)S(1)} %copy-done.32), channel_id=1, source_target_pairs={{0,2},{1,3},{2,0},{3,1},{4,6},{5,7},{6,4},{7,5},{8,10},{9,11},{10,... | collective-permute-start | bytes 1572872 | tf_op jit(solution)/shard_map/ppermute | solution.py:68
  91.3 2.0 %collective-permute-start.26 = (bf16[2,128,256]{2,1,0:T(8,128)(2,1)}, bf16[2,128,256]{2,1,0:T(8,128)(2,1)S(1)}, u32[]{:S(2)}, u32[]{:S(2)}) collective-permute-start(bf16[2,128,256]{2,1,0:T(8,128)(2,1)} %get-tuple-element.74), channel_id=1, source_target_pairs={{0,2},{1,3},{2,0},{3,1},{4,6},{5,7},{6,4},{7,5},{8,10},{9,11},{10,... | collective-permute-start | bytes 393224 | tf_op jit(solution)/shard_map/ppermute | solution.py:68
  91.4 2.2 %collective-permute-start.27 = (bf16[2,128,256]{2,1,0:T(8,128)(2,1)}, bf16[2,128,256]{2,1,0:T(8,128)(2,1)S(1)}, u32[]{:S(2)}, u32[]{:S(2)}) collective-permute-start(bf16[2,128,256]{2,1,0:T(8,128)(2,1)} %get-tuple-element.75), channel_id=1, source_target_pairs={{0,2},{1,3},{2,0},{3,1},{4,6},{5,7},{6,4},{7,5},{8,10},{9,11},{10,... | collective-permute-start | bytes 393224 | tf_op jit(solution)/shard_map/ppermute | solution.py:68
  92.3 1.6 %copy-start.23 = (bf16[2,128,256]{2,1,0:T(8,128)(2,1)}, bf16[2,128,256]{2,1,0:T(8,128)(2,1)S(1)}, u32[]{:S(2)}) copy-start(bf16[2,128,256]{2,1,0:T(8,128)(2,1)S(1)} %collective-permute-done.25.refs_0_) | copy-start | bytes 393220
  92.3 1.6 %collective-permute-start.28 = (bf16[2,128,256]{2,1,0:T(8,128)(2,1)}, bf16[2,128,256]{2,1,0:T(8,128)(2,1)S(1)}, u32[]{:S(2)}, u32[]{:S(2)}) collective-permute-start(bf16[2,128,256]{2,1,0:T(8,128)(2,1)} %get-tuple-element.76), channel_id=1, source_target_pairs={{0,2},{1,3},{2,0},{3,1},{4,6},{5,7},{6,4},{7,5},{8,10},{9,11},{10,... | collective-permute-start | bytes 393224 | tf_op jit(solution)/shard_map/ppermute | solution.py:68
  93.3 0.7 copy-start.26
  93.3 12.7 %collective-permute-start.24 = (bf16[4,2,128,256]{3,2,1,0:T(8,128)(2,1)}, bf16[4,2,128,256]{3,2,1,0:T(8,128)(2,1)S(1)}, u32[]{:S(2)}, u32[]{:S(2)}) collective-permute-start(bf16[4,2,128,256]{3,2,1,0:T(8,128)(2,1)} %get-tuple-element.71), channel_id=1, source_target_pairs={{0,2},{1,3},{2,0},{3,1},{4,6},{5,7},{6,4},{7,5},{8,10},{9,11},{10,... | collective-permute-start | bytes 1572872 | tf_op jit(solution)/shard_map/ppermute | solution.py:68
  93.6 0.6 copy-start.28
  93.9 0.7 copy-start.30
  93.9 0.8 copy-start
  96.9 14.2 %collective-permute-start.29 = (bf16[4,2,128,256]{3,2,1,0:T(8,128)(2,1)}, bf16[4,2,128,256]{3,2,1,0:T(8,128)(2,1)S(1)}, u32[]{:S(2)}, u32[]{:S(2)}) collective-permute-start(bf16[4,2,128,256]{3,2,1,0:T(8,128)(2,1)} %add_before.3), channel_id=1, source_target_pairs={{0,24},{1,25},{2,26},{3,27},{4,28},{5,29},{6,30},{7,31},{8,0},{9,1... | collective-permute-start | bytes 1572872 | tf_op jit(solution)/shard_map/ppermute | solution.py:71
  99.1 0.8 copy-start.12
  102.5 14.5 %collective-permute-start.21 = (bf16[2,128,512]{2,1,0:T(8,128)(2,1)}, bf16[2,128,512]{2,1,0:T(8,128)(2,1)S(1)}, u32[]{:S(2)}, u32[]{:S(2)}) collective-permute-start(bf16[2,128,512]{2,1,0:T(8,128)(2,1)} %get-tuple-element.67), channel_id=1, source_target_pairs={{0,5},{1,4},{2,7},{3,6},{4,1},{5,0},{6,3},{7,2},{8,13},{9,12},{10,... | collective-permute-start | bytes 786440 | tf_op jit(solution)/shard_map/ppermute | solution.py:65
  104.9 12.7 %collective-permute-start.22 = (bf16[2,128,512]{2,1,0:T(8,128)(2,1)}, bf16[2,128,512]{2,1,0:T(8,128)(2,1)S(1)}, u32[]{:S(2)}, u32[]{:S(2)}) collective-permute-start(bf16[2,128,512]{2,1,0:T(8,128)(2,1)} %get-tuple-element.68), channel_id=1, source_target_pairs={{0,1},{1,0},{2,3},{3,2},{4,5},{5,4},{6,7},{7,6},{8,9},{9,8},{10,11... | collective-permute-start | bytes 786440 | tf_op jit(solution)/shard_map/ppermute | solution.py:65
  105.4 12.2 %collective-permute-start.23 = (bf16[2,128,512]{2,1,0:T(8,128)(2,1)}, bf16[2,128,512]{2,1,0:T(8,128)(2,1)S(1)}, u32[]{:S(2)}, u32[]{:S(2)}) collective-permute-start(bf16[2,128,512]{2,1,0:T(8,128)(2,1)} %get-tuple-element.69), channel_id=1, source_target_pairs={{0,4},{1,5},{2,6},{3,7},{4,0},{5,1},{6,2},{7,3},{8,12},{9,13},{10,... | collective-permute-start | bytes 786440 | tf_op jit(solution)/shard_map/ppermute | solution.py:65
  105.9 5.1 %copy-start.7 = (bf16[4,2,128,256]{3,2,1,0:T(8,128)(2,1)}, bf16[4,2,128,256]{3,2,1,0:T(8,128)(2,1)S(1)}, u32[]{:S(2)}) copy-start(bf16[4,2,128,256]{3,2,1,0:T(8,128)(2,1)S(1)} %collective-permute-done.24.far_ref) | copy-start | bytes 1572868
  111.1 0.8 copy-start.8
  114.1 6.9 %collective-permute-start.30 = (bf16[2,128,256]{2,1,0:T(8,128)(2,1)}, bf16[2,128,256]{2,1,0:T(8,128)(2,1)S(1)}, u32[]{:S(2)}, u32[]{:S(2)}) collective-permute-start(bf16[2,128,256]{2,1,0:T(8,128)(2,1)} %get-tuple-element.78), channel_id=1, source_target_pairs={{0,5},{1,4},{2,7},{3,6},{4,1},{5,0},{6,3},{7,2},{8,13},{9,12},{10,... | collective-permute-start | bytes 393224 | tf_op jit(solution)/shard_map/ppermute | solution.py:65
  116.4 6.5 %collective-permute-start.31 = (bf16[2,128,256]{2,1,0:T(8,128)(2,1)}, bf16[2,128,256]{2,1,0:T(8,128)(2,1)S(1)}, u32[]{:S(2)}, u32[]{:S(2)}) collective-permute-start(bf16[2,128,256]{2,1,0:T(8,128)(2,1)} %get-tuple-element.79), channel_id=1, source_target_pairs={{0,1},{1,0},{2,3},{3,2},{4,5},{5,4},{6,7},{7,6},{8,9},{9,8},{10,11... | collective-permute-start | bytes 393224 | tf_op jit(solution)/shard_map/ppermute | solution.py:65
  116.9 0.7 copy-start.1
  116.9 6.1 %collective-permute-start.32 = (bf16[2,128,256]{2,1,0:T(8,128)(2,1)}, bf16[2,128,256]{2,1,0:T(8,128)(2,1)S(1)}, u32[]{:S(2)}, u32[]{:S(2)}) collective-permute-start(bf16[2,128,256]{2,1,0:T(8,128)(2,1)} %get-tuple-element.80), channel_id=1, source_target_pairs={{0,4},{1,5},{2,6},{3,7},{4,0},{5,1},{6,2},{7,3},{8,12},{9,13},{10,... | collective-permute-start | bytes 393224 | tf_op jit(solution)/shard_map/ppermute | solution.py:65
  117.6 0.7 copy-start.2
  117.6 0.8 copy-start.3
  121.0 2.0 %copy-start.20 = (bf16[2,128,256]{2,1,0:T(8,128)(2,1)}, bf16[2,128,256]{2,1,0:T(8,128)(2,1)S(1)}, u32[]{:S(2)}) copy-start(bf16[2,128,256]{2,1,0:T(8,128)(2,1)S(1)} %collective-permute-done.30.refs_9_) | copy-start | bytes 393220
  123.0 0.7 copy-start.25
  (2 other events, 1.3 us)

commit v4 on v3

--- a/solution.py
+++ b/solution.py
@@ -120,26 +120,19 @@
     return [out[chunk * plan.groups : (chunk + 1) * plan.groups] for chunk in range(chunks)]
 
 
-def gather_pieces(plan, pieces, cost, after=()):
+def ordered(value, cost, after):
     def kernel(*refs):
-        sources, target, sem = refs[: plan.groups], refs[-2], refs[-1]
-        _, _, group = plan.place()
-        run_copies(
-            [
-                pltpu.make_async_copy(source, target.at[group ^ flip], sem.at[flip])
-                for flip, source in zip(plan.flips, sources)
-            ]
-        )
+        pass
 
     return pl.pallas_call(
         kernel,
-        out_shape=jax.ShapeDtypeStruct((plan.groups,) + pieces[0].shape, jnp.bfloat16),
-        in_specs=[ANY] * (plan.groups + len(after)),
-        out_specs=VMEM,
-        scratch_shapes=[pltpu.SemaphoreType.DMA((plan.groups,))],
+        out_shape=jax.ShapeDtypeStruct(value.shape, value.dtype),
+        in_specs=[ANY] * (1 + len(after)),
+        out_specs=ANY,
+        input_output_aliases={0: 0},
         cost_estimate=traffic(cost),
-        name="gather_keys",
-    )(*pieces, *after)
+        name="ordered",
+    )(value, *after)
 
 
 def backward(plan, chunk, doc_lengths, query_pieces, key_arrays, after):
@@ -149,7 +142,7 @@
     wide = GROUP * block
     query_width = HEAD_SIZE * GROUP
     exponent_scale = attn_scale * math.log2(math.e)
-    loads = heads * (2 * groups + 8 * plan.ways)
+    loads = heads * 5 * groups
     stores = heads * (2 * groups + 3)
 
     def kernel(docs, *refs):
@@ -160,10 +153,15 @@
         before_mine, own_mine, own_far, refs = *refs[:3], refs[3:]
         parts = (before_mine, None, own_mine, own_far)
         before_far, refs = refs[:groups], refs[groups:]
-        q_s, o_s, k_s, v_s, dq_s, dk_s, dv_s, part_s, score_s, prob_grad_s, prob_s, grad_s, sem, out_sem = refs
+        qo_s, kv_s, dq_s, dk_s, dv_s, part_s, score_s, prob_grad_s, prob_s, grad_s, sem, out_sem = refs
+        q_s, o_s, k_s, v_s = qo_s.at[0], qo_s.at[1], kv_s.at[0], kv_s.at[1]
         slab_seq, core, group = plan.place()
 
         copies, results = [], []
+
+        def block_of(late, away, flip):
+            side = core + away * (cores - 1 - 2 * core)
+            return late * plan.pieces + ((group ^ flip) // tp * cores + side) * tp + lax.rem(group ^ flip, tp)
 
         def load(source, target):
             copies.append(pltpu.make_async_copy(source, target, sem.at[len(copies)]))
@@ -176,15 +174,11 @@
         for head in range(heads):
             here, there = pl.ds(head * query_width, query_width), pl.ds((chunk * heads + head) * query_width, query_width)
             for flip, piece in zip(plan.flips, pieces):
-                load(piece.at[0, :, there], q_s.at[group ^ flip, :, here])
-                load(piece.at[1, :, there], o_s.at[group ^ flip, :, here])
+                load(piece.at[:, :, there], qo_s.at[:, group ^ flip, :, here])
             here, there = pl.ds(head * HEAD_SIZE, HEAD_SIZE), pl.ds((chunk * heads + head) * HEAD_SIZE, HEAD_SIZE)
             for source, (late, away) in zip(key_refs, itertools.product((1, 0), (0, 1))):
-                side = core + away * (cores - 1 - 2 * core)
-                for way in range(plan.ways):
-                    start = late * plan.pieces + (way * cores + side) * tp
-                    for index, target in enumerate((k_s, v_s)):
-                        load(source.at[pl.ds(way * tp, tp), index, :, there], target.at[pl.ds(start, tp), :, here])
+                for at, flip in enumerate(plan.flips):
+                    load(source.at[at, :, :, there], kv_s.at[:, block_of(late, away, flip), :, here])
         dk_s[...] = jnp.zeros_like(dk_s)
         dv_s[...] = jnp.zeros_like(dv_s)
 
@@ -272,12 +266,10 @@
                 step(head, way)
             head_cols = pl.ds(head * HEAD_SIZE, HEAD_SIZE)
             for late, away in itertools.product((0, 1), (0, 1)):
-                side = core + away * (cores - 1 - 2 * core)
                 staged = part_s.at[late, away]
-                for way, index in itertools.product(range(plan.ways), (0, 1)):
-                    at = pl.ds(late * plan.pieces + (way * cores + side) * tp, tp)
-                    total = (dk_s, dv_s)[index][at, :, head_cols]
-                    staged[pl.ds(way * tp, tp), index, :, head_cols] = total.astype(jnp.bfloat16)
+                for (at, flip), index in itertools.product(enumerate(plan.flips), (0, 1)):
+                    total = (dk_s, dv_s)[index][block_of(late, away, flip), :, head_cols]
+                    staged[at, index, :, head_cols] = total.astype(jnp.bfloat16)
                 if late or not away:
                     store(staged.at[:, :, :, head_cols], parts[2 * late + away].at[:, :, :, head_cols])
                 else:
@@ -301,10 +293,8 @@
         in_specs=[SMEM] + [ANY] * (groups + 4 + len(after)),
         out_specs=[ANY] * (2 * groups + 3),
         scratch_shapes=[
-            pltpu.VMEM((groups, plan.rows, query_cols), bf),
-            pltpu.VMEM((groups, plan.rows, query_cols), bf),
-            pltpu.VMEM((span, plan.rows, key_cols), bf),
-            pltpu.VMEM((span, plan.rows, key_cols), bf),
+            pltpu.VMEM((2, groups, plan.rows, query_cols), bf),
+            pltpu.VMEM((2, span, plan.rows, key_cols), bf),
             pltpu.VMEM((groups, plan.rows, query_cols), bf),
             pltpu.VMEM((span, plan.rows, key_cols), fl),
             pltpu.VMEM((span, plan.rows, key_cols), fl),
@@ -323,45 +313,11 @@
     return out[:groups], out[groups : groups + 3], out[groups + 3 :]
 
 
-def add_before(plan, mine, far, after):
-    def kernel(mine_ref, *refs):
-        for piece in range(plan.groups):
-            total = mine_ref[piece].astype(jnp.float32) + refs[piece][...].astype(jnp.float32)
-            refs[-1][piece] = total.astype(jnp.bfloat16)
-
-    return pl.pallas_call(
-        kernel,
-        out_shape=jax.ShapeDtypeStruct(mine.shape, jnp.bfloat16),
-        in_specs=[VMEM] * (1 + plan.groups) + [ANY] * len(after),
-        out_specs=VMEM,
-        cost_estimate=traffic(3 * mine.nbytes),
-        name="add_before",
-    )(mine, *far, *after)
-
-
-def add_up(plan, mine, far, later, cost, riders):
-    def kernel(mine_ref, far_ref, later_ref, *refs):
-        _, _, group = plan.place()
-        for at, flip in enumerate(plan.flips):
-            piece, target = group ^ flip, refs[len(riders) + at]
-            total = mine_ref[piece].astype(jnp.float32) + far_ref[piece].astype(jnp.float32)
-            total = (total + later_ref[piece].astype(jnp.float32)).astype(jnp.bfloat16)
-            if riders:
-                target[0] = refs[at][0]
-                target[1, :, : plan.key_cols] = total[0]
-                target[1, :, plan.key_cols :] = total[1]
-            else:
-                target[...] = total
-
-    shape = (2, plan.rows, 2 * plan.key_cols if riders else plan.key_cols)
-    return pl.pallas_call(
-        kernel,
-        out_shape=[jax.ShapeDtypeStruct(shape, jnp.bfloat16)] * plan.groups,
-        in_specs=[VMEM] * (3 + len(riders)),
-        out_specs=[VMEM] * plan.groups,
-        cost_estimate=traffic(cost),
-        name="add_up",
-    )(mine, far, later, *riders)
+def add_up(*parts):
+    total = parts[0].astype(jnp.float32)
+    for part in parts[1:]:
+        total = total + part.astype(jnp.float32)
+    return total.astype(jnp.bfloat16)
 
 
 def join_columns(plan, sources, targets, width, name):
@@ -409,29 +365,45 @@
     query_parts = split_columns(plan, (queries, out_grad), query_width, 1, "split_queries", after=(key_parts[0],))[0]
     pieces = exchange(key_parts)
     arrived = exchange(query_parts)
-    own = gather_pieces(plan, pieces, HARD)
-    before = gather_pieces(plan, [plan.to_slab(piece, 1) for piece in pieces], HARD, (own, *arrived[1:]))
-    key_arrays = (own, plan.to_core(own), before, plan.to_core(before))
-    after, wait = (), ()
+    own_first = ordered(pieces[0], HARD, pieces[1:])
+    own = jnp.stack([own_first, *pieces[1:]])
+    own_other = plan.to_core(own)
+    moved = [plan.to_slab(pieces[0], 1), plan.to_slab(pieces[1], 1)]
+    if plan.groups > 2:
+        rest = plan.to_slab(jnp.stack(pieces[2:]), 1)
+        moved = moved + [rest[at] for at in range(plan.groups - 2)]
+    before = jnp.stack([ordered(moved[0], HARD, (own_first, *arrived[1:])), *moved[1:]])
+    before_other = plan.to_core(before)
+    key_arrays = (own, own_other, before, before_other)
+    after, hold = (), ()
     sums, query_outs, sent = [], [], []
     for chunk in range(plan.chunks):
         query_out, (before_mine, own_mine, own_far), before_far = backward(plan, chunk, doc_lengths, arrived, key_arrays, after)
-        before_sum = add_before(plan, before_mine, [plan.to_core(piece) for piece in before_far], wait)
+        if hold:
+            before_mine = ordered(before_mine, EASY, hold)
+        before_sum = add_up(before_mine, jnp.stack([plan.to_core(piece) for piece in before_far]))
         later = plan.to_slab(before_sum, -1)
         sums.append((own_mine, plan.to_core(own_far), later))
         query_outs.append(query_out)
         if chunk < plan.chunks - 1 or plan.chunks == 1:
             sent.append(exchange(query_out))
             after = (before_sum, *sent[-1][1:])
-        wait = (later,)
+        hold = (later,)
     query_from, key_from, value_from = ([(chunk, 0, 0) for chunk in range(len(sent))], [], [])
     for chunk in range(plan.chunks):
-        last, first = chunk == plan.chunks - 1, chunk == 0
-        riders = query_outs[-1] if first and not last else ()
-        sent.append(exchange(add_up(plan, *sums[chunk], EASY if last else HARD, riders)))
+        own_mine, own_far, later = sums[chunk]
+        riders = chunk == 0 and plan.chunks > 1
+        if riders:
+            own_mine = ordered(own_mine, HARD, query_outs[-1][:1])
+        messages = [add_up(own_mine[at], own_far[at], later[at]) for at in range(plan.groups)]
+        if riders:
+            messages = [
+                jnp.concatenate([rider, jnp.concatenate([message[0], message[1]], axis=1)[None]])
+                for rider, message in zip(query_outs[-1], messages)
+            ]
+            query_from.append((len(sent), 0, 0))
+        sent.append(exchange(messages))
         at = len(sent) - 1
-        if riders:
-            query_from.append((at, 0, 0))
         key_from.append((at, 1, 0) if riders else (at, 0, 0))
         value_from.append((at, 1, plan.key_cols) if riders else (at, 1, 0))
     (query_grad,) = join_columns(plan, sent[: plan.chunks], [query_from], query_width, "join_queries")

time: 127 us -> 120 us (0.945)
  Pallas kernels: 52.1 us -> 38.1 us
  other arithmetic: 0 us -> 6.74 us
    pallas_call x6 -> x4, Pallas kernels: 13.8 us -> 0.01 us  [ordered(): pl.pallas_call(kernel, out_shape=jax.ShapeDtypeStruct(value.shape, value....]
    ppermute x15, waiting for transfers between devices: 10.1 us -> 22.4 us  [to_group(): lax.ppermute(value, AXES, self.routes(lambda slab, core, group: (slab, co...]
    ppermute x6 -> x5, waiting for transfers between devices: 15.1 us -> 5.54 us  [to_slab(): lax.ppermute(value, AXES, self.routes(lambda slab, core, group: (slab + s...]
    convert_element_type x0 -> x4, other arithmetic: none -> 3.47 us  [add_up(): return total.astype(jnp.bfloat16)]
    another operation x0 -> x3, other arithmetic: none -> 2.43 us  [the longest x1 1.21 us: per_device(): jnp.stack([ordered(moved[0], HARD, (own_first, *arrived[1:])), *moved[1:]])]
    ppermute x12, waiting for transfers between devices: 4.57 us -> 2.83 us  [to_core(): lax.ppermute(value, AXES, self.routes(lambda slab, core, group: (slab, se...]
    unnamed x66 -> x58, local copies, waits for them, and re-layouts: 8.22 us -> 7.62 us
    ppermute x6 -> x5, starting transfers between devices: 12.5 us -> 12.9 us  [to_slab(): lax.ppermute(value, AXES, self.routes(lambda slab, core, group: (slab + s...]
  transfers between devices with their start and end apart: 33 -> 32, of which waited for: 14 -> 9; matrix products, arithmetic and copies ran while one was open for 0% -> 6% of each run, Pallas kernels for 26% -> 16%
where the time goes in v4:
time: 120 us
  Pallas kernels  38.1 us (32%)
  starting transfers between devices  35.3 us (29%)
  waiting for transfers between devices  30.7 us (26%)
  local copies, waits for them, and re-layouts  7.66 us (6%)
  other arithmetic  6.74 us (6%)
    pallas_call x2, Pallas kernels, backward(): pl.pallas_call(kernel, out_shape=[jax.ShapeDtypeStruct((1, plan.rows, que...  28.2 us
    ppermute x15, waiting for transfers between devices, to_group(): lax.ppermute(value, AXES, self.routes(lambda slab, core, group: (slab, co...  22.4 us
    ppermute x15, starting transfers between devices, to_group(): lax.ppermute(value, AXES, self.routes(lambda slab, core, group: (slab, co...  19.7 us
    ppermute x5, starting transfers between devices, to_slab(): lax.ppermute(value, AXES, self.routes(lambda slab, core, group: (slab + s...  12.9 us
    unnamed x58, local copies, waits for them, and re-layouts  7.62 us
    ppermute x5, waiting for transfers between devices, to_slab(): lax.ppermute(value, AXES, self.routes(lambda slab, core, group: (slab + s...  5.54 us
    pallas_call x2, Pallas kernels, split_columns(): pl.pallas_call(kernel, out_shape=[shape] * count, in_specs=[ANY] * (len(a...  5.23 us
    pallas_call x2, Pallas kernels, join_columns(): pl.pallas_call(kernel, out_shape=[jax.ShapeDtypeStruct((plan.rows, width...  4.65 us
  transfers between devices with their start and end apart: 32, of which 9 were waited for; matrix products, arithmetic and copies ran while one was open for 6% of the time, Pallas kernels for 16%

profile of v4, /device:TPU:0, one launch (start us, length us, event | category | flops | bytes accessed | tf_op | source)
XLA Modules:
  0.0 119.7 jit_solution(10581923211227998928)
XLA Ops:
  0.6 2.3 %split_keys.1 = (bf16[2,128,512]{2,1,0:T(8,128)(2,1)}, bf16[2,128,512]{2,1,0:T(8,128)(2,1)}, bf16[2,128,512]{2,1,0:T(8,128)(2,1)}, bf16[2,128,512]{2,1,0:T(8,128)(2,1)}) custom-call(bf16[128,2048]{1,0:T(8,128)(2,1)} %refs_0_.2, bf16[128,2048]{1,0:T(8,128)(2,1)} %refs_1_.2), custom_call_target="tpu_custom_call" | custom-call | bytes 2097152 | tf_op jit(solution)/shard_map/split_keys/pallas_call | solution.py:111
  3.0 3.0 %collective-permute-start.4 = (bf16[2,128,512]{2,1,0:T(8,128)(2,1)}, bf16[2,128,512]{2,1,0:T(8,128)(2,1)S(1)}, u32[]{:S(2)}, u32[]{:S(2)}) collective-permute-start(bf16[2,128,512]{2,1,0:T(8,128)(2,1)} %get-tuple-element.41), channel_id=1, source_target_pairs={{0,1},{1,0},{2,3},{3,2},{4,5},{5,4},{6,7},{7,6},{8,9},{9,8},{10,11... | collective-permute-start | bytes 786440 | tf_op jit(solution)/shard_map/ppermute | solution.py:65
  6.0 1.5 %collective-permute-start.5 = (bf16[2,128,512]{2,1,0:T(8,128)(2,1)}, bf16[2,128,512]{2,1,0:T(8,128)(2,1)S(1)}, u32[]{:S(2)}, u32[]{:S(2)}) collective-permute-start(bf16[2,128,512]{2,1,0:T(8,128)(2,1)} %get-tuple-element.42), channel_id=1, source_target_pairs={{0,4},{1,5},{2,6},{3,7},{4,0},{5,1},{6,2},{7,3},{8,12},{9,13},{10,... | collective-permute-start | bytes 786440 | tf_op jit(solution)/shard_map/ppermute | solution.py:65
  7.5 0.0 collective-permute-start.3
  7.5 2.0 %collective-permute-start.7 = (bf16[2,128,512]{2,1,0:T(8,128)(2,1)}, bf16[2,128,512]{2,1,0:T(8,128)(2,1)S(1)}, u32[]{:S(2)}, u32[]{:S(2)}) collective-permute-start(bf16[2,128,512]{2,1,0:T(8,128)(2,1)} %get-tuple-element.35.refs_2_.refs_0_), channel_id=1, source_target_pairs={{0,8},{1,9},{2,10},{3,11},{4,12},{5,13},{6,14},{7,15},{8,16},{9,17... | collective-permute-start | bytes 786440 | tf_op jit(solution)/shard_map/ppermute | solution.py:71
  9.5 2.9 %split_queries.1 = (bf16[2,128,1024]{2,1,0:T(8,128)(2,1)}, bf16[2,128,1024]{2,1,0:T(8,128)(2,1)}, bf16[2,128,1024]{2,1,0:T(8,128)(2,1)}, bf16[2,128,1024]{2,1,0:T(8,128)(2,1)}) custom-call(bf16[128,4096]{1,0:T(8,128)(2,1)} %refs_0_.3, bf16[128,4096]{1,0:T(8,128)(2,1)} %refs_1_.3, bf16[2,128,512]{2,1,0:T(8,128)(2,1)} %get-tuple-element.35.refs_2_.refs_0_), custom_call_target="tpu_custom_call" | custom-call | bytes 4194304 | tf_op jit(solution)/shard_map/split_queries/pallas_call | solution.py:111
  12.5 2.5 %collective-permute-start = (bf16[2,128,1024]{2,1,0:T(8,128)(2,1)}, bf16[2,128,1024]{2,1,0:T(8,128)(2,1)S(1)}, u32[]{:S(2)}, u32[]{:S(2)}) collective-permute-start(bf16[2,128,1024]{2,1,0:T(8,128)(2,1)} %get-tuple-element.37), channel_id=1, source_target_pairs={{0,5},{1,4},{2,7},{3,6},{4,1},{5,0},{6,3},{7,2},{8,13},{9,12},{10,... | collective-permute-start | bytes 1572872 | tf_op jit(solution)/shard_map/ppermute | solution.py:65
  15.0 0.5 collective-permute-start.1
  15.5 1.5 %collective-permute-start.2 = (bf16[2,128,1024]{2,1,0:T(8,128)(2,1)}, bf16[2,128,1024]{2,1,0:T(8,128)(2,1)}, u32[]{:S(2)}, u32[]{:S(2)}) collective-permute-start(bf16[2,128,1024]{2,1,0:T(8,128)(2,1)} %get-tuple-element.39), channel_id=1, source_target_pairs={{0,4},{1,5},{2,6},{3,7},{4,0},{5,1},{6,2},{7,3},{8,12},{9,13},{10,... | collective-permute-start | bytes 1572872 | tf_op jit(solution)/shard_map/ppermute | solution.py:65
  16.9 0.1 pad_maximum_fusion.2
  17.0 3.6 %collective-permute-done.3.refs_1_ = bf16[2,128,512]{2,1,0:T(8,128)(2,1)S(1)} collective-permute-done((bf16[2,128,512]{2,1,0:T(8,128)(2,1)}, bf16[2,128,512]{2,1,0:T(8,128)(2,1)S(1)}, u32[]{:S(2)}, u32[]{:S(2)}) %collective-permute-start.3) | collective-permute-done | bytes 262176 | tf_op jit(solution)/shard_map/ppermute | solution.py:65
  20.6 2.0 %collective-permute-start.9 = (bf16[2,2,128,512]{3,2,1,0:T(8,128)(2,1)S(1)}, bf16[2,2,128,512]{3,2,1,0:T(8,128)(2,1)}, u32[]{:S(2)}, u32[]{:S(2)}) collective-permute-start(bf16[2,2,128,512]{3,2,1,0:T(8,128)(2,1)S(1)} %pad_maximum_fusion.2), channel_id=1, source_target_pairs={{0,8},{1,9},{2,10},{3,11},{4,12},{5,13},{6,14},{7,15},{8,16},{9,17... | collective-permute-start | bytes 1572872 | tf_op jit(solution)/shard_map/ppermute | solution.py:71
  22.7 1.6 %collective-permute-start.8 = (bf16[2,128,512]{2,1,0:T(8,128)(2,1)S(1)}, bf16[2,128,512]{2,1,0:T(8,128)(2,1)S(1)}, u32[]{:S(2)}, u32[]{:S(2)}) collective-permute-start(bf16[2,128,512]{2,1,0:T(8,128)(2,1)S(1)} %collective-permute-done.3.refs_1_), channel_id=1, source_target_pairs={{0,8},{1,9},{2,10},{3,11},{4,12},{5,13},{6,14},{7,15},{8,16},{9,17... | collective-permute-start | bytes 786440 | tf_op jit(solution)/shard_map/ppermute | solution.py:71
  24.3 1.2 pad_maximum_fusion.refs_4_
  25.5 6.3 %collective-permute-done.refs_2_.refs_1_ = bf16[2,128,1024]{2,1,0:T(8,128)(2,1)S(1)} collective-permute-done((bf16[2,128,1024]{2,1,0:T(8,128)(2,1)}, bf16[2,128,1024]{2,1,0:T(8,128)(2,1)S(1)}, u32[]{:S(2)}, u32[]{:S(2)}) %collective-permute-start) | collective-permute-done | bytes 524320 | tf_op jit(solution)/shard_map/ppermute | solution.py:65
  31.8 10.1 %collective-permute-done.1.refs_3_.refs_2_ = bf16[2,128,1024]{2,1,0:T(8,128)(2,1)} collective-permute-done((bf16[2,128,1024]{2,1,0:T(8,128)(2,1)}, bf16[2,128,1024]{2,1,0:T(8,128)(2,1)}, u32[]{:S(2)}, u32[]{:S(2)}) %collective-permute-start.1) | collective-permute-done | bytes 524320 | tf_op jit(solution)/shard_map/ppermute | solution.py:65
  42.0 0.3 collective-permute-done.2.refs_4_.refs_3_
  42.2 1.2 %pad_maximum_fusion.1.refs_6_ = bf16[4,2,128,512]{3,2,1,0:T(8,128)(2,1)S(1)} fusion(bf16[2,2,128,512]{3,2,1,0:T(8,128)(2,1)} %collective-permute-done.9, bf16[1,2,128,512]{3,2,1,0:T(8,128)(2,1)S(1)} %bitcast.53, bf16[1,2,128,512]{3,2,1,0:T(8,128)(2,1)} %bitcast.52), kind=kLoop, calls=%fused_computation.1 | loop fusion | flops 1048576 | bytes 2097152 | tf_op jit(solution)/shard_map/stack | solution.py:375
  43.5 0.1 collective-permute-start.10
  43.6 2.6 %collective-permute-done.10.refs_7_ = bf16[4,2,128,512]{3,2,1,0:T(8,128)(2,1)S(1)} collective-permute-done((bf16[4,2,128,512]{3,2,1,0:T(8,128)(2,1)S(1)}, bf16[4,2,128,512]{3,2,1,0:T(8,128)(2,1)S(1)}, u32[]{:S(2)}, u32[]{:S(2)}) %collective-permute-start.10) | collective-permute-done | bytes 1048608 | tf_op jit(solution)/shard_map/ppermute | solution.py:68
  46.2 1.0 copy-done.27
  47.2 14.1 %backward.2 = (bf16[1,128,512]{2,1,0:T(8,128)(2,1)}, bf16[1,128,512]{2,1,0:T(8,128)(2,1)}, bf16[1,128,512]{2,1,0:T(8,128)(2,1)}, bf16[1,128,512]{2,1,0:T(8,128)(...) custom-call(s32[4]{0:T(128)} %docs.3, ...), custom_call_target="tpu_custom_call" | custom-call | flops 53687091200 | bytes 6291456 | tf_op jit(solution)/shard_map/backward/pallas_call | solution.py:288
  61.2 0.2 collective-permute-start.14
  61.4 0.4 collective-permute-start.15
  61.8 0.1 collective-permute-start.16
  62.0 0.4 collective-permute-start.17
  62.3 1.9 %collective-permute-start.11 = (bf16[1,128,512]{2,1,0:T(8,128)(2,1)}, bf16[1,128,512]{2,1,0:T(8,128)(2,1)S(1)}, u32[]{:S(2)}, u32[]{:S(2)}) collective-permute-start(bf16[1,128,512]{2,1,0:T(8,128)(2,1)} %get-tuple-element.44), channel_id=1, source_target_pairs={{0,5},{1,4},{2,7},{3,6},{4,1},{5,0},{6,3},{7,2},{8,13},{9,12},{10,... | collective-permute-start | bytes 393224 | tf_op jit(solution)/shard_map/ppermute | solution.py:65
  64.2 1.0 collective-permute-start.12
  65.3 0.5 collective-permute-start.13
  65.8 1.2 add_convert_fusion.1.refs_8_
  67.0 3.6 %collective-permute-start.19 = (bf16[4,2,128,256]{3,2,1,0:T(8,128)(2,1)S(1)}, bf16[4,2,128,256]{3,2,1,0:T(8,128)(2,1)S(1)}, u32[]{:S(2)}, u32[]{:S(2)}) collective-permute-start(bf16[4,2,128,256]{3,2,1,0:T(8,128)(2,1)S(1)} %add_convert_fusion.1.refs_8_), channel_id=1, source_target_pairs={{0,24},{1,25},{2,26},{3,27},{4,28},{5,29},{6,30},{7,31},{8,0},{9,1... | collective-permute-start | bytes 1572872 | tf_op jit(solution)/shard_map/ppermute | solution.py:71
  70.7 1.1 collective-permute-done.12.refs_10_.refs_2_
  71.8 0.6 copy-done.16
  72.4 0.6 copy-done.17
  73.1 14.1 %backward.3 = (bf16[1,128,512]{2,1,0:T(8,128)(2,1)}, bf16[1,128,512]{2,1,0:T(8,128)(2,1)}, bf16[1,128,512]{2,1,0:T(8,128)(2,1)}, bf16[1,128,512]{2,1,0:T(8,128)(...) custom-call(s32[4]{0:T(128)} %docs.3, ...), custom_call_target="tpu_custom_call" | custom-call | flops 53687091200 | bytes 6291456 | tf_op jit(solution)/shard_map/backward/pallas_call | solution.py:288
  87.2 0.1 collective-permute-start.24
  87.3 0.5 collective-permute-start.25
  87.8 0.1 collective-permute-start.26
  87.9 0.4 collective-permute-start.27
  88.3 0.4 copy-done.4
  88.7 0.2 collective-permute-done.24
  88.8 0.9 copy-done.28
  89.7 0.4 collective-permute-start.23
  90.2 1.3 %add_convert_fusion = bf16[4,2,128,256]{3,2,1,0:T(8,128)(2,1)S(1)} fusion(bf16[4,2,128,256]{3,2,1,0:T(8,128)(2,1)} %ordered.7, bf16[1,2,128,256]{3,2,1,0:T(8,128)(2,1)S(1)} %bitcast.61, bf16[1,2,128,256]{3,2,1,0:T(8,128)(2,1)S(1)} %bitcast.60, bf16[1,2,128,256]{3,2,1,0:T(8,128)(2,1)S(1)} %bitcast.58, bf16[1,2,128,256]{3,2,1,0:T(8,128)(2,1)S(1)} %bitcast.56), kind=kLoop, calls=%fused_computation.2 | loop fusion | flops 1835008 | bytes 1572864 | tf_op jit(solution)/shard_map/convert_element_type | solution.py:320
  91.4 3.7 %collective-permute-start.28 = (bf16[4,2,128,256]{3,2,1,0:T(8,128)(2,1)S(1)}, bf16[4,2,128,256]{3,2,1,0:T(8,128)(2,1)S(1)}, u32[]{:S(2)}, u32[]{:S(2)}) collective-permute-start(bf16[4,2,128,256]{3,2,1,0:T(8,128)(2,1)S(1)} %add_convert_fusion), channel_id=1, source_target_pairs={{0,24},{1,25},{2,26},{3,27},{4,28},{5,29},{6,30},{7,31},{8,0},{9,1... | collective-permute-start | bytes 1572872 | tf_op jit(solution)/shard_map/ppermute | solution.py:71
  95.1 0.2 add_convert_fusion.6
  95.4 0.9 copy-done.26
  96.3 1.8 %collective-permute-start.20 = (bf16[2,128,512]{2,1,0:T(8,128)(2,1)S(1)}, bf16[2,128,512]{2,1,0:T(8,128)(2,1)S(1)}, u32[]{:S(2)}, u32[]{:S(2)}) collective-permute-start(bf16[2,128,512]{2,1,0:T(8,128)(2,1)S(1)} %pad_maximum_fusion.4), channel_id=1, source_target_pairs={{0,5},{1,4},{2,7},{3,6},{4,1},{5,0},{6,3},{7,2},{8,13},{9,12},{10,... | collective-permute-start | bytes 786440 | tf_op jit(solution)/shard_map/ppermute | solution.py:65
  98.1 0.9 copy-done.25
  99.1 1.0 collective-permute-start.21
  100.2 0.8 collective-permute-start.22
  101.0 5.5 %collective-permute-done.28 = bf16[4,2,128,256]{3,2,1,0:T(8,128)(2,1)S(1)} collective-permute-done((bf16[4,2,128,256]{3,2,1,0:T(8,128)(2,1)S(1)}, bf16[4,2,128,256]{3,2,1,0:T(8,128)(2,1)S(1)}, u32[]{:S(2)}, u32[]{:S(2)}) %collective-permute-start.28) | collective-permute-done | bytes 524320 | tf_op jit(solution)/shard_map/ppermute | solution.py:71
  106.5 0.8 fusion.3
  107.4 1.3 %collective-permute-start.31 = (bf16[2,128,256]{2,1,0:T(8,128)(2,1)S(1)}, bf16[2,128,256]{2,1,0:T(8,128)(2,1)S(1)}, u32[]{:S(2)}, u32[]{:S(2)}) collective-permute-start(bf16[2,128,256]{2,1,0:T(8,128)(2,1)S(1)} %get-tuple-element.67), channel_id=1, source_target_pairs={{0,4},{1,5},{2,6},{3,7},{4,0},{5,1},{6,2},{7,3},{8,12},{9,13},{10,... | collective-permute-start | bytes 393224 | tf_op jit(solution)/shard_map/ppermute | solution.py:65
  108.6 1.0 collective-permute-start.30
  109.7 1.2 collective-permute-start.29
  110.9 0.9 copy-done.18
  111.8 0.7 pad_maximum_fusion.3.refs_4_
  112.5 0.7 copy-done.10
  113.2 0.1 copy-done.11
  113.3 2.3 %join_queries.1 = bf16[128,4096]{1,0:T(8,128)(2,1)} custom-call(bf16[1,128,512]{2,1,0:T(8,128)(2,1)} %get-tuple-element.43.refs_0_, bf16[1,128,512]{2,1,0:T(8,128)(2,1)} %copy-done.15, bf16[1,128,512]{2,1,0:T(8,128)(2,1)} %copy-done.16, bf16[1,128,512]{2,1,0:T(8,128)(2,1)} %copy-done.17, bf16[2,128,512]{2,1,0:T(8,128)(2,1)} %pad_maximum_fusion.3.refs_4_, ...), custom_call_target="tpu_custom_call" | custom-call | bytes 3145728 | tf_op jit(solution)/shard_map/join_queries/pallas_call | solution.py:345
  115.6 0.9 collective-permute-done.29.refs_9_
  116.5 0.6 copy-done.23
  117.2 2.3 %join_keys.1 = (bf16[128,2048]{1,0:T(8,128)(2,1)}, bf16[128,2048]{1,0:T(8,128)(2,1)}) custom-call(bf16[1,128,512]{2,1,0:T(8,128)(2,1)} %get-tuple-element.43.refs_0_, bf16[1,128,512]{2,1,0:T(8,128)(2,1)} %copy-done.15, bf16[1,128,512]{2,1,0:T(8,128)(2,1)} %copy-done.16, bf16[1,128,512]{2,1,0:T(8,128)(2,1)} %copy-done.17, ...), custom_call_target="tpu_custom_call" | custom-call | bytes 4194304 | tf_op jit(solution)/shard_map/join_keys/pallas_call | solution.py:345
  (85 shorter events, 0.3 us)
Async XLA Ops:
  3.0 12.0 %collective-permute-start.4 = (bf16[2,128,512]{2,1,0:T(8,128)(2,1)}, bf16[2,128,512]{2,1,0:T(8,128)(2,1)S(1)}, u32[]{:S(2)}, u32[]{:S(2)}) collective-permute-start(bf16[2,128,512]{2,1,0:T(8,128)(2,1)} %get-tuple-element.41), channel_id=1, source_target_pairs={{0,1},{1,0},{2,3},{3,2},{4,5},{5,4},{6,7},{7,6},{8,9},{9,8},{10,11... | collective-permute-start | bytes 786440 | tf_op jit(solution)/shard_map/ppermute | solution.py:65
  6.0 9.5 %collective-permute-start.5 = (bf16[2,128,512]{2,1,0:T(8,128)(2,1)}, bf16[2,128,512]{2,1,0:T(8,128)(2,1)S(1)}, u32[]{:S(2)}, u32[]{:S(2)}) collective-permute-start(bf16[2,128,512]{2,1,0:T(8,128)(2,1)} %get-tuple-element.42), channel_id=1, source_target_pairs={{0,4},{1,5},{2,6},{3,7},{4,0},{5,1},{6,2},{7,3},{8,12},{9,13},{10,... | collective-permute-start | bytes 786440 | tf_op jit(solution)/shard_map/ppermute | solution.py:65
  7.5 13.1 %collective-permute-start.3 = (bf16[2,128,512]{2,1,0:T(8,128)(2,1)}, bf16[2,128,512]{2,1,0:T(8,128)(2,1)S(1)}, u32[]{:S(2)}, u32[]{:S(2)}) collective-permute-start(bf16[2,128,512]{2,1,0:T(8,128)(2,1)} %get-tuple-element.40), channel_id=1, source_target_pairs={{0,5},{1,4},{2,7},{3,6},{4,1},{5,0},{6,3},{7,2},{8,13},{9,12},{10,... | collective-permute-start | bytes 786440 | tf_op jit(solution)/shard_map/ppermute | solution.py:65
  7.5 15.1 %collective-permute-start.7 = (bf16[2,128,512]{2,1,0:T(8,128)(2,1)}, bf16[2,128,512]{2,1,0:T(8,128)(2,1)S(1)}, u32[]{:S(2)}, u32[]{:S(2)}) collective-permute-start(bf16[2,128,512]{2,1,0:T(8,128)(2,1)} %get-tuple-element.35.refs_2_.refs_0_), channel_id=1, source_target_pairs={{0,8},{1,9},{2,10},{3,11},{4,12},{5,13},{6,14},{7,15},{8,16},{9,17... | collective-permute-start | bytes 786440 | tf_op jit(solution)/shard_map/ppermute | solution.py:71
  12.5 19.4 %collective-permute-start = (bf16[2,128,1024]{2,1,0:T(8,128)(2,1)}, bf16[2,128,1024]{2,1,0:T(8,128)(2,1)S(1)}, u32[]{:S(2)}, u32[]{:S(2)}) collective-permute-start(bf16[2,128,1024]{2,1,0:T(8,128)(2,1)} %get-tuple-element.37), channel_id=1, source_target_pairs={{0,5},{1,4},{2,7},{3,6},{4,1},{5,0},{6,3},{7,2},{8,13},{9,12},{10,... | collective-permute-start | bytes 1572872 | tf_op jit(solution)/shard_map/ppermute | solution.py:65
  15.0 2.0 %copy-start = (bf16[2,128,512]{2,1,0:T(8,128)(2,1)}, bf16[2,128,512]{2,1,0:T(8,128)(2,1)S(1)}, u32[]{:S(2)}) copy-start(bf16[2,128,512]{2,1,0:T(8,128)(2,1)S(1)} %collective-permute-done.4.refs_2_) | copy-start | bytes 786436
  15.0 27.0 %collective-permute-start.1 = (bf16[2,128,1024]{2,1,0:T(8,128)(2,1)}, bf16[2,128,1024]{2,1,0:T(8,128)(2,1)}, u32[]{:S(2)}, u32[]{:S(2)}) collective-permute-start(bf16[2,128,1024]{2,1,0:T(8,128)(2,1)} %get-tuple-element.38), channel_id=1, source_target_pairs={{0,1},{1,0},{2,3},{3,2},{4,5},{5,4},{6,7},{7,6},{8,9},{9,8},{10,11... | collective-permute-start | bytes 1572872 | tf_op jit(solution)/shard_map/ppermute | solution.py:65
  15.5 1.5 %copy-start.2 = (bf16[2,128,512]{2,1,0:T(8,128)(2,1)}, bf16[2,128,512]{2,1,0:T(8,128)(2,1)S(1)}, u32[]{:S(2)}) copy-start(bf16[2,128,512]{2,1,0:T(8,128)(2,1)S(1)} %collective-permute-done.5.refs_3_) | copy-start | bytes 786436
  15.5 26.7 %collective-permute-start.2 = (bf16[2,128,1024]{2,1,0:T(8,128)(2,1)}, bf16[2,128,1024]{2,1,0:T(8,128)(2,1)}, u32[]{:S(2)}, u32[]{:S(2)}) collective-permute-start(bf16[2,128,1024]{2,1,0:T(8,128)(2,1)} %get-tuple-element.39), channel_id=1, source_target_pairs={{0,4},{1,5},{2,6},{3,7},{4,0},{5,1},{6,2},{7,3},{8,12},{9,13},{10,... | collective-permute-start | bytes 1572872 | tf_op jit(solution)/shard_map/ppermute | solution.py:65
  20.6 3.6 %copy-start.12 = (bf16[2,128,512]{2,1,0:T(8,128)(2,1)}, bf16[2,128,512]{2,1,0:T(8,128)(2,1)S(1)}, u32[]{:S(2)}) copy-start(bf16[2,128,512]{2,1,0:T(8,128)(2,1)S(1)} %collective-permute-done.3.refs_1_) | copy-start | bytes 786436
  20.6 3.6 %copy-start.1 = (bf16[2,128,512]{2,1,0:T(8,128)(2,1)S(1)}, bf16[2,128,512]{2,1,0:T(8,128)(2,1)}, u32[]{:S(2)}) copy-start(bf16[2,128,512]{2,1,0:T(8,128)(2,1)} %copy-done) | copy-start | bytes 786436
  20.6 3.6 %copy-start.3 = (bf16[2,128,512]{2,1,0:T(8,128)(2,1)S(1)}, bf16[2,128,512]{2,1,0:T(8,128)(2,1)}, u32[]{:S(2)}) copy-start(bf16[2,128,512]{2,1,0:T(8,128)(2,1)} %copy-done.2) | copy-start | bytes 786436
  20.6 21.6 %collective-permute-start.9 = (bf16[2,2,128,512]{3,2,1,0:T(8,128)(2,1)S(1)}, bf16[2,2,128,512]{3,2,1,0:T(8,128)(2,1)}, u32[]{:S(2)}, u32[]{:S(2)}) collective-permute-start(bf16[2,2,128,512]{3,2,1,0:T(8,128)(2,1)S(1)} %pad_maximum_fusion.2), channel_id=1, source_target_pairs={{0,8},{1,9},{2,10},{3,11},{4,12},{5,13},{6,14},{7,15},{8,16},{9,17... | collective-permute-start | bytes 1572872 | tf_op jit(solution)/shard_map/ppermute | solution.py:71
  22.7 1.6 %copy-start.13 = (bf16[2,128,512]{2,1,0:T(8,128)(2,1)}, bf16[2,128,512]{2,1,0:T(8,128)(2,1)S(1)}, u32[]{:S(2)}) copy-start(bf16[2,128,512]{2,1,0:T(8,128)(2,1)S(1)} %collective-permute-done.7.refs_0_) | copy-start | bytes 786436
  22.7 19.5 %collective-permute-start.8 = (bf16[2,128,512]{2,1,0:T(8,128)(2,1)S(1)}, bf16[2,128,512]{2,1,0:T(8,128)(2,1)S(1)}, u32[]{:S(2)}, u32[]{:S(2)}) collective-permute-start(bf16[2,128,512]{2,1,0:T(8,128)(2,1)S(1)} %collective-permute-done.3.refs_1_), channel_id=1, source_target_pairs={{0,8},{1,9},{2,10},{3,11},{4,12},{5,13},{6,14},{7,15},{8,16},{9,17... | collective-permute-start | bytes 786440 | tf_op jit(solution)/shard_map/ppermute | solution.py:71
  25.5 16.8 %copy-start.7 = (bf16[4,2,128,512]{3,2,1,0:T(8,128)(2,1)}, bf16[4,2,128,512]{3,2,1,0:T(8,128)(2,1)S(1)}, u32[]{:S(2)}) copy-start(bf16[4,2,128,512]{3,2,1,0:T(8,128)(2,1)S(1)} %pad_maximum_fusion.refs_4_) | copy-start | bytes 3145732
  31.8 10.4 %copy-start.19 = (bf16[2,128,1024]{2,1,0:T(8,128)(2,1)}, bf16[2,128,1024]{2,1,0:T(8,128)(2,1)S(1)}, u32[]{:S(2)}) copy-start(bf16[2,128,1024]{2,1,0:T(8,128)(2,1)S(1)} %collective-permute-done.refs_2_.refs_1_) | copy-start | bytes 1572868
  31.8 11.7 %collective-permute-start.6 = (bf16[4,2,128,512]{3,2,1,0:T(8,128)(2,1)S(1)}, bf16[4,2,128,512]{3,2,1,0:T(8,128)(2,1)}, u32[]{:S(2)}, u32[]{:S(2)}) collective-permute-start(bf16[4,2,128,512]{3,2,1,0:T(8,128)(2,1)S(1)} %pad_maximum_fusion.refs_4_), channel_id=1, source_target_pairs={{0,2},{1,3},{2,0},{3,1},{4,6},{5,7},{6,4},{7,5},{8,10},{9,11},{10,... | collective-permute-start | bytes 3145736 | tf_op jit(solution)/shard_map/ppermute | solution.py:68
  43.5 2.7 %copy-start.8 = (bf16[4,2,128,512]{3,2,1,0:T(8,128)(2,1)}, bf16[4,2,128,512]{3,2,1,0:T(8,128)(2,1)S(1)}, u32[]{:S(2)}) copy-start(bf16[4,2,128,512]{3,2,1,0:T(8,128)(2,1)S(1)} %pad_maximum_fusion.1.refs_6_) | copy-start | bytes 3145732
  43.5 2.7 %collective-permute-start.10 = (bf16[4,2,128,512]{3,2,1,0:T(8,128)(2,1)S(1)}, bf16[4,2,128,512]{3,2,1,0:T(8,128)(2,1)S(1)}, u32[]{:S(2)}, u32[]{:S(2)}) collective-permute-start(bf16[4,2,128,512]{3,2,1,0:T(8,128)(2,1)S(1)} %pad_maximum_fusion.1.refs_6_), channel_id=1, source_target_pairs={{0,2},{1,3},{2,0},{3,1},{4,6},{5,7},{6,4},{7,5},{8,10},{9,11},{10,... | collective-permute-start | bytes 3145736 | tf_op jit(solution)/shard_map/ppermute | solution.py:68
  46.2 1.0 copy-start.27
  61.2 3.0 %collective-permute-start.14 = (bf16[2,128,256]{2,1,0:T(8,128)(2,1)}, bf16[2,128,256]{2,1,0:T(8,128)(2,1)S(1)}, u32[]{:S(2)}, u32[]{:S(2)}) collective-permute-start(bf16[2,128,256]{2,1,0:T(8,128)(2,1)} %get-tuple-element.48), channel_id=1, source_target_pairs={{0,2},{1,3},{2,0},{3,1},{4,6},{5,7},{6,4},{7,5},{8,10},{9,11},{10,... | collective-permute-start | bytes 393224 | tf_op jit(solution)/shard_map/ppermute | solution.py:68
  61.4 3.8 %collective-permute-start.15 = (bf16[2,128,256]{2,1,0:T(8,128)(2,1)}, bf16[2,128,256]{2,1,0:T(8,128)(2,1)S(1)}, u32[]{:S(2)}, u32[]{:S(2)}) collective-permute-start(bf16[2,128,256]{2,1,0:T(8,128)(2,1)} %get-tuple-element.49), channel_id=1, source_target_pairs={{0,2},{1,3},{2,0},{3,1},{4,6},{5,7},{6,4},{7,5},{8,10},{9,11},{10,... | collective-permute-start | bytes 393224 | tf_op jit(solution)/shard_map/ppermute | solution.py:68
  61.8 4.0 %collective-permute-start.16 = (bf16[2,128,256]{2,1,0:T(8,128)(2,1)}, bf16[2,128,256]{2,1,0:T(8,128)(2,1)S(1)}, u32[]{:S(2)}, u32[]{:S(2)}) collective-permute-start(bf16[2,128,256]{2,1,0:T(8,128)(2,1)} %get-tuple-element.50), channel_id=1, source_target_pairs={{0,2},{1,3},{2,0},{3,1},{4,6},{5,7},{6,4},{7,5},{8,10},{9,11},{10,... | collective-permute-start | bytes 393224 | tf_op jit(solution)/shard_map/ppermute | solution.py:68
  62.0 3.9 %collective-permute-start.17 = (bf16[2,128,256]{2,1,0:T(8,128)(2,1)}, bf16[2,128,256]{2,1,0:T(8,128)(2,1)S(1)}, u32[]{:S(2)}, u32[]{:S(2)}) collective-permute-start(bf16[2,128,256]{2,1,0:T(8,128)(2,1)} %get-tuple-element.51), channel_id=1, source_target_pairs={{0,2},{1,3},{2,0},{3,1},{4,6},{5,7},{6,4},{7,5},{8,10},{9,11},{10,... | collective-permute-start | bytes 393224 | tf_op jit(solution)/shard_map/ppermute | solution.py:68
  62.3 8.3 %collective-permute-start.11 = (bf16[1,128,512]{2,1,0:T(8,128)(2,1)}, bf16[1,128,512]{2,1,0:T(8,128)(2,1)S(1)}, u32[]{:S(2)}, u32[]{:S(2)}) collective-permute-start(bf16[1,128,512]{2,1,0:T(8,128)(2,1)} %get-tuple-element.44), channel_id=1, source_target_pairs={{0,5},{1,4},{2,7},{3,6},{4,1},{5,0},{6,3},{7,2},{8,13},{9,12},{10,... | collective-permute-start | bytes 393224 | tf_op jit(solution)/shard_map/ppermute | solution.py:65
  64.2 7.5 %collective-permute-start.12 = (bf16[1,128,512]{2,1,0:T(8,128)(2,1)}, bf16[1,128,512]{2,1,0:T(8,128)(2,1)S(1)}, u32[]{:S(2)}, u32[]{:S(2)}) collective-permute-start(bf16[1,128,512]{2,1,0:T(8,128)(2,1)} %get-tuple-element.45), channel_id=1, source_target_pairs={{0,1},{1,0},{2,3},{3,2},{4,5},{5,4},{6,7},{7,6},{8,9},{9,8},{10,11... | collective-permute-start | bytes 393224 | tf_op jit(solution)/shard_map/ppermute | solution.py:65
  65.3 6.5 %collective-permute-start.13 = (bf16[1,128,512]{2,1,0:T(8,128)(2,1)}, bf16[1,128,512]{2,1,0:T(8,128)(2,1)S(1)}, u32[]{:S(2)}, u32[]{:S(2)}) collective-permute-start(bf16[1,128,512]{2,1,0:T(8,128)(2,1)} %get-tuple-element.46), channel_id=1, source_target_pairs={{0,4},{1,5},{2,6},{3,7},{4,0},{5,1},{6,2},{7,3},{8,12},{9,13},{10,... | collective-permute-start | bytes 393224 | tf_op jit(solution)/shard_map/ppermute | solution.py:65
  65.8 29.3 %collective-permute-start.18 = (bf16[4,2,128,256]{3,2,1,0:T(8,128)(2,1)}, bf16[4,2,128,256]{3,2,1,0:T(8,128)(2,1)S(1)}, u32[]{:S(2)}, u32[]{:S(2)}) collective-permute-start(bf16[4,2,128,256]{3,2,1,0:T(8,128)(2,1)} %get-tuple-element.54), channel_id=1, source_target_pairs={{0,2},{1,3},{2,0},{3,1},{4,6},{5,7},{6,4},{7,5},{8,10},{9,11},{10,... | collective-permute-start | bytes 1572872 | tf_op jit(solution)/shard_map/ppermute | solution.py:68
  67.0 4.8 %copy-start.14 = (bf16[4,2,128,256]{3,2,1,0:T(8,128)(2,1)}, bf16[4,2,128,256]{3,2,1,0:T(8,128)(2,1)S(1)}, u32[]{:S(2)}) copy-start(bf16[4,2,128,256]{3,2,1,0:T(8,128)(2,1)S(1)} %add_convert_fusion.1.refs_8_) | copy-start | bytes 1572868
  67.0 20.8 %collective-permute-start.19 = (bf16[4,2,128,256]{3,2,1,0:T(8,128)(2,1)S(1)}, bf16[4,2,128,256]{3,2,1,0:T(8,128)(2,1)S(1)}, u32[]{:S(2)}, u32[]{:S(2)}) collective-permute-start(bf16[4,2,128,256]{3,2,1,0:T(8,128)(2,1)S(1)} %add_convert_fusion.1.refs_8_), channel_id=1, source_target_pairs={{0,24},{1,25},{2,26},{3,27},{4,28},{5,29},{6,30},{7,31},{8,0},{9,1... | collective-permute-start | bytes 1572872 | tf_op jit(solution)/shard_map/ppermute | solution.py:71
  70.7 1.1 copy-start.15
  71.8 0.7 copy-start.16
  72.4 0.6 copy-start.17
  87.2 1.6 %collective-permute-start.24 = (bf16[2,128,256]{2,1,0:T(8,128)(2,1)}, bf16[2,128,256]{2,1,0:T(8,128)(2,1)S(1)}, u32[]{:S(2)}, u32[]{:S(2)}) collective-permute-start(bf16[2,128,256]{2,1,0:T(8,128)(2,1)} %get-tuple-element.61), channel_id=1, source_target_pairs={{0,2},{1,3},{2,0},{3,1},{4,6},{5,7},{6,4},{7,5},{8,10},{9,11},{10,... | collective-permute-start | bytes 393224 | tf_op jit(solution)/shard_map/ppermute | solution.py:68
  87.3 2.9 %collective-permute-start.25 = (bf16[2,128,256]{2,1,0:T(8,128)(2,1)}, bf16[2,128,256]{2,1,0:T(8,128)(2,1)S(1)}, u32[]{:S(2)}, u32[]{:S(2)}) collective-permute-start(bf16[2,128,256]{2,1,0:T(8,128)(2,1)} %get-tuple-element.62), channel_id=1, source_target_pairs={{0,2},{1,3},{2,0},{3,1},{4,6},{5,7},{6,4},{7,5},{8,10},{9,11},{10,... | collective-permute-start | bytes 393224 | tf_op jit(solution)/shard_map/ppermute | solution.py:68
  87.8 2.4 %collective-permute-start.26 = (bf16[2,128,256]{2,1,0:T(8,128)(2,1)}, bf16[2,128,256]{2,1,0:T(8,128)(2,1)S(1)}, u32[]{:S(2)}, u32[]{:S(2)}) collective-permute-start(bf16[2,128,256]{2,1,0:T(8,128)(2,1)} %get-tuple-element.63), channel_id=1, source_target_pairs={{0,2},{1,3},{2,0},{3,1},{4,6},{5,7},{6,4},{7,5},{8,10},{9,11},{10,... | collective-permute-start | bytes 393224 | tf_op jit(solution)/shard_map/ppermute | solution.py:68
  87.9 0.8 copy-start.4
  87.9 2.3 %collective-permute-start.27 = (bf16[2,128,256]{2,1,0:T(8,128)(2,1)}, bf16[2,128,256]{2,1,0:T(8,128)(2,1)S(1)}, u32[]{:S(2)}, u32[]{:S(2)}) collective-permute-start(bf16[2,128,256]{2,1,0:T(8,128)(2,1)} %get-tuple-element.64), channel_id=1, source_target_pairs={{0,2},{1,3},{2,0},{3,1},{4,6},{5,7},{6,4},{7,5},{8,10},{9,11},{10,... | collective-permute-start | bytes 393224 | tf_op jit(solution)/shard_map/ppermute | solution.py:68
  88.7 1.0 copy-start.28
  89.7 11.3 %collective-permute-start.23 = (bf16[4,2,128,256]{3,2,1,0:T(8,128)(2,1)S(1)}, bf16[4,2,128,256]{3,2,1,0:T(8,128)(2,1)S(1)}, u32[]{:S(2)}, u32[]{:S(2)}) collective-permute-start(bf16[4,2,128,256]{3,2,1,0:T(8,128)(2,1)S(1)} %copy-done.28), channel_id=1, source_target_pairs={{0,2},{1,3},{2,0},{3,1},{4,6},{5,7},{6,4},{7,5},{8,10},{9,11},{10,... | collective-permute-start | bytes 1572872 | tf_op jit(solution)/shard_map/ppermute | solution.py:68
  90.1 4.9 %copy-start.5 = (bf16[4,2,128,256]{3,2,1,0:T(8,128)(2,1)S(1)}, bf16[4,2,128,256]{3,2,1,0:T(8,128)(2,1)}, u32[]{:S(2)}) copy-start(bf16[4,2,128,256]{3,2,1,0:T(8,128)(2,1)} %copy-done.4) | copy-start | bytes 1572868
  90.2 4.9 %copy-start.6 = (bf16[4,2,128,256]{3,2,1,0:T(8,128)(2,1)S(1)}, bf16[4,2,128,256]{3,2,1,0:T(8,128)(2,1)}, u32[]{:S(2)}) copy-start(bf16[4,2,128,256]{3,2,1,0:T(8,128)(2,1)} %ordered.6) | copy-start | bytes 1572868
  91.4 15.1 %collective-permute-start.28 = (bf16[4,2,128,256]{3,2,1,0:T(8,128)(2,1)S(1)}, bf16[4,2,128,256]{3,2,1,0:T(8,128)(2,1)S(1)}, u32[]{:S(2)}, u32[]{:S(2)}) collective-permute-start(bf16[4,2,128,256]{3,2,1,0:T(8,128)(2,1)S(1)} %add_convert_fusion), channel_id=1, source_target_pairs={{0,24},{1,25},{2,26},{3,27},{4,28},{5,29},{6,30},{7,31},{8,0},{9,1... | collective-permute-start | bytes 1572872 | tf_op jit(solution)/shard_map/ppermute | solution.py:71
  95.3 0.9 copy-start.26
  96.3 13.4 %collective-permute-start.20 = (bf16[2,128,512]{2,1,0:T(8,128)(2,1)S(1)}, bf16[2,128,512]{2,1,0:T(8,128)(2,1)S(1)}, u32[]{:S(2)}, u32[]{:S(2)}) collective-permute-start(bf16[2,128,512]{2,1,0:T(8,128)(2,1)S(1)} %pad_maximum_fusion.4), channel_id=1, source_target_pairs={{0,5},{1,4},{2,7},{3,6},{4,1},{5,0},{6,3},{7,2},{8,13},{9,12},{10,... | collective-permute-start | bytes 786440 | tf_op jit(solution)/shard_map/ppermute | solution.py:65
  98.1 0.9 copy-start.25
  99.0 1.1 copy-start.24
  99.0 7.5 %copy-start.20 = (bf16[4,2,128,256]{3,2,1,0:T(8,128)(2,1)S(1)}, bf16[4,2,128,256]{3,2,1,0:T(8,128)(2,1)}, u32[]{:S(2)}) copy-start(bf16[4,2,128,256]{3,2,1,0:T(8,128)(2,1)} %get-tuple-element.58) | copy-start | bytes 1572868
  99.1 13.4 %collective-permute-start.21 = (bf16[2,128,512]{2,1,0:T(8,128)(2,1)S(1)}, bf16[2,128,512]{2,1,0:T(8,128)(2,1)S(1)}, u32[]{:S(2)}, u32[]{:S(2)}) collective-permute-start(bf16[2,128,512]{2,1,0:T(8,128)(2,1)S(1)} %pad_maximum_fusion.5), channel_id=1, source_target_pairs={{0,1},{1,0},{2,3},{3,2},{4,5},{5,4},{6,7},{7,6},{8,9},{9,8},{10,11... | collective-permute-start | bytes 786440 | tf_op jit(solution)/shard_map/ppermute | solution.py:65
  100.2 12.3 %collective-permute-start.22 = (bf16[2,128,512]{2,1,0:T(8,128)(2,1)S(1)}, bf16[2,128,512]{2,1,0:T(8,128)(2,1)S(1)}, u32[]{:S(2)}, u32[]{:S(2)}) collective-permute-start(bf16[2,128,512]{2,1,0:T(8,128)(2,1)S(1)} %pad_maximum_fusion.6), channel_id=1, source_target_pairs={{0,4},{1,5},{2,6},{3,7},{4,0},{5,1},{6,2},{7,3},{8,12},{9,13},{10,... | collective-permute-start | bytes 786440 | tf_op jit(solution)/shard_map/ppermute | solution.py:65
  107.4 8.2 %collective-permute-start.31 = (bf16[2,128,256]{2,1,0:T(8,128)(2,1)S(1)}, bf16[2,128,256]{2,1,0:T(8,128)(2,1)S(1)}, u32[]{:S(2)}, u32[]{:S(2)}) collective-permute-start(bf16[2,128,256]{2,1,0:T(8,128)(2,1)S(1)} %get-tuple-element.67), channel_id=1, source_target_pairs={{0,4},{1,5},{2,6},{3,7},{4,0},{5,1},{6,2},{7,3},{8,12},{9,13},{10,... | collective-permute-start | bytes 393224 | tf_op jit(solution)/shard_map/ppermute | solution.py:65
  108.6 7.0 %collective-permute-start.30 = (bf16[2,128,256]{2,1,0:T(8,128)(2,1)S(1)}, bf16[2,128,256]{2,1,0:T(8,128)(2,1)S(1)}, u32[]{:S(2)}, u32[]{:S(2)}) collective-permute-start(bf16[2,128,256]{2,1,0:T(8,128)(2,1)S(1)} %get-tuple-element.68), channel_id=1, source_target_pairs={{0,1},{1,0},{2,3},{3,2},{4,5},{5,4},{6,7},{7,6},{8,9},{9,8},{10,11... | collective-permute-start | bytes 393224 | tf_op jit(solution)/shard_map/ppermute | solution.py:65
  109.7 2.8 %copy-start.9 = (bf16[2,128,512]{2,1,0:T(8,128)(2,1)}, bf16[2,128,512]{2,1,0:T(8,128)(2,1)S(1)}, u32[]{:S(2)}) copy-start(bf16[2,128,512]{2,1,0:T(8,128)(2,1)S(1)} %collective-permute-done.20.refs_5_) | copy-start | bytes 786436
  109.7 6.8 %collective-permute-start.29 = (bf16[2,128,256]{2,1,0:T(8,128)(2,1)S(1)}, bf16[2,128,256]{2,1,0:T(8,128)(2,1)S(1)}, u32[]{:S(2)}, u32[]{:S(2)}) collective-permute-start(bf16[2,128,256]{2,1,0:T(8,128)(2,1)S(1)} %get-tuple-element.69), channel_id=1, source_target_pairs={{0,5},{1,4},{2,7},{3,6},{4,1},{5,0},{6,3},{7,2},{8,13},{9,12},{10,... | collective-permute-start | bytes 393224 | tf_op jit(solution)/shard_map/ppermute | solution.py:65
  110.9 0.9 copy-start.18
  112.5 0.7 copy-start.10
  112.5 0.8 copy-start.11
  115.6 0.9 copy-start.21
  115.6 0.9 copy-start.22
  116.5 0.6 copy-start.23

commit v5 on v4

--- a/solution.py
+++ b/solution.py
@@ -135,7 +135,7 @@
     )(value, *after)
 
 
-def backward(plan, chunk, doc_lengths, query_pieces, key_arrays, after):
+def backward(plan, chunk, doc_lengths, query_pieces, key_arrays, earlier, after):
     tiles = plan.slab + 1
     block, groups, tp, cores = plan.block, plan.groups, plan.tp, plan.cores
     heads, key_cols, query_cols = plan.heads, plan.key_cols, plan.query_cols
@@ -143,17 +143,17 @@
     query_width = HEAD_SIZE * GROUP
     exponent_scale = attn_scale * math.log2(math.e)
     loads = heads * 5 * groups
-    stores = heads * (2 * groups + 3)
+    stores = heads * (2 * groups + 3) + len(earlier)
 
     def kernel(docs, *refs):
         pieces, refs = refs[:groups], refs[groups:]
         key_refs, refs = refs[:4], refs[4:]
-        refs = refs[len(after) :]
+        early, refs = refs[: len(earlier)], refs[len(earlier) + len(after) :]
         query_out, refs = refs[:groups], refs[groups:]
         before_mine, own_mine, own_far, refs = *refs[:3], refs[3:]
         parts = (before_mine, None, own_mine, own_far)
         before_far, refs = refs[:groups], refs[groups:]
-        qo_s, kv_s, dq_s, dk_s, dv_s, part_s, score_s, prob_grad_s, prob_s, grad_s, sem, out_sem = refs
+        qo_s, kv_s, dq_s, early_s, dk_s, dv_s, part_s, score_s, prob_grad_s, prob_s, grad_s, sem, out_sem = refs
         q_s, o_s, k_s, v_s = qo_s.at[0], qo_s.at[1], kv_s.at[0], kv_s.at[1]
         slab_seq, core, group = plan.place()
 
@@ -179,6 +179,8 @@
             for source, (late, away) in zip(key_refs, itertools.product((1, 0), (0, 1))):
                 for at, flip in enumerate(plan.flips):
                     load(source.at[at, :, :, there], kv_s.at[:, block_of(late, away, flip), :, here])
+        for at, source in enumerate(early):
+            load(source, early_s.at[at])
         dk_s[...] = jnp.zeros_like(dk_s)
         dv_s[...] = jnp.zeros_like(dv_s)
 
@@ -264,6 +266,11 @@
                 copy.wait()
             for way in range(plan.ways):
                 step(head, way)
+            if head == 0:
+                for copy in copies[loads:]:
+                    copy.wait()
+                for at, target in enumerate(query_out[: len(early)]):
+                    store(early_s.at[at], target.at[pl.ds(0, chunk)])
             head_cols = pl.ds(head * HEAD_SIZE, HEAD_SIZE)
             for late, away in itertools.product((0, 1), (0, 1)):
                 staged = part_s.at[late, away]
@@ -277,7 +284,7 @@
                         store(staged.at[piece, :, :, head_cols], before_far[piece].at[:, :, head_cols])
             done_part = pl.ds(head * query_width, query_width)
             for at, flip in enumerate(plan.flips):
-                store(dq_s.at[group ^ flip, :, done_part], query_out[at].at[0, :, done_part])
+                store(dq_s.at[group ^ flip, :, done_part], query_out[at].at[chunk, :, done_part])
         for copy in results:
             copy.wait()
 
@@ -287,15 +294,16 @@
     pairs = tiles * block * wide * heads * plan.ways
     out = pl.pallas_call(
         kernel,
-        out_shape=[jax.ShapeDtypeStruct((1, plan.rows, query_cols), bf)] * groups
+        out_shape=[jax.ShapeDtypeStruct((chunk + 1, plan.rows, query_cols), bf)] * groups
         + [jax.ShapeDtypeStruct(part, bf)] * 3
         + [jax.ShapeDtypeStruct(part[1:], bf)] * groups,
-        in_specs=[SMEM] + [ANY] * (groups + 4 + len(after)),
+        in_specs=[SMEM] + [ANY] * (groups + 4 + len(earlier) + len(after)),
         out_specs=[ANY] * (2 * groups + 3),
         scratch_shapes=[
             pltpu.VMEM((2, groups, plan.rows, query_cols), bf),
             pltpu.VMEM((2, span, plan.rows, key_cols), bf),
             pltpu.VMEM((groups, plan.rows, query_cols), bf),
+            pltpu.VMEM((groups, max(chunk, 1), plan.rows, query_cols), bf),
             pltpu.VMEM((span, plan.rows, key_cols), fl),
             pltpu.VMEM((span, plan.rows, key_cols), fl),
             pltpu.VMEM((2, 2) + part, bf),
@@ -303,14 +311,18 @@
             pltpu.VMEM((tiles * block, wide), fl),
             pltpu.VMEM((tiles * block, wide), bf),
             pltpu.VMEM((tiles * block, wide), bf),
-            pltpu.SemaphoreType.DMA((loads,)),
+            pltpu.SemaphoreType.DMA((loads + len(earlier),)),
             pltpu.SemaphoreType.DMA((stores,)),
         ],
         compiler_params=pltpu.CompilerParams(vmem_limit_bytes=VMEM_LIMIT),
         cost_estimate=pl.CostEstimate(flops=160 * pairs * HEAD_SIZE, bytes_accessed=6 << 20, transcendentals=pairs),
         name="backward",
-    )(doc_lengths, *query_pieces, *key_arrays, *after)
+    )(doc_lengths, *query_pieces, *key_arrays, *earlier, *after)
     return out[:groups], out[groups : groups + 3], out[groups + 3 :]
+
+
+def token(arrays):
+    return sum(array.reshape(-1, array.shape[-1])[:16, :HEAD_SIZE] for array in arrays)
 
 
 def add_up(*parts):
@@ -321,7 +333,7 @@
 
 
 def join_columns(plan, sources, targets, width, name):
-    flat = [piece for pieces in sources for piece in pieces]
+    flat = [piece for pieces in sources for piece in pieces[::-1]]
     chunks = len(targets[0])
     chunk_width = width // chunks
 
@@ -335,7 +347,7 @@
                     start = (group ^ flip) * width + chunk * chunk_width
                     copies.append(
                         pltpu.make_async_copy(
-                            pieces[which * plan.groups + at].at[row, :, pl.ds(column, chunk_width)],
+                            pieces[(which + 1) * plan.groups - 1 - at].at[row, :, pl.ds(column, chunk_width)],
                             out.at[:, columns(start, chunk_width)],
                             sem.at[len(copies)],
                         )
@@ -375,39 +387,29 @@
     before = jnp.stack([ordered(moved[0], HARD, (own_first, *arrived[1:])), *moved[1:]])
     before_other = plan.to_core(before)
     key_arrays = (own, own_other, before, before_other)
-    after, hold = (), ()
-    sums, query_outs, sent = [], [], []
+    after, hold, query_out = (), (), ()
+    sums = []
     for chunk in range(plan.chunks):
-        query_out, (before_mine, own_mine, own_far), before_far = backward(plan, chunk, doc_lengths, arrived, key_arrays, after)
+        query_out, (before_mine, own_mine, own_far), before_far = backward(
+            plan, chunk, doc_lengths, arrived, key_arrays, query_out, after
+        )
         if hold:
             before_mine = ordered(before_mine, EASY, hold)
         before_sum = add_up(before_mine, jnp.stack([plan.to_core(piece) for piece in before_far]))
         later = plan.to_slab(before_sum, -1)
         sums.append((own_mine, plan.to_core(own_far), later))
-        query_outs.append(query_out)
-        if chunk < plan.chunks - 1 or plan.chunks == 1:
-            sent.append(exchange(query_out))
-            after = (before_sum, *sent[-1][1:])
-        hold = (later,)
-    query_from, key_from, value_from = ([(chunk, 0, 0) for chunk in range(len(sent))], [], [])
-    for chunk in range(plan.chunks):
-        own_mine, own_far, later = sums[chunk]
-        riders = chunk == 0 and plan.chunks > 1
-        if riders:
-            own_mine = ordered(own_mine, HARD, query_outs[-1][:1])
-        messages = [add_up(own_mine[at], own_far[at], later[at]) for at in range(plan.groups)]
-        if riders:
-            messages = [
-                jnp.concatenate([rider, jnp.concatenate([message[0], message[1]], axis=1)[None]])
-                for rider, message in zip(query_outs[-1], messages)
-            ]
-            query_from.append((len(sent), 0, 0))
-        sent.append(exchange(messages))
-        at = len(sent) - 1
-        key_from.append((at, 1, 0) if riders else (at, 0, 0))
-        value_from.append((at, 1, plan.key_cols) if riders else (at, 1, 0))
-    (query_grad,) = join_columns(plan, sent[: plan.chunks], [query_from], query_width, "join_queries")
-    key_gradient, value_gradient = join_columns(plan, sent, [key_from, value_from], key_width, "join_keys")
+        after, hold = (token((before_sum,)),), (later,)
+    query_sent = exchange(query_out)
+    key_sent = []
+    for chunk, (own_mine, own_far, later) in enumerate(sums):
+        if chunk < plan.chunks - 1:
+            own_mine = ordered(own_mine, HARD, query_out[:1])
+        key_sent.append(exchange([add_up(own_mine[at], own_far[at], later[at]) for at in range(plan.groups)]))
+    chunks = range(plan.chunks)
+    (query_grad,) = join_columns(plan, [query_sent], [[(0, chunk, 0) for chunk in chunks]], query_width, "join_queries")
+    key_gradient, value_gradient = join_columns(
+        plan, key_sent, [[(chunk, index, 0) for chunk in chunks] for index in (0, 1)], key_width, "join_keys"
+    )
     return query_grad, key_gradient, value_gradient
 
 

time: 120 us -> 118 us (0.983)
  local copies, waits for them, and re-layouts: 7.66 us -> 3.02 us
  waiting for transfers between devices: 30.7 us -> 34.4 us
  starting transfers between devices: 35.3 us -> 32.9 us
    unnamed x58 -> x44, local copies, waits for them, and re-layouts: 7.62 us -> 2.43 us
    ppermute x5, starting transfers between devices: 12.9 us -> 9.97 us  [to_slab(): lax.ppermute(value, AXES, self.routes(lambda slab, core, group: (slab + s...]
    convert_element_type x4, other arithmetic: 3.47 us -> 5.2 us  [add_up(): return total.astype(jnp.bfloat16)]
    ppermute x15, waiting for transfers between devices: 22.4 us -> 24 us  [to_group(): lax.ppermute(value, AXES, self.routes(lambda slab, core, group: (slab, co...]
    ppermute x12, waiting for transfers between devices: 2.83 us -> 4.23 us  [to_core(): lax.ppermute(value, AXES, self.routes(lambda slab, core, group: (slab, se...]
  transfers between devices with their start and end apart: 32 -> 32, of which waited for: 9 -> 15; matrix products, arithmetic and copies ran while one was open for 6% -> 6% of each run, Pallas kernels for 16% -> 17%
where the time goes in v5:
time: 118 us; the launch traced here: 117 us
  Pallas kernels  38.2 us (32%)
  waiting for transfers between devices  34.4 us (29%)
  starting transfers between devices  32.9 us (28%)
  other arithmetic  7.63 us (6%)
  local copies, waits for them, and re-layouts  3.02 us (3%)
    pallas_call x2, Pallas kernels, backward(): pl.pallas_call(kernel, out_shape=[jax.ShapeDtypeStruct((chunk + 1, plan.r...  28.2 us
    ppermute x15, waiting for transfers between devices, to_group(): lax.ppermute(value, AXES, self.routes(lambda slab, core, group: (slab, co...  24 us
    ppermute x15, starting transfers between devices, to_group(): lax.ppermute(value, AXES, self.routes(lambda slab, core, group: (slab, co...  20.5 us
    ppermute x5, starting transfers between devices, to_slab(): lax.ppermute(value, AXES, self.routes(lambda slab, core, group: (slab + s...  9.97 us
    ppermute x5, waiting for transfers between devices, to_slab(): lax.ppermute(value, AXES, self.routes(lambda slab, core, group: (slab + s...  6.21 us
    pallas_call x2, Pallas kernels, split_columns(): pl.pallas_call(kernel, out_shape=[shape] * count, in_specs=[ANY] * (len(a...  5.27 us
    convert_element_type x4, other arithmetic, add_up(): return total.astype(jnp.bfloat16)  5.2 us
    pallas_call x2, Pallas kernels, join_columns(): pl.pallas_call(kernel, out_shape=[jax.ShapeDtypeStruct((plan.rows, width...  4.67 us
  transfers between devices with their start and end apart: 32, of which 15 were waited for; matrix products, arithmetic and copies ran while one was open for 6% of the time, Pallas kernels for 17%

profile of v5, /device:TPU:0, one launch (start us, length us, event | category | flops | bytes accessed | tf_op | source)
XLA Modules:
  0.0 117.1 jit_solution(1341323763126913337)
XLA Ops:
  0.6 2.4 %split_keys.1 = (bf16[2,128,512]{2,1,0:T(8,128)(2,1)}, bf16[2,128,512]{2,1,0:T(8,128)(2,1)}, bf16[2,128,512]{2,1,0:T(8,128)(2,1)}, bf16[2,128,512]{2,1,0:T(8,128)(2,1)}) custom-call(bf16[128,2048]{1,0:T(8,128)(2,1)} %refs_0_.2, bf16[128,2048]{1,0:T(8,128)(2,1)} %refs_1_.2), custom_call_target="tpu_custom_call" | custom-call | bytes 2097152 | tf_op jit(solution)/shard_map/split_keys/pallas_call | solution.py:111
  3.0 3.0 %collective-permute-start.4 = (bf16[2,128,512]{2,1,0:T(8,128)(2,1)}, bf16[2,128,512]{2,1,0:T(8,128)(2,1)S(1)}, u32[]{:S(2)}, u32[]{:S(2)}) collective-permute-start(bf16[2,128,512]{2,1,0:T(8,128)(2,1)} %get-tuple-element.41), channel_id=1, source_target_pairs={{0,1},{1,0},{2,3},{3,2},{4,5},{5,4},{6,7},{7,6},{8,9},{9,8},{10,11... | collective-permute-start | bytes 786440 | tf_op jit(solution)/shard_map/ppermute | solution.py:65
  6.0 1.5 %collective-permute-start.5 = (bf16[2,128,512]{2,1,0:T(8,128)(2,1)}, bf16[2,128,512]{2,1,0:T(8,128)(2,1)S(1)}, u32[]{:S(2)}, u32[]{:S(2)}) collective-permute-start(bf16[2,128,512]{2,1,0:T(8,128)(2,1)} %get-tuple-element.42), channel_id=1, source_target_pairs={{0,4},{1,5},{2,6},{3,7},{4,0},{5,1},{6,2},{7,3},{8,12},{9,13},{10,... | collective-permute-start | bytes 786440 | tf_op jit(solution)/shard_map/ppermute | solution.py:65
  7.5 0.0 collective-permute-start.3
  7.6 2.0 %collective-permute-start.7 = (bf16[2,128,512]{2,1,0:T(8,128)(2,1)}, bf16[2,128,512]{2,1,0:T(8,128)(2,1)S(1)}, u32[]{:S(2)}, u32[]{:S(2)}) collective-permute-start(bf16[2,128,512]{2,1,0:T(8,128)(2,1)} %get-tuple-element.35.refs_2_.refs_0_), channel_id=1, source_target_pairs={{0,8},{1,9},{2,10},{3,11},{4,12},{5,13},{6,14},{7,15},{8,16},{9,17... | collective-permute-start | bytes 786440 | tf_op jit(solution)/shard_map/ppermute | solution.py:71
  9.6 2.9 %split_queries.1 = (bf16[2,128,1024]{2,1,0:T(8,128)(2,1)}, bf16[2,128,1024]{2,1,0:T(8,128)(2,1)}, bf16[2,128,1024]{2,1,0:T(8,128)(2,1)}, bf16[2,128,1024]{2,1,0:T(8,128)(2,1)}) custom-call(bf16[128,4096]{1,0:T(8,128)(2,1)} %refs_0_.3, bf16[128,4096]{1,0:T(8,128)(2,1)} %refs_1_.3, bf16[2,128,512]{2,1,0:T(8,128)(2,1)} %get-tuple-element.35.refs_2_.refs_0_), custom_call_target="tpu_custom_call" | custom-call | bytes 4194304 | tf_op jit(solution)/shard_map/split_queries/pallas_call | solution.py:111
  12.5 2.5 %collective-permute-start = (bf16[2,128,1024]{2,1,0:T(8,128)(2,1)}, bf16[2,128,1024]{2,1,0:T(8,128)(2,1)S(1)}, u32[]{:S(2)}, u32[]{:S(2)}) collective-permute-start(bf16[2,128,1024]{2,1,0:T(8,128)(2,1)} %get-tuple-element.37), channel_id=1, source_target_pairs={{0,5},{1,4},{2,7},{3,6},{4,1},{5,0},{6,3},{7,2},{8,13},{9,12},{10,... | collective-permute-start | bytes 1572872 | tf_op jit(solution)/shard_map/ppermute | solution.py:65
  15.0 0.5 collective-permute-start.1
  15.5 1.4 %collective-permute-start.2 = (bf16[2,128,1024]{2,1,0:T(8,128)(2,1)}, bf16[2,128,1024]{2,1,0:T(8,128)(2,1)}, u32[]{:S(2)}, u32[]{:S(2)}) collective-permute-start(bf16[2,128,1024]{2,1,0:T(8,128)(2,1)} %get-tuple-element.39), channel_id=1, source_target_pairs={{0,4},{1,5},{2,6},{3,7},{4,0},{5,1},{6,2},{7,3},{8,12},{9,13},{10,... | collective-permute-start | bytes 1572872 | tf_op jit(solution)/shard_map/ppermute | solution.py:65
  17.0 0.1 pad_maximum_fusion.2
  17.1 3.6 %collective-permute-done.3.refs_1_ = bf16[2,128,512]{2,1,0:T(8,128)(2,1)S(1)} collective-permute-done((bf16[2,128,512]{2,1,0:T(8,128)(2,1)}, bf16[2,128,512]{2,1,0:T(8,128)(2,1)S(1)}, u32[]{:S(2)}, u32[]{:S(2)}) %collective-permute-start.3) | collective-permute-done | bytes 262176 | tf_op jit(solution)/shard_map/ppermute | solution.py:65
  20.7 2.0 %collective-permute-start.9 = (bf16[2,2,128,512]{3,2,1,0:T(8,128)(2,1)S(1)}, bf16[2,2,128,512]{3,2,1,0:T(8,128)(2,1)}, u32[]{:S(2)}, u32[]{:S(2)}) collective-permute-start(bf16[2,2,128,512]{3,2,1,0:T(8,128)(2,1)S(1)} %pad_maximum_fusion.2), channel_id=1, source_target_pairs={{0,8},{1,9},{2,10},{3,11},{4,12},{5,13},{6,14},{7,15},{8,16},{9,17... | collective-permute-start | bytes 1572872 | tf_op jit(solution)/shard_map/ppermute | solution.py:71
  22.7 1.6 %collective-permute-start.8 = (bf16[2,128,512]{2,1,0:T(8,128)(2,1)S(1)}, bf16[2,128,512]{2,1,0:T(8,128)(2,1)S(1)}, u32[]{:S(2)}, u32[]{:S(2)}) collective-permute-start(bf16[2,128,512]{2,1,0:T(8,128)(2,1)S(1)} %collective-permute-done.3.refs_1_), channel_id=1, source_target_pairs={{0,8},{1,9},{2,10},{3,11},{4,12},{5,13},{6,14},{7,15},{8,16},{9,17... | collective-permute-start | bytes 786440 | tf_op jit(solution)/shard_map/ppermute | solution.py:71
  24.3 1.2 pad_maximum_fusion.refs_4_
  25.5 6.3 %collective-permute-done.refs_2_.refs_1_ = bf16[2,128,1024]{2,1,0:T(8,128)(2,1)S(1)} collective-permute-done((bf16[2,128,1024]{2,1,0:T(8,128)(2,1)}, bf16[2,128,1024]{2,1,0:T(8,128)(2,1)S(1)}, u32[]{:S(2)}, u32[]{:S(2)}) %collective-permute-start) | collective-permute-done | bytes 524320 | tf_op jit(solution)/shard_map/ppermute | solution.py:65
  31.9 10.1 %collective-permute-done.1.refs_3_.refs_2_ = bf16[2,128,1024]{2,1,0:T(8,128)(2,1)} collective-permute-done((bf16[2,128,1024]{2,1,0:T(8,128)(2,1)}, bf16[2,128,1024]{2,1,0:T(8,128)(2,1)}, u32[]{:S(2)}, u32[]{:S(2)}) %collective-permute-start.1) | collective-permute-done | bytes 524320 | tf_op jit(solution)/shard_map/ppermute | solution.py:65
  42.0 0.2 collective-permute-done.2.refs_4_.refs_3_
  42.3 1.2 %pad_maximum_fusion.1.refs_6_ = bf16[4,2,128,512]{3,2,1,0:T(8,128)(2,1)S(1)} fusion(bf16[2,2,128,512]{3,2,1,0:T(8,128)(2,1)} %collective-permute-done.9, bf16[1,2,128,512]{3,2,1,0:T(8,128)(2,1)S(1)} %bitcast.39, bf16[1,2,128,512]{3,2,1,0:T(8,128)(2,1)} %bitcast.37), kind=kLoop, calls=%fused_computation.1 | loop fusion | flops 1048576 | bytes 2097152 | tf_op jit(solution)/shard_map/stack | solution.py:387
  43.5 0.1 collective-permute-start.10
  43.6 2.6 %collective-permute-done.10.refs_7_ = bf16[4,2,128,512]{3,2,1,0:T(8,128)(2,1)S(1)} collective-permute-done((bf16[4,2,128,512]{3,2,1,0:T(8,128)(2,1)S(1)}, bf16[4,2,128,512]{3,2,1,0:T(8,128)(2,1)S(1)}, u32[]{:S(2)}, u32[]{:S(2)}) %collective-permute-start.10) | collective-permute-done | bytes 1048608 | tf_op jit(solution)/shard_map/ppermute | solution.py:68
  46.2 1.0 copy-done.21
  47.2 14.1 %backward.2 = (bf16[1,128,512]{2,1,0:T(8,128)(2,1)}, bf16[1,128,512]{2,1,0:T(8,128)(2,1)}, bf16[1,128,512]{2,1,0:T(8,128)(2,1)}, bf16[1,128,512]{2,1,0:T(8,128)(...) custom-call(s32[4]{0:T(128)} %docs.3, ...), custom_call_target="tpu_custom_call" | custom-call | flops 53687091200 | bytes 6291456 | tf_op jit(solution)/shard_map/backward/pallas_call | solution.py:295
  61.3 0.2 collective-permute-start.11
  61.5 0.4 collective-permute-start.12
  61.9 0.1 collective-permute-start.13
  62.0 0.4 collective-permute-start.14
  62.4 0.5 collective-permute-done.11
  62.9 0.2 collective-permute-done.12
  63.1 0.3 collective-permute-done.13
  63.4 0.2 collective-permute-done.14
  63.6 1.2 add_convert_fusion.1
  64.8 3.8 %collective-permute-start.19 = (bf16[4,2,128,256]{3,2,1,0:T(8,128)(2,1)S(1)}, bf16[4,2,128,256]{3,2,1,0:T(8,128)(2,1)S(1)}, u32[]{:S(2)}, u32[]{:S(2)}) collective-permute-start(bf16[4,2,128,256]{3,2,1,0:T(8,128)(2,1)S(1)} %add_convert_fusion.1), channel_id=1, source_target_pairs={{0,24},{1,25},{2,26},{3,27},{4,28},{5,29},{6,30},{7,31},{8,0},{9,1... | collective-permute-start | bytes 1572872 | tf_op jit(solution)/shard_map/ppermute | solution.py:71
  68.6 0.6 slice.103.refs_12_
  69.2 14.2 %backward.3 = (bf16[2,128,512]{2,1,0:T(8,128)(2,1)}, bf16[2,128,512]{2,1,0:T(8,128)(2,1)}, bf16[2,128,512]{2,1,0:T(8,128)(2,1)}, bf16[2,128,512]{2,1,0:T(8,128)(...) custom-call(s32[4]{0:T(128)} %docs.3, ...), custom_call_target="tpu_custom_call" | custom-call | flops 53687091200 | bytes 6291456 | tf_op jit(solution)/shard_map/backward/pallas_call | solution.py:295
  83.4 0.1 collective-permute-start.24
  83.5 0.5 collective-permute-start.25
  84.0 0.1 collective-permute-start.26
  84.0 0.4 collective-permute-start.27
  84.5 0.1 collective-permute-start.18
  84.6 0.7 copy-done.4
  85.3 0.1 collective-permute-start.23
  85.4 0.2 collective-permute-done.26
  85.5 0.2 collective-permute-done.27
  85.7 1.2 add_convert_fusion
  86.9 0.5 collective-permute-start.28
  87.4 1.5 %collective-permute-start.15 = (bf16[2,128,512]{2,1,0:T(8,128)(2,1)}, bf16[2,128,512]{2,1,0:T(8,128)(2,1)S(1)}, u32[]{:S(2)}, u32[]{:S(2)}) collective-permute-start(bf16[2,128,512]{2,1,0:T(8,128)(2,1)} %get-tuple-element.52), channel_id=1, source_target_pairs={{0,4},{1,5},{2,6},{3,7},{4,0},{5,1},{6,2},{7,3},{8,12},{9,13},{10,... | collective-permute-start | bytes 786440 | tf_op jit(solution)/shard_map/ppermute | solution.py:65
  88.9 1.0 collective-permute-start.16
  89.9 1.1 collective-permute-start.17
  91.0 2.0 %fusion.3 = (bf16[2,128,256]{2,1,0:T(8,128)(2,1)}, bf16[2,128,256]{2,1,0:T(8,128)(2,1)S(1)}, bf16[2,128,256]{2,1,0:T(8,128)(2,1)}, bf16[2,128,256]{2,1,0:T(8,128)(2,1)S(1)}) fusion(bf16[4,2,128,256]{3,2,1,0:T(8,128)(2,1)S(1)} %copy-done.5, bf16[4,2,128,256]{3,2,1,0:T(8,128)(2,1)S(1)} %collective-permute-done.18, bf16[4,2,128,256]{3,2,1,0:T(8,128)(2,1)} %ordered.6), kind=kLoop, calls=%fused_computation.16 | loop fusion | flops 1572864 | bytes 2097152 | tf_op jit(solution)/shard_map/convert_element_type | solution.py:332
  93.0 1.9 %collective-permute-start.22 = (bf16[2,128,256]{2,1,0:T(8,128)(2,1)S(1)}, bf16[2,128,256]{2,1,0:T(8,128)(2,1)S(1)}, u32[]{:S(2)}, u32[]{:S(2)}) collective-permute-start(bf16[2,128,256]{2,1,0:T(8,128)(2,1)S(1)} %get-tuple-element.72), channel_id=1, source_target_pairs={{0,5},{1,4},{2,7},{3,6},{4,1},{5,0},{6,3},{7,2},{8,13},{9,12},{10,... | collective-permute-start | bytes 393224 | tf_op jit(solution)/shard_map/ppermute | solution.py:65
  94.9 6.2 %collective-permute-done.28 = bf16[4,2,128,256]{3,2,1,0:T(8,128)(2,1)S(1)} collective-permute-done((bf16[4,2,128,256]{3,2,1,0:T(8,128)(2,1)S(1)}, bf16[4,2,128,256]{3,2,1,0:T(8,128)(2,1)S(1)}, u32[]{:S(2)}, u32[]{:S(2)}) %collective-permute-start.28) | collective-permute-done | bytes 524320 | tf_op jit(solution)/shard_map/ppermute | solution.py:71
  101.1 1.0 collective-permute-start.21
  102.1 0.9 fusion.7
  102.9 1.5 %collective-permute-start.20 = (bf16[2,128,256]{2,1,0:T(8,128)(2,1)S(1)}, bf16[2,128,256]{2,1,0:T(8,128)(2,1)S(1)}, u32[]{:S(2)}, u32[]{:S(2)}) collective-permute-start(bf16[2,128,256]{2,1,0:T(8,128)(2,1)S(1)} %get-tuple-element.74), channel_id=1, source_target_pairs={{0,4},{1,5},{2,6},{3,7},{4,0},{5,1},{6,2},{7,3},{8,12},{9,13},{10,... | collective-permute-start | bytes 393224 | tf_op jit(solution)/shard_map/ppermute | solution.py:65
  104.4 1.4 %collective-permute-done.16.refs_1_ = bf16[2,128,512]{2,1,0:T(8,128)(2,1)S(1)} collective-permute-done((bf16[2,128,512]{2,1,0:T(8,128)(2,1)}, bf16[2,128,512]{2,1,0:T(8,128)(2,1)S(1)}, u32[]{:S(2)}, u32[]{:S(2)}) %collective-permute-start.16) | collective-permute-done | bytes 262176 | tf_op jit(solution)/shard_map/ppermute | solution.py:65
  105.8 1.0 collective-permute-start.31
  106.8 0.4 collective-permute-start.30
  107.2 2.1 %collective-permute-start.29 = (bf16[2,128,256]{2,1,0:T(8,128)(2,1)S(1)}, bf16[2,128,256]{2,1,0:T(8,128)(2,1)S(1)}, u32[]{:S(2)}, u32[]{:S(2)}) collective-permute-start(bf16[2,128,256]{2,1,0:T(8,128)(2,1)S(1)} %get-tuple-element.70), channel_id=1, source_target_pairs={{0,4},{1,5},{2,6},{3,7},{4,0},{5,1},{6,2},{7,3},{8,12},{9,13},{10,... | collective-permute-start | bytes 393224 | tf_op jit(solution)/shard_map/ppermute | solution.py:65
  109.3 2.3 %join_queries.1 = bf16[128,4096]{1,0:T(8,128)(2,1)} custom-call(bf16[2,128,512]{2,1,0:T(8,128)(2,1)} %copy-done.12, bf16[2,128,512]{2,1,0:T(8,128)(2,1)} %copy-done.13, bf16[2,128,512]{2,1,0:T(8,128)(2,1)} %copy-done.14, bf16[2,128,512]{2,1,0:T(8,128)(2,1)} %get-tuple-element.55.refs_3_.refs_1_), custom_call_target="tpu_custom_call" | custom-call | bytes 2097152 | tf_op jit(solution)/shard_map/join_queries/pallas_call | solution.py:357
  111.7 0.9 collective-permute-done.31.refs_6_
  112.6 1.3 %collective-permute-done.30.refs_5_ = bf16[2,128,256]{2,1,0:T(8,128)(2,1)S(1)} collective-permute-done((bf16[2,128,256]{2,1,0:T(8,128)(2,1)S(1)}, bf16[2,128,256]{2,1,0:T(8,128)(2,1)S(1)}, u32[]{:S(2)}, u32[]{:S(2)}) %collective-permute-start.30) | collective-permute-done | bytes 131104 | tf_op jit(solution)/shard_map/ppermute | solution.py:65
  114.0 0.6 copy-done.19
  114.6 0.1 copy-done.20
  114.6 2.3 %join_keys.1 = (bf16[128,2048]{1,0:T(8,128)(2,1)}, bf16[128,2048]{1,0:T(8,128)(2,1)}) custom-call(bf16[2,128,256]{2,1,0:T(8,128)(2,1)} %copy-done.17, bf16[2,128,256]{2,1,0:T(8,128)(2,1)} %copy-done.16, bf16[2,128,256]{2,1,0:T(8,128)(2,1)} %copy-done.15, bf16[2,128,256]{2,1,0:T(8,128)(2,1)} %get-tuple-element.71.refs_3_, bf16[2,128,256]{2,1,0:T(8,128)(2,1)} %copy-done.20, ...), custom_call_target="tpu_custom_call" | custom-call | bytes 2097152 | tf_op jit(solution)/shard_map/join_keys/pallas_call | solution.py:357
  (62 shorter events, 0.1 us)
Async XLA Ops:
  3.0 12.0 %collective-permute-start.4 = (bf16[2,128,512]{2,1,0:T(8,128)(2,1)}, bf16[2,128,512]{2,1,0:T(8,128)(2,1)S(1)}, u32[]{:S(2)}, u32[]{:S(2)}) collective-permute-start(bf16[2,128,512]{2,1,0:T(8,128)(2,1)} %get-tuple-element.41), channel_id=1, source_target_pairs={{0,1},{1,0},{2,3},{3,2},{4,5},{5,4},{6,7},{7,6},{8,9},{9,8},{10,11... | collective-permute-start | bytes 786440 | tf_op jit(solution)/shard_map/ppermute | solution.py:65
  6.0 9.5 %collective-permute-start.5 = (bf16[2,128,512]{2,1,0:T(8,128)(2,1)}, bf16[2,128,512]{2,1,0:T(8,128)(2,1)S(1)}, u32[]{:S(2)}, u32[]{:S(2)}) collective-permute-start(bf16[2,128,512]{2,1,0:T(8,128)(2,1)} %get-tuple-element.42), channel_id=1, source_target_pairs={{0,4},{1,5},{2,6},{3,7},{4,0},{5,1},{6,2},{7,3},{8,12},{9,13},{10,... | collective-permute-start | bytes 786440 | tf_op jit(solution)/shard_map/ppermute | solution.py:65
  7.5 13.1 %collective-permute-start.3 = (bf16[2,128,512]{2,1,0:T(8,128)(2,1)}, bf16[2,128,512]{2,1,0:T(8,128)(2,1)S(1)}, u32[]{:S(2)}, u32[]{:S(2)}) collective-permute-start(bf16[2,128,512]{2,1,0:T(8,128)(2,1)} %get-tuple-element.40), channel_id=1, source_target_pairs={{0,5},{1,4},{2,7},{3,6},{4,1},{5,0},{6,3},{7,2},{8,13},{9,12},{10,... | collective-permute-start | bytes 786440 | tf_op jit(solution)/shard_map/ppermute | solution.py:65
  7.6 15.1 %collective-permute-start.7 = (bf16[2,128,512]{2,1,0:T(8,128)(2,1)}, bf16[2,128,512]{2,1,0:T(8,128)(2,1)S(1)}, u32[]{:S(2)}, u32[]{:S(2)}) collective-permute-start(bf16[2,128,512]{2,1,0:T(8,128)(2,1)} %get-tuple-element.35.refs_2_.refs_0_), channel_id=1, source_target_pairs={{0,8},{1,9},{2,10},{3,11},{4,12},{5,13},{6,14},{7,15},{8,16},{9,17... | collective-permute-start | bytes 786440 | tf_op jit(solution)/shard_map/ppermute | solution.py:71
  12.5 19.4 %collective-permute-start = (bf16[2,128,1024]{2,1,0:T(8,128)(2,1)}, bf16[2,128,1024]{2,1,0:T(8,128)(2,1)S(1)}, u32[]{:S(2)}, u32[]{:S(2)}) collective-permute-start(bf16[2,128,1024]{2,1,0:T(8,128)(2,1)} %get-tuple-element.37), channel_id=1, source_target_pairs={{0,5},{1,4},{2,7},{3,6},{4,1},{5,0},{6,3},{7,2},{8,13},{9,12},{10,... | collective-permute-start | bytes 1572872 | tf_op jit(solution)/shard_map/ppermute | solution.py:65
  15.0 2.0 %copy-start = (bf16[2,128,512]{2,1,0:T(8,128)(2,1)}, bf16[2,128,512]{2,1,0:T(8,128)(2,1)S(1)}, u32[]{:S(2)}) copy-start(bf16[2,128,512]{2,1,0:T(8,128)(2,1)S(1)} %collective-permute-done.4.refs_2_) | copy-start | bytes 786436
  15.0 27.0 %collective-permute-start.1 = (bf16[2,128,1024]{2,1,0:T(8,128)(2,1)}, bf16[2,128,1024]{2,1,0:T(8,128)(2,1)}, u32[]{:S(2)}, u32[]{:S(2)}) collective-permute-start(bf16[2,128,1024]{2,1,0:T(8,128)(2,1)} %get-tuple-element.38), channel_id=1, source_target_pairs={{0,1},{1,0},{2,3},{3,2},{4,5},{5,4},{6,7},{7,6},{8,9},{9,8},{10,11... | collective-permute-start | bytes 1572872 | tf_op jit(solution)/shard_map/ppermute | solution.py:65
  15.5 1.5 %copy-start.2 = (bf16[2,128,512]{2,1,0:T(8,128)(2,1)}, bf16[2,128,512]{2,1,0:T(8,128)(2,1)S(1)}, u32[]{:S(2)}) copy-start(bf16[2,128,512]{2,1,0:T(8,128)(2,1)S(1)} %collective-permute-done.5.refs_3_) | copy-start | bytes 786436
  15.5 26.7 %collective-permute-start.2 = (bf16[2,128,1024]{2,1,0:T(8,128)(2,1)}, bf16[2,128,1024]{2,1,0:T(8,128)(2,1)}, u32[]{:S(2)}, u32[]{:S(2)}) collective-permute-start(bf16[2,128,1024]{2,1,0:T(8,128)(2,1)} %get-tuple-element.39), channel_id=1, source_target_pairs={{0,4},{1,5},{2,6},{3,7},{4,0},{5,1},{6,2},{7,3},{8,12},{9,13},{10,... | collective-permute-start | bytes 1572872 | tf_op jit(solution)/shard_map/ppermute | solution.py:65
  20.7 3.6 %copy-start.8 = (bf16[2,128,512]{2,1,0:T(8,128)(2,1)}, bf16[2,128,512]{2,1,0:T(8,128)(2,1)S(1)}, u32[]{:S(2)}) copy-start(bf16[2,128,512]{2,1,0:T(8,128)(2,1)S(1)} %collective-permute-done.3.refs_1_) | copy-start | bytes 786436
  20.7 3.6 %copy-start.1 = (bf16[2,128,512]{2,1,0:T(8,128)(2,1)S(1)}, bf16[2,128,512]{2,1,0:T(8,128)(2,1)}, u32[]{:S(2)}) copy-start(bf16[2,128,512]{2,1,0:T(8,128)(2,1)} %copy-done) | copy-start | bytes 786436
  20.7 3.6 %copy-start.3 = (bf16[2,128,512]{2,1,0:T(8,128)(2,1)S(1)}, bf16[2,128,512]{2,1,0:T(8,128)(2,1)}, u32[]{:S(2)}) copy-start(bf16[2,128,512]{2,1,0:T(8,128)(2,1)} %copy-done.2) | copy-start | bytes 786436
  20.7 21.6 %collective-permute-start.9 = (bf16[2,2,128,512]{3,2,1,0:T(8,128)(2,1)S(1)}, bf16[2,2,128,512]{3,2,1,0:T(8,128)(2,1)}, u32[]{:S(2)}, u32[]{:S(2)}) collective-permute-start(bf16[2,2,128,512]{3,2,1,0:T(8,128)(2,1)S(1)} %pad_maximum_fusion.2), channel_id=1, source_target_pairs={{0,8},{1,9},{2,10},{3,11},{4,12},{5,13},{6,14},{7,15},{8,16},{9,17... | collective-permute-start | bytes 1572872 | tf_op jit(solution)/shard_map/ppermute | solution.py:71
  22.7 1.6 %copy-start.9 = (bf16[2,128,512]{2,1,0:T(8,128)(2,1)}, bf16[2,128,512]{2,1,0:T(8,128)(2,1)S(1)}, u32[]{:S(2)}) copy-start(bf16[2,128,512]{2,1,0:T(8,128)(2,1)S(1)} %collective-permute-done.7.refs_0_) | copy-start | bytes 786436
  22.7 19.5 %collective-permute-start.8 = (bf16[2,128,512]{2,1,0:T(8,128)(2,1)S(1)}, bf16[2,128,512]{2,1,0:T(8,128)(2,1)S(1)}, u32[]{:S(2)}, u32[]{:S(2)}) collective-permute-start(bf16[2,128,512]{2,1,0:T(8,128)(2,1)S(1)} %collective-permute-done.3.refs_1_), channel_id=1, source_target_pairs={{0,8},{1,9},{2,10},{3,11},{4,12},{5,13},{6,14},{7,15},{8,16},{9,17... | collective-permute-start | bytes 786440 | tf_op jit(solution)/shard_map/ppermute | solution.py:71
  25.5 16.8 %copy-start.6 = (bf16[4,2,128,512]{3,2,1,0:T(8,128)(2,1)}, bf16[4,2,128,512]{3,2,1,0:T(8,128)(2,1)S(1)}, u32[]{:S(2)}) copy-start(bf16[4,2,128,512]{3,2,1,0:T(8,128)(2,1)S(1)} %pad_maximum_fusion.refs_4_) | copy-start | bytes 3145732
  31.9 10.4 %copy-start.10 = (bf16[2,128,1024]{2,1,0:T(8,128)(2,1)}, bf16[2,128,1024]{2,1,0:T(8,128)(2,1)S(1)}, u32[]{:S(2)}) copy-start(bf16[2,128,1024]{2,1,0:T(8,128)(2,1)S(1)} %collective-permute-done.refs_2_.refs_1_) | copy-start | bytes 1572868
  31.9 11.7 %collective-permute-start.6 = (bf16[4,2,128,512]{3,2,1,0:T(8,128)(2,1)S(1)}, bf16[4,2,128,512]{3,2,1,0:T(8,128)(2,1)}, u32[]{:S(2)}, u32[]{:S(2)}) collective-permute-start(bf16[4,2,128,512]{3,2,1,0:T(8,128)(2,1)S(1)} %pad_maximum_fusion.refs_4_), channel_id=1, source_target_pairs={{0,2},{1,3},{2,0},{3,1},{4,6},{5,7},{6,4},{7,5},{8,10},{9,11},{10,... | collective-permute-start | bytes 3145736 | tf_op jit(solution)/shard_map/ppermute | solution.py:68
  43.5 2.7 %copy-start.7 = (bf16[4,2,128,512]{3,2,1,0:T(8,128)(2,1)}, bf16[4,2,128,512]{3,2,1,0:T(8,128)(2,1)S(1)}, u32[]{:S(2)}) copy-start(bf16[4,2,128,512]{3,2,1,0:T(8,128)(2,1)S(1)} %pad_maximum_fusion.1.refs_6_) | copy-start | bytes 3145732
  43.5 2.7 %collective-permute-start.10 = (bf16[4,2,128,512]{3,2,1,0:T(8,128)(2,1)S(1)}, bf16[4,2,128,512]{3,2,1,0:T(8,128)(2,1)S(1)}, u32[]{:S(2)}, u32[]{:S(2)}) collective-permute-start(bf16[4,2,128,512]{3,2,1,0:T(8,128)(2,1)S(1)} %pad_maximum_fusion.1.refs_6_), channel_id=1, source_target_pairs={{0,2},{1,3},{2,0},{3,1},{4,6},{5,7},{6,4},{7,5},{8,10},{9,11},{10,... | collective-permute-start | bytes 3145736 | tf_op jit(solution)/shard_map/ppermute | solution.py:68
  46.2 1.0 copy-start.21
  61.3 1.6 %collective-permute-start.11 = (bf16[2,128,256]{2,1,0:T(8,128)(2,1)}, bf16[2,128,256]{2,1,0:T(8,128)(2,1)S(1)}, u32[]{:S(2)}, u32[]{:S(2)}) collective-permute-start(bf16[2,128,256]{2,1,0:T(8,128)(2,1)} %get-tuple-element.48), channel_id=1, source_target_pairs={{0,2},{1,3},{2,0},{3,1},{4,6},{5,7},{6,4},{7,5},{8,10},{9,11},{10,... | collective-permute-start | bytes 393224 | tf_op jit(solution)/shard_map/ppermute | solution.py:68
  61.5 1.6 %collective-permute-start.12 = (bf16[2,128,256]{2,1,0:T(8,128)(2,1)}, bf16[2,128,256]{2,1,0:T(8,128)(2,1)S(1)}, u32[]{:S(2)}, u32[]{:S(2)}) collective-permute-start(bf16[2,128,256]{2,1,0:T(8,128)(2,1)} %get-tuple-element.49), channel_id=1, source_target_pairs={{0,2},{1,3},{2,0},{3,1},{4,6},{5,7},{6,4},{7,5},{8,10},{9,11},{10,... | collective-permute-start | bytes 393224 | tf_op jit(solution)/shard_map/ppermute | solution.py:68
  61.9 1.6 %collective-permute-start.13 = (bf16[2,128,256]{2,1,0:T(8,128)(2,1)}, bf16[2,128,256]{2,1,0:T(8,128)(2,1)S(1)}, u32[]{:S(2)}, u32[]{:S(2)}) collective-permute-start(bf16[2,128,256]{2,1,0:T(8,128)(2,1)} %get-tuple-element.50), channel_id=1, source_target_pairs={{0,2},{1,3},{2,0},{3,1},{4,6},{5,7},{6,4},{7,5},{8,10},{9,11},{10,... | collective-permute-start | bytes 393224 | tf_op jit(solution)/shard_map/ppermute | solution.py:68
  62.0 1.6 %collective-permute-start.14 = (bf16[2,128,256]{2,1,0:T(8,128)(2,1)}, bf16[2,128,256]{2,1,0:T(8,128)(2,1)S(1)}, u32[]{:S(2)}, u32[]{:S(2)}) collective-permute-start(bf16[2,128,256]{2,1,0:T(8,128)(2,1)} %get-tuple-element.51), channel_id=1, source_target_pairs={{0,2},{1,3},{2,0},{3,1},{4,6},{5,7},{6,4},{7,5},{8,10},{9,11},{10,... | collective-permute-start | bytes 393224 | tf_op jit(solution)/shard_map/ppermute | solution.py:68
  64.8 19.7 %collective-permute-start.19 = (bf16[4,2,128,256]{3,2,1,0:T(8,128)(2,1)S(1)}, bf16[4,2,128,256]{3,2,1,0:T(8,128)(2,1)S(1)}, u32[]{:S(2)}, u32[]{:S(2)}) collective-permute-start(bf16[4,2,128,256]{3,2,1,0:T(8,128)(2,1)S(1)} %add_convert_fusion.1), channel_id=1, source_target_pairs={{0,24},{1,25},{2,26},{3,27},{4,28},{5,29},{6,30},{7,31},{8,0},{9,1... | collective-permute-start | bytes 1572872 | tf_op jit(solution)/shard_map/ppermute | solution.py:71
  83.4 1.9 %collective-permute-start.24 = (bf16[2,128,256]{2,1,0:T(8,128)(2,1)}, bf16[2,128,256]{2,1,0:T(8,128)(2,1)S(1)}, u32[]{:S(2)}, u32[]{:S(2)}) collective-permute-start(bf16[2,128,256]{2,1,0:T(8,128)(2,1)} %get-tuple-element.61), channel_id=1, source_target_pairs={{0,2},{1,3},{2,0},{3,1},{4,6},{5,7},{6,4},{7,5},{8,10},{9,11},{10,... | collective-permute-start | bytes 393224 | tf_op jit(solution)/shard_map/ppermute | solution.py:68
  83.5 1.9 %collective-permute-start.25 = (bf16[2,128,256]{2,1,0:T(8,128)(2,1)}, bf16[2,128,256]{2,1,0:T(8,128)(2,1)S(1)}, u32[]{:S(2)}, u32[]{:S(2)}) collective-permute-start(bf16[2,128,256]{2,1,0:T(8,128)(2,1)} %get-tuple-element.62), channel_id=1, source_target_pairs={{0,2},{1,3},{2,0},{3,1},{4,6},{5,7},{6,4},{7,5},{8,10},{9,11},{10,... | collective-permute-start | bytes 393224 | tf_op jit(solution)/shard_map/ppermute | solution.py:68
  84.0 1.6 %collective-permute-start.26 = (bf16[2,128,256]{2,1,0:T(8,128)(2,1)}, bf16[2,128,256]{2,1,0:T(8,128)(2,1)S(1)}, u32[]{:S(2)}, u32[]{:S(2)}) collective-permute-start(bf16[2,128,256]{2,1,0:T(8,128)(2,1)} %get-tuple-element.63), channel_id=1, source_target_pairs={{0,2},{1,3},{2,0},{3,1},{4,6},{5,7},{6,4},{7,5},{8,10},{9,11},{10,... | collective-permute-start | bytes 393224 | tf_op jit(solution)/shard_map/ppermute | solution.py:68
  84.0 1.7 %collective-permute-start.27 = (bf16[2,128,256]{2,1,0:T(8,128)(2,1)}, bf16[2,128,256]{2,1,0:T(8,128)(2,1)S(1)}, u32[]{:S(2)}, u32[]{:S(2)}) collective-permute-start(bf16[2,128,256]{2,1,0:T(8,128)(2,1)} %get-tuple-element.64), channel_id=1, source_target_pairs={{0,2},{1,3},{2,0},{3,1},{4,6},{5,7},{6,4},{7,5},{8,10},{9,11},{10,... | collective-permute-start | bytes 393224 | tf_op jit(solution)/shard_map/ppermute | solution.py:68
  84.5 0.8 copy-start.4
  84.5 5.4 %collective-permute-start.18 = (bf16[4,2,128,256]{3,2,1,0:T(8,128)(2,1)}, bf16[4,2,128,256]{3,2,1,0:T(8,128)(2,1)S(1)}, u32[]{:S(2)}, u32[]{:S(2)}) collective-permute-start(bf16[4,2,128,256]{3,2,1,0:T(8,128)(2,1)} %get-tuple-element.57), channel_id=1, source_target_pairs={{0,2},{1,3},{2,0},{3,1},{4,6},{5,7},{6,4},{7,5},{8,10},{9,11},{10,... | collective-permute-start | bytes 1572872 | tf_op jit(solution)/shard_map/ppermute | solution.py:68
  85.3 7.7 %collective-permute-start.23 = (bf16[4,2,128,256]{3,2,1,0:T(8,128)(2,1)}, bf16[4,2,128,256]{3,2,1,0:T(8,128)(2,1)S(1)}, u32[]{:S(2)}, u32[]{:S(2)}) collective-permute-start(bf16[4,2,128,256]{3,2,1,0:T(8,128)(2,1)} %get-tuple-element.59), channel_id=1, source_target_pairs={{0,2},{1,3},{2,0},{3,1},{4,6},{5,7},{6,4},{7,5},{8,10},{9,11},{10,... | collective-permute-start | bytes 1572872 | tf_op jit(solution)/shard_map/ppermute | solution.py:68
  86.9 14.2 %collective-permute-start.28 = (bf16[4,2,128,256]{3,2,1,0:T(8,128)(2,1)S(1)}, bf16[4,2,128,256]{3,2,1,0:T(8,128)(2,1)S(1)}, u32[]{:S(2)}, u32[]{:S(2)}) collective-permute-start(bf16[4,2,128,256]{3,2,1,0:T(8,128)(2,1)S(1)} %add_convert_fusion), channel_id=1, source_target_pairs={{0,24},{1,25},{2,26},{3,27},{4,28},{5,29},{6,30},{7,31},{8,0},{9,1... | collective-permute-start | bytes 1572872 | tf_op jit(solution)/shard_map/ppermute | solution.py:71
  87.4 15.6 %collective-permute-start.15 = (bf16[2,128,512]{2,1,0:T(8,128)(2,1)}, bf16[2,128,512]{2,1,0:T(8,128)(2,1)S(1)}, u32[]{:S(2)}, u32[]{:S(2)}) collective-permute-start(bf16[2,128,512]{2,1,0:T(8,128)(2,1)} %get-tuple-element.52), channel_id=1, source_target_pairs={{0,4},{1,5},{2,6},{3,7},{4,0},{5,1},{6,2},{7,3},{8,12},{9,13},{10,... | collective-permute-start | bytes 786440 | tf_op jit(solution)/shard_map/ppermute | solution.py:65
  88.9 16.9 %collective-permute-start.16 = (bf16[2,128,512]{2,1,0:T(8,128)(2,1)}, bf16[2,128,512]{2,1,0:T(8,128)(2,1)S(1)}, u32[]{:S(2)}, u32[]{:S(2)}) collective-permute-start(bf16[2,128,512]{2,1,0:T(8,128)(2,1)} %get-tuple-element.53), channel_id=1, source_target_pairs={{0,1},{1,0},{2,3},{3,2},{4,5},{5,4},{6,7},{7,6},{8,9},{9,8},{10,11... | collective-permute-start | bytes 786440 | tf_op jit(solution)/shard_map/ppermute | solution.py:65
  89.9 1.1 copy-start.5
  89.9 12.2 %copy-start.11 = (bf16[4,2,128,256]{3,2,1,0:T(8,128)(2,1)S(1)}, bf16[4,2,128,256]{3,2,1,0:T(8,128)(2,1)}, u32[]{:S(2)}) copy-start(bf16[4,2,128,256]{3,2,1,0:T(8,128)(2,1)} %get-tuple-element.58) | copy-start | bytes 1572868
  89.9 16.9 %collective-permute-start.17 = (bf16[2,128,512]{2,1,0:T(8,128)(2,1)}, bf16[2,128,512]{2,1,0:T(8,128)(2,1)S(1)}, u32[]{:S(2)}, u32[]{:S(2)}) collective-permute-start(bf16[2,128,512]{2,1,0:T(8,128)(2,1)} %get-tuple-element.54), channel_id=1, source_target_pairs={{0,5},{1,4},{2,7},{3,6},{4,1},{5,0},{6,3},{7,2},{8,13},{9,12},{10,... | collective-permute-start | bytes 786440 | tf_op jit(solution)/shard_map/ppermute | solution.py:65
  93.0 14.2 %collective-permute-start.22 = (bf16[2,128,256]{2,1,0:T(8,128)(2,1)S(1)}, bf16[2,128,256]{2,1,0:T(8,128)(2,1)S(1)}, u32[]{:S(2)}, u32[]{:S(2)}) collective-permute-start(bf16[2,128,256]{2,1,0:T(8,128)(2,1)S(1)} %get-tuple-element.72), channel_id=1, source_target_pairs={{0,5},{1,4},{2,7},{3,6},{4,1},{5,0},{6,3},{7,2},{8,13},{9,12},{10,... | collective-permute-start | bytes 393224 | tf_op jit(solution)/shard_map/ppermute | solution.py:65
  101.1 10.6 %collective-permute-start.21 = (bf16[2,128,256]{2,1,0:T(8,128)(2,1)}, bf16[2,128,256]{2,1,0:T(8,128)(2,1)S(1)}, u32[]{:S(2)}, u32[]{:S(2)}) collective-permute-start(bf16[2,128,256]{2,1,0:T(8,128)(2,1)} %get-tuple-element.73), channel_id=1, source_target_pairs={{0,1},{1,0},{2,3},{3,2},{4,5},{5,4},{6,7},{7,6},{8,9},{9,8},{10,11... | collective-permute-start | bytes 393224 | tf_op jit(solution)/shard_map/ppermute | solution.py:65
  102.9 6.4 %copy-start.12 = (bf16[2,128,512]{2,1,0:T(8,128)(2,1)}, bf16[2,128,512]{2,1,0:T(8,128)(2,1)S(1)}, u32[]{:S(2)}) copy-start(bf16[2,128,512]{2,1,0:T(8,128)(2,1)S(1)} %collective-permute-done.15.refs_0_) | copy-start | bytes 786436
  102.9 8.7 %collective-permute-start.20 = (bf16[2,128,256]{2,1,0:T(8,128)(2,1)S(1)}, bf16[2,128,256]{2,1,0:T(8,128)(2,1)S(1)}, u32[]{:S(2)}, u32[]{:S(2)}) collective-permute-start(bf16[2,128,256]{2,1,0:T(8,128)(2,1)S(1)} %get-tuple-element.74), channel_id=1, source_target_pairs={{0,4},{1,5},{2,6},{3,7},{4,0},{5,1},{6,2},{7,3},{8,12},{9,13},{10,... | collective-permute-start | bytes 393224 | tf_op jit(solution)/shard_map/ppermute | solution.py:65
  105.8 3.5 %copy-start.13 = (bf16[2,128,512]{2,1,0:T(8,128)(2,1)}, bf16[2,128,512]{2,1,0:T(8,128)(2,1)S(1)}, u32[]{:S(2)}) copy-start(bf16[2,128,512]{2,1,0:T(8,128)(2,1)S(1)} %collective-permute-done.16.refs_1_) | copy-start | bytes 786436
  105.8 6.8 %collective-permute-start.31 = (bf16[2,128,256]{2,1,0:T(8,128)(2,1)S(1)}, bf16[2,128,256]{2,1,0:T(8,128)(2,1)S(1)}, u32[]{:S(2)}, u32[]{:S(2)}) collective-permute-start(bf16[2,128,256]{2,1,0:T(8,128)(2,1)S(1)} %get-tuple-element.68), channel_id=1, source_target_pairs={{0,5},{1,4},{2,7},{3,6},{4,1},{5,0},{6,3},{7,2},{8,13},{9,12},{10,... | collective-permute-start | bytes 393224 | tf_op jit(solution)/shard_map/ppermute | solution.py:65
  106.8 2.5 %copy-start.14 = (bf16[2,128,512]{2,1,0:T(8,128)(2,1)}, bf16[2,128,512]{2,1,0:T(8,128)(2,1)S(1)}, u32[]{:S(2)}) copy-start(bf16[2,128,512]{2,1,0:T(8,128)(2,1)S(1)} %collective-permute-done.17.refs_2_) | copy-start | bytes 786436
  106.8 7.1 %collective-permute-start.30 = (bf16[2,128,256]{2,1,0:T(8,128)(2,1)S(1)}, bf16[2,128,256]{2,1,0:T(8,128)(2,1)S(1)}, u32[]{:S(2)}, u32[]{:S(2)}) collective-permute-start(bf16[2,128,256]{2,1,0:T(8,128)(2,1)S(1)} %get-tuple-element.69), channel_id=1, source_target_pairs={{0,1},{1,0},{2,3},{3,2},{4,5},{5,4},{6,7},{7,6},{8,9},{9,8},{10,11... | collective-permute-start | bytes 393224 | tf_op jit(solution)/shard_map/ppermute | solution.py:65
  107.2 4.5 %copy-start.15 = (bf16[2,128,256]{2,1,0:T(8,128)(2,1)}, bf16[2,128,256]{2,1,0:T(8,128)(2,1)S(1)}, u32[]{:S(2)}) copy-start(bf16[2,128,256]{2,1,0:T(8,128)(2,1)S(1)} %collective-permute-done.22.refs_2_) | copy-start | bytes 393220
  107.2 6.8 %collective-permute-start.29 = (bf16[2,128,256]{2,1,0:T(8,128)(2,1)S(1)}, bf16[2,128,256]{2,1,0:T(8,128)(2,1)S(1)}, u32[]{:S(2)}, u32[]{:S(2)}) collective-permute-start(bf16[2,128,256]{2,1,0:T(8,128)(2,1)S(1)} %get-tuple-element.70), channel_id=1, source_target_pairs={{0,4},{1,5},{2,6},{3,7},{4,0},{5,1},{6,2},{7,3},{8,12},{9,13},{10,... | collective-permute-start | bytes 393224 | tf_op jit(solution)/shard_map/ppermute | solution.py:65
  111.7 2.3 %copy-start.16 = (bf16[2,128,256]{2,1,0:T(8,128)(2,1)}, bf16[2,128,256]{2,1,0:T(8,128)(2,1)S(1)}, u32[]{:S(2)}) copy-start(bf16[2,128,256]{2,1,0:T(8,128)(2,1)S(1)} %collective-permute-done.21.refs_1_) | copy-start | bytes 393220
  111.7 2.2 %copy-start.17 = (bf16[2,128,256]{2,1,0:T(8,128)(2,1)}, bf16[2,128,256]{2,1,0:T(8,128)(2,1)S(1)}, u32[]{:S(2)}) copy-start(bf16[2,128,256]{2,1,0:T(8,128)(2,1)S(1)} %collective-permute-done.20.refs_0_) | copy-start | bytes 393220
  112.6 1.3 %copy-start.18 = (bf16[2,128,256]{2,1,0:T(8,128)(2,1)}, bf16[2,128,256]{2,1,0:T(8,128)(2,1)S(1)}, u32[]{:S(2)}) copy-start(bf16[2,128,256]{2,1,0:T(8,128)(2,1)S(1)} %collective-permute-done.31.refs_6_) | copy-start | bytes 393220
  113.9 0.6 copy-start.19
  113.9 0.7 copy-start.20

commit v6 on v5

--- a/solution.py
+++ b/solution.py
@@ -235,14 +235,16 @@
                     key_rows(v_s, tile), grads, (((1,), (1,)), ((), ())), preferred_element_type=jnp.float32
                 )
                 total = total + jnp.sum(raised, axis=0, keepdims=True)
-                delta = delta + jnp.sum(raised * prob_grad, axis=0, keepdims=True)
                 score_s[tile_rows(tile), :] = raised
                 prob_grad_s[tile_rows(tile), :] = prob_grad
             inverse = 1.0 / total
-            delta = delta * inverse
+            for tile in range(tiles):
+                rounded = (score_s[tile_rows(tile), :] * inverse).astype(jnp.bfloat16)
+                prob_s[tile_rows(tile), :] = rounded
+                product = rounded.astype(jnp.float32) * prob_grad_s[tile_rows(tile), :]
+                delta = delta + jnp.sum(product, axis=0, keepdims=True)
             for tile in range(tiles):
                 probs = score_s[tile_rows(tile), :] * inverse
-                prob_s[tile_rows(tile), :] = probs.astype(jnp.bfloat16)
                 grad_scores = probs * (prob_grad_s[tile_rows(tile), :] - delta) * attn_scale
                 grad_s[tile_rows(tile), :] = grad_scores.astype(jnp.bfloat16)
             at = pl.ds(key_at, tiles * tp)

time: 118 us -> 118 us (level)
  no operation moved by 1% of the time
where the time goes in v6:
time: 118 us
  Pallas kernels  39.2 us (33%)
  waiting for transfers between devices  34.5 us (29%)
  starting transfers between devices  32.6 us (28%)
  other arithmetic  7.63 us (6%)
  local copies, waits for them, and re-layouts  3.02 us (3%)
    pallas_call x2, Pallas kernels, backward(): pl.pallas_call(kernel, out_shape=[jax.ShapeDtypeStruct((chunk + 1, plan.r...  29.2 us
    ppermute x15, waiting for transfers between devices, to_group(): lax.ppermute(value, AXES, self.routes(lambda slab, core, group: (slab, co...  24 us
    ppermute x15, starting transfers between devices, to_group(): lax.ppermute(value, AXES, self.routes(lambda slab, core, group: (slab, co...  20.5 us
    ppermute x5, starting transfers between devices, to_slab(): lax.ppermute(value, AXES, self.routes(lambda slab, core, group: (slab + s...  9.78 us
    ppermute x5, waiting for transfers between devices, to_slab(): lax.ppermute(value, AXES, self.routes(lambda slab, core, group: (slab + s...  6.24 us
    pallas_call x2, Pallas kernels, split_columns(): pl.pallas_call(kernel, out_shape=[shape] * count, in_specs=[ANY] * (len(a...  5.27 us
    convert_element_type x4, other arithmetic, add_up(): return total.astype(jnp.bfloat16)  5.2 us
    pallas_call x2, Pallas kernels, join_columns(): pl.pallas_call(kernel, out_shape=[jax.ShapeDtypeStruct((plan.rows, width...  4.67 us
  transfers between devices with their start and end apart: 32, of which 15 were waited for; matrix products, arithmetic and copies ran while one was open for 6% of the time, Pallas kernels for 17%

profile of v6, /device:TPU:0, one launch (start us, length us, event | category | flops | bytes accessed | tf_op | source)
XLA Modules:
  0.0 118.0 jit_solution(7526722033494073307)
XLA Ops:
  0.6 2.4 %split_keys.1 = (bf16[2,128,512]{2,1,0:T(8,128)(2,1)}, bf16[2,128,512]{2,1,0:T(8,128)(2,1)}, bf16[2,128,512]{2,1,0:T(8,128)(2,1)}, bf16[2,128,512]{2,1,0:T(8,128)(2,1)}) custom-call(bf16[128,2048]{1,0:T(8,128)(2,1)} %refs_0_.2, bf16[128,2048]{1,0:T(8,128)(2,1)} %refs_1_.2), custom_call_target="tpu_custom_call" | custom-call | bytes 2097152 | tf_op jit(solution)/shard_map/split_keys/pallas_call | solution.py:111
  3.0 3.0 %collective-permute-start.4 = (bf16[2,128,512]{2,1,0:T(8,128)(2,1)}, bf16[2,128,512]{2,1,0:T(8,128)(2,1)S(1)}, u32[]{:S(2)}, u32[]{:S(2)}) collective-permute-start(bf16[2,128,512]{2,1,0:T(8,128)(2,1)} %get-tuple-element.41), channel_id=1, source_target_pairs={{0,1},{1,0},{2,3},{3,2},{4,5},{5,4},{6,7},{7,6},{8,9},{9,8},{10,11... | collective-permute-start | bytes 786440 | tf_op jit(solution)/shard_map/ppermute | solution.py:65
  6.0 1.5 %collective-permute-start.5 = (bf16[2,128,512]{2,1,0:T(8,128)(2,1)}, bf16[2,128,512]{2,1,0:T(8,128)(2,1)S(1)}, u32[]{:S(2)}, u32[]{:S(2)}) collective-permute-start(bf16[2,128,512]{2,1,0:T(8,128)(2,1)} %get-tuple-element.42), channel_id=1, source_target_pairs={{0,4},{1,5},{2,6},{3,7},{4,0},{5,1},{6,2},{7,3},{8,12},{9,13},{10,... | collective-permute-start | bytes 786440 | tf_op jit(solution)/shard_map/ppermute | solution.py:65
  7.5 0.0 collective-permute-start.3
  7.6 2.0 %collective-permute-start.7 = (bf16[2,128,512]{2,1,0:T(8,128)(2,1)}, bf16[2,128,512]{2,1,0:T(8,128)(2,1)S(1)}, u32[]{:S(2)}, u32[]{:S(2)}) collective-permute-start(bf16[2,128,512]{2,1,0:T(8,128)(2,1)} %get-tuple-element.35.refs_2_.refs_0_), channel_id=1, source_target_pairs={{0,8},{1,9},{2,10},{3,11},{4,12},{5,13},{6,14},{7,15},{8,16},{9,17... | collective-permute-start | bytes 786440 | tf_op jit(solution)/shard_map/ppermute | solution.py:71
  9.6 2.9 %split_queries.1 = (bf16[2,128,1024]{2,1,0:T(8,128)(2,1)}, bf16[2,128,1024]{2,1,0:T(8,128)(2,1)}, bf16[2,128,1024]{2,1,0:T(8,128)(2,1)}, bf16[2,128,1024]{2,1,0:T(8,128)(2,1)}) custom-call(bf16[128,4096]{1,0:T(8,128)(2,1)} %refs_0_.3, bf16[128,4096]{1,0:T(8,128)(2,1)} %refs_1_.3, bf16[2,128,512]{2,1,0:T(8,128)(2,1)} %get-tuple-element.35.refs_2_.refs_0_), custom_call_target="tpu_custom_call" | custom-call | bytes 4194304 | tf_op jit(solution)/shard_map/split_queries/pallas_call | solution.py:111
  12.5 2.5 %collective-permute-start = (bf16[2,128,1024]{2,1,0:T(8,128)(2,1)}, bf16[2,128,1024]{2,1,0:T(8,128)(2,1)S(1)}, u32[]{:S(2)}, u32[]{:S(2)}) collective-permute-start(bf16[2,128,1024]{2,1,0:T(8,128)(2,1)} %get-tuple-element.37), channel_id=1, source_target_pairs={{0,5},{1,4},{2,7},{3,6},{4,1},{5,0},{6,3},{7,2},{8,13},{9,12},{10,... | collective-permute-start | bytes 1572872 | tf_op jit(solution)/shard_map/ppermute | solution.py:65
  15.0 0.5 collective-permute-start.1
  15.5 1.4 %collective-permute-start.2 = (bf16[2,128,1024]{2,1,0:T(8,128)(2,1)}, bf16[2,128,1024]{2,1,0:T(8,128)(2,1)}, u32[]{:S(2)}, u32[]{:S(2)}) collective-permute-start(bf16[2,128,1024]{2,1,0:T(8,128)(2,1)} %get-tuple-element.39), channel_id=1, source_target_pairs={{0,4},{1,5},{2,6},{3,7},{4,0},{5,1},{6,2},{7,3},{8,12},{9,13},{10,... | collective-permute-start | bytes 1572872 | tf_op jit(solution)/shard_map/ppermute | solution.py:65
  17.0 0.1 pad_maximum_fusion.2
  17.1 3.6 %collective-permute-done.3.refs_1_ = bf16[2,128,512]{2,1,0:T(8,128)(2,1)S(1)} collective-permute-done((bf16[2,128,512]{2,1,0:T(8,128)(2,1)}, bf16[2,128,512]{2,1,0:T(8,128)(2,1)S(1)}, u32[]{:S(2)}, u32[]{:S(2)}) %collective-permute-start.3) | collective-permute-done | bytes 262176 | tf_op jit(solution)/shard_map/ppermute | solution.py:65
  20.7 2.0 %collective-permute-start.9 = (bf16[2,2,128,512]{3,2,1,0:T(8,128)(2,1)S(1)}, bf16[2,2,128,512]{3,2,1,0:T(8,128)(2,1)}, u32[]{:S(2)}, u32[]{:S(2)}) collective-permute-start(bf16[2,2,128,512]{3,2,1,0:T(8,128)(2,1)S(1)} %pad_maximum_fusion.2), channel_id=1, source_target_pairs={{0,8},{1,9},{2,10},{3,11},{4,12},{5,13},{6,14},{7,15},{8,16},{9,17... | collective-permute-start | bytes 1572872 | tf_op jit(solution)/shard_map/ppermute | solution.py:71
  22.7 1.6 %collective-permute-start.8 = (bf16[2,128,512]{2,1,0:T(8,128)(2,1)S(1)}, bf16[2,128,512]{2,1,0:T(8,128)(2,1)S(1)}, u32[]{:S(2)}, u32[]{:S(2)}) collective-permute-start(bf16[2,128,512]{2,1,0:T(8,128)(2,1)S(1)} %collective-permute-done.3.refs_1_), channel_id=1, source_target_pairs={{0,8},{1,9},{2,10},{3,11},{4,12},{5,13},{6,14},{7,15},{8,16},{9,17... | collective-permute-start | bytes 786440 | tf_op jit(solution)/shard_map/ppermute | solution.py:71
  24.3 1.2 pad_maximum_fusion.refs_4_
  25.5 6.3 %collective-permute-done.refs_2_.refs_1_ = bf16[2,128,1024]{2,1,0:T(8,128)(2,1)S(1)} collective-permute-done((bf16[2,128,1024]{2,1,0:T(8,128)(2,1)}, bf16[2,128,1024]{2,1,0:T(8,128)(2,1)S(1)}, u32[]{:S(2)}, u32[]{:S(2)}) %collective-permute-start) | collective-permute-done | bytes 524320 | tf_op jit(solution)/shard_map/ppermute | solution.py:65
  31.9 10.1 %collective-permute-done.1.refs_3_.refs_2_ = bf16[2,128,1024]{2,1,0:T(8,128)(2,1)} collective-permute-done((bf16[2,128,1024]{2,1,0:T(8,128)(2,1)}, bf16[2,128,1024]{2,1,0:T(8,128)(2,1)}, u32[]{:S(2)}, u32[]{:S(2)}) %collective-permute-start.1) | collective-permute-done | bytes 524320 | tf_op jit(solution)/shard_map/ppermute | solution.py:65
  42.0 0.2 collective-permute-done.2.refs_4_.refs_3_
  42.3 1.2 %pad_maximum_fusion.1.refs_6_ = bf16[4,2,128,512]{3,2,1,0:T(8,128)(2,1)S(1)} fusion(bf16[2,2,128,512]{3,2,1,0:T(8,128)(2,1)} %collective-permute-done.9, bf16[1,2,128,512]{3,2,1,0:T(8,128)(2,1)S(1)} %bitcast.39, bf16[1,2,128,512]{3,2,1,0:T(8,128)(2,1)} %bitcast.37), kind=kLoop, calls=%fused_computation.1 | loop fusion | flops 1048576 | bytes 2097152 | tf_op jit(solution)/shard_map/stack | solution.py:389
  43.5 0.1 collective-permute-start.10
  43.6 2.6 %collective-permute-done.10.refs_7_ = bf16[4,2,128,512]{3,2,1,0:T(8,128)(2,1)S(1)} collective-permute-done((bf16[4,2,128,512]{3,2,1,0:T(8,128)(2,1)S(1)}, bf16[4,2,128,512]{3,2,1,0:T(8,128)(2,1)S(1)}, u32[]{:S(2)}, u32[]{:S(2)}) %collective-permute-start.10) | collective-permute-done | bytes 1048608 | tf_op jit(solution)/shard_map/ppermute | solution.py:68
  46.2 1.0 copy-done.21
  47.2 14.5 %backward.2 = (bf16[1,128,512]{2,1,0:T(8,128)(2,1)}, bf16[1,128,512]{2,1,0:T(8,128)(2,1)}, bf16[1,128,512]{2,1,0:T(8,128)(2,1)}, bf16[1,128,512]{2,1,0:T(8,128)(...) custom-call(s32[4]{0:T(128)} %docs.3, ...), custom_call_target="tpu_custom_call" | custom-call | flops 53687091200 | bytes 6291456 | tf_op jit(solution)/shard_map/backward/pallas_call | solution.py:297
  61.8 0.2 collective-permute-start.11
  62.0 0.4 collective-permute-start.12
  62.3 0.3 collective-permute-start.13
  62.6 0.3 collective-permute-start.14
  62.9 0.5 collective-permute-done.11
  63.4 0.3 collective-permute-done.12
  63.6 0.3 collective-permute-done.13
  63.9 0.3 collective-permute-done.14
  64.2 1.2 add_convert_fusion.1
  65.3 3.7 %collective-permute-start.19 = (bf16[4,2,128,256]{3,2,1,0:T(8,128)(2,1)S(1)}, bf16[4,2,128,256]{3,2,1,0:T(8,128)(2,1)S(1)}, u32[]{:S(2)}, u32[]{:S(2)}) collective-permute-start(bf16[4,2,128,256]{3,2,1,0:T(8,128)(2,1)S(1)} %add_convert_fusion.1), channel_id=1, source_target_pairs={{0,24},{1,25},{2,26},{3,27},{4,28},{5,29},{6,30},{7,31},{8,0},{9,1... | collective-permute-start | bytes 1572872 | tf_op jit(solution)/shard_map/ppermute | solution.py:71
  69.0 0.6 slice.103.refs_12_
  69.6 14.7 %backward.3 = (bf16[2,128,512]{2,1,0:T(8,128)(2,1)}, bf16[2,128,512]{2,1,0:T(8,128)(2,1)}, bf16[2,128,512]{2,1,0:T(8,128)(2,1)}, bf16[2,128,512]{2,1,0:T(8,128)(...) custom-call(s32[4]{0:T(128)} %docs.3, ...), custom_call_target="tpu_custom_call" | custom-call | flops 53687091200 | bytes 6291456 | tf_op jit(solution)/shard_map/backward/pallas_call | solution.py:297
  84.3 0.1 collective-permute-start.24
  84.3 0.5 collective-permute-start.25
  84.8 0.1 collective-permute-start.26
  84.9 0.4 collective-permute-start.27
  85.4 0.1 collective-permute-start.18
  85.4 0.7 copy-done.4
  86.1 0.1 collective-permute-start.23
  86.2 0.2 collective-permute-done.26
  86.4 0.2 collective-permute-done.27
  86.6 1.2 add_convert_fusion
  87.8 0.5 collective-permute-start.28
  88.2 1.5 %collective-permute-start.15 = (bf16[2,128,512]{2,1,0:T(8,128)(2,1)}, bf16[2,128,512]{2,1,0:T(8,128)(2,1)S(1)}, u32[]{:S(2)}, u32[]{:S(2)}) collective-permute-start(bf16[2,128,512]{2,1,0:T(8,128)(2,1)} %get-tuple-element.52), channel_id=1, source_target_pairs={{0,4},{1,5},{2,6},{3,7},{4,0},{5,1},{6,2},{7,3},{8,12},{9,13},{10,... | collective-permute-start | bytes 786440 | tf_op jit(solution)/shard_map/ppermute | solution.py:65
  89.8 1.0 collective-permute-start.16
  90.7 1.1 collective-permute-start.17
  91.8 2.0 %fusion.3 = (bf16[2,128,256]{2,1,0:T(8,128)(2,1)}, bf16[2,128,256]{2,1,0:T(8,128)(2,1)S(1)}, bf16[2,128,256]{2,1,0:T(8,128)(2,1)}, bf16[2,128,256]{2,1,0:T(8,128)(2,1)S(1)}) fusion(bf16[4,2,128,256]{3,2,1,0:T(8,128)(2,1)S(1)} %copy-done.5, bf16[4,2,128,256]{3,2,1,0:T(8,128)(2,1)S(1)} %collective-permute-done.18, bf16[4,2,128,256]{3,2,1,0:T(8,128)(2,1)} %ordered.6), kind=kLoop, calls=%fused_computation.16 | loop fusion | flops 1572864 | bytes 2097152 | tf_op jit(solution)/shard_map/convert_element_type | solution.py:334
  93.8 1.9 %collective-permute-start.22 = (bf16[2,128,256]{2,1,0:T(8,128)(2,1)S(1)}, bf16[2,128,256]{2,1,0:T(8,128)(2,1)S(1)}, u32[]{:S(2)}, u32[]{:S(2)}) collective-permute-start(bf16[2,128,256]{2,1,0:T(8,128)(2,1)S(1)} %get-tuple-element.72), channel_id=1, source_target_pairs={{0,5},{1,4},{2,7},{3,6},{4,1},{5,0},{6,3},{7,2},{8,13},{9,12},{10,... | collective-permute-start | bytes 393224 | tf_op jit(solution)/shard_map/ppermute | solution.py:65
  95.7 6.2 %collective-permute-done.28 = bf16[4,2,128,256]{3,2,1,0:T(8,128)(2,1)S(1)} collective-permute-done((bf16[4,2,128,256]{3,2,1,0:T(8,128)(2,1)S(1)}, bf16[4,2,128,256]{3,2,1,0:T(8,128)(2,1)S(1)}, u32[]{:S(2)}, u32[]{:S(2)}) %collective-permute-start.28) | collective-permute-done | bytes 524320 | tf_op jit(solution)/shard_map/ppermute | solution.py:71
  102.0 1.0 collective-permute-start.21
  102.9 0.9 fusion.7
  103.8 1.5 %collective-permute-start.20 = (bf16[2,128,256]{2,1,0:T(8,128)(2,1)S(1)}, bf16[2,128,256]{2,1,0:T(8,128)(2,1)S(1)}, u32[]{:S(2)}, u32[]{:S(2)}) collective-permute-start(bf16[2,128,256]{2,1,0:T(8,128)(2,1)S(1)} %get-tuple-element.74), channel_id=1, source_target_pairs={{0,4},{1,5},{2,6},{3,7},{4,0},{5,1},{6,2},{7,3},{8,12},{9,13},{10,... | collective-permute-start | bytes 393224 | tf_op jit(solution)/shard_map/ppermute | solution.py:65
  105.3 1.4 %collective-permute-done.16.refs_1_ = bf16[2,128,512]{2,1,0:T(8,128)(2,1)S(1)} collective-permute-done((bf16[2,128,512]{2,1,0:T(8,128)(2,1)}, bf16[2,128,512]{2,1,0:T(8,128)(2,1)S(1)}, u32[]{:S(2)}, u32[]{:S(2)}) %collective-permute-start.16) | collective-permute-done | bytes 262176 | tf_op jit(solution)/shard_map/ppermute | solution.py:65
  106.7 1.0 collective-permute-start.31
  107.7 0.3 collective-permute-start.30
  108.0 2.1 %collective-permute-start.29 = (bf16[2,128,256]{2,1,0:T(8,128)(2,1)S(1)}, bf16[2,128,256]{2,1,0:T(8,128)(2,1)S(1)}, u32[]{:S(2)}, u32[]{:S(2)}) collective-permute-start(bf16[2,128,256]{2,1,0:T(8,128)(2,1)S(1)} %get-tuple-element.70), channel_id=1, source_target_pairs={{0,4},{1,5},{2,6},{3,7},{4,0},{5,1},{6,2},{7,3},{8,12},{9,13},{10,... | collective-permute-start | bytes 393224 | tf_op jit(solution)/shard_map/ppermute | solution.py:65
  110.2 2.3 %join_queries.1 = bf16[128,4096]{1,0:T(8,128)(2,1)} custom-call(bf16[2,128,512]{2,1,0:T(8,128)(2,1)} %copy-done.12, bf16[2,128,512]{2,1,0:T(8,128)(2,1)} %copy-done.13, bf16[2,128,512]{2,1,0:T(8,128)(2,1)} %copy-done.14, bf16[2,128,512]{2,1,0:T(8,128)(2,1)} %get-tuple-element.55.refs_3_.refs_1_), custom_call_target="tpu_custom_call" | custom-call | bytes 2097152 | tf_op jit(solution)/shard_map/join_queries/pallas_call | solution.py:359
  112.6 0.9 collective-permute-done.31.refs_6_
  113.5 1.3 %collective-permute-done.30.refs_5_ = bf16[2,128,256]{2,1,0:T(8,128)(2,1)S(1)} collective-permute-done((bf16[2,128,256]{2,1,0:T(8,128)(2,1)S(1)}, bf16[2,128,256]{2,1,0:T(8,128)(2,1)S(1)}, u32[]{:S(2)}, u32[]{:S(2)}) %collective-permute-start.30) | collective-permute-done | bytes 131104 | tf_op jit(solution)/shard_map/ppermute | solution.py:65
  114.8 0.6 copy-done.19
  115.4 0.1 copy-done.20
  115.5 2.3 %join_keys.1 = (bf16[128,2048]{1,0:T(8,128)(2,1)}, bf16[128,2048]{1,0:T(8,128)(2,1)}) custom-call(bf16[2,128,256]{2,1,0:T(8,128)(2,1)} %copy-done.17, bf16[2,128,256]{2,1,0:T(8,128)(2,1)} %copy-done.16, bf16[2,128,256]{2,1,0:T(8,128)(2,1)} %copy-done.15, bf16[2,128,256]{2,1,0:T(8,128)(2,1)} %get-tuple-element.71.refs_3_, bf16[2,128,256]{2,1,0:T(8,128)(2,1)} %copy-done.20, ...), custom_call_target="tpu_custom_call" | custom-call | bytes 2097152 | tf_op jit(solution)/shard_map/join_keys/pallas_call | solution.py:359
  (62 shorter events, 0.1 us)
Async XLA Ops:
  3.0 12.0 %collective-permute-start.4 = (bf16[2,128,512]{2,1,0:T(8,128)(2,1)}, bf16[2,128,512]{2,1,0:T(8,128)(2,1)S(1)}, u32[]{:S(2)}, u32[]{:S(2)}) collective-permute-start(bf16[2,128,512]{2,1,0:T(8,128)(2,1)} %get-tuple-element.41), channel_id=1, source_target_pairs={{0,1},{1,0},{2,3},{3,2},{4,5},{5,4},{6,7},{7,6},{8,9},{9,8},{10,11... | collective-permute-start | bytes 786440 | tf_op jit(solution)/shard_map/ppermute | solution.py:65
  6.0 9.5 %collective-permute-start.5 = (bf16[2,128,512]{2,1,0:T(8,128)(2,1)}, bf16[2,128,512]{2,1,0:T(8,128)(2,1)S(1)}, u32[]{:S(2)}, u32[]{:S(2)}) collective-permute-start(bf16[2,128,512]{2,1,0:T(8,128)(2,1)} %get-tuple-element.42), channel_id=1, source_target_pairs={{0,4},{1,5},{2,6},{3,7},{4,0},{5,1},{6,2},{7,3},{8,12},{9,13},{10,... | collective-permute-start | bytes 786440 | tf_op jit(solution)/shard_map/ppermute | solution.py:65
  7.5 13.1 %collective-permute-start.3 = (bf16[2,128,512]{2,1,0:T(8,128)(2,1)}, bf16[2,128,512]{2,1,0:T(8,128)(2,1)S(1)}, u32[]{:S(2)}, u32[]{:S(2)}) collective-permute-start(bf16[2,128,512]{2,1,0:T(8,128)(2,1)} %get-tuple-element.40), channel_id=1, source_target_pairs={{0,5},{1,4},{2,7},{3,6},{4,1},{5,0},{6,3},{7,2},{8,13},{9,12},{10,... | collective-permute-start | bytes 786440 | tf_op jit(solution)/shard_map/ppermute | solution.py:65
  7.6 15.1 %collective-permute-start.7 = (bf16[2,128,512]{2,1,0:T(8,128)(2,1)}, bf16[2,128,512]{2,1,0:T(8,128)(2,1)S(1)}, u32[]{:S(2)}, u32[]{:S(2)}) collective-permute-start(bf16[2,128,512]{2,1,0:T(8,128)(2,1)} %get-tuple-element.35.refs_2_.refs_0_), channel_id=1, source_target_pairs={{0,8},{1,9},{2,10},{3,11},{4,12},{5,13},{6,14},{7,15},{8,16},{9,17... | collective-permute-start | bytes 786440 | tf_op jit(solution)/shard_map/ppermute | solution.py:71
  12.5 19.4 %collective-permute-start = (bf16[2,128,1024]{2,1,0:T(8,128)(2,1)}, bf16[2,128,1024]{2,1,0:T(8,128)(2,1)S(1)}, u32[]{:S(2)}, u32[]{:S(2)}) collective-permute-start(bf16[2,128,1024]{2,1,0:T(8,128)(2,1)} %get-tuple-element.37), channel_id=1, source_target_pairs={{0,5},{1,4},{2,7},{3,6},{4,1},{5,0},{6,3},{7,2},{8,13},{9,12},{10,... | collective-permute-start | bytes 1572872 | tf_op jit(solution)/shard_map/ppermute | solution.py:65
  15.0 2.0 %copy-start = (bf16[2,128,512]{2,1,0:T(8,128)(2,1)}, bf16[2,128,512]{2,1,0:T(8,128)(2,1)S(1)}, u32[]{:S(2)}) copy-start(bf16[2,128,512]{2,1,0:T(8,128)(2,1)S(1)} %collective-permute-done.4.refs_2_) | copy-start | bytes 786436
  15.0 27.0 %collective-permute-start.1 = (bf16[2,128,1024]{2,1,0:T(8,128)(2,1)}, bf16[2,128,1024]{2,1,0:T(8,128)(2,1)}, u32[]{:S(2)}, u32[]{:S(2)}) collective-permute-start(bf16[2,128,1024]{2,1,0:T(8,128)(2,1)} %get-tuple-element.38), channel_id=1, source_target_pairs={{0,1},{1,0},{2,3},{3,2},{4,5},{5,4},{6,7},{7,6},{8,9},{9,8},{10,11... | collective-permute-start | bytes 1572872 | tf_op jit(solution)/shard_map/ppermute | solution.py:65
  15.5 1.5 %copy-start.2 = (bf16[2,128,512]{2,1,0:T(8,128)(2,1)}, bf16[2,128,512]{2,1,0:T(8,128)(2,1)S(1)}, u32[]{:S(2)}) copy-start(bf16[2,128,512]{2,1,0:T(8,128)(2,1)S(1)} %collective-permute-done.5.refs_3_) | copy-start | bytes 786436
  15.5 26.7 %collective-permute-start.2 = (bf16[2,128,1024]{2,1,0:T(8,128)(2,1)}, bf16[2,128,1024]{2,1,0:T(8,128)(2,1)}, u32[]{:S(2)}, u32[]{:S(2)}) collective-permute-start(bf16[2,128,1024]{2,1,0:T(8,128)(2,1)} %get-tuple-element.39), channel_id=1, source_target_pairs={{0,4},{1,5},{2,6},{3,7},{4,0},{5,1},{6,2},{7,3},{8,12},{9,13},{10,... | collective-permute-start | bytes 1572872 | tf_op jit(solution)/shard_map/ppermute | solution.py:65
  20.7 3.6 %copy-start.8 = (bf16[2,128,512]{2,1,0:T(8,128)(2,1)}, bf16[2,128,512]{2,1,0:T(8,128)(2,1)S(1)}, u32[]{:S(2)}) copy-start(bf16[2,128,512]{2,1,0:T(8,128)(2,1)S(1)} %collective-permute-done.3.refs_1_) | copy-start | bytes 786436
  20.7 3.6 %copy-start.1 = (bf16[2,128,512]{2,1,0:T(8,128)(2,1)S(1)}, bf16[2,128,512]{2,1,0:T(8,128)(2,1)}, u32[]{:S(2)}) copy-start(bf16[2,128,512]{2,1,0:T(8,128)(2,1)} %copy-done) | copy-start | bytes 786436
  20.7 3.6 %copy-start.3 = (bf16[2,128,512]{2,1,0:T(8,128)(2,1)S(1)}, bf16[2,128,512]{2,1,0:T(8,128)(2,1)}, u32[]{:S(2)}) copy-start(bf16[2,128,512]{2,1,0:T(8,128)(2,1)} %copy-done.2) | copy-start | bytes 786436
  20.7 21.6 %collective-permute-start.9 = (bf16[2,2,128,512]{3,2,1,0:T(8,128)(2,1)S(1)}, bf16[2,2,128,512]{3,2,1,0:T(8,128)(2,1)}, u32[]{:S(2)}, u32[]{:S(2)}) collective-permute-start(bf16[2,2,128,512]{3,2,1,0:T(8,128)(2,1)S(1)} %pad_maximum_fusion.2), channel_id=1, source_target_pairs={{0,8},{1,9},{2,10},{3,11},{4,12},{5,13},{6,14},{7,15},{8,16},{9,17... | collective-permute-start | bytes 1572872 | tf_op jit(solution)/shard_map/ppermute | solution.py:71
  22.7 1.6 %copy-start.9 = (bf16[2,128,512]{2,1,0:T(8,128)(2,1)}, bf16[2,128,512]{2,1,0:T(8,128)(2,1)S(1)}, u32[]{:S(2)}) copy-start(bf16[2,128,512]{2,1,0:T(8,128)(2,1)S(1)} %collective-permute-done.7.refs_0_) | copy-start | bytes 786436
  22.7 19.5 %collective-permute-start.8 = (bf16[2,128,512]{2,1,0:T(8,128)(2,1)S(1)}, bf16[2,128,512]{2,1,0:T(8,128)(2,1)S(1)}, u32[]{:S(2)}, u32[]{:S(2)}) collective-permute-start(bf16[2,128,512]{2,1,0:T(8,128)(2,1)S(1)} %collective-permute-done.3.refs_1_), channel_id=1, source_target_pairs={{0,8},{1,9},{2,10},{3,11},{4,12},{5,13},{6,14},{7,15},{8,16},{9,17... | collective-permute-start | bytes 786440 | tf_op jit(solution)/shard_map/ppermute | solution.py:71
  25.5 16.8 %copy-start.6 = (bf16[4,2,128,512]{3,2,1,0:T(8,128)(2,1)}, bf16[4,2,128,512]{3,2,1,0:T(8,128)(2,1)S(1)}, u32[]{:S(2)}) copy-start(bf16[4,2,128,512]{3,2,1,0:T(8,128)(2,1)S(1)} %pad_maximum_fusion.refs_4_) | copy-start | bytes 3145732
  31.9 10.4 %copy-start.10 = (bf16[2,128,1024]{2,1,0:T(8,128)(2,1)}, bf16[2,128,1024]{2,1,0:T(8,128)(2,1)S(1)}, u32[]{:S(2)}) copy-start(bf16[2,128,1024]{2,1,0:T(8,128)(2,1)S(1)} %collective-permute-done.refs_2_.refs_1_) | copy-start | bytes 1572868
  31.9 11.7 %collective-permute-start.6 = (bf16[4,2,128,512]{3,2,1,0:T(8,128)(2,1)S(1)}, bf16[4,2,128,512]{3,2,1,0:T(8,128)(2,1)}, u32[]{:S(2)}, u32[]{:S(2)}) collective-permute-start(bf16[4,2,128,512]{3,2,1,0:T(8,128)(2,1)S(1)} %pad_maximum_fusion.refs_4_), channel_id=1, source_target_pairs={{0,2},{1,3},{2,0},{3,1},{4,6},{5,7},{6,4},{7,5},{8,10},{9,11},{10,... | collective-permute-start | bytes 3145736 | tf_op jit(solution)/shard_map/ppermute | solution.py:68
  43.5 2.7 %copy-start.7 = (bf16[4,2,128,512]{3,2,1,0:T(8,128)(2,1)}, bf16[4,2,128,512]{3,2,1,0:T(8,128)(2,1)S(1)}, u32[]{:S(2)}) copy-start(bf16[4,2,128,512]{3,2,1,0:T(8,128)(2,1)S(1)} %pad_maximum_fusion.1.refs_6_) | copy-start | bytes 3145732
  43.5 2.7 %collective-permute-start.10 = (bf16[4,2,128,512]{3,2,1,0:T(8,128)(2,1)S(1)}, bf16[4,2,128,512]{3,2,1,0:T(8,128)(2,1)S(1)}, u32[]{:S(2)}, u32[]{:S(2)}) collective-permute-start(bf16[4,2,128,512]{3,2,1,0:T(8,128)(2,1)S(1)} %pad_maximum_fusion.1.refs_6_), channel_id=1, source_target_pairs={{0,2},{1,3},{2,0},{3,1},{4,6},{5,7},{6,4},{7,5},{8,10},{9,11},{10,... | collective-permute-start | bytes 3145736 | tf_op jit(solution)/shard_map/ppermute | solution.py:68
  46.2 1.0 copy-start.21
  61.8 1.6 %collective-permute-start.11 = (bf16[2,128,256]{2,1,0:T(8,128)(2,1)}, bf16[2,128,256]{2,1,0:T(8,128)(2,1)S(1)}, u32[]{:S(2)}, u32[]{:S(2)}) collective-permute-start(bf16[2,128,256]{2,1,0:T(8,128)(2,1)} %get-tuple-element.48), channel_id=1, source_target_pairs={{0,2},{1,3},{2,0},{3,1},{4,6},{5,7},{6,4},{7,5},{8,10},{9,11},{10,... | collective-permute-start | bytes 393224 | tf_op jit(solution)/shard_map/ppermute | solution.py:68
  62.0 1.7 %collective-permute-start.12 = (bf16[2,128,256]{2,1,0:T(8,128)(2,1)}, bf16[2,128,256]{2,1,0:T(8,128)(2,1)S(1)}, u32[]{:S(2)}, u32[]{:S(2)}) collective-permute-start(bf16[2,128,256]{2,1,0:T(8,128)(2,1)} %get-tuple-element.49), channel_id=1, source_target_pairs={{0,2},{1,3},{2,0},{3,1},{4,6},{5,7},{6,4},{7,5},{8,10},{9,11},{10,... | collective-permute-start | bytes 393224 | tf_op jit(solution)/shard_map/ppermute | solution.py:68
  62.3 1.6 %collective-permute-start.13 = (bf16[2,128,256]{2,1,0:T(8,128)(2,1)}, bf16[2,128,256]{2,1,0:T(8,128)(2,1)S(1)}, u32[]{:S(2)}, u32[]{:S(2)}) collective-permute-start(bf16[2,128,256]{2,1,0:T(8,128)(2,1)} %get-tuple-element.50), channel_id=1, source_target_pairs={{0,2},{1,3},{2,0},{3,1},{4,6},{5,7},{6,4},{7,5},{8,10},{9,11},{10,... | collective-permute-start | bytes 393224 | tf_op jit(solution)/shard_map/ppermute | solution.py:68
  62.6 1.6 %collective-permute-start.14 = (bf16[2,128,256]{2,1,0:T(8,128)(2,1)}, bf16[2,128,256]{2,1,0:T(8,128)(2,1)S(1)}, u32[]{:S(2)}, u32[]{:S(2)}) collective-permute-start(bf16[2,128,256]{2,1,0:T(8,128)(2,1)} %get-tuple-element.51), channel_id=1, source_target_pairs={{0,2},{1,3},{2,0},{3,1},{4,6},{5,7},{6,4},{7,5},{8,10},{9,11},{10,... | collective-permute-start | bytes 393224 | tf_op jit(solution)/shard_map/ppermute | solution.py:68
  65.3 20.0 %collective-permute-start.19 = (bf16[4,2,128,256]{3,2,1,0:T(8,128)(2,1)S(1)}, bf16[4,2,128,256]{3,2,1,0:T(8,128)(2,1)S(1)}, u32[]{:S(2)}, u32[]{:S(2)}) collective-permute-start(bf16[4,2,128,256]{3,2,1,0:T(8,128)(2,1)S(1)} %add_convert_fusion.1), channel_id=1, source_target_pairs={{0,24},{1,25},{2,26},{3,27},{4,28},{5,29},{6,30},{7,31},{8,0},{9,1... | collective-permute-start | bytes 1572872 | tf_op jit(solution)/shard_map/ppermute | solution.py:71
  84.3 1.9 %collective-permute-start.24 = (bf16[2,128,256]{2,1,0:T(8,128)(2,1)}, bf16[2,128,256]{2,1,0:T(8,128)(2,1)S(1)}, u32[]{:S(2)}, u32[]{:S(2)}) collective-permute-start(bf16[2,128,256]{2,1,0:T(8,128)(2,1)} %get-tuple-element.61), channel_id=1, source_target_pairs={{0,2},{1,3},{2,0},{3,1},{4,6},{5,7},{6,4},{7,5},{8,10},{9,11},{10,... | collective-permute-start | bytes 393224 | tf_op jit(solution)/shard_map/ppermute | solution.py:68
  84.3 1.9 %collective-permute-start.25 = (bf16[2,128,256]{2,1,0:T(8,128)(2,1)}, bf16[2,128,256]{2,1,0:T(8,128)(2,1)S(1)}, u32[]{:S(2)}, u32[]{:S(2)}) collective-permute-start(bf16[2,128,256]{2,1,0:T(8,128)(2,1)} %get-tuple-element.62), channel_id=1, source_target_pairs={{0,2},{1,3},{2,0},{3,1},{4,6},{5,7},{6,4},{7,5},{8,10},{9,11},{10,... | collective-permute-start | bytes 393224 | tf_op jit(solution)/shard_map/ppermute | solution.py:68
  84.8 1.6 %collective-permute-start.26 = (bf16[2,128,256]{2,1,0:T(8,128)(2,1)}, bf16[2,128,256]{2,1,0:T(8,128)(2,1)S(1)}, u32[]{:S(2)}, u32[]{:S(2)}) collective-permute-start(bf16[2,128,256]{2,1,0:T(8,128)(2,1)} %get-tuple-element.63), channel_id=1, source_target_pairs={{0,2},{1,3},{2,0},{3,1},{4,6},{5,7},{6,4},{7,5},{8,10},{9,11},{10,... | collective-permute-start | bytes 393224 | tf_op jit(solution)/shard_map/ppermute | solution.py:68
  84.9 1.7 %collective-permute-start.27 = (bf16[2,128,256]{2,1,0:T(8,128)(2,1)}, bf16[2,128,256]{2,1,0:T(8,128)(2,1)S(1)}, u32[]{:S(2)}, u32[]{:S(2)}) collective-permute-start(bf16[2,128,256]{2,1,0:T(8,128)(2,1)} %get-tuple-element.64), channel_id=1, source_target_pairs={{0,2},{1,3},{2,0},{3,1},{4,6},{5,7},{6,4},{7,5},{8,10},{9,11},{10,... | collective-permute-start | bytes 393224 | tf_op jit(solution)/shard_map/ppermute | solution.py:68
  85.3 0.8 copy-start.4
  85.4 5.4 %collective-permute-start.18 = (bf16[4,2,128,256]{3,2,1,0:T(8,128)(2,1)}, bf16[4,2,128,256]{3,2,1,0:T(8,128)(2,1)S(1)}, u32[]{:S(2)}, u32[]{:S(2)}) collective-permute-start(bf16[4,2,128,256]{3,2,1,0:T(8,128)(2,1)} %get-tuple-element.57), channel_id=1, source_target_pairs={{0,2},{1,3},{2,0},{3,1},{4,6},{5,7},{6,4},{7,5},{8,10},{9,11},{10,... | collective-permute-start | bytes 1572872 | tf_op jit(solution)/shard_map/ppermute | solution.py:68
  86.1 7.7 %collective-permute-start.23 = (bf16[4,2,128,256]{3,2,1,0:T(8,128)(2,1)}, bf16[4,2,128,256]{3,2,1,0:T(8,128)(2,1)S(1)}, u32[]{:S(2)}, u32[]{:S(2)}) collective-permute-start(bf16[4,2,128,256]{3,2,1,0:T(8,128)(2,1)} %get-tuple-element.59), channel_id=1, source_target_pairs={{0,2},{1,3},{2,0},{3,1},{4,6},{5,7},{6,4},{7,5},{8,10},{9,11},{10,... | collective-permute-start | bytes 1572872 | tf_op jit(solution)/shard_map/ppermute | solution.py:68
  87.8 14.2 %collective-permute-start.28 = (bf16[4,2,128,256]{3,2,1,0:T(8,128)(2,1)S(1)}, bf16[4,2,128,256]{3,2,1,0:T(8,128)(2,1)S(1)}, u32[]{:S(2)}, u32[]{:S(2)}) collective-permute-start(bf16[4,2,128,256]{3,2,1,0:T(8,128)(2,1)S(1)} %add_convert_fusion), channel_id=1, source_target_pairs={{0,24},{1,25},{2,26},{3,27},{4,28},{5,29},{6,30},{7,31},{8,0},{9,1... | collective-permute-start | bytes 1572872 | tf_op jit(solution)/shard_map/ppermute | solution.py:71
  88.2 15.6 %collective-permute-start.15 = (bf16[2,128,512]{2,1,0:T(8,128)(2,1)}, bf16[2,128,512]{2,1,0:T(8,128)(2,1)S(1)}, u32[]{:S(2)}, u32[]{:S(2)}) collective-permute-start(bf16[2,128,512]{2,1,0:T(8,128)(2,1)} %get-tuple-element.52), channel_id=1, source_target_pairs={{0,4},{1,5},{2,6},{3,7},{4,0},{5,1},{6,2},{7,3},{8,12},{9,13},{10,... | collective-permute-start | bytes 786440 | tf_op jit(solution)/shard_map/ppermute | solution.py:65
  89.8 16.9 %collective-permute-start.16 = (bf16[2,128,512]{2,1,0:T(8,128)(2,1)}, bf16[2,128,512]{2,1,0:T(8,128)(2,1)S(1)}, u32[]{:S(2)}, u32[]{:S(2)}) collective-permute-start(bf16[2,128,512]{2,1,0:T(8,128)(2,1)} %get-tuple-element.53), channel_id=1, source_target_pairs={{0,1},{1,0},{2,3},{3,2},{4,5},{5,4},{6,7},{7,6},{8,9},{9,8},{10,11... | collective-permute-start | bytes 786440 | tf_op jit(solution)/shard_map/ppermute | solution.py:65
  90.7 1.1 copy-start.5
  90.7 12.2 %copy-start.11 = (bf16[4,2,128,256]{3,2,1,0:T(8,128)(2,1)S(1)}, bf16[4,2,128,256]{3,2,1,0:T(8,128)(2,1)}, u32[]{:S(2)}) copy-start(bf16[4,2,128,256]{3,2,1,0:T(8,128)(2,1)} %get-tuple-element.58) | copy-start | bytes 1572868
  90.7 16.9 %collective-permute-start.17 = (bf16[2,128,512]{2,1,0:T(8,128)(2,1)}, bf16[2,128,512]{2,1,0:T(8,128)(2,1)S(1)}, u32[]{:S(2)}, u32[]{:S(2)}) collective-permute-start(bf16[2,128,512]{2,1,0:T(8,128)(2,1)} %get-tuple-element.54), channel_id=1, source_target_pairs={{0,5},{1,4},{2,7},{3,6},{4,1},{5,0},{6,3},{7,2},{8,13},{9,12},{10,... | collective-permute-start | bytes 786440 | tf_op jit(solution)/shard_map/ppermute | solution.py:65
  93.8 14.2 %collective-permute-start.22 = (bf16[2,128,256]{2,1,0:T(8,128)(2,1)S(1)}, bf16[2,128,256]{2,1,0:T(8,128)(2,1)S(1)}, u32[]{:S(2)}, u32[]{:S(2)}) collective-permute-start(bf16[2,128,256]{2,1,0:T(8,128)(2,1)S(1)} %get-tuple-element.72), channel_id=1, source_target_pairs={{0,5},{1,4},{2,7},{3,6},{4,1},{5,0},{6,3},{7,2},{8,13},{9,12},{10,... | collective-permute-start | bytes 393224 | tf_op jit(solution)/shard_map/ppermute | solution.py:65
  102.0 10.6 %collective-permute-start.21 = (bf16[2,128,256]{2,1,0:T(8,128)(2,1)}, bf16[2,128,256]{2,1,0:T(8,128)(2,1)S(1)}, u32[]{:S(2)}, u32[]{:S(2)}) collective-permute-start(bf16[2,128,256]{2,1,0:T(8,128)(2,1)} %get-tuple-element.73), channel_id=1, source_target_pairs={{0,1},{1,0},{2,3},{3,2},{4,5},{5,4},{6,7},{7,6},{8,9},{9,8},{10,11... | collective-permute-start | bytes 393224 | tf_op jit(solution)/shard_map/ppermute | solution.py:65
  103.8 6.3 %copy-start.12 = (bf16[2,128,512]{2,1,0:T(8,128)(2,1)}, bf16[2,128,512]{2,1,0:T(8,128)(2,1)S(1)}, u32[]{:S(2)}) copy-start(bf16[2,128,512]{2,1,0:T(8,128)(2,1)S(1)} %collective-permute-done.15.refs_0_) | copy-start | bytes 786436
  103.8 8.7 %collective-permute-start.20 = (bf16[2,128,256]{2,1,0:T(8,128)(2,1)S(1)}, bf16[2,128,256]{2,1,0:T(8,128)(2,1)S(1)}, u32[]{:S(2)}, u32[]{:S(2)}) collective-permute-start(bf16[2,128,256]{2,1,0:T(8,128)(2,1)S(1)} %get-tuple-element.74), channel_id=1, source_target_pairs={{0,4},{1,5},{2,6},{3,7},{4,0},{5,1},{6,2},{7,3},{8,12},{9,13},{10,... | collective-permute-start | bytes 393224 | tf_op jit(solution)/shard_map/ppermute | solution.py:65
  106.7 3.5 %copy-start.13 = (bf16[2,128,512]{2,1,0:T(8,128)(2,1)}, bf16[2,128,512]{2,1,0:T(8,128)(2,1)S(1)}, u32[]{:S(2)}) copy-start(bf16[2,128,512]{2,1,0:T(8,128)(2,1)S(1)} %collective-permute-done.16.refs_1_) | copy-start | bytes 786436
  106.7 6.8 %collective-permute-start.31 = (bf16[2,128,256]{2,1,0:T(8,128)(2,1)S(1)}, bf16[2,128,256]{2,1,0:T(8,128)(2,1)S(1)}, u32[]{:S(2)}, u32[]{:S(2)}) collective-permute-start(bf16[2,128,256]{2,1,0:T(8,128)(2,1)S(1)} %get-tuple-element.68), channel_id=1, source_target_pairs={{0,5},{1,4},{2,7},{3,6},{4,1},{5,0},{6,3},{7,2},{8,13},{9,12},{10,... | collective-permute-start | bytes 393224 | tf_op jit(solution)/shard_map/ppermute | solution.py:65
  107.7 2.5 %copy-start.14 = (bf16[2,128,512]{2,1,0:T(8,128)(2,1)}, bf16[2,128,512]{2,1,0:T(8,128)(2,1)S(1)}, u32[]{:S(2)}) copy-start(bf16[2,128,512]{2,1,0:T(8,128)(2,1)S(1)} %collective-permute-done.17.refs_2_) | copy-start | bytes 786436
  107.7 7.1 %collective-permute-start.30 = (bf16[2,128,256]{2,1,0:T(8,128)(2,1)S(1)}, bf16[2,128,256]{2,1,0:T(8,128)(2,1)S(1)}, u32[]{:S(2)}, u32[]{:S(2)}) collective-permute-start(bf16[2,128,256]{2,1,0:T(8,128)(2,1)S(1)} %get-tuple-element.69), channel_id=1, source_target_pairs={{0,1},{1,0},{2,3},{3,2},{4,5},{5,4},{6,7},{7,6},{8,9},{9,8},{10,11... | collective-permute-start | bytes 393224 | tf_op jit(solution)/shard_map/ppermute | solution.py:65
  108.0 4.5 %copy-start.15 = (bf16[2,128,256]{2,1,0:T(8,128)(2,1)}, bf16[2,128,256]{2,1,0:T(8,128)(2,1)S(1)}, u32[]{:S(2)}) copy-start(bf16[2,128,256]{2,1,0:T(8,128)(2,1)S(1)} %collective-permute-done.22.refs_2_) | copy-start | bytes 393220
  108.0 6.8 %collective-permute-start.29 = (bf16[2,128,256]{2,1,0:T(8,128)(2,1)S(1)}, bf16[2,128,256]{2,1,0:T(8,128)(2,1)S(1)}, u32[]{:S(2)}, u32[]{:S(2)}) collective-permute-start(bf16[2,128,256]{2,1,0:T(8,128)(2,1)S(1)} %get-tuple-element.70), channel_id=1, source_target_pairs={{0,4},{1,5},{2,6},{3,7},{4,0},{5,1},{6,2},{7,3},{8,12},{9,13},{10,... | collective-permute-start | bytes 393224 | tf_op jit(solution)/shard_map/ppermute | solution.py:65
  112.5 2.3 %copy-start.16 = (bf16[2,128,256]{2,1,0:T(8,128)(2,1)}, bf16[2,128,256]{2,1,0:T(8,128)(2,1)S(1)}, u32[]{:S(2)}) copy-start(bf16[2,128,256]{2,1,0:T(8,128)(2,1)S(1)} %collective-permute-done.21.refs_1_) | copy-start | bytes 393220
  112.6 2.3 %copy-start.17 = (bf16[2,128,256]{2,1,0:T(8,128)(2,1)}, bf16[2,128,256]{2,1,0:T(8,128)(2,1)S(1)}, u32[]{:S(2)}) copy-start(bf16[2,128,256]{2,1,0:T(8,128)(2,1)S(1)} %collective-permute-done.20.refs_0_) | copy-start | bytes 393220
  113.5 1.3 %copy-start.18 = (bf16[2,128,256]{2,1,0:T(8,128)(2,1)}, bf16[2,128,256]{2,1,0:T(8,128)(2,1)S(1)}, u32[]{:S(2)}) copy-start(bf16[2,128,256]{2,1,0:T(8,128)(2,1)S(1)} %collective-permute-done.31.refs_6_) | copy-start | bytes 393220
  114.8 0.6 copy-start.19
  114.8 0.7 copy-start.20
